TPU v7x, 32 devices: a whole 2x2x4 slice. The times are simulated.
32 devices in a mesh: section: 4 (over y, x), dp: 8 (over z, core).
Axes of the slice: x: 2, y: 2, z: 4, core: 2. Of those that a mesh axis runs over, the one named last changes fastest.
Arguments:
- query_gradient_stack: float32 [4, 4096, 2048], P('section', 'dp'), may hold values from -6 to 6
- train_grads: float32 [4, 4096, 2048], P('section', 'dp'), may hold values from -6 to 6
- factor_slots: float32 [4, 8, 2048, 512], P('section', 'dp'), as said below
- owner: int32 [4, 4], P('section'), may hold values from 0 to 7, as said below
- train_count: int32 [8], P('dp'), may hold values from 128 to 512, as said below
Outputs:
- scores: float32 [8, 512, 1536], P('dp', 'section')
Inputs may be any that keep to these rules, and one draw needn't show every extreme that they name: `owner`: for each layer the 4 entries are distinct data indices. `train_count`: some data index has all 512 training examples live. `factor_slots`: the diagonal entries of each factor lie between 0.9 and 2.1.
All inputs are finite; a program needn't handle non-finite values.
Results may differ from a plain program's by a relative error of at most 0.00019.
Values sent between devices are 32-bit elements; how exact they have to be, the bound alone decides.
No kernel may reach another device: no remote copies, remote signals or barrier semaphores. Data moves between devices by JAX's collectives and lax.ppermute only.
A program may use at most 128 MiB of HBM per device.

v0:
```python
import jax
import jax.numpy as jnp
from jax import lax
from jax.sharding import PartitionSpec as P

COORDS = 2048
PANEL = 512


def spread(block, axis, source):
    block = jnp.where(lax.axis_index(axis) == source, block, jnp.zeros_like(block))
    return lax.psum(block, axis)


def shifted_2(value, axis, steps):
    count = lax.axis_size(axis)
    pairs = [(source, (source + steps) % count) for source in range(count)]
    return lax.ppermute(value, axis, pairs)


def solve_rows(row_block, slot, owner_list):
    panel_count = row_block.shape[1] // PANEL
    pending = row_block
    solved_parts = []
    for panel_number in range(panel_count):
        panel_cols = spread(slot[panel_number * PANEL :, :], "dp", owner_list[panel_number])
        diag_block = jnp.tril(panel_cols[:PANEL, :])
        solved = lax.linalg.triangular_solve(
            diag_block, pending[:, :PANEL], left_side=False, lower=True, transpose_a=True
        )
        solved_parts.append(solved)
        if panel_number + 1 < panel_count:
            update = lax.dot_general(
                solved,
                panel_cols[PANEL:, :],
                (((1,), (1,)), ((), ())),
                precision=lax.Precision.HIGHEST,
                preferred_element_type=jnp.float32,
            )
            pending = pending[:, PANEL:] - update
    return jnp.concatenate(solved_parts, axis=1)


def neighbour_blocks(blocks, counts):
    gathered = []
    current = (blocks, counts)
    for step_index in range(2):
        current = shifted_2((current[0], current[1]), "dp", 1)
        gathered.append(current)
    return gathered


def body(query_gradient_stack, train_grads, factor_slots, owner, train_count):
    layer_count = query_gradient_stack.shape[0]
    row_count = query_gradient_stack.shape[1]
    score_scale = (COORDS * layer_count * lax.axis_size("section")) ** (-0.5)
    layer_index = 0
    stacked = jnp.concatenate([query_gradient_stack[layer_index], train_grads[layer_index]], axis=0)
    solved = solve_rows(stacked, factor_slots[layer_index, 0], owner[layer_index])
    query_solved = [solved[:row_count]]
    own_solved = [solved[row_count:]]
    own_stack = jnp.stack(own_solved, axis=0)
    shifted = neighbour_blocks(own_stack, train_count)
    count_list = [train_count, shifted[0][1], shifted[1][1]]
    layer_index = 0
    column_solved = [
        jnp.concatenate(
            [own_stack[layer_index], shifted[0][0][layer_index], shifted[1][0][layer_index]], axis=0
        )
    ]
    positions = jnp.arange(row_count, dtype=jnp.int32)
    valid_cols = jnp.concatenate(
        [(positions < count_item[0]).astype(jnp.float32) for count_item in count_list], axis=0
    )
    col_factor = score_scale * valid_cols
    layer_index = 0
    query_part = query_solved[layer_index]
    running = lax.dot_general(
        query_part,
        column_solved[layer_index],
        (((1,), (1,)), ((), ())),
        precision=lax.Precision.HIGHEST,
        preferred_element_type=jnp.float32,
    )
    scores = lax.psum_scatter(
        running * col_factor[None, :], "section", scatter_dimension=0, tiled=True
    )
    return scores[None]


def solution(mesh):
    in_specs = (
        P("section", "dp", None),
        P("section", "dp", None),
        P("section", "dp", None, None),
        P("section", None),
        P("dp"),
    )
    out_specs = P("dp", "section", None)
    return jax.shard_map(body, mesh=mesh, in_specs=in_specs, out_specs=out_specs, check_vma=False)
```

profile of v0, /device:TPU:0, one launch (start us, length us, event | category | flops | bytes accessed | tf_op | source)
XLA Modules:
  0.0 725.8 jit_solution(13629908636700005185)
XLA Ops:
  6.5 1.5 fusion.140
  10.6 2.4 select_bitcast_fusion.3
  13.1 3.2 select_bitcast_fusion.2
  16.2 2.1 select_bitcast_fusion.1
  18.3 2.5 select_bitcast_fusion
  20.9 219.0 %all-reduce.3.cloned.1.call-done = (f32[2048,512]{1,0:T(8,128)}, f32[1536,512]{1,0:T(8,128)}, f32[1024,512]{1,0:T(8,128)}, f32[512,512]{1,0:T(8,128)}) async-done(((f32[2048,512]{1,0:T(8,128)}, f32[1536,512]{1,0:T(8,128)}, f32[1024,512]{1,0:T(8,128)}, f32[512,512]{1,0:T(8,128)}), (f32[2048,512]{1,0:T(8,128)}, f32[1536,512]{1,0:T(8,128)}, f32[1024,512]{1,0:T(8,128)}, ...) | async-done | bytes 10485776 | tf_op jit(solution)/shard_map/psum | solution.py:12
  239.8 3.4 select_select_fusion
  243.3 11.6 %while.11 = (s32[]{:T(128)}, f32[512,512]{1,0:T(8,128)}, s32[4,2]{0,1:T(2,128)S(1)}, f32[4,128,128]{2,1,0:T(8,128)S(1)}, s32[]{:T(128)}) while((s32[]{:T(128)}, f32[512,512]{1,0:T(8,128)}, s32[4,2]{0,1:T(2,128)S(1)}, f32[4,128,128]{2,1,0:T(8,128)S(1)}, s32[]{:T(128)}) %tuple.78), condition=%wide.while_cond.clone.2, body=%wide.while_body.clone.2.sunk | while | flops 2 | bytes 131189 | solution.py:28
  243.9 2.2 bitcast_dynamic-update-slice_fusion.11
  246.8 2.2 bitcast_dynamic-update-slice_fusion.11
  249.7 2.2 bitcast_dynamic-update-slice_fusion.11
  252.7 2.2 bitcast_dynamic-update-slice_fusion.11
  254.8 39.9 %custom-call.9 = f32[4,128,128]{1,2,0:T(8,128)} custom-call(f32[4,128,128]{2,1,0:T(8,128)S(1)} %get-tuple-element.35), custom_call_target="InvertDiagBlocksLowerTriangular" | custom-call | tf_op jit(solution)/shard_map/triangular_solve/custom-call.1 | solution.py:28
  294.8 11.6 %while.10 = (s32[]{:T(128)}, f32[512,512]{1,0:T(8,128)}, s32[4,2]{0,1:T(2,128)S(1)}, f32[4,128,128]{2,1,0:T(8,128)S(1)}, s32[]{:T(128)}) while((s32[]{:T(128)}, f32[512,512]{1,0:T(8,128)}, s32[4,2]{0,1:T(2,128)S(1)}, f32[4,128,128]{2,1,0:T(8,128)S(1)}, s32[]{:T(128)}) %tuple.86), condition=%wide.while_cond.clone.1, body=%wide.while_body.clone.1.sunk | while | flops 2 | bytes 131189 | solution.py:28
  295.5 2.2 bitcast_dynamic-update-slice_fusion.10
  298.4 2.2 bitcast_dynamic-update-slice_fusion.10
  301.3 2.2 bitcast_dynamic-update-slice_fusion.10
  304.2 2.2 bitcast_dynamic-update-slice_fusion.10
  306.4 39.9 %custom-call.8 = f32[4,128,128]{1,2,0:T(8,128)} custom-call(f32[4,128,128]{2,1,0:T(8,128)S(1)} %get-tuple-element.34), custom_call_target="InvertDiagBlocksLowerTriangular" | custom-call | tf_op jit(solution)/shard_map/triangular_solve/custom-call.1 | solution.py:28
  346.3 2.8 select_select_fusion.2
  349.2 11.5 %while.9 = (s32[]{:T(128)}, f32[512,512]{1,0:T(8,128)}, s32[4,2]{0,1:T(2,128)S(1)}, f32[4,128,128]{2,1,0:T(8,128)S(1)}, s32[]{:T(128)}) while((s32[]{:T(128)}, f32[512,512]{1,0:T(8,128)}, s32[4,2]{0,1:T(2,128)S(1)}, f32[4,128,128]{2,1,0:T(8,128)S(1)}, s32[]{:T(128)}) %tuple.87), condition=%wide.while_cond.clone, body=%wide.while_body.clone.sunk | while | flops 2 | bytes 131189 | solution.py:28
  349.8 2.2 bitcast_dynamic-update-slice_fusion.9
  352.7 2.2 bitcast_dynamic-update-slice_fusion.9
  355.6 2.2 bitcast_dynamic-update-slice_fusion.9
  358.5 2.2 bitcast_dynamic-update-slice_fusion.9
  360.7 39.9 %custom-call.7 = f32[4,128,128]{1,2,0:T(8,128)} custom-call(f32[4,128,128]{2,1,0:T(8,128)S(1)} %get-tuple-element.33), custom_call_target="InvertDiagBlocksLowerTriangular" | custom-call | tf_op jit(solution)/shard_map/triangular_solve/custom-call.1 | solution.py:28
  400.6 11.7 %while.8 = (s32[]{:T(128)}, f32[512,512]{1,0:T(8,128)}, s32[4,2]{0,1:T(2,128)S(1)}, f32[4,128,128]{2,1,0:T(8,128)S(1)}, s32[]{:T(128)}) while((s32[]{:T(128)}, f32[512,512]{1,0:T(8,128)}, s32[4,2]{0,1:T(2,128)S(1)}, f32[4,128,128]{2,1,0:T(8,128)S(1)}, s32[]{:T(128)}) %tuple.88), condition=%wide.while_cond, body=%wide.while_body.sunk | while | flops 2 | bytes 131189 | solution.py:28
  401.3 2.3 bitcast_dynamic-update-slice_fusion.8
  404.3 2.3 bitcast_dynamic-update-slice_fusion.8
  407.2 2.3 bitcast_dynamic-update-slice_fusion.8
  410.2 2.2 bitcast_dynamic-update-slice_fusion.8
  412.4 0.7 copy-done.10
  413.1 40.3 %custom-call.6 = f32[4,128,128]{1,2,0:T(8,128)S(1)} custom-call(f32[4,128,128]{2,1,0:T(8,128)} %copy-done.10), custom_call_target="InvertDiagBlocksLowerTriangular" | custom-call | tf_op jit(solution)/shard_map/triangular_solve/custom-call.1 | solution.py:28
  453.4 1.8 fusion.94
  455.8 1.3 copy-done.1
  457.0 1.8 convolution_subtract_fusion.7
  458.9 0.6 fusion.120
  459.5 2.7 convolution_subtract_fusion.3
  462.9 3.8 fusion.72
  466.7 0.6 fusion.118
  467.3 21.1 %fusion.6 = f32[1024,1536]{1,0:T(8,128)S(1)} fusion(f32[512,2048]{1,0:T(8,128)S(1)} %bitcast.135, f32[512,2048]{1,0:T(8,128)S(1)} %bitcast.140, f32[2048,512]{1,0:T(8,128)S(1)} %copy-done.4, f32[1024,128]{0,1:T(8,128)S(1)} %fusion.118, f32[1024,128]{0,1:T(8,128)S(1)} %fusion.119, f32[1024,128]{0,1:T(8,128)S(1)} %fusion.120, f32[1024,128]{0,1:T(8,128)S(1)} %bitcast.151), kind=kOutput, calls=%fused_computation.16 | convolution fusion | flops 9668395008 | bytes 19922944 | tf_op jit(solution)/shard_map/dot_general | solution.py:33
  488.5 0.6 fusion.92
  489.1 1.8 convolution_subtract_fusion.6
  491.6 2.7 convolution_subtract_fusion.2
  495.0 3.6 fusion.69
  499.3 14.6 %slice_subtract_fusion = f32[1024,1024]{1,0:T(8,128)S(1)} fusion(f32[1024,1536]{1,0:T(8,128)S(1)} %fusion.6, f32[1536,512]{1,0:T(8,128)S(1)} %copy-done.5, f32[1024,128]{0,1:T(8,128)S(1)} %fusion.114, f32[1024,128]{0,1:T(8,128)S(1)} %fusion.115, f32[1024,128]{0,1:T(8,128)S(1)} %fusion.116, f32[1024,128]{0,1:T(8,128)S(1)} %bitcast.147), kind=kOutput, calls=%fused_computation.18 | convolution fusion | flops 6445072384 | bytes 12582912 | tf_op jit(solution)/shard_map/dot_general | solution.py:33
  513.9 0.7 fusion.90
  514.6 1.8 convolution_subtract_fusion.5
  517.1 2.8 convolution_subtract_fusion.1
  520.4 3.7 fusion.66
  524.7 7.1 slice_subtract_fusion.1
  531.9 0.6 fusion.88
  532.5 1.8 convolution_subtract_fusion.4
  535.0 2.8 convolution_subtract_fusion
  538.4 3.8 fusion.63
  542.2 1.4 fusion.106
  543.7 3.3 maximum_maximum_fusion
  547.0 1.1 fusion.139
  548.2 49.7 %collective-permute-done = f32[1,512,2048]{1,2,0:T(8,128)S(1)} collective-permute-done((f32[1,512,2048]{1,2,0:T(8,128)S(1)}, f32[1,512,2048]{1,2,0:T(8,128)S(1)}, u32[]{:S(2)}, u32[]{:S(2)}) %collective-permute-start) | collective-permute-done | bytes 4194336 | tf_op jit(solution)/shard_map/ppermute | solution.py:18
  598.6 49.2 %collective-permute-done.2 = s32[1]{0:T(128)} collective-permute-done((s32[1]{0:T(128)}, s32[1]{0:T(128)}, u32[]{:S(2)}, u32[]{:S(2)}) %collective-permute-start.2) | collective-permute-done | bytes 36 | tf_op jit(solution)/shard_map/ppermute | solution.py:18
  648.0 0.6 iota_compare_fusion.2
  648.7 4.1 collective-permute-done.3
  653.4 22.8 %fusion.8 = f32[512,1536]{1,0:T(8,128)} fusion(f32[512,2048]{0,1:T(8,128)S(1)} %bitcast.157, f32[512,2048]{0,1:T(8,128)S(1)} %bitcast.156, f32[512,2048]{0,1:T(8,128)S(1)} %get-tuple-element.80, f32[1024,2048]{0,1:T(8,128)S(1)} %maximum_maximum_fusion, f32[1536]{0:T(1024)S(1)} %add_select_fusion), kind=kOutput, calls=%fused_computation.20 | convolution fusion | flops 19334430720 | bytes 19931136 | tf_op jit(solution)/shard_map/dot_general | solution.py:78
  676.3 42.2 %reduce-scatter.2.cloned.1.call-done = f32[128,1536]{1,0:T(8,128)} async-done(((f32[512,1536]{1,0:T(8,128)}), f32[128,1536]{1,0:T(8,128)}) %reduce-scatter.2.cloned.1.call-update) | async-done | bytes 786448 | tf_op jit(solution)/shard_map/reduce_scatter | solution.py:85
  (79 shorter events, 17.6 us)
Async XLA Ops:
  6.5 233.3 %all-reduce.3.cloned.1.call-start = ((), (), s32[]{:S(2)}) async-start(), calls=%async_computation.2 | async-start | bytes 20971520 | tf_op jit(solution)/shard_map/psum | solution.py:12
  10.6 5.6 copy-start.2
  20.8 697.7 %reduce-scatter.2.cloned.1.call-start = ((), (), s32[]{:S(2)}) async-start(), calls=%async_computation.1 | async-start | bytes 3932160 | tf_op jit(solution)/shard_map/reduce_scatter | solution.py:85
  239.8 106.5 %copy-start.5 = (f32[1536,512]{1,0:T(8,128)S(1)}, f32[1536,512]{1,0:T(8,128)}, u32[]{:S(2)}) copy-start(f32[1536,512]{1,0:T(8,128)} %get-tuple-element.69) | copy-start | bytes 9437188
  412.3 0.7 copy-start.10
  453.4 2.4 copy-start
  453.4 3.6 copy-start.1
  462.9 4.4 copy-start.4
  467.3 21.1 %copy-start.9 = (f32[4,128,128]{1,2,0:T(8,128)S(1)}, f32[4,128,128]{1,2,0:T(8,128)}, u32[]{:S(2)}) copy-start(f32[4,128,128]{1,2,0:T(8,128)} %custom-call.7) | copy-start | bytes 786436
  499.3 14.6 %copy-start.8 = (f32[4,128,128]{1,2,0:T(8,128)S(1)}, f32[4,128,128]{1,2,0:T(8,128)}, u32[]{:S(2)}) copy-start(f32[4,128,128]{1,2,0:T(8,128)} %custom-call.8) | copy-start | bytes 786436
  516.4 8.3 %copy-start.6 = (f32[1024,512]{1,0:T(8,128)S(1)}, f32[1024,512]{1,0:T(8,128)}, u32[]{:S(2)}) copy-start(f32[1024,512]{1,0:T(8,128)} %get-tuple-element.70) | copy-start | bytes 6291460
  524.1 7.8 %copy-start.7 = (f32[4,128,128]{1,2,0:T(8,128)S(1)}, f32[4,128,128]{1,2,0:T(8,128)}, u32[]{:S(2)}) copy-start(f32[4,128,128]{1,2,0:T(8,128)} %custom-call.9) | copy-start | bytes 786436
  538.4 3.9 copy-start.3
  548.1 49.8 %collective-permute-start = (f32[1,512,2048]{1,2,0:T(8,128)S(1)}, f32[1,512,2048]{1,2,0:T(8,128)S(1)}, u32[]{:S(2)}, u32[]{:S(2)}) collective-permute-start(f32[1,512,2048]{1,2,0:T(8,128)S(1)} %get-tuple-element.81), channel_id=1, source_target_pairs={{0,1},{1,2},{2,3},{3,4},{4,5},{5,6},{6,7},{7,0},{8,9},{9,10},{10,1... | collective-permute-start | bytes 12582920 | tf_op jit(solution)/shard_map/ppermute | solution.py:18
  597.9 55.5 %collective-permute-start.1 = (f32[1,512,2048]{1,2,0:T(8,128)S(1)}, f32[1,512,2048]{1,2,0:T(8,128)S(1)}, u32[]{:S(2)}, u32[]{:S(2)}) collective-permute-start(f32[1,512,2048]{1,2,0:T(8,128)S(1)} %collective-permute-done), channel_id=1, source_target_pairs={{0,1},{1,2},{2,3},{3,4},{4,5},{5,6},{6,7},{7,0},{8,9},{9,10},{10,1... | collective-permute-start | bytes 12582920 | tf_op jit(solution)/shard_map/ppermute | solution.py:18
  597.9 49.9 %collective-permute-start.2 = (s32[1]{0:T(128)}, s32[1]{0:T(128)}, u32[]{:S(2)}, u32[]{:S(2)}) collective-permute-start(s32[1]{0:T(128)} %param.11), channel_id=1, source_target_pairs={{0,1},{1,2},{2,3},{3,4},{4,5},{5,6},{6,7},{7,0},{8,9},{9,10},{10,1... | collective-permute-start | bytes 20 | tf_op jit(solution)/shard_map/ppermute | solution.py:18
  647.8 5.0 collective-permute-start.3
Sparse Core Ops, SparseCore 0:
  20.9 218.8 all-reduce.2
  676.4 42.0 reduce-scatter.1
where the time goes:
time: 735 us; the launch traced here: 726 us
  waiting for transfers between devices  364 us (50%)
  other arithmetic  181 us (25%)
  matrix products  111 us (15%)
  local copies, waits for them, and re-layouts  51.2 us (7%)
  between operations  17.6 us (2%)
    psum x1, waiting for transfers between devices, spread(): return lax.psum(block, axis)  219 us
    another operation x7, other arithmetic, solve_rows(): lax.linalg.triangular_solve(diag_block, pending[:, :PANEL], left_side=Fal...  166 us
    ppermute x4, waiting for transfers between devices, shifted_2(): return lax.ppermute(value, axis, pairs)  103 us
    another operation x52, local copies, waits for them, and re-layouts, solve_rows(): lax.linalg.triangular_solve(diag_block, pending[:, :PANEL], left_side=Fal...  46.1 us
    another operation x28, matrix products, solve_rows(): lax.linalg.triangular_solve(diag_block, pending[:, :PANEL], left_side=Fal...  45.3 us
    dot_general x3, matrix products, solve_rows(): lax.dot_general(solved, panel_cols[PANEL:, :], (((1,), (1,)), ((), ())),...  42.8 us
    reduce_scatter x1, waiting for transfers between devices, body(): lax.psum_scatter(running * col_factor[None, :], 'section', scatter_dimens...  42.2 us
    dot_general x1, matrix products, body(): lax.dot_general(query_part, column_solved[layer_index], (((1,), (1,)), ((...  22.8 us
  transfers between devices with their start and end apart: 6, of which 5 were waited for; matrix products, arithmetic and copies ran while one was open for 0% of the time, Pallas kernels for 0%

commit v1 on v0

v1 whole, which is shorter than its diff:
```python
import functools

import jax
import jax.numpy as jnp
from jax import lax
from jax.experimental import pallas as pl
from jax.experimental.pallas import tpu as pltpu
from jax.sharding import PartitionSpec as P

HIGHEST = lax.Precision.HIGHEST
CHUNKS = 8
SKEW = 2
GROUPS = ((0, 5), (5, 8))
TRAIN_CUTS = (128, 128, 128, 96, 32)
MIB = 1024 * 1024
ANY = pl.BlockSpec(memory_space=pl.ANY)
SMEM = pl.BlockSpec(memory_space=pltpu.SMEM)
VMEM = pl.BlockSpec(memory_space=pltpu.VMEM)


def dot(a, b, contract, precision=None):
    return lax.dot_general(
        a, b, (((1,), (contract,)), ((), ())), precision=precision, preferred_element_type=jnp.float32
    )


def parts_of(value):
    high = value.astype(jnp.bfloat16)
    return high, (value - high.astype(jnp.float32)).astype(jnp.bfloat16)


def dot_parts(a, b, contract):
    return dot(a[0], b[0], contract) + (dot(a[0], b[1], contract) + dot(a[1], b[0], contract))


def after(value, *others):
    return lax.optimization_barrier((value, *others))[0]


def partner(section, k, n_sec):
    if n_sec & (n_sec - 1) == 0:
        return section ^ k
    return lax.rem(section + k, n_sec)


def param(limit_mib):
    return pltpu.CompilerParams(vmem_limit_bytes=limit_mib * MIB)


def cost(flops, moved):
    return pl.CostEstimate(flops=flops, bytes_accessed=moved, transcendentals=0)


def invert_kernel(panel_ref, block_ref, packed_ref):
    size = block_ref.shape[0]
    count = 4
    tile = size // count
    row = lax.broadcasted_iota(jnp.int32, (tile, tile), 0)
    col = lax.broadcasted_iota(jnp.int32, (tile, tile), 1)
    spans = [slice(i * tile, (i + 1) * tile) for i in range(count)]
    low = [block_ref[s, s] for s in spans]
    inv = []
    for block in low:
        diagonal = jnp.sum(jnp.where(row == col, block, 0.0), axis=1, keepdims=True)
        inv.append(jnp.where(row == col, 1.0 / diagonal, 0.0))
    width = 1
    while width < tile:
        joins = (row // (2 * width) == col // (2 * width)) & (row // width > col // width)
        half = [dot(jnp.where(joins, low[i], 0.0), inv[i], 0, HIGHEST) for i in range(count)]
        inv = [inv[i] - dot(inv[i], half[i], 0, HIGHEST) for i in range(count)]
        width *= 2
    while len(inv) > 1:
        width = inv[0].shape[0]
        zero = jnp.zeros((width, width), jnp.float32)
        merged = []
        for i in range(0, len(inv), 2):
            below = block_ref[(i + 1) * width : (i + 2) * width, i * width : (i + 1) * width]
            corner = -dot(inv[i + 1], dot(below, inv[i], 0, HIGHEST), 0, HIGHEST)
            top = jnp.concatenate([inv[i], zero], axis=1)
            merged.append(jnp.concatenate([top, jnp.concatenate([corner, inv[i + 1]], axis=1)], axis=0))
        inv = merged
    whole = inv[0]
    mid = tile + tile // 2
    packed_ref[0:tile, :] = whole[3 * tile :, :]
    packed_ref[tile : 2 * tile, 0 : 3 * tile] = whole[2 * tile : 3 * tile, 0 : 3 * tile]
    packed_ref[tile : 2 * tile, 3 * tile :] = whole[0:tile, 0:tile]
    packed_ref[2 * tile :, 0 : 2 * tile] = whole[tile:mid, 0 : 2 * tile]
    packed_ref[2 * tile :, 2 * tile :] = whole[mid : 2 * tile, 0 : 2 * tile]


def inverted_diagonal(slot, panel):
    size = slot.shape[1]
    rows = size // 2 + size // 8
    return pl.pallas_call(
        invert_kernel,
        out_shape=jax.ShapeDtypeStruct((rows, size), jnp.float32),
        grid_spec=pltpu.PrefetchScalarGridSpec(
            num_scalar_prefetch=1,
            grid=(1,),
            in_specs=[pl.BlockSpec((size, size), lambda i, which: (which[0], 0))],
            out_specs=pl.BlockSpec((rows, size), lambda i, which: (0, 0)),
        ),
        compiler_params=param(16),
        cost_estimate=cost(4_000_000_000, 2_000_000),
    )(panel, slot)


class Stream:
    def __init__(self, panels, size):
        self.panels, self.size, self.half = panels, size, size // 2
        self.packed = (size // 2 + size // 8) // 2
        self.pieces, self.starts, start = [], [], 0
        for j in range(panels):
            for k in [*range(j + 1, panels), None]:
                self.pieces.append((j, k))
                self.starts.append(start)
                start += self.packed if k is None else self.half
        self.total = start
        self.step = start // CHUNKS

    def rows(self, piece):
        return self.packed if self.pieces[piece][1] is None else self.half

    def panel_start(self, j):
        last = self.panels - 1
        return j * self.packed + self.half * (j * last - (j * (j - 1)) // 2)

    def panel_ends(self):
        return [self.panel_start(j + 1) for j in range(self.panels)]


def build_kernel(stream, chips, info, slot, peer, packed, peer_packed, up, down, sems):
    chip, core, me = info[0], info[1], info[2]
    shift = SKEW * stream.step
    number = 0
    pending = []
    for piece, (j, k) in enumerate(stream.pieces):
        count = stream.rows(piece)
        if k is None:
            mine = packed.at[pl.ds(pl.multiple_of(core * count, 8), count)]
            theirs = peer_packed
        else:
            mine = slot.at[pl.ds(pl.multiple_of(k * stream.size + core * count, 8), count)]
            theirs = peer.at[k - 1]
        is_mine = info[4 + j] == me
        for place, out in ((chip, up), (chips - 1 - chip, down)):
            target = out.at[pl.ds(pl.multiple_of(place * shift + stream.starts[piece], 8), count)]
            own_copy = pltpu.make_async_copy(mine, target, sems.at[number])
            peer_copy = pltpu.make_async_copy(theirs, target, sems.at[number])
            pl.when(is_mine)(own_copy.start)
            pl.when(jnp.logical_not(is_mine))(peer_copy.start)
            pending.append(peer_copy)
            number += 1
    for copy in pending:
        copy.wait()


def build_streams(stream, chips, info, slot, peer, packed, peer_packed):
    rows = stream.total + SKEW * stream.step * (chips - 1)
    shape = jax.ShapeDtypeStruct((rows, stream.size), jnp.float32)
    return pl.pallas_call(
        functools.partial(build_kernel, stream, chips),
        out_shape=(shape, shape),
        in_specs=[SMEM, ANY, ANY, ANY, ANY],
        out_specs=(ANY, ANY),
        scratch_shapes=[pltpu.SemaphoreType.DMA((2 * len(stream.pieces),))],
        compiler_params=param(8),
        cost_estimate=cost(0, 16_000_000),
    )(info, slot, peer, packed, peer_packed)


def collect_kernel(stream, chips, first, last, info, up, *refs):
    sent = SKEW * (chips - 2) + last - first
    ups, downs, out, sems = refs[:sent], refs[sent : 2 * sent], refs[-2], refs[-1]
    chip = info[0]
    pending = []
    number = 0
    for i in range(first, last):
        for piece, (j, _) in enumerate(stream.pieces):
            low = max(stream.starts[piece], i * stream.step)
            high = min(stream.starts[piece] + stream.rows(piece), (i + 1) * stream.step)
            if low >= high:
                continue
            count = high - low
            origin = info[4 + j] >> 1
            target = out.at[pl.ds(low - first * stream.step, count)]
            inside = pl.ds(low - i * stream.step, count)
            start = pl.multiple_of(chip * SKEW * stream.step + low, 8)
            own_copy = pltpu.make_async_copy(up.at[pl.ds(start, count)], target, sems.at[number])
            pl.when(origin == chip)(own_copy.start)
            for p in range(1, chips):
                at = i - first + SKEW * (p - 1)
                rising = pltpu.make_async_copy(ups[at].at[inside], target, sems.at[number])
                pl.when((chip == p) & (origin < chip))(rising.start)
                falling = pltpu.make_async_copy(downs[at].at[inside], target, sems.at[number])
                pl.when((chip == chips - 1 - p) & (origin > chip))(falling.start)
            pending.append(own_copy)
            number += 1
    for copy in pending:
        copy.wait()


def collected(stream, chips, first, last, info, up, got_up, got_down):
    steps = range(first, last + SKEW * (chips - 2))
    received = [got_up[s] for s in steps] + [got_down[s] for s in steps]
    return pl.pallas_call(
        functools.partial(collect_kernel, stream, chips, first, last),
        out_shape=jax.ShapeDtypeStruct(((last - first) * stream.step, stream.size), jnp.float32),
        in_specs=[SMEM] + [ANY] * (1 + len(received)),
        out_specs=ANY,
        scratch_shapes=[pltpu.SemaphoreType.DMA(((last - first) * len(stream.pieces),))],
        compiler_params=param(8),
        cost_estimate=cost(0, 4_000_000),
    )(info, up, *received)


def sweep_kernel(stream, n_sec, info, query, *refs):
    groups = len(GROUPS)
    own, other = refs[:groups], refs[groups : 2 * groups]
    out_high, out_low, low_high, low_low, inv_high, inv_low, pending, part_high, part_low = refs[2 * groups :]
    core, section = info[1], info[3]
    panels, size, half = stream.panels, stream.size, stream.half
    rows = query.shape[0]
    block = rows // n_sec
    tile = size // 4
    step = stream.step

    for (first, last), mine, theirs in zip(GROUPS, own, other):
        for source, place in ((mine, core), (theirs, 1 - core)):

            @pl.loop(0, last - first)
            def _(i):
                start = pl.multiple_of(i * step, 16)
                target = pl.ds(pl.multiple_of((first + i) * step, 16), step)
                high, low = parts_of(source[pl.ds(start, step), :])
                low_high[place, target, :] = high
                low_low[place, target, :] = low

    for k in range(n_sec):
        start = pl.multiple_of(partner(section, k, n_sec) * block, block)
        for j in range(panels):
            pending[j, k * block : (k + 1) * block, :] = query[pl.ds(start, block), j * size : (j + 1) * size]

    split = stream.packed - tile
    for j in range(panels):
        s = stream.panel_start(j + 1) - stream.packed
        for source, target in ((low_high, inv_high), (low_low, inv_low)):
            target[j] = jnp.zeros((size, size), jnp.bfloat16)
            target[j, 3 * tile :, :] = source[0, s : s + tile, :]
            target[j, 2 * tile : 2 * tile + split, : 3 * tile] = source[0, s + tile : s + tile + split, : 3 * tile]
            target[j, 2 * tile + split : 3 * tile, : 3 * tile] = source[1, s : s + tile - split, : 3 * tile]
            target[j, :split, :tile] = source[0, s + tile : s + tile + split, 3 * tile :]
            target[j, split:tile, :tile] = source[1, s : s + tile - split, 3 * tile :]
            rest = source[1, s + tile - split : s + stream.packed, :]
            target[j, tile : tile + tile // 2, : 2 * tile] = rest[:, : 2 * tile]
            target[j, tile + tile // 2 : 2 * tile, : 2 * tile] = rest[:, 2 * tile :]

    def below(j, k, h):
        start = stream.panel_start(j) + (k - j - 1) * half
        span = pl.ds(pl.multiple_of(start, 16), half)
        return low_high[h, span, :], low_low[h, span, :]

    @pl.loop(0, panels)
    def _(j):
        solved = dot_parts(parts_of(pending[j]), (inv_high[j], inv_low[j]), 1)
        pending[j] = solved
        part_high[...], part_low[...] = parts_of(solved)

        @pl.loop(j + 1, panels)
        def _(k):
            for h in range(2):
                span = slice(h * half, (h + 1) * half)
                update = dot_parts((part_high[...], part_low[...]), below(j, k, h), 1)
                pending[k, :, span] = pending[k, :, span] - update

    @pl.loop(0, panels)
    def _(step_number):
        j = panels - 1 - step_number

        @pl.loop(j + 1, panels)
        def _(k):
            update = jnp.zeros((rows, size), jnp.float32)
            for h in range(2):
                span = slice(h * half, (h + 1) * half)
                update += dot_parts((out_high[k, :, span], out_low[k, :, span]), below(j, k, h), 0)
            pending[j] = pending[j] - update

        answer = dot_parts(parts_of(pending[j]), (inv_high[j], inv_low[j]), 0)
        out_high[j], out_low[j] = parts_of(answer)


def swept(stream, n_sec, info, query, own, other):
    rows = query.shape[0]
    panels, size, total = stream.panels, stream.size, stream.total
    out = jax.ShapeDtypeStruct((panels, rows, size), jnp.bfloat16)
    return pl.pallas_call(
        functools.partial(sweep_kernel, stream, n_sec),
        out_shape=(out, out),
        in_specs=[SMEM] + [VMEM] * (1 + len(own) + len(other)),
        out_specs=(VMEM, VMEM),
        scratch_shapes=[
            pltpu.VMEM((2, total, size), jnp.bfloat16),
            pltpu.VMEM((2, total, size), jnp.bfloat16),
            pltpu.VMEM((panels, size, size), jnp.bfloat16),
            pltpu.VMEM((panels, size, size), jnp.bfloat16),
            pltpu.VMEM((panels, rows, size), jnp.float32),
            pltpu.VMEM((rows, size), jnp.bfloat16),
            pltpu.VMEM((rows, size), jnp.bfloat16),
        ],
        compiler_params=param(46),
        cost_estimate=cost(18_000_000_000, 20_000_000),
    )(info, query, *own, *other)


def score_kernel(n_sec, scale, first, counts, high, low, *refs):
    blocks = len(refs) - n_sec - 3
    trains, outs = refs[:blocks], refs[blocks : blocks + n_sec]
    train_high, train_low, total = refs[-3:]
    panels, rows, size = high.shape
    length = trains[0].shape[0]
    for b, train in enumerate(trains):
        for p in range(panels):
            span = slice(b * length, (b + 1) * length)
            train_high[p, span, :], train_low[p, span, :] = parts_of(train[:, p * size : (p + 1) * size])
    total[...] = jnp.zeros_like(total)

    @pl.loop(0, panels)
    def _(p):
        total[...] += dot_parts((high[p], low[p]), (train_high[p], train_low[p]), 1)

    col = lax.broadcasted_iota(jnp.int32, (1, blocks * length), 1)
    limit = jnp.full_like(col, counts[0] - first)
    for b in range(1, blocks):
        limit = jnp.where(col >= b * length, counts[b] - first + b * length, limit)
    factor = jnp.where(col < limit, scale, 0.0).astype(jnp.float32)
    share = rows // n_sec
    for k in range(n_sec):
        outs[k][...] = total[k * share : (k + 1) * share, :] * factor


def scored(n_sec, scale, first, counts, high, low, trains):
    panels, rows, size = high.shape
    cols = sum(t.shape[0] for t in trains)
    return pl.pallas_call(
        functools.partial(score_kernel, n_sec, scale, first),
        out_shape=tuple(jax.ShapeDtypeStruct((rows // n_sec, cols), jnp.float32) for _ in range(n_sec)),
        in_specs=[SMEM] + [VMEM] * (2 + len(trains)),
        out_specs=tuple(VMEM for _ in range(n_sec)),
        scratch_shapes=[
            pltpu.VMEM((panels, cols, size), jnp.bfloat16),
            pltpu.VMEM((panels, cols, size), jnp.bfloat16),
            pltpu.VMEM((rows, cols), jnp.float32),
        ],
        compiler_params=param(24),
        cost_estimate=cost(6 * panels * size * rows * cols, 4_000_000 + 12 * cols * panels * size),
    )(counts, high, low, *trains)


def body(query_gradient_stack, train_grads, factor_slots, owner, train_count):
    query, train, slot, owners = query_gradient_stack[0], train_grads[0], factor_slots[0, 0], owner[0]
    rows, coords = query.shape
    size = slot.shape[1]
    panels = coords // size
    half = size // 2
    n_dp, n_sec = lax.axis_size("dp"), lax.axis_size("section")
    chips = n_dp // 2
    stream = Stream(panels, size)
    step_rows = stream.step
    me = lax.axis_index("dp")
    section = lax.axis_index("section")
    chip, core = lax.shift_right_logical(me, 1), me & 1
    first_core = core == 0
    info = jnp.concatenate([jnp.stack([chip, core, me, section]).astype(jnp.int32), owners])

    swap_pairs = [(d, d ^ 1) for d in range(n_dp)]
    next_chip = [(d, (d + 2) % n_dp) for d in range(n_dp)]

    def swapped(value):
        return lax.ppermute(value, "dp", swap_pairs)

    cuts = [sum(TRAIN_CUTS[:i]) for i in range(len(TRAIN_CUTS) + 1)]
    train_parts = [train[a:b] for a, b in zip(cuts, cuts[1:])]
    far = [None] * len(train_parts)

    def send_train(index, *deps):
        part = after(train_parts[index], *deps) if deps else train_parts[index]
        far[index] = lax.ppermute(part, "dp", next_chip)

    send_train(0)

    split = slot.reshape(panels, 2, half, size)
    to_peer = jnp.where(first_core, split[1:, 1], split[1:, 0])
    peer = swapped(to_peer)
    held = jnp.argmax(owners == me).astype(jnp.int32).reshape(1)
    packed = inverted_diagonal(slot, held)
    peer_packed = swapped(jnp.where(first_core, packed[stream.packed :], packed[: stream.packed]))
    up, down = build_streams(stream, chips, info, slot, peer, packed, peer_packed)

    position = lax.broadcasted_iota(jnp.int32, up.shape[:1] + (1,), 0)
    owner_chip = lax.shift_right_logical(owners, 1)

    def origin(place):
        row = position - place * (SKEW * step_rows)
        value = jnp.broadcast_to(owner_chip[0], row.shape)
        for j, end in enumerate(stream.panel_ends()[:-1]):
            value = jnp.where(row >= end, owner_chip[j + 1], value)
        return value

    lines = []
    for place, own_rows in ((lambda z: z, up), (lambda z: chips - 1 - z, down)):
        from_before = origin(place(chip)) < chip if own_rows is up else origin(place(chip)) > chip
        lines.append((place, own_rows, from_before, {}))

    def move(line, number):
        place, own_rows, from_before, got = line
        span = slice(number * step_rows, (number + 1) * step_rows)
        block = own_rows[span]
        if number >= SKEW:
            block = jnp.where(from_before[span], got[number - SKEW], block)
        pairs = []
        for z in range(chips):
            if place(z) < chips - 1 and 0 <= number - SKEW * place(z) < CHUNKS:
                to = [y for y in range(chips) if place(y) == place(z) + 1][0]
                pairs += [(2 * z + c, 2 * to + c) for c in range(2)]
        got[number] = lax.ppermute(block, "dp", pairs)
        return block

    own, other = [], []
    for number in range(CHUNKS + SKEW * (chips - 2)):
        sent = [move(line, number) for line in lines]
        for first, last in GROUPS:
            if number == last - 1 + SKEW * (chips - 2):
                value = collected(stream, chips, first, last, info, up, lines[0][3], lines[1][3])
                own.append(value)
                other.append(swapped(value))
    send_train(1, *sent)
    send_train(2, *sent)
    for index in range(3, len(train_parts)):
        send_train(index, far[index - 2])

    high, low = swept(stream, n_sec, info, query, own, other)

    count_2 = lax.ppermute(train_count, "dp", next_chip)
    count_1 = lax.ppermute(train_count, "dp", [(d, (d + 1) % n_dp) for d in range(n_dp)])
    near_counts = jnp.concatenate([count_1, count_2])
    scale = (coords * n_sec) ** (-0.5)

    def summed(parts):
        total = parts[0]
        for k in range(1, n_sec):
            if n_sec & (n_sec - 1) == 0:
                pairs = [(s, s ^ k) for s in range(n_sec)]
            else:
                pairs = [(s, (s + k) % n_sec) for s in range(n_sec)]
            total = total + lax.ppermute(parts[k], "section", pairs)
        return total

    own_scores = summed(scored(n_sec, scale, 0, train_count, high, low, [train]))
    near_scores, far_scores = [], []
    for index, far_part in enumerate(far):
        near_part = swapped(jnp.where(first_core, train_parts[index], far_part))
        length = cuts[index + 1] - cuts[index]
        both = summed(scored(n_sec, scale, cuts[index], near_counts, high, low, [near_part, far_part]))
        near_scores.append(both[:, :length])
        far_scores.append(both[:, length:])
    return jnp.concatenate([own_scores] + near_scores + far_scores, axis=1)[None]


def solution(mesh):
    in_specs = (
        P("section", "dp", None),
        P("section", "dp", None),
        P("section", "dp", None, None),
        P("section", None),
        P("dp"),
    )
    out_specs = P("dp", "section", None)
    return jax.shard_map(body, mesh=mesh, in_specs=in_specs, out_specs=out_specs, check_vma=False)
```

time: 735 us -> 383 us (0.52); the launches traced: 726 us -> 383 us
  other arithmetic: 181 us -> 13.6 us
  waiting for transfers between devices: 364 us -> 218 us
  matrix products: 111 us -> 0 us
  starting transfers between devices: 0.3 us -> 76.7 us
  Pallas kernels: 0 us -> 63 us
  local copies, waits for them, and re-layouts: 51.2 us -> 10 us
  between operations: 17.6 us -> 1.36 us
    psum x1 -> x0, waiting for transfers between devices: 219 us -> none  [spread(): return lax.psum(block, axis)]
    another operation x7 -> x1, other arithmetic: 166 us -> 0.65 us  [body(): held = jnp.argmax(owners == me).astype(jnp.int32).reshape(1)]
    ppermute x4 -> x58, waiting for transfers between devices: 103 us -> 218 us  [the longest x24 122 us: move(): got[number] = lax.ppermute(block, 'dp', pairs)]
    ppermute x4 -> x58, starting transfers between devices: 0.26 us -> 76.7 us  [the longest x24 51.9 us: move(): got[number] = lax.ppermute(block, 'dp', pairs)]
    dot_general x4 -> x0, matrix products: 65.7 us -> none  [the longest x3 42.8 us: solve_rows(): lax.dot_general(solved, panel_cols[PANEL:, :], (((1,), (1,)), ((), ())),...]
    pallas_call x0 -> x11, Pallas kernels: none -> 63 us  [the longest x1 26.2 us: swept(): pl.pallas_call(functools.partial(sweep_kernel, stream, n_sec), out_shape=...]
    another operation x52 -> x0, local copies, waits for them, and re-layouts: 46.1 us -> none  [solve_rows(): lax.linalg.triangular_solve(diag_block, pending[:, :PANEL], left_side=Fal...]
    another operation x28 -> x0, matrix products: 45.3 us -> none  [solve_rows(): lax.linalg.triangular_solve(diag_block, pending[:, :PANEL], left_side=Fal...]
  transfers between devices with their start and end apart: 6 -> 58, of which waited for: 5 -> 25; matrix products, arithmetic and copies ran while one was open for 0% -> 3% of each run, Pallas kernels for 0% -> 16%
where the time goes in v1:
time: 383 us
  waiting for transfers between devices  218 us (57%)
  starting transfers between devices  76.7 us (20%)
  Pallas kernels  63 us (16%)
  other arithmetic  13.6 us (4%)
  local copies, waits for them, and re-layouts  10 us (3%)
    ppermute x24, waiting for transfers between devices, move(): got[number] = lax.ppermute(block, 'dp', pairs)  122 us
    ppermute x24, starting transfers between devices, move(): got[number] = lax.ppermute(block, 'dp', pairs)  51.9 us
    ppermute x1, waiting for transfers between devices, body(): count_2 = lax.ppermute(train_count, 'dp', next_chip)  41.8 us
    pallas_call x1, Pallas kernels, swept(): pl.pallas_call(functools.partial(sweep_kernel, stream, n_sec), out_shape=...  26.2 us
    ppermute x18, waiting for transfers between devices, summed(): total = total + lax.ppermute(parts[k], 'section', pairs)  24.8 us
    pallas_call x6, Pallas kernels, scored(): pl.pallas_call(functools.partial(score_kernel, n_sec, scale, first), out_...  23.4 us
    ppermute x5, waiting for transfers between devices, send_train(): far[index] = lax.ppermute(part, 'dp', next_chip)  23.1 us
    ppermute x18, starting transfers between devices, summed(): total = total + lax.ppermute(parts[k], 'section', pairs)  16.9 us
  transfers between devices with their start and end apart: 58, of which 25 were waited for; matrix products, arithmetic and copies ran while one was open for 3% of the time, Pallas kernels for 16%

profile of v1, /device:TPU:0, one launch (start us, length us, event | category | flops | bytes accessed | tf_op | source)
XLA Modules:
  0.0 382.5 jit_solution(3729983788849852879)
XLA Ops:
  0.0 3.6 fusion.1
  4.7 5.4 %shard_map.55.packed = f32[320,512]{1,0:T(8,128)S(1)} custom-call(s32[1]{0:T(128)} %bitcast.9.panel_ref, f32[2048,512]{1,0:T(8,128)S(1)} %bitcast.51), custom_call_target="tpu_custom_call" | custom-call | flops 4000000000 | bytes 2000000 | tf_op jit(solution)/shard_map/pallas_call | solution.py:94
  11.8 2.2 copy-done.2
  14.0 2.2 shard_map.56
  17.8 4.7 %collective-permute-start.3 = (f32[272,512]{1,0:T(8,128)S(1)}, f32[272,512]{1,0:T(8,128)S(1)}, u32[]{:S(2)}, u32[]{:S(2)}) collective-permute-start(f32[272,512]{1,0:T(8,128)S(1)} %get-tuple-element.113), channel_id=1, source_target_pairs={{0,2},{1,3},{8,10},{9,11},{16,18},{17,19},{24,26},{25,27}} | collective-permute-start | bytes 1671176 | tf_op jit(solution)/shard_map/ppermute | solution.py:425
  22.4 1.3 collective-permute-start.2
  23.8 2.6 fusion.2
  28.3 7.1 %collective-permute-done.3.refs_1_ = f32[272,512]{1,0:T(8,128)S(1)} collective-permute-done((f32[272,512]{1,0:T(8,128)S(1)}, f32[272,512]{1,0:T(8,128)S(1)}, u32[]{:S(2)}, u32[]{:S(2)}) %collective-permute-start.3) | collective-permute-done | bytes 557088 | tf_op jit(solution)/shard_map/ppermute | solution.py:425
  35.3 11.4 %collective-permute-done.2.refs_0_ = f32[272,512]{1,0:T(8,128)S(1)} collective-permute-done((f32[272,512]{1,0:T(8,128)S(1)}, f32[272,512]{1,0:T(8,128)S(1)}, u32[]{:S(2)}, u32[]{:S(2)}) %collective-permute-start.2) | collective-permute-done | bytes 557088 | tf_op jit(solution)/shard_map/ppermute | solution.py:425
  46.9 4.4 %collective-permute-start.5 = (f32[272,512]{1,0:T(8,128)S(1)}, f32[272,512]{1,0:T(8,128)S(1)}, u32[]{:S(2)}, u32[]{:S(2)}) collective-permute-start(f32[272,512]{1,0:T(8,128)S(1)} %get-tuple-element.111), channel_id=1, source_target_pairs={{0,2},{1,3},{2,4},{3,5},{8,10},{9,11},{10,12},{11,13},{16,18},{17,... | collective-permute-start | bytes 1671176 | tf_op jit(solution)/shard_map/ppermute | solution.py:425
  51.4 6.1 %collective-permute-start.4 = (f32[272,512]{1,0:T(8,128)S(1)}, f32[272,512]{1,0:T(8,128)S(1)}, u32[]{:S(2)}, u32[]{:S(2)}) collective-permute-start(f32[272,512]{1,0:T(8,128)S(1)} %get-tuple-element.112), channel_id=1, source_target_pairs={{0,2},{1,3},{2,4},{3,5},{8,10},{9,11},{10,12},{11,13},{16,18},{17,... | collective-permute-start | bytes 1671176 | tf_op jit(solution)/shard_map/ppermute | solution.py:425
  57.7 1.3 collective-permute-start.16
  59.0 1.3 collective-permute-start.15
  60.3 4.1 %collective-permute-done.5.refs_3_ = f32[272,512]{1,0:T(8,128)S(1)} collective-permute-done((f32[272,512]{1,0:T(8,128)S(1)}, f32[272,512]{1,0:T(8,128)S(1)}, u32[]{:S(2)}, u32[]{:S(2)}) %collective-permute-start.5) | collective-permute-done | bytes 557088 | tf_op jit(solution)/shard_map/ppermute | solution.py:425
  64.4 10.5 %collective-permute-done.4.refs_2_ = f32[272,512]{1,0:T(8,128)S(1)} collective-permute-done((f32[272,512]{1,0:T(8,128)S(1)}, f32[272,512]{1,0:T(8,128)S(1)}, u32[]{:S(2)}, u32[]{:S(2)}) %collective-permute-start.4) | collective-permute-done | bytes 557088 | tf_op jit(solution)/shard_map/ppermute | solution.py:425
  75.0 6.8 %collective-permute-start.7 = (f32[272,512]{1,0:T(8,128)S(1)}, f32[272,512]{1,0:T(8,128)S(1)}, u32[]{:S(2)}, u32[]{:S(2)}) collective-permute-start(f32[272,512]{1,0:T(8,128)S(1)} %get-tuple-element.109), channel_id=1, source_target_pairs={{0,2},{1,3},{2,4},{3,5},{4,6},{5,7},{8,10},{9,11},{10,12},{11,13},... | collective-permute-start | bytes 1671176 | tf_op jit(solution)/shard_map/ppermute | solution.py:425
  81.9 3.9 %collective-permute-start.6 = (f32[272,512]{1,0:T(8,128)S(1)}, f32[272,512]{1,0:T(8,128)S(1)}, u32[]{:S(2)}, u32[]{:S(2)}) collective-permute-start(f32[272,512]{1,0:T(8,128)S(1)} %get-tuple-element.110), channel_id=1, source_target_pairs={{0,2},{1,3},{2,4},{3,5},{4,6},{5,7},{8,10},{9,11},{10,12},{11,13},... | collective-permute-start | bytes 1671176 | tf_op jit(solution)/shard_map/ppermute | solution.py:425
  85.8 5.5 %collective-permute-done.16.refs_14_.refs_7_ = f32[272,512]{1,0:T(8,128)S(1)} collective-permute-done((f32[272,512]{1,0:T(8,128)S(1)}, f32[272,512]{1,0:T(8,128)S(1)}, u32[]{:S(2)}, u32[]{:S(2)}) %collective-permute-start.16) | collective-permute-done | bytes 557088 | tf_op jit(solution)/shard_map/ppermute | solution.py:425
  91.3 10.2 %collective-permute-done.15.refs_13_ = f32[272,512]{1,0:T(8,128)S(1)} collective-permute-done((f32[272,512]{1,0:T(8,128)S(1)}, f32[272,512]{1,0:T(8,128)S(1)}, u32[]{:S(2)}, u32[]{:S(2)}) %collective-permute-start.15) | collective-permute-done | bytes 557088 | tf_op jit(solution)/shard_map/ppermute | solution.py:425
  101.7 1.3 collective-permute-start.18
  103.0 1.3 collective-permute-start.17
  105.0 4.7 %collective-permute-start.9 = (f32[272,512]{1,0:T(8,128)S(1)}, f32[272,512]{1,0:T(8,128)S(1)}, u32[]{:S(2)}, u32[]{:S(2)}) collective-permute-start(f32[272,512]{1,0:T(8,128)S(1)} %get-tuple-element.107), channel_id=1, source_target_pairs={{0,2},{1,3},{2,4},{3,5},{4,6},{5,7},{8,10},{9,11},{10,12},{11,13},... | collective-permute-start | bytes 1671176 | tf_op jit(solution)/shard_map/ppermute | solution.py:425
  109.7 3.9 %collective-permute-start.8 = (f32[272,512]{1,0:T(8,128)S(1)}, f32[272,512]{1,0:T(8,128)S(1)}, u32[]{:S(2)}, u32[]{:S(2)}) collective-permute-start(f32[272,512]{1,0:T(8,128)S(1)} %get-tuple-element.108), channel_id=1, source_target_pairs={{0,2},{1,3},{2,4},{3,5},{4,6},{5,7},{8,10},{9,11},{10,12},{11,13},... | collective-permute-start | bytes 1671176 | tf_op jit(solution)/shard_map/ppermute | solution.py:425
  113.6 5.5 %collective-permute-done.18.refs_16_.refs_9_ = f32[272,512]{1,0:T(8,128)S(1)} collective-permute-done((f32[272,512]{1,0:T(8,128)S(1)}, f32[272,512]{1,0:T(8,128)S(1)}, u32[]{:S(2)}, u32[]{:S(2)}) %collective-permute-start.18) | collective-permute-done | bytes 557088 | tf_op jit(solution)/shard_map/ppermute | solution.py:425
  119.1 9.2 %collective-permute-done.17.refs_15_.refs_8_ = f32[272,512]{1,0:T(8,128)S(1)} collective-permute-done((f32[272,512]{1,0:T(8,128)S(1)}, f32[272,512]{1,0:T(8,128)S(1)}, u32[]{:S(2)}, u32[]{:S(2)}) %collective-permute-start.17) | collective-permute-done | bytes 557088 | tf_op jit(solution)/shard_map/ppermute | solution.py:425
  128.5 1.3 collective-permute-start.23
  129.8 1.3 collective-permute-start.19
  133.3 12.7 %collective-permute-done.23.refs_11_ = f32[272,512]{1,0:T(8,128)S(1)} collective-permute-done((f32[272,512]{1,0:T(8,128)S(1)}, f32[272,512]{1,0:T(8,128)S(1)}, u32[]{:S(2)}, u32[]{:S(2)}) %collective-permute-start.23) | collective-permute-done | bytes 557088 | tf_op jit(solution)/shard_map/ppermute | solution.py:425
  146.0 8.3 %collective-permute-done.19.refs_17_.refs_10_ = f32[272,512]{1,0:T(8,128)S(1)} collective-permute-done((f32[272,512]{1,0:T(8,128)S(1)}, f32[272,512]{1,0:T(8,128)S(1)}, u32[]{:S(2)}, u32[]{:S(2)}) %collective-permute-start.19) | collective-permute-done | bytes 557088 | tf_op jit(solution)/shard_map/ppermute | solution.py:425
  154.5 1.3 collective-permute-start.24
  155.8 1.3 collective-permute-start.25
  158.1 3.5 shard_map.57.refs_0_
  162.0 2.5 collective-permute-start.33
  164.6 29.8 %collective-permute-done.24.refs_12_ = f32[272,512]{1,0:T(8,128)S(1)} collective-permute-done((f32[272,512]{1,0:T(8,128)S(1)}, f32[272,512]{1,0:T(8,128)S(1)}, u32[]{:S(2)}, u32[]{:S(2)}) %collective-permute-start.24) | collective-permute-done | bytes 557088 | tf_op jit(solution)/shard_map/ppermute | solution.py:425
  195.1 6.7 %collective-permute-done.25.refs_13_ = f32[272,512]{1,0:T(8,128)S(1)} collective-permute-done((f32[272,512]{1,0:T(8,128)S(1)}, f32[272,512]{1,0:T(8,128)S(1)}, u32[]{:S(2)}, u32[]{:S(2)}) %collective-permute-start.25) | collective-permute-done | bytes 557088 | tf_op jit(solution)/shard_map/ppermute | solution.py:425
  202.7 2.5 shard_map.58.refs_1_
  205.1 41.8 %collective-permute-done.32 = s32[1]{0:T(128)} collective-permute-done((s32[1]{0:T(128)}, s32[1]{0:T(128)}, u32[]{:S(2)}, u32[]{:S(2)}) %collective-permute-start.32) | collective-permute-done | bytes 36 | tf_op jit(solution)/shard_map/ppermute | solution.py:443
  246.9 5.0 %collective-permute-done.31 = s32[1]{0:T(128)} collective-permute-done((s32[1]{0:T(128)}, s32[1]{0:T(128)}, u32[]{:S(2)}, u32[]{:S(2)}) %collective-permute-start.31) | collective-permute-done | bytes 36 | tf_op jit(solution)/shard_map/ppermute | solution.py:444
  254.1 2.6 collective-permute-start.53
  256.7 1.8 broadcast_select_fusion
  258.5 23.1 %collective-permute-done.53.refs_1_ = f32[32,2048]{1,0:T(8,128)S(1)} collective-permute-done((f32[32,2048]{1,0:T(8,128)S(1)}, f32[32,2048]{1,0:T(8,128)S(1)}, u32[]{:S(2)}, u32[]{:S(2)}) %collective-permute-start.53) | collective-permute-done | bytes 262176 | tf_op jit(solution)/shard_map/ppermute | solution.py:387
  286.7 1.4 copy-done.5
  288.2 1.4 copy-done.7
  289.6 26.2 %shard_map.59 = (bf16[4,512,512]{2,1,0:T(8,128)(2,1)S(1)}, bf16[4,512,512]{2,1,0:T(8,128)(2,1)S(1)}) custom-call(s32[8]{0:T(128)S(1)} %concatenate.9.info, f32[512,2048]{1,0:T(8,128)} %bitcast.54, f32[1360,512]{1,0:T(8,128)} %copy-done.3, f32[816,512]{1,0:T(8,128)S(1)} %copy-done.5, f32[1360,512]{1,0:T(8,128)} %copy-done.9, f32[816,512]{1,0:T(8,128)S(1)} %copy-done.7), custom_call_target="tpu_custom_call" | custom-call | flops 17999998976 | bytes 20000000 | tf_op jit(solution)/shard_map/pallas_call | solution.py:296
  315.8 3.3 shard_map.65
  319.1 1.6 collective-permute-start.55
  320.6 1.4 collective-permute-start.56
  322.1 3.2 shard_map.64
  325.9 4.1 %shard_map.63 = (f32[128,256]{1,0:T(8,128)S(1)}, f32[128,256]{1,0:T(8,128)S(1)}, f32[128,256]{1,0:T(8,128)S(1)}, f32[128,256]{1,0:T(8,128)S(1)}) custom-call(s32[2]{0:T(128)S(1)} %pad_add_fusion.counts, bf16[4,512,512]{2,1,0:T(8,128)(2,1)S(1)} %get-tuple-element.41.high, bf16[4,512,512]{2,1,0:T(8,128)(2,1)S(1)} %get-tuple-element.42.low, ...), custom_call_target="tpu_custom_call" | custom-call | flops 1610612736 | bytes 10291456 | tf_op jit(solution)/shard_map/pallas_call | solution.py:344
  330.0 1.6 collective-permute-start.50
  331.5 4.1 %shard_map.62 = (f32[128,256]{1,0:T(8,128)S(1)}, f32[128,256]{1,0:T(8,128)S(1)}, f32[128,256]{1,0:T(8,128)S(1)}, f32[128,256]{1,0:T(8,128)S(1)}) custom-call(s32[2]{0:T(128)S(1)} %pad_add_fusion.counts, bf16[4,512,512]{2,1,0:T(8,128)(2,1)S(1)} %get-tuple-element.41.high, bf16[4,512,512]{2,1,0:T(8,128)(2,1)S(1)} %get-tuple-element.42.low, ...), custom_call_target="tpu_custom_call" | custom-call | flops 1610612736 | bytes 10291456 | tf_op jit(solution)/shard_map/pallas_call | solution.py:344
  335.6 4.7 %shard_map.60 = (f32[128,512]{1,0:T(8,128)S(1)}, f32[128,512]{1,0:T(8,128)S(1)}, f32[128,512]{1,0:T(8,128)S(1)}, f32[128,512]{1,0:T(8,128)S(1)}) custom-call(s32[1]{0:T(128)S(6)} %copy.10.counts, bf16[4,512,512]{2,1,0:T(8,128)(2,1)S(1)} %get-tuple-element.41.high, bf16[4,512,512]{2,1,0:T(8,128)(2,1)S(1)} %get-tuple-element.42.low, f32[512,2048]{1,0:T(8,128)S(1)} %bitcast.49), custom_call_target="tpu_custom_call" | custom-call | flops 3221225472 | bytes 16582912 | tf_op jit(solution)/shard_map/pallas_call | solution.py:344
  340.4 1.5 collective-permute-start.51
  341.9 4.1 %shard_map.61 = (f32[128,256]{1,0:T(8,128)S(1)}, f32[128,256]{1,0:T(8,128)S(1)}, f32[128,256]{1,0:T(8,128)S(1)}, f32[128,256]{1,0:T(8,128)S(1)}) custom-call(s32[2]{0:T(128)S(1)} %pad_add_fusion.counts, bf16[4,512,512]{2,1,0:T(8,128)(2,1)S(1)} %get-tuple-element.41.high, bf16[4,512,512]{2,1,0:T(8,128)(2,1)S(1)} %get-tuple-element.42.low, ...), custom_call_target="tpu_custom_call" | custom-call | flops 1610612736 | bytes 10291456 | tf_op jit(solution)/shard_map/pallas_call | solution.py:344
  346.6 1.5 collective-permute-start.28
  348.1 1.4 collective-permute-start.29
  350.8 2.5 collective-permute-done.52
  354.0 6.9 %collective-permute-done.45 = f32[128,256]{1,0:T(8,128)S(1)} collective-permute-done((f32[128,256]{1,0:T(8,128)S(1)}, f32[128,256]{1,0:T(8,128)S(1)}, u32[]{:S(2)}, u32[]{:S(2)}) %collective-permute-start.45) | collective-permute-done | bytes 131104 | tf_op jit(solution)/shard_map/ppermute | solution.py:455
  361.4 1.4 collective-permute-start.41
  362.9 1.3 collective-permute-done.47
  364.7 2.5 collective-permute-done.40
  368.7 1.4 collective-permute-done.42
  370.8 2.8 collective-permute-done.35
  374.1 7.2 %collective-permute-done.36 = f32[128,256]{1,0:T(8,128)S(1)} collective-permute-done((f32[128,256]{1,0:T(8,128)S(1)}, f32[128,256]{1,0:T(8,128)S(1)}, u32[]{:S(2)}, u32[]{:S(2)}) %collective-permute-start.36) | collective-permute-done | bytes 131104 | tf_op jit(solution)/shard_map/ppermute | solution.py:455
  (123 shorter events, 27.6 us)
Async XLA Ops:
  0.0 4.0 %copy-start.8 = (s32[1,4]{1,0:T(1,128)S(1)}, s32[1,4]{1,0:T(1,128)}, u32[]{:S(2)}) copy-start(s32[1,4]{1,0:T(1,128)} %param.8) | copy-start | bytes 52
  0.0 4.7 %copy-start.1 = (f32[1,1,2048,512]{3,2,1,0:T(8,128)S(1)}, f32[1,1,2048,512]{3,2,1,0:T(8,128)}, u32[]{:S(2)}) copy-start(f32[1,1,2048,512]{3,2,1,0:T(8,128)} %param.7) | copy-start | bytes 12582916
  3.6 8.3 %collective-permute-start = (f32[3,256,512]{2,1,0:T(8,128)}, f32[3,256,512]{2,1,0:T(8,128)S(1)}, u32[]{:S(2)}, u32[]{:S(2)}) collective-permute-start(f32[3,256,512]{2,1,0:T(8,128)} %fusion.1), channel_id=1, source_target_pairs={{0,1},{1,0},{2,3},{3,2},{4,5},{5,4},{6,7},{7,6},{8,9},{9,8},{10,11... | collective-permute-start | bytes 4718600 | tf_op jit(solution)/shard_map/ppermute | solution.py:379
  10.1 1.7 collective-permute-start.1
  11.8 2.2 copy-start.2
  16.3 10.4 %collective-permute-start.12 = (f32[272,512]{1,0:T(8,128)S(1)}, f32[272,512]{1,0:T(8,128)S(1)}, u32[]{:S(2)}, u32[]{:S(2)}) collective-permute-start(f32[272,512]{1,0:T(8,128)S(1)} %get-tuple-element.105), channel_id=1, source_target_pairs={{6,4},{7,5},{14,12},{15,13},{22,20},{23,21},{30,28},{31,29}} | collective-permute-start | bytes 1671176 | tf_op jit(solution)/shard_map/ppermute | solution.py:425
  17.0 9.7 %collective-permute-start.11 = (f32[272,512]{1,0:T(8,128)S(1)}, f32[272,512]{1,0:T(8,128)S(1)}, u32[]{:S(2)}, u32[]{:S(2)}) collective-permute-start(f32[272,512]{1,0:T(8,128)S(1)} %get-tuple-element.106), channel_id=1, source_target_pairs={{6,4},{7,5},{14,12},{15,13},{22,20},{23,21},{30,28},{31,29}} | collective-permute-start | bytes 1671176 | tf_op jit(solution)/shard_map/ppermute | solution.py:425
  17.8 17.6 %collective-permute-start.3 = (f32[272,512]{1,0:T(8,128)S(1)}, f32[272,512]{1,0:T(8,128)S(1)}, u32[]{:S(2)}, u32[]{:S(2)}) collective-permute-start(f32[272,512]{1,0:T(8,128)S(1)} %get-tuple-element.113), channel_id=1, source_target_pairs={{0,2},{1,3},{8,10},{9,11},{16,18},{17,19},{24,26},{25,27}} | collective-permute-start | bytes 1671176 | tf_op jit(solution)/shard_map/ppermute | solution.py:425
  22.4 24.3 %collective-permute-start.2 = (f32[272,512]{1,0:T(8,128)S(1)}, f32[272,512]{1,0:T(8,128)S(1)}, u32[]{:S(2)}, u32[]{:S(2)}) collective-permute-start(f32[272,512]{1,0:T(8,128)S(1)} %get-tuple-element.114), channel_id=1, source_target_pairs={{0,2},{1,3},{8,10},{9,11},{16,18},{17,19},{24,26},{25,27}} | collective-permute-start | bytes 1671176 | tf_op jit(solution)/shard_map/ppermute | solution.py:425
  26.9 30.6 %collective-permute-start.14 = (f32[272,512]{1,0:T(8,128)S(1)}, f32[272,512]{1,0:T(8,128)S(1)}, u32[]{:S(2)}, u32[]{:S(2)}) collective-permute-start(f32[272,512]{1,0:T(8,128)S(1)} %get-tuple-element.103), channel_id=1, source_target_pairs={{4,2},{5,3},{6,4},{7,5},{12,10},{13,11},{14,12},{15,13},{20,18},{2... | collective-permute-start | bytes 1671176 | tf_op jit(solution)/shard_map/ppermute | solution.py:425
  27.6 29.9 %collective-permute-start.13 = (f32[272,512]{1,0:T(8,128)S(1)}, f32[272,512]{1,0:T(8,128)S(1)}, u32[]{:S(2)}, u32[]{:S(2)}) collective-permute-start(f32[272,512]{1,0:T(8,128)S(1)} %get-tuple-element.104), channel_id=1, source_target_pairs={{4,2},{5,3},{6,4},{7,5},{12,10},{13,11},{14,12},{15,13},{20,18},{2... | collective-permute-start | bytes 1671176 | tf_op jit(solution)/shard_map/ppermute | solution.py:425
  46.9 17.4 %collective-permute-start.5 = (f32[272,512]{1,0:T(8,128)S(1)}, f32[272,512]{1,0:T(8,128)S(1)}, u32[]{:S(2)}, u32[]{:S(2)}) collective-permute-start(f32[272,512]{1,0:T(8,128)S(1)} %get-tuple-element.111), channel_id=1, source_target_pairs={{0,2},{1,3},{2,4},{3,5},{8,10},{9,11},{10,12},{11,13},{16,18},{17,... | collective-permute-start | bytes 1671176 | tf_op jit(solution)/shard_map/ppermute | solution.py:425
  51.4 23.5 %collective-permute-start.4 = (f32[272,512]{1,0:T(8,128)S(1)}, f32[272,512]{1,0:T(8,128)S(1)}, u32[]{:S(2)}, u32[]{:S(2)}) collective-permute-start(f32[272,512]{1,0:T(8,128)S(1)} %get-tuple-element.112), channel_id=1, source_target_pairs={{0,2},{1,3},{2,4},{3,5},{8,10},{9,11},{10,12},{11,13},{16,18},{17,... | collective-permute-start | bytes 1671176 | tf_op jit(solution)/shard_map/ppermute | solution.py:425
  57.7 33.7 %collective-permute-start.16 = (f32[272,512]{1,0:T(8,128)S(1)}, f32[272,512]{1,0:T(8,128)S(1)}, u32[]{:S(2)}, u32[]{:S(2)}) collective-permute-start(f32[272,512]{1,0:T(8,128)S(1)} %get-tuple-element.101), channel_id=1, source_target_pairs={{2,0},{3,1},{4,2},{5,3},{6,4},{7,5},{10,8},{11,9},{12,10},{13,11},... | collective-permute-start | bytes 1671176 | tf_op jit(solution)/shard_map/ppermute | solution.py:425
  59.0 42.5 %collective-permute-start.15 = (f32[272,512]{1,0:T(8,128)S(1)}, f32[272,512]{1,0:T(8,128)S(1)}, u32[]{:S(2)}, u32[]{:S(2)}) collective-permute-start(f32[272,512]{1,0:T(8,128)S(1)} %get-tuple-element.102), channel_id=1, source_target_pairs={{2,0},{3,1},{4,2},{5,3},{6,4},{7,5},{10,8},{11,9},{12,10},{13,11},... | collective-permute-start | bytes 1671176 | tf_op jit(solution)/shard_map/ppermute | solution.py:425
  75.0 29.2 %collective-permute-start.7 = (f32[272,512]{1,0:T(8,128)S(1)}, f32[272,512]{1,0:T(8,128)S(1)}, u32[]{:S(2)}, u32[]{:S(2)}) collective-permute-start(f32[272,512]{1,0:T(8,128)S(1)} %get-tuple-element.109), channel_id=1, source_target_pairs={{0,2},{1,3},{2,4},{3,5},{4,6},{5,7},{8,10},{9,11},{10,12},{11,13},... | collective-permute-start | bytes 1671176 | tf_op jit(solution)/shard_map/ppermute | solution.py:425
  81.9 22.9 %collective-permute-start.6 = (f32[272,512]{1,0:T(8,128)S(1)}, f32[272,512]{1,0:T(8,128)S(1)}, u32[]{:S(2)}, u32[]{:S(2)}) collective-permute-start(f32[272,512]{1,0:T(8,128)S(1)} %get-tuple-element.110), channel_id=1, source_target_pairs={{0,2},{1,3},{2,4},{3,5},{4,6},{5,7},{8,10},{9,11},{10,12},{11,13},... | collective-permute-start | bytes 1671176 | tf_op jit(solution)/shard_map/ppermute | solution.py:425
  101.7 17.5 %collective-permute-start.18 = (f32[272,512]{1,0:T(8,128)S(1)}, f32[272,512]{1,0:T(8,128)S(1)}, u32[]{:S(2)}, u32[]{:S(2)}) collective-permute-start(f32[272,512]{1,0:T(8,128)S(1)} %get-tuple-element.99), channel_id=1, source_target_pairs={{2,0},{3,1},{4,2},{5,3},{6,4},{7,5},{10,8},{11,9},{12,10},{13,11},... | collective-permute-start | bytes 1671176 | tf_op jit(solution)/shard_map/ppermute | solution.py:425
  103.0 25.4 %collective-permute-start.17 = (f32[272,512]{1,0:T(8,128)S(1)}, f32[272,512]{1,0:T(8,128)S(1)}, u32[]{:S(2)}, u32[]{:S(2)}) collective-permute-start(f32[272,512]{1,0:T(8,128)S(1)} %get-tuple-element.100), channel_id=1, source_target_pairs={{2,0},{3,1},{4,2},{5,3},{6,4},{7,5},{10,8},{11,9},{12,10},{13,11},... | collective-permute-start | bytes 1671176 | tf_op jit(solution)/shard_map/ppermute | solution.py:425
  105.0 26.1 %collective-permute-start.9 = (f32[272,512]{1,0:T(8,128)S(1)}, f32[272,512]{1,0:T(8,128)S(1)}, u32[]{:S(2)}, u32[]{:S(2)}) collective-permute-start(f32[272,512]{1,0:T(8,128)S(1)} %get-tuple-element.107), channel_id=1, source_target_pairs={{0,2},{1,3},{2,4},{3,5},{4,6},{5,7},{8,10},{9,11},{10,12},{11,13},... | collective-permute-start | bytes 1671176 | tf_op jit(solution)/shard_map/ppermute | solution.py:425
  109.7 22.0 %collective-permute-start.8 = (f32[272,512]{1,0:T(8,128)S(1)}, f32[272,512]{1,0:T(8,128)S(1)}, u32[]{:S(2)}, u32[]{:S(2)}) collective-permute-start(f32[272,512]{1,0:T(8,128)S(1)} %get-tuple-element.108), channel_id=1, source_target_pairs={{0,2},{1,3},{2,4},{3,5},{4,6},{5,7},{8,10},{9,11},{10,12},{11,13},... | collective-permute-start | bytes 1671176 | tf_op jit(solution)/shard_map/ppermute | solution.py:425
  128.5 17.5 %collective-permute-start.23 = (f32[272,512]{1,0:T(8,128)S(1)}, f32[272,512]{1,0:T(8,128)S(1)}, u32[]{:S(2)}, u32[]{:S(2)}) collective-permute-start(f32[272,512]{1,0:T(8,128)S(1)} %get-tuple-element.93), channel_id=1, source_target_pairs={{2,0},{3,1},{4,2},{5,3},{10,8},{11,9},{12,10},{13,11},{18,16},{19,... | collective-permute-start | bytes 1671176 | tf_op jit(solution)/shard_map/ppermute | solution.py:425
  129.8 24.5 %collective-permute-start.19 = (f32[272,512]{1,0:T(8,128)S(1)}, f32[272,512]{1,0:T(8,128)S(1)}, u32[]{:S(2)}, u32[]{:S(2)}) collective-permute-start(f32[272,512]{1,0:T(8,128)S(1)} %get-tuple-element.94), channel_id=1, source_target_pairs={{2,0},{3,1},{4,2},{5,3},{10,8},{11,9},{12,10},{13,11},{18,16},{19,... | collective-permute-start | bytes 1671176 | tf_op jit(solution)/shard_map/ppermute | solution.py:425
  131.9 25.2 %collective-permute-start.20 = (f32[272,512]{1,0:T(8,128)S(1)}, f32[272,512]{1,0:T(8,128)S(1)}, u32[]{:S(2)}, u32[]{:S(2)}) collective-permute-start(f32[272,512]{1,0:T(8,128)S(1)} %get-tuple-element.97), channel_id=1, source_target_pairs={{2,4},{3,5},{4,6},{5,7},{10,12},{11,13},{12,14},{13,15},{18,20},{1... | collective-permute-start | bytes 1671176 | tf_op jit(solution)/shard_map/ppermute | solution.py:425
  132.6 24.5 %collective-permute-start.10 = (f32[272,512]{1,0:T(8,128)S(1)}, f32[272,512]{1,0:T(8,128)S(1)}, u32[]{:S(2)}, u32[]{:S(2)}) collective-permute-start(f32[272,512]{1,0:T(8,128)S(1)} %get-tuple-element.98), channel_id=1, source_target_pairs={{2,4},{3,5},{4,6},{5,7},{10,12},{11,13},{12,14},{13,15},{18,20},{1... | collective-permute-start | bytes 1671176 | tf_op jit(solution)/shard_map/ppermute | solution.py:425
  154.5 39.9 %collective-permute-start.24 = (f32[272,512]{1,0:T(8,128)S(1)}, f32[272,512]{1,0:T(8,128)S(1)}, u32[]{:S(2)}, u32[]{:S(2)}) collective-permute-start(f32[272,512]{1,0:T(8,128)S(1)} %get-tuple-element.92), channel_id=1, source_target_pairs={{2,0},{3,1},{10,8},{11,9},{18,16},{19,17},{26,24},{27,25}} | collective-permute-start | bytes 1671176 | tf_op jit(solution)/shard_map/ppermute | solution.py:425
  155.8 46.0 %collective-permute-start.25 = (f32[272,512]{1,0:T(8,128)S(1)}, f32[272,512]{1,0:T(8,128)S(1)}, u32[]{:S(2)}, u32[]{:S(2)}) collective-permute-start(f32[272,512]{1,0:T(8,128)S(1)} %get-tuple-element.91), channel_id=1, source_target_pairs={{2,0},{3,1},{10,8},{11,9},{18,16},{19,17},{26,24},{27,25}} | collective-permute-start | bytes 1671176 | tf_op jit(solution)/shard_map/ppermute | solution.py:425
  157.3 4.4 %copy-start = (f32[1,512,2048]{2,1,0:T(8,128)S(1)}, f32[1,512,2048]{2,1,0:T(8,128)}, u32[]{:S(2)}) copy-start(f32[1,512,2048]{2,1,0:T(8,128)} %param.6) | copy-start | bytes 12582916
  157.3 44.5 %collective-permute-start.21 = (f32[272,512]{1,0:T(8,128)S(1)}, f32[272,512]{1,0:T(8,128)S(1)}, u32[]{:S(2)}, u32[]{:S(2)}) collective-permute-start(f32[272,512]{1,0:T(8,128)S(1)} %get-tuple-element.96), channel_id=1, source_target_pairs={{4,6},{5,7},{12,14},{13,15},{20,22},{21,23},{28,30},{29,31}} | collective-permute-start | bytes 1671176 | tf_op jit(solution)/shard_map/ppermute | solution.py:425
  161.6 40.9 %copy-start.3 = (f32[1360,512]{1,0:T(8,128)}, f32[1360,512]{1,0:T(8,128)S(1)}, u32[]{:S(2)}) copy-start(f32[1360,512]{1,0:T(8,128)S(1)} %shard_map.57.refs_0_) | copy-start | bytes 8355844
  161.6 123.5 %collective-permute-start.26 = (f32[1360,512]{1,0:T(8,128)S(1)}, f32[1360,512]{1,0:T(8,128)S(1)}, u32[]{:S(2)}, u32[]{:S(2)}) collective-permute-start(f32[1360,512]{1,0:T(8,128)S(1)} %shard_map.57.refs_0_), channel_id=1, source_target_pairs={{0,1},{1,0},{2,3},{3,2},{4,5},{5,4},{6,7},{7,6},{8,9},{9,8},{10,11... | collective-permute-start | bytes 8355848 | tf_op jit(solution)/shard_map/ppermute | solution.py:379
  162.0 94.7 %collective-permute-start.33 = (f32[128,2048]{1,0:T(8,128)S(1)}, f32[128,2048]{1,0:T(8,128)S(1)}, u32[]{:S(2)}, u32[]{:S(2)}) collective-permute-start(f32[128,2048]{1,0:T(8,128)S(1)} %get-tuple-element.120), channel_id=1, source_target_pairs={{0,2},{1,3},{2,4},{3,5},{4,6},{5,7},{6,0},{7,1},{8,10},{9,11},{10,... | collective-permute-start | bytes 3145736 | tf_op jit(solution)/shard_map/ppermute | solution.py:387
  194.4 8.2 %collective-permute-start.22 = (f32[272,512]{1,0:T(8,128)S(1)}, f32[272,512]{1,0:T(8,128)S(1)}, u32[]{:S(2)}, u32[]{:S(2)}) collective-permute-start(f32[272,512]{1,0:T(8,128)S(1)} %get-tuple-element.95), channel_id=1, source_target_pairs={{4,6},{5,7},{12,14},{13,15},{20,22},{21,23},{28,30},{29,31}} | collective-permute-start | bytes 1671176 | tf_op jit(solution)/shard_map/ppermute | solution.py:425
  201.8 51.3 %collective-permute-start.38 = (f32[128,2048]{1,0:T(8,128)S(1)}, f32[128,2048]{1,0:T(8,128)S(1)}, u32[]{:S(2)}, u32[]{:S(2)}) collective-permute-start(f32[128,2048]{1,0:T(8,128)S(1)} %get-tuple-element.51), channel_id=1, source_target_pairs={{0,2},{1,3},{2,4},{3,5},{4,6},{5,7},{6,0},{7,1},{8,10},{9,11},{10,... | collective-permute-start | bytes 3145736 | tf_op jit(solution)/shard_map/ppermute | solution.py:387
  201.8 52.3 %collective-permute-start.43 = (f32[128,2048]{1,0:T(8,128)S(1)}, f32[128,2048]{1,0:T(8,128)S(1)}, u32[]{:S(2)}, u32[]{:S(2)}) collective-permute-start(f32[128,2048]{1,0:T(8,128)S(1)} %get-tuple-element.56), channel_id=1, source_target_pairs={{0,2},{1,3},{2,4},{3,5},{4,6},{5,7},{6,0},{7,1},{8,10},{9,11},{10,... | collective-permute-start | bytes 3145736 | tf_op jit(solution)/shard_map/ppermute | solution.py:387
  202.6 44.3 %collective-permute-start.32 = (s32[1]{0:T(128)}, s32[1]{0:T(128)}, u32[]{:S(2)}, u32[]{:S(2)}) collective-permute-start(s32[1]{0:T(128)} %param.9), channel_id=1, source_target_pairs={{0,2},{1,3},{2,4},{3,5},{4,6},{5,7},{6,0},{7,1},{8,10},{9,11},{10,... | collective-permute-start | bytes 20 | tf_op jit(solution)/shard_map/ppermute | solution.py:443
  205.1 53.4 %copy-start.4 = (f32[816,512]{1,0:T(8,128)}, f32[816,512]{1,0:T(8,128)S(1)}, u32[]{:S(2)}) copy-start(f32[816,512]{1,0:T(8,128)S(1)} %shard_map.58.refs_1_) | copy-start | bytes 5013508
  246.9 5.0 %collective-permute-start.31 = (s32[1]{0:T(128)}, s32[1]{0:T(128)}, u32[]{:S(2)}, u32[]{:S(2)}) collective-permute-start(s32[1]{0:T(128)} %param.9), channel_id=1, source_target_pairs={{0,1},{1,2},{2,3},{3,4},{4,5},{5,6},{6,7},{7,0},{8,9},{9,10},{10,1... | collective-permute-start | bytes 20 | tf_op jit(solution)/shard_map/ppermute | solution.py:444
  251.9 32.0 %collective-permute-start.27 = (f32[816,512]{1,0:T(8,128)S(1)}, f32[816,512]{1,0:T(8,128)S(1)}, u32[]{:S(2)}, u32[]{:S(2)}) collective-permute-start(f32[816,512]{1,0:T(8,128)S(1)} %shard_map.58.refs_1_), channel_id=1, source_target_pairs={{0,1},{1,0},{2,3},{3,2},{4,5},{5,4},{6,7},{7,6},{8,9},{9,8},{10,11... | collective-permute-start | bytes 5013512 | tf_op jit(solution)/shard_map/ppermute | solution.py:379
  253.1 29.3 %collective-permute-start.48 = (f32[96,2048]{1,0:T(8,128)S(1)}, f32[96,2048]{1,0:T(8,128)S(1)}, u32[]{:S(2)}, u32[]{:S(2)}) collective-permute-start(f32[96,2048]{1,0:T(8,128)S(1)} %slice_bitcast_fusion.5), channel_id=1, source_target_pairs={{0,2},{1,3},{2,4},{3,5},{4,6},{5,7},{6,0},{7,1},{8,10},{9,11},{10,... | collective-permute-start | bytes 2359304 | tf_op jit(solution)/shard_map/ppermute | solution.py:387
  254.1 27.5 %collective-permute-start.53 = (f32[32,2048]{1,0:T(8,128)S(1)}, f32[32,2048]{1,0:T(8,128)S(1)}, u32[]{:S(2)}, u32[]{:S(2)}) collective-permute-start(f32[32,2048]{1,0:T(8,128)S(1)} %slice_bitcast_fusion.6), channel_id=1, source_target_pairs={{0,2},{1,3},{2,4},{3,5},{4,6},{5,7},{6,0},{7,1},{8,10},{9,11},{10,... | collective-permute-start | bytes 786440 | tf_op jit(solution)/shard_map/ppermute | solution.py:387
  258.5 66.8 %collective-permute-start.44 = (f32[128,2048]{1,0:T(8,128)}, f32[128,2048]{1,0:T(8,128)}, u32[]{:S(2)}, u32[]{:S(2)}) collective-permute-start(f32[128,2048]{1,0:T(8,128)} %get-tuple-element.115), channel_id=1, source_target_pairs={{0,1},{1,0},{2,3},{3,2},{4,5},{5,4},{6,7},{7,6},{8,9},{9,8},{10,11... | collective-permute-start | bytes 3145736 | tf_op jit(solution)/shard_map/ppermute | solution.py:379
  281.7 48.3 %collective-permute-start.39 = (f32[128,2048]{1,0:T(8,128)}, f32[128,2048]{1,0:T(8,128)}, u32[]{:S(2)}, u32[]{:S(2)}) collective-permute-start(f32[128,2048]{1,0:T(8,128)} %get-tuple-element.116), channel_id=1, source_target_pairs={{0,1},{1,0},{2,3},{3,2},{4,5},{5,4},{6,7},{7,6},{8,9},{9,8},{10,11... | collective-permute-start | bytes 3145736 | tf_op jit(solution)/shard_map/ppermute | solution.py:379
  282.4 57.9 %collective-permute-start.34 = (f32[128,2048]{1,0:T(8,128)}, f32[128,2048]{1,0:T(8,128)}, u32[]{:S(2)}, u32[]{:S(2)}) collective-permute-start(f32[128,2048]{1,0:T(8,128)} %get-tuple-element.117), channel_id=1, source_target_pairs={{0,1},{1,0},{2,3},{3,2},{4,5},{5,4},{6,7},{7,6},{8,9},{9,8},{10,11... | collective-permute-start | bytes 3145736 | tf_op jit(solution)/shard_map/ppermute | solution.py:379
  285.1 30.6 %collective-permute-start.54 = (f32[32,2048]{1,0:T(8,128)}, f32[32,2048]{1,0:T(8,128)}, u32[]{:S(2)}, u32[]{:S(2)}) collective-permute-start(f32[32,2048]{1,0:T(8,128)} %broadcast_select_fusion.4), channel_id=1, source_target_pairs={{0,1},{1,0},{2,3},{3,2},{4,5},{5,4},{6,7},{7,6},{8,9},{9,8},{10,11... | collective-permute-start | bytes 786440 | tf_op jit(solution)/shard_map/ppermute | solution.py:379
  285.2 35.5 %collective-permute-start.49 = (f32[96,2048]{1,0:T(8,128)}, f32[96,2048]{1,0:T(8,128)S(1)}, u32[]{:S(2)}, u32[]{:S(2)}) collective-permute-start(f32[96,2048]{1,0:T(8,128)} %broadcast_select_fusion.3), channel_id=1, source_target_pairs={{0,1},{1,0},{2,3},{3,2},{4,5},{5,4},{6,7},{7,6},{8,9},{9,8},{10,11... | collective-permute-start | bytes 2359304 | tf_op jit(solution)/shard_map/ppermute | solution.py:379
  319.1 26.9 %collective-permute-start.55 = (f32[128,64]{1,0:T(8,128)S(1)}, f32[128,64]{1,0:T(8,128)S(1)}, u32[]{:S(2)}, u32[]{:S(2)}) collective-permute-start(f32[128,64]{1,0:T(8,128)S(1)} %get-tuple-element.68), channel_id=1, source_target_pairs={{0,8},{8,0},{16,24},{24,16},{1,9},{9,1},{17,25},{25,17},{2,10},{10... | collective-permute-start | bytes 98312 | tf_op jit(solution)/shard_map/ppermute | solution.py:455
  320.6 25.9 %collective-permute-start.56 = (f32[128,64]{1,0:T(8,128)S(1)}, f32[128,64]{1,0:T(8,128)S(1)}, u32[]{:S(2)}, u32[]{:S(2)}) collective-permute-start(f32[128,64]{1,0:T(8,128)S(1)} %get-tuple-element.69), channel_id=1, source_target_pairs={{0,16},{8,24},{16,0},{24,8},{1,17},{9,25},{17,1},{25,9},{2,18},{10... | collective-permute-start | bytes 98312 | tf_op jit(solution)/shard_map/ppermute | solution.py:455
  325.3 22.8 %collective-permute-start.57 = (f32[128,64]{1,0:T(8,128)S(1)}, f32[128,64]{1,0:T(8,128)S(1)}, u32[]{:S(2)}, u32[]{:S(2)}) collective-permute-start(f32[128,64]{1,0:T(8,128)S(1)} %get-tuple-element.70), channel_id=1, source_target_pairs={{0,24},{8,16},{16,8},{24,0},{1,25},{9,17},{17,9},{25,1},{2,26},{10... | collective-permute-start | bytes 98312 | tf_op jit(solution)/shard_map/ppermute | solution.py:455
  330.0 19.6 %collective-permute-start.50 = (f32[128,192]{1,0:T(8,128)S(1)}, f32[128,192]{1,0:T(8,128)S(1)}, u32[]{:S(2)}, u32[]{:S(2)}) collective-permute-start(f32[128,192]{1,0:T(8,128)S(1)} %get-tuple-element.63), channel_id=1, source_target_pairs={{0,8},{8,0},{16,24},{24,16},{1,9},{9,1},{17,25},{25,17},{2,10},{10... | collective-permute-start | bytes 294920 | tf_op jit(solution)/shard_map/ppermute | solution.py:455
  340.4 9.9 %collective-permute-start.51 = (f32[128,192]{1,0:T(8,128)S(1)}, f32[128,192]{1,0:T(8,128)S(1)}, u32[]{:S(2)}, u32[]{:S(2)}) collective-permute-start(f32[128,192]{1,0:T(8,128)S(1)} %get-tuple-element.64), channel_id=1, source_target_pairs={{0,16},{8,24},{16,0},{24,8},{1,17},{9,25},{17,1},{25,9},{2,18},{10... | collective-permute-start | bytes 294920 | tf_op jit(solution)/shard_map/ppermute | solution.py:455
  346.0 7.4 %collective-permute-start.52 = (f32[128,192]{1,0:T(8,128)S(1)}, f32[128,192]{1,0:T(8,128)S(1)}, u32[]{:S(2)}, u32[]{:S(2)}) collective-permute-start(f32[128,192]{1,0:T(8,128)S(1)} %get-tuple-element.65), channel_id=1, source_target_pairs={{0,24},{8,16},{16,8},{24,0},{1,25},{9,17},{17,9},{25,1},{2,26},{10... | collective-permute-start | bytes 294920 | tf_op jit(solution)/shard_map/ppermute | solution.py:455
  346.6 34.8 %collective-permute-start.28 = (f32[128,512]{1,0:T(8,128)S(1)}, f32[128,512]{1,0:T(8,128)S(1)}, u32[]{:S(2)}, u32[]{:S(2)}) collective-permute-start(f32[128,512]{1,0:T(8,128)S(1)} %get-tuple-element.44), channel_id=1, source_target_pairs={{0,8},{8,0},{16,24},{24,16},{1,9},{9,1},{17,25},{25,17},{2,10},{10... | collective-permute-start | bytes 786440 | tf_op jit(solution)/shard_map/ppermute | solution.py:455
  348.1 33.3 %collective-permute-start.29 = (f32[128,512]{1,0:T(8,128)S(1)}, f32[128,512]{1,0:T(8,128)S(1)}, u32[]{:S(2)}, u32[]{:S(2)}) collective-permute-start(f32[128,512]{1,0:T(8,128)S(1)} %get-tuple-element.45), channel_id=1, source_target_pairs={{0,16},{8,24},{16,0},{24,8},{1,17},{9,25},{17,1},{25,9},{2,18},{10... | collective-permute-start | bytes 786440 | tf_op jit(solution)/shard_map/ppermute | solution.py:455
  349.6 11.3 %collective-permute-start.45 = (f32[128,256]{1,0:T(8,128)S(1)}, f32[128,256]{1,0:T(8,128)S(1)}, u32[]{:S(2)}, u32[]{:S(2)}) collective-permute-start(f32[128,256]{1,0:T(8,128)S(1)} %get-tuple-element.58), channel_id=1, source_target_pairs={{0,8},{8,0},{16,24},{24,16},{1,9},{9,1},{17,25},{25,17},{2,10},{10... | collective-permute-start | bytes 393224 | tf_op jit(solution)/shard_map/ppermute | solution.py:455
  350.2 11.2 %collective-permute-start.46 = (f32[128,256]{1,0:T(8,128)S(1)}, f32[128,256]{1,0:T(8,128)S(1)}, u32[]{:S(2)}, u32[]{:S(2)}) collective-permute-start(f32[128,256]{1,0:T(8,128)S(1)} %get-tuple-element.59), channel_id=1, source_target_pairs={{0,16},{8,24},{16,0},{24,8},{1,17},{9,25},{17,1},{25,9},{2,18},{10... | collective-permute-start | bytes 393224 | tf_op jit(solution)/shard_map/ppermute | solution.py:455
  353.4 10.9 %collective-permute-start.47 = (f32[128,256]{1,0:T(8,128)S(1)}, f32[128,256]{1,0:T(8,128)S(1)}, u32[]{:S(2)}, u32[]{:S(2)}) collective-permute-start(f32[128,256]{1,0:T(8,128)S(1)} %get-tuple-element.60), channel_id=1, source_target_pairs={{0,24},{8,16},{16,8},{24,0},{1,25},{9,17},{17,9},{25,1},{2,26},{10... | collective-permute-start | bytes 393224 | tf_op jit(solution)/shard_map/ppermute | solution.py:455
  360.9 6.4 %collective-permute-start.40 = (f32[128,256]{1,0:T(8,128)S(1)}, f32[128,256]{1,0:T(8,128)S(1)}, u32[]{:S(2)}, u32[]{:S(2)}) collective-permute-start(f32[128,256]{1,0:T(8,128)S(1)} %get-tuple-element.53), channel_id=1, source_target_pairs={{0,8},{8,0},{16,24},{24,16},{1,9},{9,1},{17,25},{25,17},{2,10},{10... | collective-permute-start | bytes 393224 | tf_op jit(solution)/shard_map/ppermute | solution.py:455
  361.4 6.4 %collective-permute-start.41 = (f32[128,256]{1,0:T(8,128)S(1)}, f32[128,256]{1,0:T(8,128)S(1)}, u32[]{:S(2)}, u32[]{:S(2)}) collective-permute-start(f32[128,256]{1,0:T(8,128)S(1)} %get-tuple-element.54), channel_id=1, source_target_pairs={{0,16},{8,24},{16,0},{24,8},{1,17},{9,25},{17,1},{25,9},{2,18},{10... | collective-permute-start | bytes 393224 | tf_op jit(solution)/shard_map/ppermute | solution.py:455
  364.2 5.9 %collective-permute-start.42 = (f32[128,256]{1,0:T(8,128)S(1)}, f32[128,256]{1,0:T(8,128)S(1)}, u32[]{:S(2)}, u32[]{:S(2)}) collective-permute-start(f32[128,256]{1,0:T(8,128)S(1)} %get-tuple-element.55), channel_id=1, source_target_pairs={{0,24},{8,16},{16,8},{24,0},{1,25},{9,17},{17,9},{25,1},{2,26},{10... | collective-permute-start | bytes 393224 | tf_op jit(solution)/shard_map/ppermute | solution.py:455
  367.3 6.4 %collective-permute-start.35 = (f32[128,256]{1,0:T(8,128)S(1)}, f32[128,256]{1,0:T(8,128)S(1)}, u32[]{:S(2)}, u32[]{:S(2)}) collective-permute-start(f32[128,256]{1,0:T(8,128)S(1)} %get-tuple-element.48), channel_id=1, source_target_pairs={{0,8},{8,0},{16,24},{24,16},{1,9},{9,1},{17,25},{25,17},{2,10},{10... | collective-permute-start | bytes 393224 | tf_op jit(solution)/shard_map/ppermute | solution.py:455
  367.8 13.5 %collective-permute-start.36 = (f32[128,256]{1,0:T(8,128)S(1)}, f32[128,256]{1,0:T(8,128)S(1)}, u32[]{:S(2)}, u32[]{:S(2)}) collective-permute-start(f32[128,256]{1,0:T(8,128)S(1)} %get-tuple-element.49), channel_id=1, source_target_pairs={{0,16},{8,24},{16,0},{24,8},{1,17},{9,25},{17,1},{25,9},{2,18},{10... | collective-permute-start | bytes 393224 | tf_op jit(solution)/shard_map/ppermute | solution.py:455
  370.1 11.2 %collective-permute-start.37 = (f32[128,256]{1,0:T(8,128)S(1)}, f32[128,256]{1,0:T(8,128)S(1)}, u32[]{:S(2)}, u32[]{:S(2)}) collective-permute-start(f32[128,256]{1,0:T(8,128)S(1)} %get-tuple-element.50), channel_id=1, source_target_pairs={{0,24},{8,16},{16,8},{24,0},{1,25},{9,17},{17,9},{25,1},{2,26},{10... | collective-permute-start | bytes 393224 | tf_op jit(solution)/shard_map/ppermute | solution.py:455
  373.6 7.8 %collective-permute-start.30 = (f32[128,512]{1,0:T(8,128)S(1)}, f32[128,512]{1,0:T(8,128)S(1)}, u32[]{:S(2)}, u32[]{:S(2)}) collective-permute-start(f32[128,512]{1,0:T(8,128)S(1)} %get-tuple-element.46), channel_id=1, source_target_pairs={{0,24},{8,16},{16,8},{24,0},{1,25},{9,17},{17,9},{25,1},{2,26},{10... | collective-permute-start | bytes 786440 | tf_op jit(solution)/shard_map/ppermute | solution.py:455
  (4 other events, 5.7 us)

commit v2 on v1

--- a/solution.py
+++ b/solution.py
@@ -11,7 +11,7 @@
 CHUNKS = 8
 SKEW = 2
 GROUPS = ((0, 5), (5, 8))
-TRAIN_CUTS = (128, 128, 128, 96, 32)
+TRAIN_CUTS = (128, 256, 96, 32)
 MIB = 1024 * 1024
 ANY = pl.BlockSpec(memory_space=pl.ANY)
 SMEM = pl.BlockSpec(memory_space=pltpu.SMEM)
@@ -217,7 +217,8 @@
 def sweep_kernel(stream, n_sec, info, query, *refs):
     groups = len(GROUPS)
     own, other = refs[:groups], refs[groups : 2 * groups]
-    out_high, out_low, low_high, low_low, inv_high, inv_low, pending, part_high, part_low = refs[2 * groups :]
+    out_high, out_low, low_high, low_low, inv_high, inv_low, pending, part_high, part_low = refs[2 * groups : -2]
+    arrived, sems = refs[-2:]
     core, section = info[1], info[3]
     panels, size, half = stream.panels, stream.size, stream.half
     rows = query.shape[0]
@@ -225,21 +226,28 @@
     tile = size // 4
     step = stream.step
 
-    for (first, last), mine, theirs in zip(GROUPS, own, other):
-        for source, place in ((mine, core), (theirs, 1 - core)):
-
-            @pl.loop(0, last - first)
-            def _(i):
-                start = pl.multiple_of(i * step, 16)
-                target = pl.ds(pl.multiple_of((first + i) * step, 16), step)
-                high, low = parts_of(source[pl.ds(start, step), :])
-                low_high[place, target, :] = high
-                low_low[place, target, :] = low
+    copies = []
+    for number, ((first, last), mine, theirs) in enumerate(zip(GROUPS, own, other)):
+        span = pl.ds(first * step, (last - first) * step)
+        for side, source in enumerate((mine, theirs)):
+            copies.append(pltpu.make_async_copy(source, arrived.at[side, span], sems.at[2 * number + side]))
+            copies[-1].start()
 
     for k in range(n_sec):
         start = pl.multiple_of(partner(section, k, n_sec) * block, block)
         for j in range(panels):
             pending[j, k * block : (k + 1) * block, :] = query[pl.ds(start, block), j * size : (j + 1) * size]
+
+    for number, (first, last) in enumerate(GROUPS):
+        for side, place in ((0, core), (1, 1 - core)):
+            copies[2 * number + side].wait()
+
+            @pl.loop(first, last)
+            def _(i):
+                span = pl.ds(pl.multiple_of(i * step, 16), step)
+                high, low = parts_of(arrived[side, span, :])
+                low_high[place, span, :] = high
+                low_low[place, span, :] = low
 
     split = stream.packed - tile
     for j in range(panels):
@@ -296,7 +304,7 @@
     return pl.pallas_call(
         functools.partial(sweep_kernel, stream, n_sec),
         out_shape=(out, out),
-        in_specs=[SMEM] + [VMEM] * (1 + len(own) + len(other)),
+        in_specs=[SMEM, VMEM] + [ANY] * (len(own) + len(other)),
         out_specs=(VMEM, VMEM),
         scratch_shapes=[
             pltpu.VMEM((2, total, size), jnp.bfloat16),
@@ -306,6 +314,8 @@
             pltpu.VMEM((panels, rows, size), jnp.float32),
             pltpu.VMEM((rows, size), jnp.bfloat16),
             pltpu.VMEM((rows, size), jnp.bfloat16),
+            pltpu.VMEM((2, total, size), jnp.float32),
+            pltpu.SemaphoreType.DMA((2 * len(own),)),
         ],
         compiler_params=param(46),
         cost_estimate=cost(18_000_000_000, 20_000_000),
@@ -386,6 +396,9 @@
         part = after(train_parts[index], *deps) if deps else train_parts[index]
         far[index] = lax.ppermute(part, "dp", next_chip)
 
+    count_2 = lax.ppermute(train_count, "dp", next_chip)
+    count_1 = lax.ppermute(train_count, "dp", [(d, (d + 1) % n_dp) for d in range(n_dp)])
+    near_counts = jnp.concatenate([count_1, count_2])
     send_train(0)
 
     split = slot.reshape(panels, 2, half, size)
@@ -411,12 +424,14 @@
         from_before = origin(place(chip)) < chip if own_rows is up else origin(place(chip)) > chip
         lines.append((place, own_rows, from_before, {}))
 
-    def move(line, number):
+    def move(line, number, *deps):
         place, own_rows, from_before, got = line
         span = slice(number * step_rows, (number + 1) * step_rows)
         block = own_rows[span]
         if number >= SKEW:
-            block = jnp.where(from_before[span], got[number - SKEW], block)
+            block = jnp.where(from_before[span], after(got[number - SKEW], *deps), block)
+        else:
+            block = after(block, *deps)
         pairs = []
         for z in range(chips):
             if place(z) < chips - 1 and 0 <= number - SKEW * place(z) < CHUNKS:
@@ -426,23 +441,19 @@
         return block
 
     own, other = [], []
+    sent = [far[0], near_counts]
     for number in range(CHUNKS + SKEW * (chips - 2)):
-        sent = [move(line, number) for line in lines]
+        sent = [move(line, number, *sent) for line in lines]
         for first, last in GROUPS:
             if number == last - 1 + SKEW * (chips - 2):
                 value = collected(stream, chips, first, last, info, up, lines[0][3], lines[1][3])
                 own.append(value)
                 other.append(swapped(value))
     send_train(1, *sent)
-    send_train(2, *sent)
-    for index in range(3, len(train_parts)):
-        send_train(index, far[index - 2])
-
     high, low = swept(stream, n_sec, info, query, own, other)
-
-    count_2 = lax.ppermute(train_count, "dp", next_chip)
-    count_1 = lax.ppermute(train_count, "dp", [(d, (d + 1) % n_dp) for d in range(n_dp)])
-    near_counts = jnp.concatenate([count_1, count_2])
+    for index in range(2, len(train_parts)):
+        send_train(index, high)
+
     scale = (coords * n_sec) ** (-0.5)
 
     def summed(parts):
@@ -455,12 +466,16 @@
             total = total + lax.ppermute(parts[k], "section", pairs)
         return total
 
-    own_scores = summed(scored(n_sec, scale, 0, train_count, high, low, [train]))
+    near = []
+    for part, far_part in zip(train_parts, far):
+        near.append(swapped(jnp.where(first_core, part, after(far_part, high))))
+    parts = scored(n_sec, scale, 0, train_count, high, low, [train])
+    own_scores = summed(parts)
     near_scores, far_scores = [], []
-    for index, far_part in enumerate(far):
-        near_part = swapped(jnp.where(first_core, train_parts[index], far_part))
+    for index, pair in enumerate(zip(near, far)):
         length = cuts[index + 1] - cuts[index]
-        both = summed(scored(n_sec, scale, cuts[index], near_counts, high, low, [near_part, far_part]))
+        parts = scored(n_sec, scale, cuts[index], after(near_counts, *parts), high, low, list(pair))
+        both = summed(parts)
         near_scores.append(both[:, :length])
         far_scores.append(both[:, length:])
     return jnp.concatenate([own_scores] + near_scores + far_scores, axis=1)[None]

time: 383 us -> 309 us (0.81)
  waiting for transfers between devices: 218 us -> 133 us
  starting transfers between devices: 76.7 us -> 85.1 us
  local copies, waits for them, and re-layouts: 10 us -> 15.1 us
    ppermute x24, waiting for transfers between devices: 122 us -> 79.9 us  [move(): got[number] = lax.ppermute(block, 'dp', pairs)]
    ppermute x1, waiting for transfers between devices: 41.8 us -> 0.01 us  [body(): count_2 = lax.ppermute(train_count, 'dp', next_chip)]
    ppermute x5 -> x4, waiting for transfers between devices: 23.1 us -> 37.2 us  [send_train(): far[index] = lax.ppermute(part, 'dp', next_chip)]
    ppermute x18 -> x15, waiting for transfers between devices: 24.8 us -> 15.6 us  [summed(): total = total + lax.ppermute(parts[k], 'section', pairs)]
    ppermute x1, waiting for transfers between devices: 5 us -> 0.01 us  [body(): lax.ppermute(train_count, 'dp', [(d, (d + 1) % n_dp) for d in range(n_dp)])]
    ppermute x18 -> x15, starting transfers between devices: 16.9 us -> 21.6 us  [summed(): total = total + lax.ppermute(parts[k], 'section', pairs)]
    slice x3 -> x4, local copies, waits for them, and re-layouts: 0.37 us -> 4.81 us  [body(): train_parts = [train[a:b] for a, b in zip(cuts, cuts[1:])]]
    pallas_call x6 -> x5, Pallas kernels: 23.4 us -> 19.6 us  [scored(): pl.pallas_call(functools.partial(score_kernel, n_sec, scale, first), out_...]
  transfers between devices with their start and end apart: 58 -> 53, of which waited for: 25 -> 26; matrix products, arithmetic and copies ran while one was open for 3% -> 6% of each run, Pallas kernels for 16% -> 19%
where the time goes in v2:
time: 309 us; the launch traced here: 308 us
  waiting for transfers between devices  133 us (43%)
  starting transfers between devices  85.1 us (28%)
  Pallas kernels  60.9 us (20%)
  local copies, waits for them, and re-layouts  15.1 us (5%)
  other arithmetic  12.5 us (4%)
    ppermute x24, waiting for transfers between devices, move(): got[number] = lax.ppermute(block, 'dp', pairs)  79.9 us
    ppermute x24, starting transfers between devices, move(): got[number] = lax.ppermute(block, 'dp', pairs)  49.4 us
    ppermute x4, waiting for transfers between devices, send_train(): far[index] = lax.ppermute(part, 'dp', next_chip)  37.2 us
    pallas_call x1, Pallas kernels, swept(): pl.pallas_call(functools.partial(sweep_kernel, stream, n_sec), out_shape=...  26.4 us
    ppermute x15, starting transfers between devices, summed(): total = total + lax.ppermute(parts[k], 'section', pairs)  21.6 us
    pallas_call x5, Pallas kernels, scored(): pl.pallas_call(functools.partial(score_kernel, n_sec, scale, first), out_...  19.6 us
    ppermute x15, waiting for transfers between devices, summed(): total = total + lax.ppermute(parts[k], 'section', pairs)  15.6 us
    ppermute x4, starting transfers between devices, send_train(): far[index] = lax.ppermute(part, 'dp', next_chip)  8.69 us
  transfers between devices with their start and end apart: 53, of which 26 were waited for; matrix products, arithmetic and copies ran while one was open for 6% of the time, Pallas kernels for 19%

profile of v2, /device:TPU:0, one launch (start us, length us, event | category | flops | bytes accessed | tf_op | source)
XLA Modules:
  0.0 308.0 jit_solution(11398822782710578151)
XLA Ops:
  0.5 2.6 collective-permute-start.4
  3.1 3.5 %fusion.1 = f32[3,256,512]{2,1,0:T(8,128)} fusion(f32[4,2,256,512]{3,2,1,0:T(8,128)} %bitcast.46, pred[]{:T(512)S(6)} %eq.11), kind=kLoop, calls=%fused_computation.3 | loop fusion | flops 393216 | bytes 4718593 | tf_op jit(solution)/shard_map/jit(_where)/select_n | solution.py:405
  6.6 1.4 collective-permute-start
  8.0 2.3 slice_bitcast_fusion.3
  10.3 1.6 collective-permute-start.2
  12.6 5.5 %shard_map.55.packed = f32[320,512]{1,0:T(8,128)S(1)} custom-call(s32[1]{0:T(128)} %bitcast.9.panel_ref, f32[2048,512]{1,0:T(8,128)S(1)} %bitcast.47), custom_call_target="tpu_custom_call" | custom-call | flops 4000000000 | bytes 2000000 | tf_op jit(solution)/shard_map/pallas_call | solution.py:94
  19.7 1.4 pad_add_fusion.counts
  21.1 2.2 copy-done.2
  23.3 3.4 %shard_map.56 = (f32[3808,512]{1,0:T(8,128)S(1)}, f32[3808,512]{1,0:T(8,128)S(1)}) custom-call(s32[8]{0:T(128)S(1)} %concatenate.9.info, f32[2048,512]{1,0:T(8,128)S(1)} %bitcast.48, f32[3,256,512]{2,1,0:T(8,128)S(1)} %collective-permute-done.peer, f32[320,512]{1,0:T(8,128)S(1)} %shard_map.55.packed, f32[160,512]{1,0:T(8,128)} %collective-permute-done.1.peer_packed), custom_call_target="tpu_custom_call" | custom-call | bytes 16000000 | tf_op jit(solution)/shard_map/pallas_call | solution.py:161
  27.0 10.4 %collective-permute-done.2.refs_1_ = f32[128,2048]{1,0:T(8,128)S(1)} collective-permute-done((f32[128,2048]{1,0:T(8,128)}, f32[128,2048]{1,0:T(8,128)S(1)}, u32[]{:S(2)}, u32[]{:S(2)}) %collective-permute-start.2) | collective-permute-done | bytes 1048608 | tf_op jit(solution)/shard_map/ppermute | solution.py:397
  38.0 1.7 collective-permute-start.5
  39.8 2.5 fusion.2
  43.3 1.3 collective-permute-start.6
  44.6 8.2 %collective-permute-done.5.refs_0_ = f32[272,512]{1,0:T(8,128)S(1)} collective-permute-done((f32[272,512]{1,0:T(8,128)S(1)}, f32[272,512]{1,0:T(8,128)S(1)}, u32[]{:S(2)}, u32[]{:S(2)}) %collective-permute-start.5) | collective-permute-done | bytes 557088 | tf_op jit(solution)/shard_map/ppermute | solution.py:440
  53.8 5.0 %collective-permute-start.7 = (f32[272,512]{1,0:T(8,128)S(1)}, f32[272,512]{1,0:T(8,128)S(1)}, u32[]{:S(2)}, u32[]{:S(2)}) collective-permute-start(f32[272,512]{1,0:T(8,128)S(1)} %slice_select_fusion.19), channel_id=1, source_target_pairs={{0,2},{1,3},{2,4},{3,5},{8,10},{9,11},{10,12},{11,13},{16,18},{17,... | collective-permute-start | bytes 1671176 | tf_op jit(solution)/shard_map/ppermute | solution.py:440
  58.9 5.9 %collective-permute-done.6.refs_1_ = f32[272,512]{1,0:T(8,128)S(1)} collective-permute-done((f32[272,512]{1,0:T(8,128)S(1)}, f32[272,512]{1,0:T(8,128)S(1)}, u32[]{:S(2)}, u32[]{:S(2)}) %collective-permute-start.6) | collective-permute-done | bytes 557088 | tf_op jit(solution)/shard_map/ppermute | solution.py:440
  65.8 5.0 %collective-permute-start.9 = (f32[272,512]{1,0:T(8,128)S(1)}, f32[272,512]{1,0:T(8,128)S(1)}, u32[]{:S(2)}, u32[]{:S(2)}) collective-permute-start(f32[272,512]{1,0:T(8,128)S(1)} %slice_select_fusion.17), channel_id=1, source_target_pairs={{0,2},{1,3},{2,4},{3,5},{8,10},{9,11},{10,12},{11,13},{16,18},{17,... | collective-permute-start | bytes 1671176 | tf_op jit(solution)/shard_map/ppermute | solution.py:440
  70.8 5.9 %collective-permute-done.7.refs_2_ = f32[272,512]{1,0:T(8,128)S(1)} collective-permute-done((f32[272,512]{1,0:T(8,128)S(1)}, f32[272,512]{1,0:T(8,128)S(1)}, u32[]{:S(2)}, u32[]{:S(2)}) %collective-permute-start.7) | collective-permute-done | bytes 557088 | tf_op jit(solution)/shard_map/ppermute | solution.py:440
  76.8 1.3 collective-permute-start.16
  78.3 5.0 %collective-permute-start.11 = (f32[272,512]{1,0:T(8,128)S(1)}, f32[272,512]{1,0:T(8,128)S(1)}, u32[]{:S(2)}, u32[]{:S(2)}) collective-permute-start(f32[272,512]{1,0:T(8,128)S(1)} %slice_select_fusion.15), channel_id=1, source_target_pairs={{0,2},{1,3},{2,4},{3,5},{4,6},{5,7},{8,10},{9,11},{10,12},{11,13},... | collective-permute-start | bytes 1671176 | tf_op jit(solution)/shard_map/ppermute | solution.py:440
  83.4 5.2 %collective-permute-done.9.refs_3_ = f32[272,512]{1,0:T(8,128)S(1)} collective-permute-done((f32[272,512]{1,0:T(8,128)S(1)}, f32[272,512]{1,0:T(8,128)S(1)}, u32[]{:S(2)}, u32[]{:S(2)}) %collective-permute-start.9) | collective-permute-done | bytes 557088 | tf_op jit(solution)/shard_map/ppermute | solution.py:440
  88.8 1.3 collective-permute-start.18
  90.2 5.0 %collective-permute-start.13 = (f32[272,512]{1,0:T(8,128)S(1)}, f32[272,512]{1,0:T(8,128)S(1)}, u32[]{:S(2)}, u32[]{:S(2)}) collective-permute-start(f32[272,512]{1,0:T(8,128)S(1)} %slice_select_fusion.13), channel_id=1, source_target_pairs={{0,2},{1,3},{2,4},{3,5},{4,6},{5,7},{8,10},{9,11},{10,12},{11,13},... | collective-permute-start | bytes 1671176 | tf_op jit(solution)/shard_map/ppermute | solution.py:440
  95.3 5.2 %collective-permute-done.11.refs_4_ = f32[272,512]{1,0:T(8,128)S(1)} collective-permute-done((f32[272,512]{1,0:T(8,128)S(1)}, f32[272,512]{1,0:T(8,128)S(1)}, u32[]{:S(2)}, u32[]{:S(2)}) %collective-permute-start.11) | collective-permute-done | bytes 557088 | tf_op jit(solution)/shard_map/ppermute | solution.py:440
  102.1 5.0 %collective-permute-start.15 = (f32[272,512]{1,0:T(8,128)S(1)}, f32[272,512]{1,0:T(8,128)S(1)}, u32[]{:S(2)}, u32[]{:S(2)}) collective-permute-start(f32[272,512]{1,0:T(8,128)S(1)} %slice_select_fusion.11), channel_id=1, source_target_pairs={{0,2},{1,3},{2,4},{3,5},{4,6},{5,7},{8,10},{9,11},{10,12},{11,13},... | collective-permute-start | bytes 1671176 | tf_op jit(solution)/shard_map/ppermute | solution.py:440
  107.2 5.3 %collective-permute-done.13.refs_5_.refs_0_ = f32[272,512]{1,0:T(8,128)S(1)} collective-permute-done((f32[272,512]{1,0:T(8,128)S(1)}, f32[272,512]{1,0:T(8,128)S(1)}, u32[]{:S(2)}, u32[]{:S(2)}) %collective-permute-start.13) | collective-permute-done | bytes 557088 | tf_op jit(solution)/shard_map/ppermute | solution.py:440
  114.0 5.0 %collective-permute-start.17 = (f32[272,512]{1,0:T(8,128)S(1)}, f32[272,512]{1,0:T(8,128)S(1)}, u32[]{:S(2)}, u32[]{:S(2)}) collective-permute-start(f32[272,512]{1,0:T(8,128)S(1)} %slice_select_fusion.9), channel_id=1, source_target_pairs={{0,2},{1,3},{2,4},{3,5},{4,6},{5,7},{8,10},{9,11},{10,12},{11,13},... | collective-permute-start | bytes 1671176 | tf_op jit(solution)/shard_map/ppermute | solution.py:440
  119.1 5.3 %collective-permute-done.15.refs_6_.refs_1_ = f32[272,512]{1,0:T(8,128)S(1)} collective-permute-done((f32[272,512]{1,0:T(8,128)S(1)}, f32[272,512]{1,0:T(8,128)S(1)}, u32[]{:S(2)}, u32[]{:S(2)}) %collective-permute-start.15) | collective-permute-done | bytes 557088 | tf_op jit(solution)/shard_map/ppermute | solution.py:440
  126.7 7.8 %collective-permute-done.17.refs_7_.refs_2_ = f32[272,512]{1,0:T(8,128)S(1)} collective-permute-done((f32[272,512]{1,0:T(8,128)S(1)}, f32[272,512]{1,0:T(8,128)S(1)}, u32[]{:S(2)}, u32[]{:S(2)}) %collective-permute-start.17) | collective-permute-done | bytes 557088 | tf_op jit(solution)/shard_map/ppermute | solution.py:440
  136.7 1.4 collective-permute-done.22.refs_17_.refs_10_
  138.1 3.5 %shard_map.57.refs_0_ = f32[1360,512]{1,0:T(8,128)S(1)} custom-call(s32[8]{0:T(128)S(1)} %concatenate.9.info, f32[3808,512]{1,0:T(8,128)S(1)} %get-tuple-element.66.up, f32[272,512]{1,0:T(8,128)S(1)} %collective-permute-done.5.refs_0_, f32[272,512]{1,0:T(8,128)S(1)} %collective-permute-done.6.refs_1_, f32[272,512]{1,0:T(8,128)S(1)} %collective-permute-done.7.refs_2_, ...), custom_call_target="tpu_custom_call" | custom-call | bytes 4000000 | tf_op jit(solution)/shard_map/pallas_call | solution.py:206
  141.9 8.1 %collective-permute-done.26.refs_11_ = f32[272,512]{1,0:T(8,128)S(1)} collective-permute-done((f32[272,512]{1,0:T(8,128)S(1)}, f32[272,512]{1,0:T(8,128)S(1)}, u32[]{:S(2)}, u32[]{:S(2)}) %collective-permute-start.26) | collective-permute-done | bytes 557088 | tf_op jit(solution)/shard_map/ppermute | solution.py:440
  152.5 1.4 collective-permute-start.27
  154.7 13.0 %collective-permute-done.28.refs_13_ = f32[272,512]{1,0:T(8,128)S(1)} collective-permute-done((f32[272,512]{1,0:T(8,128)S(1)}, f32[272,512]{1,0:T(8,128)S(1)}, u32[]{:S(2)}, u32[]{:S(2)}) %collective-permute-start.28) | collective-permute-done | bytes 557088 | tf_op jit(solution)/shard_map/ppermute | solution.py:440
  167.7 8.5 %collective-permute-done.27.refs_12_ = f32[272,512]{1,0:T(8,128)S(1)} collective-permute-done((f32[272,512]{1,0:T(8,128)S(1)}, f32[272,512]{1,0:T(8,128)S(1)}, u32[]{:S(2)}, u32[]{:S(2)}) %collective-permute-start.27) | collective-permute-done | bytes 557088 | tf_op jit(solution)/shard_map/ppermute | solution.py:440
  176.2 2.4 shard_map.58.refs_1_
  180.4 1.6 slice_bitcast_fusion
  183.5 1.6 copy-done.9
  185.1 1.4 copy-done.5
  186.5 1.4 copy-done.7
  188.0 26.4 %shard_map.59 = (bf16[4,512,512]{2,1,0:T(8,128)(2,1)S(1)}, bf16[4,512,512]{2,1,0:T(8,128)(2,1)S(1)}) custom-call(s32[8]{0:T(128)S(1)} %concatenate.9.info, f32[512,2048]{1,0:T(8,128)} %bitcast.50, f32[1360,512]{1,0:T(8,128)} %copy-done.3, f32[816,512]{1,0:T(8,128)S(1)} %copy-done.5, f32[1360,512]{1,0:T(8,128)} %copy-done.9, f32[816,512]{1,0:T(8,128)S(1)} %copy-done.7), custom_call_target="tpu_custom_call" | custom-call | flops 17999998976 | bytes 20000000 | tf_op jit(solution)/shard_map/pallas_call | solution.py:304
  214.4 4.5 %collective-permute-start.48 = (f32[32,2048]{1,0:T(8,128)S(1)}, f32[32,2048]{1,0:T(8,128)S(1)}, u32[]{:S(2)}, u32[]{:S(2)}) collective-permute-start(f32[32,2048]{1,0:T(8,128)S(1)} %slice_bitcast_fusion.5), channel_id=1, source_target_pairs={{0,2},{1,3},{2,4},{3,5},{4,6},{5,7},{6,0},{7,1},{8,10},{9,11},{10,... | collective-permute-start | bytes 786440 | tf_op jit(solution)/shard_map/ppermute | solution.py:397
  218.9 2.6 collective-permute-start.43
  221.5 13.4 %collective-permute-done.38.refs_1_ = f32[256,2048]{1,0:T(8,128)S(1)} collective-permute-done((f32[256,2048]{1,0:T(8,128)}, f32[256,2048]{1,0:T(8,128)S(1)}, u32[]{:S(2)}, u32[]{:S(2)}) %collective-permute-start.38) | collective-permute-done | bytes 2097184 | tf_op jit(solution)/shard_map/ppermute | solution.py:397
  235.9 4.7 %shard_map.60 = (f32[128,512]{1,0:T(8,128)S(1)}, f32[128,512]{1,0:T(8,128)S(1)}, f32[128,512]{1,0:T(8,128)S(1)}, f32[128,512]{1,0:T(8,128)S(1)}) custom-call(s32[1]{0:T(128)S(6)} %copy.10.counts, bf16[4,512,512]{2,1,0:T(8,128)(2,1)S(1)} %get-tuple-element.92.high, bf16[4,512,512]{2,1,0:T(8,128)(2,1)S(1)} %get-tuple-element.93.low, f32[512,2048]{1,0:T(8,128)S(1)} %bitcast.45), custom_call_target="tpu_custom_call" | custom-call | flops 3221225472 | bytes 16582912 | tf_op jit(solution)/shard_map/pallas_call | solution.py:354
  240.7 1.5 collective-permute-start.31
  242.2 1.5 collective-permute-start.32
  243.8 13.4 %collective-permute-done.43.refs_1_ = f32[96,2048]{1,0:T(8,128)S(1)} collective-permute-done((f32[96,2048]{1,0:T(8,128)}, f32[96,2048]{1,0:T(8,128)S(1)}, u32[]{:S(2)}, u32[]{:S(2)}) %collective-permute-start.43) | collective-permute-done | bytes 786464 | tf_op jit(solution)/shard_map/ppermute | solution.py:397
  257.2 2.4 collective-permute-start.33
  259.8 3.4 %shard_map.61 = (f32[128,256]{1,0:T(8,128)S(1)}, f32[128,256]{1,0:T(8,128)S(1)}, f32[128,256]{1,0:T(8,128)S(1)}, f32[128,256]{1,0:T(8,128)S(1)}) custom-call(s32[2]{0:T(128)S(1)} %pad_add_fusion.counts, bf16[4,512,512]{2,1,0:T(8,128)(2,1)S(1)} %get-tuple-element.92.high, bf16[4,512,512]{2,1,0:T(8,128)(2,1)S(1)} %get-tuple-element.93.low, ...), custom_call_target="tpu_custom_call" | custom-call | flops 1610612736 | bytes 10291456 | tf_op jit(solution)/shard_map/pallas_call | solution.py:354
  264.3 1.9 collective-permute-done.33
  266.2 3.2 %collective-permute-start.37 = (f32[128,256]{1,0:T(8,128)S(1)}, f32[128,256]{1,0:T(8,128)S(1)}, u32[]{:S(2)}, u32[]{:S(2)}) collective-permute-start(f32[128,256]{1,0:T(8,128)S(1)} %get-tuple-element.103), channel_id=1, source_target_pairs={{0,24},{8,16},{16,8},{24,0},{1,25},{9,17},{17,9},{25,1},{2,26},{10... | collective-permute-start | bytes 393224 | tf_op jit(solution)/shard_map/ppermute | solution.py:466
  270.8 1.5 collective-permute-done.37
  272.4 5.5 %shard_map.62 = (f32[128,512]{1,0:T(8,128)S(1)}, f32[128,512]{1,0:T(8,128)S(1)}, f32[128,512]{1,0:T(8,128)S(1)}, f32[128,512]{1,0:T(8,128)S(1)}) custom-call(s32[2]{0:T(128)S(1)} %pad_add_fusion.counts, bf16[4,512,512]{2,1,0:T(8,128)(2,1)S(1)} %get-tuple-element.92.high, bf16[4,512,512]{2,1,0:T(8,128)(2,1)S(1)} %get-tuple-element.93.low, ...), custom_call_target="tpu_custom_call" | custom-call | flops 3221225472 | bytes 16582912 | tf_op jit(solution)/shard_map/pallas_call | solution.py:354
  277.9 3.2 %shard_map.63 = (f32[128,192]{1,0:T(8,128)S(1)}, f32[128,192]{1,0:T(8,128)S(1)}, f32[128,192]{1,0:T(8,128)S(1)}, f32[128,192]{1,0:T(8,128)S(1)}) custom-call(s32[2]{0:T(128)S(1)} %pad_add_fusion.counts, bf16[4,512,512]{2,1,0:T(8,128)(2,1)S(1)} %get-tuple-element.92.high, bf16[4,512,512]{2,1,0:T(8,128)(2,1)S(1)} %get-tuple-element.93.low, ...), custom_call_target="tpu_custom_call" | custom-call | flops 1207959552 | bytes 8718592 | tf_op jit(solution)/shard_map/pallas_call | solution.py:354
  281.1 2.8 shard_map.64
  283.9 2.0 collective-permute-start.50
  286.0 1.5 collective-permute-start.51
  287.5 2.0 collective-permute-start.45
  289.5 1.5 collective-permute-start.46
  295.3 1.6 collective-permute-start.42
  296.9 2.2 collective-permute-done.47
  299.3 4.0 %collective-permute-done.40 = f32[128,512]{1,0:T(8,128)S(1)} collective-permute-done((f32[128,512]{1,0:T(8,128)S(1)}, f32[128,512]{1,0:T(8,128)S(1)}, u32[]{:S(2)}, u32[]{:S(2)}) %collective-permute-start.40) | collective-permute-done | bytes 262176 | tf_op jit(solution)/shard_map/ppermute | solution.py:466
  303.2 2.6 collective-permute-done.41
  (121 shorter events, 31.1 us)
Async XLA Ops:
  0.0 11.9 %copy-start.8 = (s32[1,4]{1,0:T(1,128)S(1)}, s32[1,4]{1,0:T(1,128)}, u32[]{:S(2)}) copy-start(s32[1,4]{1,0:T(1,128)} %param.8) | copy-start | bytes 52
  0.0 19.7 %collective-permute-start.3 = (s32[1]{0:T(128)}, s32[1]{0:T(128)}, u32[]{:S(2)}, u32[]{:S(2)}) collective-permute-start(s32[1]{0:T(128)} %param.9), channel_id=1, source_target_pairs={{0,1},{1,2},{2,3},{3,4},{4,5},{5,6},{6,7},{7,0},{8,9},{9,10},{10,1... | collective-permute-start | bytes 20 | tf_op jit(solution)/shard_map/ppermute | solution.py:400
  0.5 19.2 %collective-permute-start.4 = (s32[1]{0:T(128)}, s32[1]{0:T(128)}, u32[]{:S(2)}, u32[]{:S(2)}) collective-permute-start(s32[1]{0:T(128)} %param.9), channel_id=1, source_target_pairs={{0,2},{1,3},{2,4},{3,5},{4,6},{5,7},{6,0},{7,1},{8,10},{9,11},{10,... | collective-permute-start | bytes 20 | tf_op jit(solution)/shard_map/ppermute | solution.py:399
  3.1 9.5 %copy-start.1 = (f32[1,1,2048,512]{3,2,1,0:T(8,128)S(1)}, f32[1,1,2048,512]{3,2,1,0:T(8,128)}, u32[]{:S(2)}) copy-start(f32[1,1,2048,512]{3,2,1,0:T(8,128)} %param.7) | copy-start | bytes 12582916
  6.6 14.5 %collective-permute-start = (f32[3,256,512]{2,1,0:T(8,128)}, f32[3,256,512]{2,1,0:T(8,128)S(1)}, u32[]{:S(2)}, u32[]{:S(2)}) collective-permute-start(f32[3,256,512]{2,1,0:T(8,128)} %fusion.1), channel_id=1, source_target_pairs={{0,1},{1,0},{2,3},{3,2},{4,5},{5,4},{6,7},{7,6},{8,9},{9,8},{10,11... | collective-permute-start | bytes 4718600 | tf_op jit(solution)/shard_map/ppermute | solution.py:389
  10.3 27.1 %collective-permute-start.2 = (f32[128,2048]{1,0:T(8,128)}, f32[128,2048]{1,0:T(8,128)S(1)}, u32[]{:S(2)}, u32[]{:S(2)}) collective-permute-start(f32[128,2048]{1,0:T(8,128)} %slice_bitcast_fusion.3), channel_id=1, source_target_pairs={{0,2},{1,3},{2,4},{3,5},{4,6},{5,7},{6,0},{7,1},{8,10},{9,11},{10,... | collective-permute-start | bytes 3145736 | tf_op jit(solution)/shard_map/ppermute | solution.py:397
  18.9 2.2 collective-permute-start.1
  21.1 2.2 copy-start.2
  37.4 7.2 %collective-permute-start.8 = (f32[272,512]{1,0:T(8,128)S(1)}, f32[272,512]{1,0:T(8,128)S(1)}, u32[]{:S(2)}, u32[]{:S(2)}) collective-permute-start(f32[272,512]{1,0:T(8,128)S(1)} %get-tuple-element.69), channel_id=1, source_target_pairs={{6,4},{7,5},{14,12},{15,13},{22,20},{23,21},{30,28},{31,29}} | collective-permute-start | bytes 1671176 | tf_op jit(solution)/shard_map/ppermute | solution.py:440
  38.0 14.8 %collective-permute-start.5 = (f32[272,512]{1,0:T(8,128)S(1)}, f32[272,512]{1,0:T(8,128)S(1)}, u32[]{:S(2)}, u32[]{:S(2)}) collective-permute-start(f32[272,512]{1,0:T(8,128)S(1)} %get-tuple-element.67), channel_id=1, source_target_pairs={{0,2},{1,3},{8,10},{9,11},{16,18},{17,19},{24,26},{25,27}} | collective-permute-start | bytes 1671176 | tf_op jit(solution)/shard_map/ppermute | solution.py:440
  42.5 16.3 %collective-permute-start.10 = (f32[272,512]{1,0:T(8,128)S(1)}, f32[272,512]{1,0:T(8,128)S(1)}, u32[]{:S(2)}, u32[]{:S(2)}) collective-permute-start(f32[272,512]{1,0:T(8,128)S(1)} %get-tuple-element.71), channel_id=1, source_target_pairs={{6,4},{7,5},{14,12},{15,13},{22,20},{23,21},{30,28},{31,29}} | collective-permute-start | bytes 1671176 | tf_op jit(solution)/shard_map/ppermute | solution.py:440
  43.3 21.5 %collective-permute-start.6 = (f32[272,512]{1,0:T(8,128)S(1)}, f32[272,512]{1,0:T(8,128)S(1)}, u32[]{:S(2)}, u32[]{:S(2)}) collective-permute-start(f32[272,512]{1,0:T(8,128)S(1)} %get-tuple-element.70), channel_id=1, source_target_pairs={{0,2},{1,3},{8,10},{9,11},{16,18},{17,19},{24,26},{25,27}} | collective-permute-start | bytes 1671176 | tf_op jit(solution)/shard_map/ppermute | solution.py:440
  53.0 17.8 %collective-permute-start.12 = (f32[272,512]{1,0:T(8,128)S(1)}, f32[272,512]{1,0:T(8,128)S(1)}, u32[]{:S(2)}, u32[]{:S(2)}) collective-permute-start(f32[272,512]{1,0:T(8,128)S(1)} %slice_select_fusion.18), channel_id=1, source_target_pairs={{4,2},{5,3},{6,4},{7,5},{12,10},{13,11},{14,12},{15,13},{20,18},{2... | collective-permute-start | bytes 1671176 | tf_op jit(solution)/shard_map/ppermute | solution.py:440
  53.8 22.9 %collective-permute-start.7 = (f32[272,512]{1,0:T(8,128)S(1)}, f32[272,512]{1,0:T(8,128)S(1)}, u32[]{:S(2)}, u32[]{:S(2)}) collective-permute-start(f32[272,512]{1,0:T(8,128)S(1)} %slice_select_fusion.19), channel_id=1, source_target_pairs={{0,2},{1,3},{2,4},{3,5},{8,10},{9,11},{10,12},{11,13},{16,18},{17,... | collective-permute-start | bytes 1671176 | tf_op jit(solution)/shard_map/ppermute | solution.py:440
  64.9 18.5 %collective-permute-start.14 = (f32[272,512]{1,0:T(8,128)S(1)}, f32[272,512]{1,0:T(8,128)S(1)}, u32[]{:S(2)}, u32[]{:S(2)}) collective-permute-start(f32[272,512]{1,0:T(8,128)S(1)} %slice_select_fusion.16), channel_id=1, source_target_pairs={{4,2},{5,3},{6,4},{7,5},{12,10},{13,11},{14,12},{15,13},{20,18},{2... | collective-permute-start | bytes 1671176 | tf_op jit(solution)/shard_map/ppermute | solution.py:440
  65.8 22.8 %collective-permute-start.9 = (f32[272,512]{1,0:T(8,128)S(1)}, f32[272,512]{1,0:T(8,128)S(1)}, u32[]{:S(2)}, u32[]{:S(2)}) collective-permute-start(f32[272,512]{1,0:T(8,128)S(1)} %slice_select_fusion.17), channel_id=1, source_target_pairs={{0,2},{1,3},{2,4},{3,5},{8,10},{9,11},{10,12},{11,13},{16,18},{17,... | collective-permute-start | bytes 1671176 | tf_op jit(solution)/shard_map/ppermute | solution.py:440
  76.8 18.5 %collective-permute-start.16 = (f32[272,512]{1,0:T(8,128)S(1)}, f32[272,512]{1,0:T(8,128)S(1)}, u32[]{:S(2)}, u32[]{:S(2)}) collective-permute-start(f32[272,512]{1,0:T(8,128)S(1)} %slice_select_fusion.14), channel_id=1, source_target_pairs={{2,0},{3,1},{4,2},{5,3},{6,4},{7,5},{10,8},{11,9},{12,10},{13,11},... | collective-permute-start | bytes 1671176 | tf_op jit(solution)/shard_map/ppermute | solution.py:440
  78.3 22.2 %collective-permute-start.11 = (f32[272,512]{1,0:T(8,128)S(1)}, f32[272,512]{1,0:T(8,128)S(1)}, u32[]{:S(2)}, u32[]{:S(2)}) collective-permute-start(f32[272,512]{1,0:T(8,128)S(1)} %slice_select_fusion.15), channel_id=1, source_target_pairs={{0,2},{1,3},{2,4},{3,5},{4,6},{5,7},{8,10},{9,11},{10,12},{11,13},... | collective-permute-start | bytes 1671176 | tf_op jit(solution)/shard_map/ppermute | solution.py:440
  88.8 18.4 %collective-permute-start.18 = (f32[272,512]{1,0:T(8,128)S(1)}, f32[272,512]{1,0:T(8,128)S(1)}, u32[]{:S(2)}, u32[]{:S(2)}) collective-permute-start(f32[272,512]{1,0:T(8,128)S(1)} %slice_select_fusion.12), channel_id=1, source_target_pairs={{2,0},{3,1},{4,2},{5,3},{6,4},{7,5},{10,8},{11,9},{12,10},{13,11},... | collective-permute-start | bytes 1671176 | tf_op jit(solution)/shard_map/ppermute | solution.py:440
  90.2 22.2 %collective-permute-start.13 = (f32[272,512]{1,0:T(8,128)S(1)}, f32[272,512]{1,0:T(8,128)S(1)}, u32[]{:S(2)}, u32[]{:S(2)}) collective-permute-start(f32[272,512]{1,0:T(8,128)S(1)} %slice_select_fusion.13), channel_id=1, source_target_pairs={{0,2},{1,3},{2,4},{3,5},{4,6},{5,7},{8,10},{9,11},{10,12},{11,13},... | collective-permute-start | bytes 1671176 | tf_op jit(solution)/shard_map/ppermute | solution.py:440
  100.7 18.4 %collective-permute-start.20 = (f32[272,512]{1,0:T(8,128)S(1)}, f32[272,512]{1,0:T(8,128)S(1)}, u32[]{:S(2)}, u32[]{:S(2)}) collective-permute-start(f32[272,512]{1,0:T(8,128)S(1)} %slice_select_fusion.10), channel_id=1, source_target_pairs={{2,0},{3,1},{4,2},{5,3},{6,4},{7,5},{10,8},{11,9},{12,10},{13,11},... | collective-permute-start | bytes 1671176 | tf_op jit(solution)/shard_map/ppermute | solution.py:440
  102.1 22.3 %collective-permute-start.15 = (f32[272,512]{1,0:T(8,128)S(1)}, f32[272,512]{1,0:T(8,128)S(1)}, u32[]{:S(2)}, u32[]{:S(2)}) collective-permute-start(f32[272,512]{1,0:T(8,128)S(1)} %slice_select_fusion.11), channel_id=1, source_target_pairs={{0,2},{1,3},{2,4},{3,5},{4,6},{5,7},{8,10},{9,11},{10,12},{11,13},... | collective-permute-start | bytes 1671176 | tf_op jit(solution)/shard_map/ppermute | solution.py:440
  112.6 14.1 %collective-permute-start.21 = (f32[272,512]{1,0:T(8,128)S(1)}, f32[272,512]{1,0:T(8,128)S(1)}, u32[]{:S(2)}, u32[]{:S(2)}) collective-permute-start(f32[272,512]{1,0:T(8,128)S(1)} %slice_select_fusion.8), channel_id=1, source_target_pairs={{2,0},{3,1},{4,2},{5,3},{6,4},{7,5},{10,8},{11,9},{12,10},{13,11},... | collective-permute-start | bytes 1671176 | tf_op jit(solution)/shard_map/ppermute | solution.py:440
  114.0 20.4 %collective-permute-start.17 = (f32[272,512]{1,0:T(8,128)S(1)}, f32[272,512]{1,0:T(8,128)S(1)}, u32[]{:S(2)}, u32[]{:S(2)}) collective-permute-start(f32[272,512]{1,0:T(8,128)S(1)} %slice_select_fusion.9), channel_id=1, source_target_pairs={{0,2},{1,3},{2,4},{3,5},{4,6},{5,7},{8,10},{9,11},{10,12},{11,13},... | collective-permute-start | bytes 1671176 | tf_op jit(solution)/shard_map/ppermute | solution.py:440
  124.5 13.6 %collective-permute-start.22 = (f32[272,512]{1,0:T(8,128)S(1)}, f32[272,512]{1,0:T(8,128)S(1)}, u32[]{:S(2)}, u32[]{:S(2)}) collective-permute-start(f32[272,512]{1,0:T(8,128)S(1)} %slice_select_fusion.6), channel_id=1, source_target_pairs={{2,0},{3,1},{4,2},{5,3},{10,8},{11,9},{12,10},{13,11},{18,16},{19,... | collective-permute-start | bytes 1671176 | tf_op jit(solution)/shard_map/ppermute | solution.py:440
  126.0 12.1 %collective-permute-start.19 = (f32[272,512]{1,0:T(8,128)S(1)}, f32[272,512]{1,0:T(8,128)S(1)}, u32[]{:S(2)}, u32[]{:S(2)}) collective-permute-start(f32[272,512]{1,0:T(8,128)S(1)} %slice_select_fusion.7), channel_id=1, source_target_pairs={{2,4},{3,5},{4,6},{5,7},{10,12},{11,13},{12,14},{13,15},{18,20},{1... | collective-permute-start | bytes 1671176 | tf_op jit(solution)/shard_map/ppermute | solution.py:440
  134.6 15.4 %collective-permute-start.26 = (f32[272,512]{1,0:T(8,128)S(1)}, f32[272,512]{1,0:T(8,128)S(1)}, u32[]{:S(2)}, u32[]{:S(2)}) collective-permute-start(f32[272,512]{1,0:T(8,128)S(1)} %slice_select_fusion.4), channel_id=1, source_target_pairs={{2,0},{3,1},{4,2},{5,3},{10,8},{11,9},{12,10},{13,11},{18,16},{19,... | collective-permute-start | bytes 1671176 | tf_op jit(solution)/shard_map/ppermute | solution.py:440
  136.0 15.5 %collective-permute-start.23 = (f32[272,512]{1,0:T(8,128)S(1)}, f32[272,512]{1,0:T(8,128)S(1)}, u32[]{:S(2)}, u32[]{:S(2)}) collective-permute-start(f32[272,512]{1,0:T(8,128)S(1)} %slice_select_fusion.5), channel_id=1, source_target_pairs={{2,4},{3,5},{4,6},{5,7},{10,12},{11,13},{12,14},{13,15},{18,20},{1... | collective-permute-start | bytes 1671176 | tf_op jit(solution)/shard_map/ppermute | solution.py:440
  141.6 37.1 %copy-start.3 = (f32[1360,512]{1,0:T(8,128)}, f32[1360,512]{1,0:T(8,128)S(1)}, u32[]{:S(2)}) copy-start(f32[1360,512]{1,0:T(8,128)S(1)} %shard_map.57.refs_0_) | copy-start | bytes 8355844
  141.6 41.9 %collective-permute-start.29 = (f32[1360,512]{1,0:T(8,128)S(1)}, f32[1360,512]{1,0:T(8,128)S(1)}, u32[]{:S(2)}, u32[]{:S(2)}) collective-permute-start(f32[1360,512]{1,0:T(8,128)S(1)} %shard_map.57.refs_0_), channel_id=1, source_target_pairs={{0,1},{1,0},{2,3},{3,2},{4,5},{5,4},{6,7},{7,6},{8,9},{9,8},{10,11... | collective-permute-start | bytes 8355848 | tf_op jit(solution)/shard_map/ppermute | solution.py:389
  150.2 17.5 %collective-permute-start.28 = (f32[272,512]{1,0:T(8,128)S(1)}, f32[272,512]{1,0:T(8,128)S(1)}, u32[]{:S(2)}, u32[]{:S(2)}) collective-permute-start(f32[272,512]{1,0:T(8,128)S(1)} %slice_select_fusion), channel_id=1, source_target_pairs={{2,0},{3,1},{10,8},{11,9},{18,16},{19,17},{26,24},{27,25}} | collective-permute-start | bytes 1671176 | tf_op jit(solution)/shard_map/ppermute | solution.py:440
  151.7 27.7 %copy-start = (f32[1,512,2048]{2,1,0:T(8,128)S(1)}, f32[1,512,2048]{2,1,0:T(8,128)}, u32[]{:S(2)}) copy-start(f32[1,512,2048]{2,1,0:T(8,128)} %param.6) | copy-start | bytes 12582916
  151.7 16.0 %collective-permute-start.25 = (f32[272,512]{1,0:T(8,128)S(1)}, f32[272,512]{1,0:T(8,128)S(1)}, u32[]{:S(2)}, u32[]{:S(2)}) collective-permute-start(f32[272,512]{1,0:T(8,128)S(1)} %slice_select_fusion.1), channel_id=1, source_target_pairs={{4,6},{5,7},{12,14},{13,15},{20,22},{21,23},{28,30},{29,31}} | collective-permute-start | bytes 1671176 | tf_op jit(solution)/shard_map/ppermute | solution.py:440
  152.5 23.7 %collective-permute-start.27 = (f32[272,512]{1,0:T(8,128)S(1)}, f32[272,512]{1,0:T(8,128)S(1)}, u32[]{:S(2)}, u32[]{:S(2)}) collective-permute-start(f32[272,512]{1,0:T(8,128)S(1)} %slice_select_fusion.2), channel_id=1, source_target_pairs={{2,0},{3,1},{10,8},{11,9},{18,16},{19,17},{26,24},{27,25}} | collective-permute-start | bytes 1671176 | tf_op jit(solution)/shard_map/ppermute | solution.py:440
  154.0 22.2 %collective-permute-start.24 = (f32[272,512]{1,0:T(8,128)S(1)}, f32[272,512]{1,0:T(8,128)S(1)}, u32[]{:S(2)}, u32[]{:S(2)}) collective-permute-start(f32[272,512]{1,0:T(8,128)S(1)} %slice_select_fusion.3), channel_id=1, source_target_pairs={{4,6},{5,7},{12,14},{13,15},{20,22},{21,23},{28,30},{29,31}} | collective-permute-start | bytes 1671176 | tf_op jit(solution)/shard_map/ppermute | solution.py:440
  178.7 4.8 %copy-start.4 = (f32[816,512]{1,0:T(8,128)}, f32[816,512]{1,0:T(8,128)S(1)}, u32[]{:S(2)}) copy-start(f32[816,512]{1,0:T(8,128)S(1)} %shard_map.58.refs_1_) | copy-start | bytes 5013508
  178.7 3.6 %collective-permute-start.30 = (f32[816,512]{1,0:T(8,128)S(1)}, f32[816,512]{1,0:T(8,128)S(1)}, u32[]{:S(2)}, u32[]{:S(2)}) collective-permute-start(f32[816,512]{1,0:T(8,128)S(1)} %shard_map.58.refs_1_), channel_id=1, source_target_pairs={{0,1},{1,0},{2,3},{3,2},{4,5},{5,4},{6,7},{7,6},{8,9},{9,8},{10,11... | collective-permute-start | bytes 5013512 | tf_op jit(solution)/shard_map/ppermute | solution.py:389
  181.9 53.0 %collective-permute-start.38 = (f32[256,2048]{1,0:T(8,128)}, f32[256,2048]{1,0:T(8,128)S(1)}, u32[]{:S(2)}, u32[]{:S(2)}) collective-permute-start(f32[256,2048]{1,0:T(8,128)} %slice_bitcast_fusion), channel_id=1, source_target_pairs={{0,2},{1,3},{2,4},{3,5},{4,6},{5,7},{6,0},{7,1},{8,10},{9,11},{10,... | collective-permute-start | bytes 6291464 | tf_op jit(solution)/shard_map/ppermute | solution.py:397
  182.3 1.2 copy-start.6
  183.5 1.6 copy-start.9
  185.1 1.4 copy-start.5
  186.5 1.4 copy-start.7
  214.4 27.8 %collective-permute-start.48 = (f32[32,2048]{1,0:T(8,128)S(1)}, f32[32,2048]{1,0:T(8,128)S(1)}, u32[]{:S(2)}, u32[]{:S(2)}) collective-permute-start(f32[32,2048]{1,0:T(8,128)S(1)} %slice_bitcast_fusion.5), channel_id=1, source_target_pairs={{0,2},{1,3},{2,4},{3,5},{4,6},{5,7},{6,0},{7,1},{8,10},{9,11},{10,... | collective-permute-start | bytes 786440 | tf_op jit(solution)/shard_map/ppermute | solution.py:397
  218.9 38.3 %collective-permute-start.43 = (f32[96,2048]{1,0:T(8,128)}, f32[96,2048]{1,0:T(8,128)S(1)}, u32[]{:S(2)}, u32[]{:S(2)}) collective-permute-start(f32[96,2048]{1,0:T(8,128)} %slice_bitcast_fusion.4), channel_id=1, source_target_pairs={{0,2},{1,3},{2,4},{3,5},{4,6},{5,7},{6,0},{7,1},{8,10},{9,11},{10,... | collective-permute-start | bytes 2359304 | tf_op jit(solution)/shard_map/ppermute | solution.py:397
  235.2 37.2 %collective-permute-start.39 = (f32[256,2048]{1,0:T(8,128)S(1)}, f32[256,2048]{1,0:T(8,128)S(1)}, u32[]{:S(2)}, u32[]{:S(2)}) collective-permute-start(f32[256,2048]{1,0:T(8,128)S(1)} %broadcast_select_fusion), channel_id=1, source_target_pairs={{0,1},{1,0},{2,3},{3,2},{4,5},{5,4},{6,7},{7,6},{8,9},{9,8},{10,11... | collective-permute-start | bytes 6291464 | tf_op jit(solution)/shard_map/ppermute | solution.py:389
  235.4 24.3 %collective-permute-start.34 = (f32[128,2048]{1,0:T(8,128)S(1)}, f32[128,2048]{1,0:T(8,128)S(1)}, u32[]{:S(2)}, u32[]{:S(2)}) collective-permute-start(f32[128,2048]{1,0:T(8,128)S(1)} %broadcast_select_fusion.1), channel_id=1, source_target_pairs={{0,1},{1,0},{2,3},{3,2},{4,5},{5,4},{6,7},{7,6},{8,9},{9,8},{10,11... | collective-permute-start | bytes 3145736 | tf_op jit(solution)/shard_map/ppermute | solution.py:389
  240.7 22.5 %collective-permute-start.31 = (f32[128,512]{1,0:T(8,128)S(1)}, f32[128,512]{1,0:T(8,128)S(1)}, u32[]{:S(2)}, u32[]{:S(2)}) collective-permute-start(f32[128,512]{1,0:T(8,128)S(1)} %get-tuple-element.95), channel_id=1, source_target_pairs={{0,8},{8,0},{16,24},{24,16},{1,9},{9,1},{17,25},{25,17},{2,10},{10... | collective-permute-start | bytes 786440 | tf_op jit(solution)/shard_map/ppermute | solution.py:466
  242.2 21.6 %collective-permute-start.32 = (f32[128,512]{1,0:T(8,128)S(1)}, f32[128,512]{1,0:T(8,128)S(1)}, u32[]{:S(2)}, u32[]{:S(2)}) collective-permute-start(f32[128,512]{1,0:T(8,128)S(1)} %get-tuple-element.96), channel_id=1, source_target_pairs={{0,16},{8,24},{16,0},{24,8},{1,17},{9,25},{17,1},{25,9},{2,18},{10... | collective-permute-start | bytes 786440 | tf_op jit(solution)/shard_map/ppermute | solution.py:466
  257.2 9.0 %collective-permute-start.33 = (f32[128,512]{1,0:T(8,128)S(1)}, f32[128,512]{1,0:T(8,128)S(1)}, u32[]{:S(2)}, u32[]{:S(2)}) collective-permute-start(f32[128,512]{1,0:T(8,128)S(1)} %get-tuple-element.97), channel_id=1, source_target_pairs={{0,24},{8,16},{16,8},{24,0},{1,25},{9,17},{17,9},{25,1},{2,26},{10... | collective-permute-start | bytes 786440 | tf_op jit(solution)/shard_map/ppermute | solution.py:466
  259.7 18.1 %collective-permute-start.44 = (f32[96,2048]{1,0:T(8,128)S(1)}, f32[96,2048]{1,0:T(8,128)S(1)}, u32[]{:S(2)}, u32[]{:S(2)}) collective-permute-start(f32[96,2048]{1,0:T(8,128)S(1)} %broadcast_select_fusion.2), channel_id=1, source_target_pairs={{0,1},{1,0},{2,3},{3,2},{4,5},{5,4},{6,7},{7,6},{8,9},{9,8},{10,11... | collective-permute-start | bytes 2359304 | tf_op jit(solution)/shard_map/ppermute | solution.py:389
  263.2 6.3 %collective-permute-start.35 = (f32[128,256]{1,0:T(8,128)S(1)}, f32[128,256]{1,0:T(8,128)S(1)}, u32[]{:S(2)}, u32[]{:S(2)}) collective-permute-start(f32[128,256]{1,0:T(8,128)S(1)} %get-tuple-element.101), channel_id=1, source_target_pairs={{0,8},{8,0},{16,24},{24,16},{1,9},{9,1},{17,25},{25,17},{2,10},{10... | collective-permute-start | bytes 393224 | tf_op jit(solution)/shard_map/ppermute | solution.py:466
  263.8 7.0 %collective-permute-start.36 = (f32[128,256]{1,0:T(8,128)S(1)}, f32[128,256]{1,0:T(8,128)S(1)}, u32[]{:S(2)}, u32[]{:S(2)}) collective-permute-start(f32[128,256]{1,0:T(8,128)S(1)} %get-tuple-element.102), channel_id=1, source_target_pairs={{0,16},{8,24},{16,0},{24,8},{1,17},{9,25},{17,1},{25,9},{2,18},{10... | collective-permute-start | bytes 393224 | tf_op jit(solution)/shard_map/ppermute | solution.py:466
  266.2 6.2 %collective-permute-start.37 = (f32[128,256]{1,0:T(8,128)S(1)}, f32[128,256]{1,0:T(8,128)S(1)}, u32[]{:S(2)}, u32[]{:S(2)}) collective-permute-start(f32[128,256]{1,0:T(8,128)S(1)} %get-tuple-element.103), channel_id=1, source_target_pairs={{0,24},{8,16},{16,8},{24,0},{1,25},{9,17},{17,9},{25,1},{2,26},{10... | collective-permute-start | bytes 393224 | tf_op jit(solution)/shard_map/ppermute | solution.py:466
  269.5 11.6 %collective-permute-start.49 = (f32[32,2048]{1,0:T(8,128)S(1)}, f32[32,2048]{1,0:T(8,128)S(1)}, u32[]{:S(2)}, u32[]{:S(2)}) collective-permute-start(f32[32,2048]{1,0:T(8,128)S(1)} %broadcast_select_fusion.3), channel_id=1, source_target_pairs={{0,1},{1,0},{2,3},{3,2},{4,5},{5,4},{6,7},{7,6},{8,9},{9,8},{10,11... | collective-permute-start | bytes 786440 | tf_op jit(solution)/shard_map/ppermute | solution.py:389
  283.9 7.1 %collective-permute-start.50 = (f32[128,64]{1,0:T(8,128)S(1)}, f32[128,64]{1,0:T(8,128)S(1)}, u32[]{:S(2)}, u32[]{:S(2)}) collective-permute-start(f32[128,64]{1,0:T(8,128)S(1)} %get-tuple-element.122), channel_id=1, source_target_pairs={{0,8},{8,0},{16,24},{24,16},{1,9},{9,1},{17,25},{25,17},{2,10},{10... | collective-permute-start | bytes 98312 | tf_op jit(solution)/shard_map/ppermute | solution.py:466
  286.0 6.0 %collective-permute-start.51 = (f32[128,64]{1,0:T(8,128)S(1)}, f32[128,64]{1,0:T(8,128)S(1)}, u32[]{:S(2)}, u32[]{:S(2)}) collective-permute-start(f32[128,64]{1,0:T(8,128)S(1)} %get-tuple-element.123), channel_id=1, source_target_pairs={{0,16},{8,24},{16,0},{24,8},{1,17},{9,25},{17,1},{25,9},{2,18},{10... | collective-permute-start | bytes 98312 | tf_op jit(solution)/shard_map/ppermute | solution.py:466
  287.5 5.9 %collective-permute-start.52 = (f32[128,64]{1,0:T(8,128)S(1)}, f32[128,64]{1,0:T(8,128)S(1)}, u32[]{:S(2)}, u32[]{:S(2)}) collective-permute-start(f32[128,64]{1,0:T(8,128)S(1)} %get-tuple-element.124), channel_id=1, source_target_pairs={{0,24},{8,16},{16,8},{24,0},{1,25},{9,17},{17,9},{25,1},{2,26},{10... | collective-permute-start | bytes 98312 | tf_op jit(solution)/shard_map/ppermute | solution.py:466
  287.5 7.8 %collective-permute-start.45 = (f32[128,192]{1,0:T(8,128)S(1)}, f32[128,192]{1,0:T(8,128)S(1)}, u32[]{:S(2)}, u32[]{:S(2)}) collective-permute-start(f32[128,192]{1,0:T(8,128)S(1)} %get-tuple-element.115), channel_id=1, source_target_pairs={{0,8},{8,0},{16,24},{24,16},{1,9},{9,1},{17,25},{25,17},{2,10},{10... | collective-permute-start | bytes 294920 | tf_op jit(solution)/shard_map/ppermute | solution.py:466
  289.5 7.4 %collective-permute-start.46 = (f32[128,192]{1,0:T(8,128)S(1)}, f32[128,192]{1,0:T(8,128)S(1)}, u32[]{:S(2)}, u32[]{:S(2)}) collective-permute-start(f32[128,192]{1,0:T(8,128)S(1)} %get-tuple-element.116), channel_id=1, source_target_pairs={{0,16},{8,24},{16,0},{24,8},{1,17},{9,25},{17,1},{25,9},{2,18},{10... | collective-permute-start | bytes 294920 | tf_op jit(solution)/shard_map/ppermute | solution.py:466
  291.1 8.1 %collective-permute-start.47 = (f32[128,192]{1,0:T(8,128)S(1)}, f32[128,192]{1,0:T(8,128)S(1)}, u32[]{:S(2)}, u32[]{:S(2)}) collective-permute-start(f32[128,192]{1,0:T(8,128)S(1)} %get-tuple-element.117), channel_id=1, source_target_pairs={{0,24},{8,16},{16,8},{24,0},{1,25},{9,17},{17,9},{25,1},{2,26},{10... | collective-permute-start | bytes 294920 | tf_op jit(solution)/shard_map/ppermute | solution.py:466
  291.9 11.3 %collective-permute-start.40 = (f32[128,512]{1,0:T(8,128)S(1)}, f32[128,512]{1,0:T(8,128)S(1)}, u32[]{:S(2)}, u32[]{:S(2)}) collective-permute-start(f32[128,512]{1,0:T(8,128)S(1)} %get-tuple-element.108), channel_id=1, source_target_pairs={{0,8},{8,0},{16,24},{24,16},{1,9},{9,1},{17,25},{25,17},{2,10},{10... | collective-permute-start | bytes 786440 | tf_op jit(solution)/shard_map/ppermute | solution.py:466
  293.4 12.4 %collective-permute-start.41 = (f32[128,512]{1,0:T(8,128)S(1)}, f32[128,512]{1,0:T(8,128)S(1)}, u32[]{:S(2)}, u32[]{:S(2)}) collective-permute-start(f32[128,512]{1,0:T(8,128)S(1)} %get-tuple-element.109), channel_id=1, source_target_pairs={{0,16},{8,24},{16,0},{24,8},{1,17},{9,25},{17,1},{25,9},{2,18},{10... | collective-permute-start | bytes 786440 | tf_op jit(solution)/shard_map/ppermute | solution.py:466
  295.3 11.6 %collective-permute-start.42 = (f32[128,512]{1,0:T(8,128)S(1)}, f32[128,512]{1,0:T(8,128)S(1)}, u32[]{:S(2)}, u32[]{:S(2)}) collective-permute-start(f32[128,512]{1,0:T(8,128)S(1)} %get-tuple-element.110), channel_id=1, source_target_pairs={{0,24},{8,16},{16,8},{24,0},{1,25},{9,17},{17,9},{25,1},{2,26},{10... | collective-permute-start | bytes 786440 | tf_op jit(solution)/shard_map/ppermute | solution.py:466

commit v3 on v2

v3 whole, which is shorter than its diff:
```python
import functools

import jax
import jax.numpy as jnp
from jax import lax
from jax.experimental import pallas as pl
from jax.experimental.pallas import tpu as pltpu
from jax.sharding import PartitionSpec as P

HIGHEST = lax.Precision.HIGHEST
CHUNKS = 17
SKEW = 2
GROUPS = ((0, 9), (9, 14), (14, 17))
TRAIN_CUTS = (128, 256, 128)
MIB = 1024 * 1024
ANY = pl.BlockSpec(memory_space=pl.ANY)
SMEM = pl.BlockSpec(memory_space=pltpu.SMEM)
VMEM = pl.BlockSpec(memory_space=pltpu.VMEM)


def dot(a, b, contract, precision=None):
    return lax.dot_general(
        a, b, (((1,), (contract,)), ((), ())), precision=precision, preferred_element_type=jnp.float32
    )


def parts_of(value):
    high = value.astype(jnp.bfloat16)
    return high, (value - high.astype(jnp.float32)).astype(jnp.bfloat16)


def dot_parts(a, b, contract):
    return dot(a[0], b[0], contract) + (dot(a[0], b[1], contract) + dot(a[1], b[0], contract))


def after(value, *others):
    return lax.optimization_barrier((value, *others))[0]


def partner(section, k, n_sec):
    if n_sec & (n_sec - 1) == 0:
        return section ^ k
    return lax.rem(section + k, n_sec)


def param(limit_mib):
    return pltpu.CompilerParams(vmem_limit_bytes=limit_mib * MIB)


def cost(flops, moved):
    return pl.CostEstimate(flops=flops, bytes_accessed=moved, transcendentals=0)


def invert_kernel(panel_ref, block_ref, packed_ref):
    size = block_ref.shape[0]
    count = 4
    tile = size // count
    row = lax.broadcasted_iota(jnp.int32, (tile, tile), 0)
    col = lax.broadcasted_iota(jnp.int32, (tile, tile), 1)
    spans = [slice(i * tile, (i + 1) * tile) for i in range(count)]
    low = [block_ref[s, s] for s in spans]
    inv = []
    for block in low:
        diagonal = jnp.sum(jnp.where(row == col, block, 0.0), axis=1, keepdims=True)
        inv.append(jnp.where(row == col, 1.0 / diagonal, 0.0))
    width = 1
    while width < tile:
        joins = (row // (2 * width) == col // (2 * width)) & (row // width > col // width)
        half = [dot(jnp.where(joins, low[i], 0.0), inv[i], 0, HIGHEST) for i in range(count)]
        inv = [inv[i] - dot(inv[i], half[i], 0, HIGHEST) for i in range(count)]
        width *= 2
    while len(inv) > 1:
        width = inv[0].shape[0]
        zero = jnp.zeros((width, width), jnp.float32)
        merged = []
        for i in range(0, len(inv), 2):
            below = block_ref[(i + 1) * width : (i + 2) * width, i * width : (i + 1) * width]
            corner = -dot(inv[i + 1], dot(below, inv[i], 0, HIGHEST), 0, HIGHEST)
            top = jnp.concatenate([inv[i], zero], axis=1)
            merged.append(jnp.concatenate([top, jnp.concatenate([corner, inv[i + 1]], axis=1)], axis=0))
        inv = merged
    whole = inv[0]
    mid = tile + tile // 2
    packed_ref[0:tile, :] = whole[3 * tile :, :]
    packed_ref[tile : 2 * tile, 0 : 3 * tile] = whole[2 * tile : 3 * tile, 0 : 3 * tile]
    packed_ref[tile : 2 * tile, 3 * tile :] = whole[0:tile, 0:tile]
    packed_ref[2 * tile :, 0 : 2 * tile] = whole[tile:mid, 0 : 2 * tile]
    packed_ref[2 * tile :, 2 * tile :] = whole[mid : 2 * tile, 0 : 2 * tile]


def inverted_diagonal(slot, panel):
    size = slot.shape[1]
    rows = size // 2 + size // 8
    return pl.pallas_call(
        invert_kernel,
        out_shape=jax.ShapeDtypeStruct((rows, size), jnp.float32),
        grid_spec=pltpu.PrefetchScalarGridSpec(
            num_scalar_prefetch=1,
            grid=(1,),
            in_specs=[pl.BlockSpec((size, size), lambda i, which: (which[0], 0))],
            out_specs=pl.BlockSpec((rows, size), lambda i, which: (0, 0)),
        ),
        compiler_params=param(16),
        cost_estimate=cost(0, 1000),
    )(panel, slot)


class Stream:
    def __init__(self, panels, size):
        self.panels, self.size = panels, size
        self.packed = size // 2 + size // 8
        self.pieces, self.starts, start = [], [], 0
        for j in range(panels):
            for k in [*range(j + 1, panels), None]:
                self.pieces.append((j, k))
                self.starts.append(start)
                start += self.packed if k is None else size
        self.total = start
        self.step = start // CHUNKS

    def rows(self, piece):
        return self.packed if self.pieces[piece][1] is None else self.size

    def panel_start(self, j):
        last = self.panels - 1
        return j * self.packed + self.size * (j * last - (j * (j - 1)) // 2)

    def cuts(self, edges):
        found = []
        for piece, (j, _) in enumerate(self.pieces):
            stop = self.starts[piece] + self.rows(piece)
            for number, (low, high) in enumerate(edges):
                low, high = max(low, self.starts[piece]), min(high, stop)
                if low < high:
                    found.append((j, number, low, high - low))
        return found


def build_kernel(stream, info, slot, peer, packed, peer_packed, out, sems):
    place, me = info[2], info[3]
    pending = []
    for piece, (j, k) in enumerate(stream.pieces):
        count = stream.rows(piece)
        mine, theirs = packed, peer_packed
        if k is not None:
            span = pl.ds(k * stream.size, count)
            mine, theirs = slot.at[span], peer.at[span]
        is_mine = info[5 + j] == me
        target = out.at[pl.ds(pl.multiple_of(place * (SKEW * stream.step) + stream.starts[piece], 8), count)]
        own_copy = pltpu.make_async_copy(mine, target, sems.at[piece])
        peer_copy = pltpu.make_async_copy(theirs, target, sems.at[piece])
        pl.when(is_mine)(own_copy.start)
        pl.when(jnp.logical_not(is_mine))(peer_copy.start)
        pending.append(peer_copy)
    for copy in pending:
        copy.wait()


def build_stream(stream, chips, info, slot, peer, packed, peer_packed):
    rows = stream.total + SKEW * stream.step * (chips - 1)
    return pl.pallas_call(
        functools.partial(build_kernel, stream),
        out_shape=jax.ShapeDtypeStruct((rows, stream.size), jnp.float32),
        in_specs=[SMEM, ANY, ANY, ANY, ANY],
        out_specs=ANY,
        scratch_shapes=[pltpu.SemaphoreType.DMA((len(stream.pieces),))],
        compiler_params=param(4),
        cost_estimate=cost(0, 1000),
    )(info, slot, peer, packed, peer_packed)


def collect_kernel(stream, chips, first, last, info, own, *refs):
    received, out, sems = refs[:-2], refs[-2], refs[-1]
    place = info[2]
    pending = []
    step = stream.step
    edges = [(i * step, (i + 1) * step) for i in range(first, last)]
    for number, (j, i, low, count) in enumerate(stream.cuts(edges)):
        here = info[5 + stream.panels + j] >= place
        target = out.at[pl.ds(low - first * step, count)]
        start = pl.multiple_of(place * (SKEW * step) + low, 8)
        own_copy = pltpu.make_async_copy(own.at[pl.ds(start, count)], target, sems.at[number])
        pl.when(here)(own_copy.start)
        for p in range(1, chips):
            source = received[i + SKEW * (p - 1)].at[pl.ds(low - (first + i) * step, count)]
            copy = pltpu.make_async_copy(source, target, sems.at[number])
            pl.when(jnp.logical_not(here) & (place == p))(copy.start)
        pending.append(own_copy)
    for copy in pending:
        copy.wait()


def collected(stream, chips, first, last, info, own, got):
    received = [got[s] for s in range(first, last + SKEW * (chips - 2))]
    return pl.pallas_call(
        functools.partial(collect_kernel, stream, chips, first, last),
        out_shape=jax.ShapeDtypeStruct(((last - first) * stream.step, stream.size), jnp.float32),
        in_specs=[SMEM] + [ANY] * (1 + len(received)),
        out_specs=ANY,
        scratch_shapes=[pltpu.SemaphoreType.DMA(((last - first) * len(stream.pieces),))],
        compiler_params=param(4),
        cost_estimate=cost(0, 1000),
    )(info, own, *received)


def sweep_kernel(stream, n_sec, info, query, *refs):
    groups = len(GROUPS)
    own, other = refs[:groups], refs[groups : 2 * groups]
    out_high, out_low, low_high, low_low, inv_high, inv_low, pending, part_high, part_low = refs[2 * groups : -2]
    arrived, sems = refs[-2:]
    place, section = info[2], info[4]
    panels, size, step = stream.panels, stream.size, stream.step
    rows = query.shape[0]
    block = rows // n_sec
    tile = size // 4

    copies = []
    for j, group, low, count in stream.cuts([(first * step, last * step) for first, last in GROUPS]):
        inside = pl.ds(low - GROUPS[group][0] * step, count)
        target = arrived.at[pl.ds(low, count)]
        number = len(copies)
        own_copy = pltpu.make_async_copy(own[group].at[inside], target, sems.at[number])
        other_copy = pltpu.make_async_copy(other[group].at[inside], target, sems.at[number])
        ahead = info[5 + panels + j] > place
        pl.when(ahead)(other_copy.start)
        pl.when(jnp.logical_not(ahead))(own_copy.start)
        copies.append((low, count, own_copy))

    for k in range(n_sec):
        start = pl.multiple_of(partner(section, k, n_sec) * block, block)
        for j in range(panels):
            pending[j, k * block : (k + 1) * block, :] = query[pl.ds(start, block), j * size : (j + 1) * size]

    for low, count, copy in copies:
        copy.wait()

        @pl.loop(0, count // 64)
        def _(i):
            span = pl.ds(pl.multiple_of(low + i * 64, 64), 64)
            low_high[span, :], low_low[span, :] = parts_of(arrived[span, :])

    for j in range(panels):
        s = stream.panel_start(j + 1) - stream.packed
        for source, target in ((low_high, inv_high), (low_low, inv_low)):
            target[j] = jnp.zeros((size, size), jnp.bfloat16)
            target[j, 3 * tile :, :] = source[s : s + tile, :]
            target[j, 2 * tile : 3 * tile, : 3 * tile] = source[s + tile : s + 2 * tile, : 3 * tile]
            target[j, :tile, :tile] = source[s + tile : s + 2 * tile, 3 * tile :]
            middle = tile + tile // 2
            target[j, tile:middle, : 2 * tile] = source[s + 2 * tile : s + stream.packed, : 2 * tile]
            target[j, middle : 2 * tile, : 2 * tile] = source[s + 2 * tile : s + stream.packed, 2 * tile :]

    def below(j, k):
        span = pl.ds(pl.multiple_of(stream.panel_start(j) + (k - j - 1) * size, 64), size)
        return low_high[span, :], low_low[span, :]

    @pl.loop(0, panels)
    def _(j):
        solved = dot_parts(parts_of(pending[j]), (inv_high[j], inv_low[j]), 1)
        pending[j] = solved
        part_high[...], part_low[...] = parts_of(solved)

        @pl.loop(j + 1, panels)
        def _(k):
            pending[k] = pending[k] - dot_parts((part_high[...], part_low[...]), below(j, k), 1)

    @pl.loop(0, panels)
    def _(step_number):
        j = panels - 1 - step_number

        @pl.loop(j + 1, panels)
        def _(k):
            pending[j] = pending[j] - dot_parts((out_high[k], out_low[k]), below(j, k), 0)

        answer = dot_parts(parts_of(pending[j]), (inv_high[j], inv_low[j]), 0)
        out_high[j], out_low[j] = parts_of(answer)


def swept(stream, n_sec, info, query, own, other):
    rows = query.shape[0]
    panels, size, total = stream.panels, stream.size, stream.total
    out = jax.ShapeDtypeStruct((panels, rows, size), jnp.bfloat16)
    return pl.pallas_call(
        functools.partial(sweep_kernel, stream, n_sec),
        out_shape=(out, out),
        in_specs=[SMEM, VMEM] + [ANY] * (len(own) + len(other)),
        out_specs=(VMEM, VMEM),
        scratch_shapes=[
            pltpu.VMEM((total, size), jnp.bfloat16),
            pltpu.VMEM((total, size), jnp.bfloat16),
            pltpu.VMEM((panels, size, size), jnp.bfloat16),
            pltpu.VMEM((panels, size, size), jnp.bfloat16),
            pltpu.VMEM((panels, rows, size), jnp.float32),
            pltpu.VMEM((rows, size), jnp.bfloat16),
            pltpu.VMEM((rows, size), jnp.bfloat16),
            pltpu.VMEM((total, size), jnp.float32),
            pltpu.SemaphoreType.DMA((len(stream.pieces) + len(GROUPS),)),
        ],
        compiler_params=param(46),
        cost_estimate=cost(0, 1000),
    )(info, query, *own, *other)


def score_kernel(n_sec, scale, first, counts, high, low, *refs):
    blocks = len(refs) - n_sec - 3
    trains, outs = refs[:blocks], refs[blocks : blocks + n_sec]
    train_high, train_low, total = refs[-3:]
    panels, rows, size = high.shape
    length = trains[0].shape[0]
    for b, train in enumerate(trains):
        for p in range(panels):
            span = slice(b * length, (b + 1) * length)
            train_high[p, span, :], train_low[p, span, :] = parts_of(train[:, p * size : (p + 1) * size])
    total[...] = jnp.zeros_like(total)

    @pl.loop(0, panels)
    def _(p):
        total[...] += dot_parts((high[p], low[p]), (train_high[p], train_low[p]), 1)

    col = lax.broadcasted_iota(jnp.int32, (1, blocks * length), 1)
    limit = jnp.full_like(col, counts[0] - first)
    for b in range(1, blocks):
        limit = jnp.where(col >= b * length, counts[b] - first + b * length, limit)
    factor = jnp.where(col < limit, scale, 0.0).astype(jnp.float32)
    share = rows // n_sec
    for k in range(n_sec):
        outs[k][...] = total[k * share : (k + 1) * share, :] * factor


def scored(n_sec, scale, first, counts, high, low, trains):
    panels, rows, size = high.shape
    cols = sum(t.shape[0] for t in trains)
    return pl.pallas_call(
        functools.partial(score_kernel, n_sec, scale, first),
        out_shape=tuple(jax.ShapeDtypeStruct((rows // n_sec, cols), jnp.float32) for _ in range(n_sec)),
        in_specs=[SMEM] + [VMEM] * (2 + len(trains)),
        out_specs=tuple(VMEM for _ in range(n_sec)),
        scratch_shapes=[
            pltpu.VMEM((panels, cols, size), jnp.bfloat16),
            pltpu.VMEM((panels, cols, size), jnp.bfloat16),
            pltpu.VMEM((rows, cols), jnp.float32),
        ],
        compiler_params=param(24),
        cost_estimate=cost(0, 1000),
    )(counts, high, low, *trains)


def body(query_gradient_stack, train_grads, factor_slots, owner, train_count):
    query, train, slot, owners = query_gradient_stack[0], train_grads[0], factor_slots[0, 0], owner[0]
    rows, coords = query.shape
    size = slot.shape[1]
    panels = coords // size
    n_dp, n_sec = lax.axis_size("dp"), lax.axis_size("section")
    chips = n_dp // 2
    stream = Stream(panels, size)
    step_rows = stream.step
    me = lax.axis_index("dp")
    section = lax.axis_index("section")
    chip, core = lax.shift_right_logical(me, 1), me & 1
    first_core = core == 0
    place = jnp.where(first_core, chip, chips - 1 - chip)
    owner_chip = lax.shift_right_logical(owners, 1)
    owner_place = jnp.where(first_core, owner_chip, chips - 1 - owner_chip)
    info = jnp.concatenate([jnp.stack([chip, core, place, me, section]), owners, owner_place])

    swap_pairs = [(d, d ^ 1) for d in range(n_dp)]
    next_chip = [(d, (d + 2) % n_dp) for d in range(n_dp)]

    def swapped(value):
        return lax.ppermute(value, "dp", swap_pairs)

    cuts = [sum(TRAIN_CUTS[:i]) for i in range(len(TRAIN_CUTS) + 1)]
    train_parts = [train[a:b] for a, b in zip(cuts, cuts[1:])]
    far = [None] * len(train_parts)

    def send_train(index, *deps):
        part = after(train_parts[index], *deps) if deps else train_parts[index]
        far[index] = lax.ppermute(part, "dp", next_chip)

    send_train(0)
    slot, train_count, owners = lax.optimization_barrier((slot, train_count, owners, train_parts[0]))[:3]
    count_2 = lax.ppermute(train_count, "dp", next_chip)
    count_1 = lax.ppermute(train_count, "dp", [(d, (d + 1) % n_dp) for d in range(n_dp)])
    near_counts = jnp.concatenate([count_1, count_2])

    peer = swapped(slot)
    held = jnp.argmax(owners == me).astype(jnp.int32).reshape(1)
    packed = inverted_diagonal(slot, held)
    own_rows = build_stream(stream, chips, info, slot, peer, packed, swapped(packed))

    row = lax.broadcasted_iota(jnp.int32, own_rows.shape[:1] + (1,), 0) - place * (SKEW * step_rows)
    origin = jnp.broadcast_to(owner_place[0], row.shape)
    for j in range(1, panels):
        origin = jnp.where(row >= stream.panel_start(j), owner_place[j], origin)
    from_before = origin < place

    got, own, other = {}, [], []
    sent = [far[0], near_counts]
    for number in range(CHUNKS + SKEW * (chips - 2)):
        span = slice(number * step_rows, (number + 1) * step_rows)
        if number >= SKEW:
            block = jnp.where(from_before[span], after(got[number - SKEW], *sent), own_rows[span])
        else:
            block = after(own_rows[span], *sent)
        pairs = []
        for p in range(chips - 1):
            if 0 <= number - SKEW * p < CHUNKS:
                pairs += [(2 * p, 2 * p + 2), (2 * (chips - 1 - p) + 1, 2 * (chips - 2 - p) + 1)]
        got[number] = lax.ppermute(block, "dp", pairs)
        sent = [block]
        for first, last in GROUPS:
            if number == last - 1 + SKEW * (chips - 2):
                value = collected(stream, chips, first, last, info, own_rows, got)
                own.append(value)
                other.append(swapped(value))
    send_train(1, *sent)
    high, low = swept(stream, n_sec, info, query, own, other)
    for index in range(2, len(train_parts)):
        send_train(index, high)

    scale = (coords * n_sec) ** (-0.5)

    def summed(parts):
        total = parts[0]
        for k in range(1, n_sec):
            if n_sec & (n_sec - 1) == 0:
                pairs = [(s, s ^ k) for s in range(n_sec)]
            else:
                pairs = [(s, (s + k) % n_sec) for s in range(n_sec)]
            total = total + lax.ppermute(parts[k], "section", pairs)
        return total

    parts = scored(n_sec, scale, 0, train_count, high, low, [train])
    own_scores = summed(parts)
    near_scores, far_scores = [], []
    for index, (part, far_part) in enumerate(zip(train_parts, far)):
        near_part = swapped(jnp.where(first_core, part, after(far_part, high if index < 2 else parts[0])))
        length = cuts[index + 1] - cuts[index]
        parts = scored(n_sec, scale, cuts[index], after(near_counts, parts[0]), high, low, [near_part, far_part])
        both = summed(parts)
        near_scores.append(both[:, :length])
        far_scores.append(both[:, length:])
    return jnp.concatenate([own_scores] + near_scores + far_scores, axis=1)[None]


def solution(mesh):
    in_specs = (
        P("section", "dp", None),
        P("section", "dp", None),
        P("section", "dp", None, None),
        P("section", None),
        P("dp"),
    )
    out_specs = P("dp", "section", None)
    return jax.shard_map(body, mesh=mesh, in_specs=in_specs, out_specs=out_specs, check_vma=False)
```

time: 309 us -> 315 us (1.019)
  waiting for transfers between devices: 133 us -> 60.4 us
  starting transfers between devices: 85.1 us -> 155 us
  other arithmetic: 12.5 us -> 21 us
  local copies, waits for them, and re-layouts: 15.1 us -> 18.5 us
  Pallas kernels: 60.9 us -> 57.7 us
    ppermute x24 -> x21, waiting for transfers between devices: 79.9 us -> 18.5 us  [body(): got[number] = lax.ppermute(block, 'dp', pairs)]
    ppermute x8, starting transfers between devices: 2.27 us -> 60.6 us  [swapped(): return lax.ppermute(value, 'dp', swap_pairs)]
    ppermute x4 -> x3, waiting for transfers between devices: 37.2 us -> 9.04 us  [send_train(): far[index] = lax.ppermute(part, 'dp', next_chip)]
    ppermute x24 -> x21, starting transfers between devices: 49.4 us -> 70.6 us  [body(): got[number] = lax.ppermute(block, 'dp', pairs)]
    ppermute x1, waiting for transfers between devices: 0.01 us -> 14.4 us  [body(): count_2 = lax.ppermute(train_count, 'dp', next_chip)]
    select_n x26 -> x23, other arithmetic: 7.55 us -> 15.4 us  [the longest x19 14.8 us: body(): jnp.where(from_before[span], after(got[number - SKEW], *sent), own_rows[s...]
    unnamed x20 -> x41, local copies, waits for them, and re-layouts: 7.88 us -> 13 us
    ppermute x15 -> x12, starting transfers between devices: 21.6 us -> 17 us  [summed(): total = total + lax.ppermute(parts[k], 'section', pairs)]
  transfers between devices with their start and end apart: 53 -> 46, of which waited for: 26 -> 23; matrix products, arithmetic and copies ran while one was open for 6% -> 7% of each run, Pallas kernels for 19% -> 17%
where the time goes in v3:
time: 315 us; the launch traced here: 314 us
  starting transfers between devices  155 us (49%)
  waiting for transfers between devices  60.4 us (19%)
  Pallas kernels  57.7 us (18%)
  other arithmetic  21 us (7%)
  local copies, waits for them, and re-layouts  18.5 us (6%)
    ppermute x21, starting transfers between devices, body(): got[number] = lax.ppermute(block, 'dp', pairs)  70.6 us
    ppermute x8, starting transfers between devices, swapped(): return lax.ppermute(value, 'dp', swap_pairs)  60.6 us
    pallas_call x1, Pallas kernels, swept(): pl.pallas_call(functools.partial(sweep_kernel, stream, n_sec), out_shape=...  26.2 us
    ppermute x21, waiting for transfers between devices, body(): got[number] = lax.ppermute(block, 'dp', pairs)  18.5 us
    pallas_call x4, Pallas kernels, scored(): pl.pallas_call(functools.partial(score_kernel, n_sec, scale, first), out_...  17.1 us
    ppermute x12, starting transfers between devices, summed(): total = total + lax.ppermute(parts[k], 'section', pairs)  17 us
    ppermute x12, waiting for transfers between devices, summed(): total = total + lax.ppermute(parts[k], 'section', pairs)  16.6 us
    select_n x19, other arithmetic, body(): jnp.where(from_before[span], after(got[number - SKEW], *sent), own_rows[s...  14.8 us
  transfers between devices with their start and end apart: 46, of which 23 were waited for; matrix products, arithmetic and copies ran while one was open for 7% of the time, Pallas kernels for 17%

profile of v3, /device:TPU:0, one launch (start us, length us, event | category | flops | bytes accessed | tf_op | source)
XLA Modules:
  0.0 313.9 jit_solution(15951996562538777528)
XLA Ops:
  0.0 3.1 slice_bitcast_fusion.1
  3.6 2.6 collective-permute-start.2
  6.1 1.4 compare_reduce_fusion
  7.5 2.2 copy-done.4
  9.7 5.5 %shard_map.55.packed = f32[320,512]{1,0:T(8,128)S(1)} custom-call(s32[1]{0:T(128)} %bitcast.9.panel_ref, f32[2048,512]{1,0:T(8,128)S(1)} %bitcast.30), custom_call_target="tpu_custom_call" | custom-call | bytes 1000 | tf_op jit(solution)/shard_map/pallas_call | solution.py:94
  15.5 1.6 collective-permute-start.4
  17.8 14.4 %collective-permute-done.4 = s32[1]{0:T(128)} collective-permute-done((s32[1]{0:T(128)}, s32[1]{0:T(128)}, u32[]{:S(2)}, u32[]{:S(2)}) %collective-permute-start.4) | collective-permute-done | bytes 36 | tf_op jit(solution)/shard_map/ppermute | solution.py:382
  32.2 1.3 pad_add_fusion.counts
  33.6 2.2 copy-done.5
  35.7 3.2 %shard_map.56.own = f32[5888,512]{1,0:T(8,128)S(1)} custom-call(s32[13]{0:T(128)S(1)} %concatenate.9.info, f32[2048,512]{1,0:T(8,128)S(1)} %bitcast.31, f32[2048,512]{1,0:T(8,128)} %collective-permute-done.peer, f32[320,512]{1,0:T(8,128)S(1)} %shard_map.55.packed, f32[320,512]{1,0:T(8,128)S(1)} %collective-permute-done.1.peer_packed), custom_call_target="tpu_custom_call" | custom-call | bytes 1000 | tf_op jit(solution)/shard_map/pallas_call | solution.py:161
  39.1 1.4 collective-permute-start.5
  40.5 2.7 fusion
  43.2 1.3 collective-permute-start.6
  44.6 2.6 collective-permute-done.5.refs_0_
  47.3 4.4 %collective-permute-start.7 = (f32[256,512]{1,0:T(8,128)S(1)}, f32[256,512]{1,0:T(8,128)S(1)}, u32[]{:S(2)}, u32[]{:S(2)}) collective-permute-start(f32[256,512]{1,0:T(8,128)S(1)} %slice_select_fusion.18), channel_id=1, source_target_pairs={{0,2},{7,5},{2,4},{5,3},{8,10},{15,13},{10,12},{13,11},{16,18},{23... | collective-permute-start | bytes 1572872 | tf_op jit(solution)/shard_map/ppermute | solution.py:409
  53.9 4.4 %collective-permute-start.8 = (f32[256,512]{1,0:T(8,128)S(1)}, f32[256,512]{1,0:T(8,128)S(1)}, u32[]{:S(2)}, u32[]{:S(2)}) collective-permute-start(f32[256,512]{1,0:T(8,128)S(1)} %slice_select_fusion.17), channel_id=1, source_target_pairs={{0,2},{7,5},{2,4},{5,3},{8,10},{15,13},{10,12},{13,11},{16,18},{23... | collective-permute-start | bytes 1572872 | tf_op jit(solution)/shard_map/ppermute | solution.py:409
  59.5 4.4 %collective-permute-start.9 = (f32[256,512]{1,0:T(8,128)S(1)}, f32[256,512]{1,0:T(8,128)S(1)}, u32[]{:S(2)}, u32[]{:S(2)}) collective-permute-start(f32[256,512]{1,0:T(8,128)S(1)} %slice_select_fusion.16), channel_id=1, source_target_pairs={{0,2},{7,5},{2,4},{5,3},{4,6},{3,1},{8,10},{15,13},{10,12},{13,11}... | collective-permute-start | bytes 1572872 | tf_op jit(solution)/shard_map/ppermute | solution.py:409
  66.2 4.4 %collective-permute-start.10 = (f32[256,512]{1,0:T(8,128)S(1)}, f32[256,512]{1,0:T(8,128)S(1)}, u32[]{:S(2)}, u32[]{:S(2)}) collective-permute-start(f32[256,512]{1,0:T(8,128)S(1)} %slice_select_fusion.15), channel_id=1, source_target_pairs={{0,2},{7,5},{2,4},{5,3},{4,6},{3,1},{8,10},{15,13},{10,12},{13,11}... | collective-permute-start | bytes 1572872 | tf_op jit(solution)/shard_map/ppermute | solution.py:409
  71.8 4.4 %collective-permute-start.11 = (f32[256,512]{1,0:T(8,128)S(1)}, f32[256,512]{1,0:T(8,128)S(1)}, u32[]{:S(2)}, u32[]{:S(2)}) collective-permute-start(f32[256,512]{1,0:T(8,128)S(1)} %slice_select_fusion.14), channel_id=1, source_target_pairs={{0,2},{7,5},{2,4},{5,3},{4,6},{3,1},{8,10},{15,13},{10,12},{13,11}... | collective-permute-start | bytes 1572872 | tf_op jit(solution)/shard_map/ppermute | solution.py:409
  77.2 1.3 slice_select_fusion.13
  78.6 4.7 %collective-permute-start.12 = (f32[256,512]{1,0:T(8,128)S(1)}, f32[256,512]{1,0:T(8,128)S(1)}, u32[]{:S(2)}, u32[]{:S(2)}) collective-permute-start(f32[256,512]{1,0:T(8,128)S(1)} %slice_select_fusion.13), channel_id=1, source_target_pairs={{0,2},{7,5},{2,4},{5,3},{4,6},{3,1},{8,10},{15,13},{10,12},{13,11}... | collective-permute-start | bytes 1572872 | tf_op jit(solution)/shard_map/ppermute | solution.py:409
  84.4 4.0 %collective-permute-start.13 = (f32[256,512]{1,0:T(8,128)S(1)}, f32[256,512]{1,0:T(8,128)S(1)}, u32[]{:S(2)}, u32[]{:S(2)}) collective-permute-start(f32[256,512]{1,0:T(8,128)S(1)} %slice_select_fusion.12), channel_id=1, source_target_pairs={{0,2},{7,5},{2,4},{5,3},{4,6},{3,1},{8,10},{15,13},{10,12},{13,11}... | collective-permute-start | bytes 1572872 | tf_op jit(solution)/shard_map/ppermute | solution.py:409
  88.4 1.5 collective-permute-done.12.refs_7_
  91.0 4.4 %collective-permute-start.14 = (f32[256,512]{1,0:T(8,128)S(1)}, f32[256,512]{1,0:T(8,128)S(1)}, u32[]{:S(2)}, u32[]{:S(2)}) collective-permute-start(f32[256,512]{1,0:T(8,128)S(1)} %slice_select_fusion.11), channel_id=1, source_target_pairs={{0,2},{7,5},{2,4},{5,3},{4,6},{3,1},{8,10},{15,13},{10,12},{13,11}... | collective-permute-start | bytes 1572872 | tf_op jit(solution)/shard_map/ppermute | solution.py:409
  95.5 1.2 slice_select_fusion.10
  96.7 4.4 %collective-permute-start.15 = (f32[256,512]{1,0:T(8,128)S(1)}, f32[256,512]{1,0:T(8,128)S(1)}, u32[]{:S(2)}, u32[]{:S(2)}) collective-permute-start(f32[256,512]{1,0:T(8,128)S(1)} %slice_select_fusion.10), channel_id=1, source_target_pairs={{0,2},{7,5},{2,4},{5,3},{4,6},{3,1},{8,10},{15,13},{10,12},{13,11}... | collective-permute-start | bytes 1572872 | tf_op jit(solution)/shard_map/ppermute | solution.py:409
  103.3 4.4 %collective-permute-start.16 = (f32[256,512]{1,0:T(8,128)S(1)}, f32[256,512]{1,0:T(8,128)S(1)}, u32[]{:S(2)}, u32[]{:S(2)}) collective-permute-start(f32[256,512]{1,0:T(8,128)S(1)} %slice_select_fusion.9), channel_id=1, source_target_pairs={{0,2},{7,5},{2,4},{5,3},{4,6},{3,1},{8,10},{15,13},{10,12},{13,11}... | collective-permute-start | bytes 1572872 | tf_op jit(solution)/shard_map/ppermute | solution.py:409
  107.8 1.2 slice_select_fusion.8
  109.0 4.4 %collective-permute-start.17 = (f32[256,512]{1,0:T(8,128)S(1)}, f32[256,512]{1,0:T(8,128)S(1)}, u32[]{:S(2)}, u32[]{:S(2)}) collective-permute-start(f32[256,512]{1,0:T(8,128)S(1)} %slice_select_fusion.8), channel_id=1, source_target_pairs={{0,2},{7,5},{2,4},{5,3},{4,6},{3,1},{8,10},{15,13},{10,12},{13,11}... | collective-permute-start | bytes 1572872 | tf_op jit(solution)/shard_map/ppermute | solution.py:409
  115.5 4.4 %collective-permute-start.18 = (f32[256,512]{1,0:T(8,128)S(1)}, f32[256,512]{1,0:T(8,128)S(1)}, u32[]{:S(2)}, u32[]{:S(2)}) collective-permute-start(f32[256,512]{1,0:T(8,128)S(1)} %slice_select_fusion.7), channel_id=1, source_target_pairs={{0,2},{7,5},{2,4},{5,3},{4,6},{3,1},{8,10},{15,13},{10,12},{13,11}... | collective-permute-start | bytes 1572872 | tf_op jit(solution)/shard_map/ppermute | solution.py:409
  121.2 4.4 %collective-permute-start.19 = (f32[256,512]{1,0:T(8,128)S(1)}, f32[256,512]{1,0:T(8,128)S(1)}, u32[]{:S(2)}, u32[]{:S(2)}) collective-permute-start(f32[256,512]{1,0:T(8,128)S(1)} %slice_select_fusion.6), channel_id=1, source_target_pairs={{0,2},{7,5},{2,4},{5,3},{4,6},{3,1},{8,10},{15,13},{10,12},{13,11}... | collective-permute-start | bytes 1572872 | tf_op jit(solution)/shard_map/ppermute | solution.py:409
  126.6 2.2 shard_map.57.refs_0_
  129.0 4.4 %collective-permute-start.20 = (f32[256,512]{1,0:T(8,128)S(1)}, f32[256,512]{1,0:T(8,128)S(1)}, u32[]{:S(2)}, u32[]{:S(2)}) collective-permute-start(f32[256,512]{1,0:T(8,128)S(1)} %slice_select_fusion.5), channel_id=1, source_target_pairs={{0,2},{7,5},{2,4},{5,3},{4,6},{3,1},{8,10},{15,13},{10,12},{13,11}... | collective-permute-start | bytes 1572872 | tf_op jit(solution)/shard_map/ppermute | solution.py:409
  133.6 3.2 %collective-permute-start.21 = (f32[256,512]{1,0:T(8,128)S(1)}, f32[256,512]{1,0:T(8,128)S(1)}, u32[]{:S(2)}, u32[]{:S(2)}) collective-permute-start(f32[256,512]{1,0:T(8,128)S(1)} %slice_select_fusion.4), channel_id=1, source_target_pairs={{0,2},{7,5},{2,4},{5,3},{4,6},{3,1},{8,10},{15,13},{10,12},{13,11}... | collective-permute-start | bytes 1572872 | tf_op jit(solution)/shard_map/ppermute | solution.py:409
  136.8 3.3 %collective-permute-done.20.refs_6_.refs_1_ = f32[256,512]{1,0:T(8,128)S(1)} collective-permute-done((f32[256,512]{1,0:T(8,128)S(1)}, f32[256,512]{1,0:T(8,128)S(1)}, u32[]{:S(2)}, u32[]{:S(2)}) %collective-permute-start.20) | collective-permute-done | bytes 524320 | tf_op jit(solution)/shard_map/ppermute | solution.py:409
  140.9 4.8 %collective-permute-done.21.refs_7_.refs_2_ = f32[256,512]{1,0:T(8,128)S(1)} collective-permute-done((f32[256,512]{1,0:T(8,128)S(1)}, f32[256,512]{1,0:T(8,128)S(1)}, u32[]{:S(2)}, u32[]{:S(2)}) %collective-permute-start.21) | collective-permute-done | bytes 524320 | tf_op jit(solution)/shard_map/ppermute | solution.py:409
  147.5 2.2 shard_map.58.refs_1_
  149.7 5.7 %collective-permute-start.27 = (f32[1280,512]{1,0:T(8,128)S(1)}, f32[1280,512]{1,0:T(8,128)S(1)}, u32[]{:S(2)}, u32[]{:S(2)}) collective-permute-start(f32[1280,512]{1,0:T(8,128)S(1)} %shard_map.58.refs_1_), channel_id=1, source_target_pairs={{0,1},{1,0},{2,3},{3,2},{4,5},{5,4},{6,7},{7,6},{8,9},{9,8},{10,11... | collective-permute-start | bytes 7864328 | tf_op jit(solution)/shard_map/ppermute | solution.py:370
  156.2 1.5 slice_bitcast_fusion
  157.8 2.4 collective-permute-start.36
  160.2 1.4 shard_map.59.refs_2_
  161.6 53.1 %collective-permute-start.28 = (f32[768,512]{1,0:T(8,128)S(1)}, f32[768,512]{1,0:T(8,128)S(1)}, u32[]{:S(2)}, u32[]{:S(2)}) collective-permute-start(f32[768,512]{1,0:T(8,128)S(1)} %shard_map.59.refs_2_), channel_id=1, source_target_pairs={{0,1},{1,0},{2,3},{3,2},{4,5},{5,4},{6,7},{7,6},{8,9},{9,8},{10,11... | collective-permute-start | bytes 4718600 | tf_op jit(solution)/shard_map/ppermute | solution.py:370
  215.9 1.9 collective-permute-done.28.refs_5_
  218.9 2.2 copy-done.13
  221.0 1.4 copy-done.8
  222.4 1.4 copy-done.12
  223.9 26.2 %shard_map.60 = (bf16[4,512,512]{2,1,0:T(8,128)(2,1)S(1)}, bf16[4,512,512]{2,1,0:T(8,128)(2,1)S(1)}) custom-call(s32[13]{0:T(128)S(1)} %concatenate.9.info, f32[512,2048]{1,0:T(8,128)} %bitcast.32, f32[2304,512]{1,0:T(8,128)} %copy-done.3, f32[1280,512]{1,0:T(8,128)} %copy-done.6, f32[768,512]{1,0:T(8,128)S(1)} %copy-done.8, f32[2304,512]{1,0:T(8,128)} %copy-done.13, ...), custom_call_target="tpu_custom_call" | custom-call | bytes 1000 | tf_op jit(solution)/shard_map/pallas_call | solution.py:283
  252.5 4.8 %shard_map.61 = (f32[128,512]{1,0:T(8,128)S(1)}, f32[128,512]{1,0:T(8,128)S(1)}, f32[128,512]{1,0:T(8,128)S(1)}, f32[128,512]{1,0:T(8,128)S(1)}) custom-call(s32[1]{0:T(128)S(6)} %copy.12.counts, bf16[4,512,512]{2,1,0:T(8,128)(2,1)S(1)} %get-tuple-element.81.high, bf16[4,512,512]{2,1,0:T(8,128)(2,1)S(1)} %get-tuple-element.82.low, f32[512,2048]{1,0:T(8,128)S(1)} %bitcast.28), custom_call_target="tpu_custom_call" | custom-call | bytes 1000 | tf_op jit(solution)/shard_map/pallas_call | solution.py:333
  257.4 2.7 collective-permute-start.31
  260.9 3.4 %shard_map.62 = (f32[128,256]{1,0:T(8,128)S(1)}, f32[128,256]{1,0:T(8,128)S(1)}, f32[128,256]{1,0:T(8,128)S(1)}, f32[128,256]{1,0:T(8,128)S(1)}) custom-call(s32[2]{0:T(128)S(1)} %pad_add_fusion.counts, bf16[4,512,512]{2,1,0:T(8,128)(2,1)S(1)} %get-tuple-element.81.high, bf16[4,512,512]{2,1,0:T(8,128)(2,1)S(1)} %get-tuple-element.82.low, ...), custom_call_target="tpu_custom_call" | custom-call | bytes 1000 | tf_op jit(solution)/shard_map/pallas_call | solution.py:333
  264.3 5.5 %shard_map.63 = (f32[128,512]{1,0:T(8,128)S(1)}, f32[128,512]{1,0:T(8,128)S(1)}, f32[128,512]{1,0:T(8,128)S(1)}, f32[128,512]{1,0:T(8,128)S(1)}) custom-call(s32[2]{0:T(128)S(1)} %pad_add_fusion.counts, bf16[4,512,512]{2,1,0:T(8,128)(2,1)S(1)} %get-tuple-element.81.high, bf16[4,512,512]{2,1,0:T(8,128)(2,1)S(1)} %get-tuple-element.82.low, ...), custom_call_target="tpu_custom_call" | custom-call | bytes 1000 | tf_op jit(solution)/shard_map/pallas_call | solution.py:333
  269.8 9.0 %collective-permute-done.41.refs_1_ = f32[128,2048]{1,0:T(8,128)S(1)} collective-permute-done((f32[128,2048]{1,0:T(8,128)S(1)}, f32[128,2048]{1,0:T(8,128)S(1)}, u32[]{:S(2)}, u32[]{:S(2)}) %collective-permute-start.41) | collective-permute-done | bytes 1048608 | tf_op jit(solution)/shard_map/ppermute | solution.py:378
  279.1 2.7 collective-permute-start.35
  282.8 2.7 collective-permute-start.40
  286.0 2.1 collective-permute-start.39
  288.2 1.6 collective-permute-done.34
  289.8 1.5 collective-permute-start.38
  291.3 4.0 %collective-permute-done.40 = f32[128,512]{1,0:T(8,128)S(1)} collective-permute-done((f32[128,512]{1,0:T(8,128)S(1)}, f32[128,512]{1,0:T(8,128)S(1)}, u32[]{:S(2)}, u32[]{:S(2)}) %collective-permute-start.40) | collective-permute-done | bytes 262176 | tf_op jit(solution)/shard_map/ppermute | solution.py:430
  295.3 4.6 %collective-permute-done.39 = f32[128,512]{1,0:T(8,128)S(1)} collective-permute-done((f32[128,512]{1,0:T(8,128)S(1)}, f32[128,512]{1,0:T(8,128)S(1)}, u32[]{:S(2)}, u32[]{:S(2)}) %collective-permute-start.39) | collective-permute-done | bytes 262176 | tf_op jit(solution)/shard_map/ppermute | solution.py:430
  300.4 3.4 %shard_map.64 = (f32[128,256]{1,0:T(8,128)S(1)}, f32[128,256]{1,0:T(8,128)S(1)}, f32[128,256]{1,0:T(8,128)S(1)}, f32[128,256]{1,0:T(8,128)S(1)}) custom-call(s32[2]{0:T(128)S(1)} %pad_add_fusion.counts, bf16[4,512,512]{2,1,0:T(8,128)(2,1)S(1)} %get-tuple-element.81.high, bf16[4,512,512]{2,1,0:T(8,128)(2,1)S(1)} %get-tuple-element.82.low, ...), custom_call_target="tpu_custom_call" | custom-call | bytes 1000 | tf_op jit(solution)/shard_map/pallas_call | solution.py:333
  303.9 1.8 collective-permute-start.45
  305.7 1.3 collective-permute-start.44
  307.4 3.5 %collective-permute-done.45 = f32[128,256]{1,0:T(8,128)S(1)} collective-permute-done((f32[128,256]{1,0:T(8,128)S(1)}, f32[128,256]{1,0:T(8,128)S(1)}, u32[]{:S(2)}, u32[]{:S(2)}) %collective-permute-start.45) | collective-permute-done | bytes 131104 | tf_op jit(solution)/shard_map/ppermute | solution.py:430
  311.0 1.7 collective-permute-done.44
  (116 shorter events, 30.8 us)
Async XLA Ops:
  0.0 17.1 %copy-start.17 = (s32[1,4]{1,0:T(1,128)S(1)}, s32[1,4]{1,0:T(1,128)}, u32[]{:S(2)}) copy-start(s32[1,4]{1,0:T(1,128)} %param.8) | copy-start | bytes 52
  3.1 30.4 %collective-permute-start = (f32[2048,512]{1,0:T(8,128)}, f32[2048,512]{1,0:T(8,128)}, u32[]{:S(2)}, u32[]{:S(2)}) collective-permute-start(f32[2048,512]{1,0:T(8,128)} %bitcast.29), channel_id=1, source_target_pairs={{0,1},{1,0},{2,3},{3,2},{4,5},{5,4},{6,7},{7,6},{8,9},{9,8},{10,11... | collective-permute-start | bytes 12582920 | tf_op jit(solution)/shard_map/ppermute | solution.py:370
  3.6 35.5 %collective-permute-start.2 = (f32[128,2048]{1,0:T(8,128)}, f32[128,2048]{1,0:T(8,128)S(1)}, u32[]{:S(2)}, u32[]{:S(2)}) collective-permute-start(f32[128,2048]{1,0:T(8,128)} %get-tuple-element.129), channel_id=1, source_target_pairs={{0,2},{1,3},{2,4},{3,5},{4,6},{5,7},{6,0},{7,1},{8,10},{9,11},{10,... | collective-permute-start | bytes 3145736 | tf_op jit(solution)/shard_map/ppermute | solution.py:378
  7.5 2.2 copy-start.4
  15.2 18.3 %collective-permute-start.1 = (f32[320,512]{1,0:T(8,128)S(1)}, f32[320,512]{1,0:T(8,128)S(1)}, u32[]{:S(2)}, u32[]{:S(2)}) collective-permute-start(f32[320,512]{1,0:T(8,128)S(1)} %shard_map.55.packed), channel_id=1, source_target_pairs={{0,1},{1,0},{2,3},{3,2},{4,5},{5,4},{6,7},{7,6},{8,9},{9,8},{10,11... | collective-permute-start | bytes 1966088 | tf_op jit(solution)/shard_map/ppermute | solution.py:370
  15.5 16.7 %collective-permute-start.4 = (s32[1]{0:T(128)}, s32[1]{0:T(128)}, u32[]{:S(2)}, u32[]{:S(2)}) collective-permute-start(s32[1]{0:T(128)} %param.9), channel_id=1, source_target_pairs={{0,2},{1,3},{2,4},{3,5},{4,6},{5,7},{6,0},{7,1},{8,10},{9,11},{10,... | collective-permute-start | bytes 20 | tf_op jit(solution)/shard_map/ppermute | solution.py:382
  17.1 15.1 %collective-permute-start.3 = (s32[1]{0:T(128)}, s32[1]{0:T(128)}, u32[]{:S(2)}, u32[]{:S(2)}) collective-permute-start(s32[1]{0:T(128)} %param.9), channel_id=1, source_target_pairs={{0,1},{1,2},{2,3},{3,4},{4,5},{5,6},{6,7},{7,0},{8,9},{9,10},{10,1... | collective-permute-start | bytes 20 | tf_op jit(solution)/shard_map/ppermute | solution.py:383
  33.6 2.2 copy-start.5
  38.9 13.8 %copy-start = (f32[5888,512]{1,0:T(8,128)}, f32[5888,512]{1,0:T(8,128)S(1)}, u32[]{:S(2)}) copy-start(f32[5888,512]{1,0:T(8,128)S(1)} %shard_map.56.own) | copy-start | bytes 36175876
  39.0 39.5 %copy-start.9 = (f32[128,2048]{1,0:T(8,128)}, f32[128,2048]{1,0:T(8,128)S(1)}, u32[]{:S(2)}) copy-start(f32[128,2048]{1,0:T(8,128)S(1)} %collective-permute-done.2.refs_1_) | copy-start | bytes 3145732
  39.1 8.1 %collective-permute-start.5 = (f32[256,512]{1,0:T(8,128)S(1)}, f32[256,512]{1,0:T(8,128)S(1)}, u32[]{:S(2)}, u32[]{:S(2)}) collective-permute-start(f32[256,512]{1,0:T(8,128)S(1)} %get-tuple-element.60), channel_id=1, source_target_pairs={{0,2},{7,5},{8,10},{15,13},{16,18},{23,21},{24,26},{31,29}} | collective-permute-start | bytes 1572872 | tf_op jit(solution)/shard_map/ppermute | solution.py:409
  43.2 9.6 %collective-permute-start.6 = (f32[256,512]{1,0:T(8,128)S(1)}, f32[256,512]{1,0:T(8,128)S(1)}, u32[]{:S(2)}, u32[]{:S(2)}) collective-permute-start(f32[256,512]{1,0:T(8,128)S(1)} %get-tuple-element.61), channel_id=1, source_target_pairs={{0,2},{7,5},{8,10},{15,13},{16,18},{23,21},{24,26},{31,29}} | collective-permute-start | bytes 1572872 | tf_op jit(solution)/shard_map/ppermute | solution.py:409
  47.3 11.1 %collective-permute-start.7 = (f32[256,512]{1,0:T(8,128)S(1)}, f32[256,512]{1,0:T(8,128)S(1)}, u32[]{:S(2)}, u32[]{:S(2)}) collective-permute-start(f32[256,512]{1,0:T(8,128)S(1)} %slice_select_fusion.18), channel_id=1, source_target_pairs={{0,2},{7,5},{2,4},{5,3},{8,10},{15,13},{10,12},{13,11},{16,18},{23... | collective-permute-start | bytes 1572872 | tf_op jit(solution)/shard_map/ppermute | solution.py:409
  53.9 11.1 %collective-permute-start.8 = (f32[256,512]{1,0:T(8,128)S(1)}, f32[256,512]{1,0:T(8,128)S(1)}, u32[]{:S(2)}, u32[]{:S(2)}) collective-permute-start(f32[256,512]{1,0:T(8,128)S(1)} %slice_select_fusion.17), channel_id=1, source_target_pairs={{0,2},{7,5},{2,4},{5,3},{8,10},{15,13},{10,12},{13,11},{16,18},{23... | collective-permute-start | bytes 1572872 | tf_op jit(solution)/shard_map/ppermute | solution.py:409
  59.5 11.1 %collective-permute-start.9 = (f32[256,512]{1,0:T(8,128)S(1)}, f32[256,512]{1,0:T(8,128)S(1)}, u32[]{:S(2)}, u32[]{:S(2)}) collective-permute-start(f32[256,512]{1,0:T(8,128)S(1)} %slice_select_fusion.16), channel_id=1, source_target_pairs={{0,2},{7,5},{2,4},{5,3},{4,6},{3,1},{8,10},{15,13},{10,12},{13,11}... | collective-permute-start | bytes 1572872 | tf_op jit(solution)/shard_map/ppermute | solution.py:409
  66.2 11.1 %collective-permute-start.10 = (f32[256,512]{1,0:T(8,128)S(1)}, f32[256,512]{1,0:T(8,128)S(1)}, u32[]{:S(2)}, u32[]{:S(2)}) collective-permute-start(f32[256,512]{1,0:T(8,128)S(1)} %slice_select_fusion.15), channel_id=1, source_target_pairs={{0,2},{7,5},{2,4},{5,3},{4,6},{3,1},{8,10},{15,13},{10,12},{13,11}... | collective-permute-start | bytes 1572872 | tf_op jit(solution)/shard_map/ppermute | solution.py:409
  71.8 11.5 %collective-permute-start.11 = (f32[256,512]{1,0:T(8,128)S(1)}, f32[256,512]{1,0:T(8,128)S(1)}, u32[]{:S(2)}, u32[]{:S(2)}) collective-permute-start(f32[256,512]{1,0:T(8,128)S(1)} %slice_select_fusion.14), channel_id=1, source_target_pairs={{0,2},{7,5},{2,4},{5,3},{4,6},{3,1},{8,10},{15,13},{10,12},{13,11}... | collective-permute-start | bytes 1572872 | tf_op jit(solution)/shard_map/ppermute | solution.py:409
  77.2 49.4 %copy-start.1 = (f32[5888,512]{1,0:T(8,128)S(1)}, f32[5888,512]{1,0:T(8,128)}, u32[]{:S(2)}) copy-start(f32[5888,512]{1,0:T(8,128)} %copy-done) | copy-start | bytes 36175876
  78.6 11.3 %collective-permute-start.12 = (f32[256,512]{1,0:T(8,128)S(1)}, f32[256,512]{1,0:T(8,128)S(1)}, u32[]{:S(2)}, u32[]{:S(2)}) collective-permute-start(f32[256,512]{1,0:T(8,128)S(1)} %slice_select_fusion.13), channel_id=1, source_target_pairs={{0,2},{7,5},{2,4},{5,3},{4,6},{3,1},{8,10},{15,13},{10,12},{13,11}... | collective-permute-start | bytes 1572872 | tf_op jit(solution)/shard_map/ppermute | solution.py:409
  84.4 11.1 %collective-permute-start.13 = (f32[256,512]{1,0:T(8,128)S(1)}, f32[256,512]{1,0:T(8,128)S(1)}, u32[]{:S(2)}, u32[]{:S(2)}) collective-permute-start(f32[256,512]{1,0:T(8,128)S(1)} %slice_select_fusion.12), channel_id=1, source_target_pairs={{0,2},{7,5},{2,4},{5,3},{4,6},{3,1},{8,10},{15,13},{10,12},{13,11}... | collective-permute-start | bytes 1572872 | tf_op jit(solution)/shard_map/ppermute | solution.py:409
  91.0 11.1 %collective-permute-start.14 = (f32[256,512]{1,0:T(8,128)S(1)}, f32[256,512]{1,0:T(8,128)S(1)}, u32[]{:S(2)}, u32[]{:S(2)}) collective-permute-start(f32[256,512]{1,0:T(8,128)S(1)} %slice_select_fusion.11), channel_id=1, source_target_pairs={{0,2},{7,5},{2,4},{5,3},{4,6},{3,1},{8,10},{15,13},{10,12},{13,11}... | collective-permute-start | bytes 1572872 | tf_op jit(solution)/shard_map/ppermute | solution.py:409
  96.7 11.1 %collective-permute-start.15 = (f32[256,512]{1,0:T(8,128)S(1)}, f32[256,512]{1,0:T(8,128)S(1)}, u32[]{:S(2)}, u32[]{:S(2)}) collective-permute-start(f32[256,512]{1,0:T(8,128)S(1)} %slice_select_fusion.10), channel_id=1, source_target_pairs={{0,2},{7,5},{2,4},{5,3},{4,6},{3,1},{8,10},{15,13},{10,12},{13,11}... | collective-permute-start | bytes 1572872 | tf_op jit(solution)/shard_map/ppermute | solution.py:409
  103.3 11.1 %collective-permute-start.16 = (f32[256,512]{1,0:T(8,128)S(1)}, f32[256,512]{1,0:T(8,128)S(1)}, u32[]{:S(2)}, u32[]{:S(2)}) collective-permute-start(f32[256,512]{1,0:T(8,128)S(1)} %slice_select_fusion.9), channel_id=1, source_target_pairs={{0,2},{7,5},{2,4},{5,3},{4,6},{3,1},{8,10},{15,13},{10,12},{13,11}... | collective-permute-start | bytes 1572872 | tf_op jit(solution)/shard_map/ppermute | solution.py:409
  109.0 11.1 %collective-permute-start.17 = (f32[256,512]{1,0:T(8,128)S(1)}, f32[256,512]{1,0:T(8,128)S(1)}, u32[]{:S(2)}, u32[]{:S(2)}) collective-permute-start(f32[256,512]{1,0:T(8,128)S(1)} %slice_select_fusion.8), channel_id=1, source_target_pairs={{0,2},{7,5},{2,4},{5,3},{4,6},{3,1},{8,10},{15,13},{10,12},{13,11}... | collective-permute-start | bytes 1572872 | tf_op jit(solution)/shard_map/ppermute | solution.py:409
  115.5 11.1 %collective-permute-start.18 = (f32[256,512]{1,0:T(8,128)S(1)}, f32[256,512]{1,0:T(8,128)S(1)}, u32[]{:S(2)}, u32[]{:S(2)}) collective-permute-start(f32[256,512]{1,0:T(8,128)S(1)} %slice_select_fusion.7), channel_id=1, source_target_pairs={{0,2},{7,5},{2,4},{5,3},{4,6},{3,1},{8,10},{15,13},{10,12},{13,11}... | collective-permute-start | bytes 1572872 | tf_op jit(solution)/shard_map/ppermute | solution.py:409
  121.2 12.3 %collective-permute-start.19 = (f32[256,512]{1,0:T(8,128)S(1)}, f32[256,512]{1,0:T(8,128)S(1)}, u32[]{:S(2)}, u32[]{:S(2)}) collective-permute-start(f32[256,512]{1,0:T(8,128)S(1)} %slice_select_fusion.6), channel_id=1, source_target_pairs={{0,2},{7,5},{2,4},{5,3},{4,6},{3,1},{8,10},{15,13},{10,12},{13,11}... | collective-permute-start | bytes 1572872 | tf_op jit(solution)/shard_map/ppermute | solution.py:409
  128.8 20.9 %copy-start.3 = (f32[2304,512]{1,0:T(8,128)}, f32[2304,512]{1,0:T(8,128)S(1)}, u32[]{:S(2)}) copy-start(f32[2304,512]{1,0:T(8,128)S(1)} %shard_map.57.refs_0_) | copy-start | bytes 14155780
  128.8 90.0 %collective-permute-start.26 = (f32[2304,512]{1,0:T(8,128)S(1)}, f32[2304,512]{1,0:T(8,128)S(1)}, u32[]{:S(2)}, u32[]{:S(2)}) collective-permute-start(f32[2304,512]{1,0:T(8,128)S(1)} %shard_map.57.refs_0_), channel_id=1, source_target_pairs={{0,1},{1,0},{2,3},{3,2},{4,5},{5,4},{6,7},{7,6},{8,9},{9,8},{10,11... | collective-permute-start | bytes 14155784 | tf_op jit(solution)/shard_map/ppermute | solution.py:370
  129.0 11.1 %collective-permute-start.20 = (f32[256,512]{1,0:T(8,128)S(1)}, f32[256,512]{1,0:T(8,128)S(1)}, u32[]{:S(2)}, u32[]{:S(2)}) collective-permute-start(f32[256,512]{1,0:T(8,128)S(1)} %slice_select_fusion.5), channel_id=1, source_target_pairs={{0,2},{7,5},{2,4},{5,3},{4,6},{3,1},{8,10},{15,13},{10,12},{13,11}... | collective-permute-start | bytes 1572872 | tf_op jit(solution)/shard_map/ppermute | solution.py:409
  133.6 12.1 %collective-permute-start.21 = (f32[256,512]{1,0:T(8,128)S(1)}, f32[256,512]{1,0:T(8,128)S(1)}, u32[]{:S(2)}, u32[]{:S(2)}) collective-permute-start(f32[256,512]{1,0:T(8,128)S(1)} %slice_select_fusion.4), channel_id=1, source_target_pairs={{0,2},{7,5},{2,4},{5,3},{4,6},{3,1},{8,10},{15,13},{10,12},{13,11}... | collective-permute-start | bytes 1572872 | tf_op jit(solution)/shard_map/ppermute | solution.py:409
  140.2 6.3 %collective-permute-start.22 = (f32[256,512]{1,0:T(8,128)S(1)}, f32[256,512]{1,0:T(8,128)S(1)}, u32[]{:S(2)}, u32[]{:S(2)}) collective-permute-start(f32[256,512]{1,0:T(8,128)S(1)} %slice_select_fusion.3), channel_id=1, source_target_pairs={{2,4},{5,3},{4,6},{3,1},{10,12},{13,11},{12,14},{11,9},{18,20},{21... | collective-permute-start | bytes 1572872 | tf_op jit(solution)/shard_map/ppermute | solution.py:409
  145.9 9.6 %collective-permute-start.23 = (f32[256,512]{1,0:T(8,128)S(1)}, f32[256,512]{1,0:T(8,128)S(1)}, u32[]{:S(2)}, u32[]{:S(2)}) collective-permute-start(f32[256,512]{1,0:T(8,128)S(1)} %slice_select_fusion.2), channel_id=1, source_target_pairs={{2,4},{5,3},{4,6},{3,1},{10,12},{13,11},{12,14},{11,9},{18,20},{21... | collective-permute-start | bytes 1572872 | tf_op jit(solution)/shard_map/ppermute | solution.py:409
  146.7 9.6 %copy-start.2 = (f32[1,512,2048]{2,1,0:T(8,128)S(1)}, f32[1,512,2048]{2,1,0:T(8,128)}, u32[]{:S(2)}) copy-start(f32[1,512,2048]{2,1,0:T(8,128)} %param.6) | copy-start | bytes 12582916
  146.7 13.5 %collective-permute-start.24 = (f32[256,512]{1,0:T(8,128)S(1)}, f32[256,512]{1,0:T(8,128)S(1)}, u32[]{:S(2)}, u32[]{:S(2)}) collective-permute-start(f32[256,512]{1,0:T(8,128)S(1)} %slice_select_fusion.1), channel_id=1, source_target_pairs={{4,6},{3,1},{12,14},{11,9},{20,22},{19,17},{28,30},{27,25}} | collective-permute-start | bytes 1572872 | tf_op jit(solution)/shard_map/ppermute | solution.py:409
  149.7 11.8 %copy-start.6 = (f32[1280,512]{1,0:T(8,128)}, f32[1280,512]{1,0:T(8,128)S(1)}, u32[]{:S(2)}) copy-start(f32[1280,512]{1,0:T(8,128)S(1)} %shard_map.58.refs_1_) | copy-start | bytes 7864324
  149.7 66.1 %collective-permute-start.27 = (f32[1280,512]{1,0:T(8,128)S(1)}, f32[1280,512]{1,0:T(8,128)S(1)}, u32[]{:S(2)}, u32[]{:S(2)}) collective-permute-start(f32[1280,512]{1,0:T(8,128)S(1)} %shard_map.58.refs_1_), channel_id=1, source_target_pairs={{0,1},{1,0},{2,3},{3,2},{4,5},{5,4},{6,7},{7,6},{8,9},{9,8},{10,11... | collective-permute-start | bytes 7864328 | tf_op jit(solution)/shard_map/ppermute | solution.py:370
  155.5 4.7 %collective-permute-start.25 = (f32[256,512]{1,0:T(8,128)S(1)}, f32[256,512]{1,0:T(8,128)S(1)}, u32[]{:S(2)}, u32[]{:S(2)}) collective-permute-start(f32[256,512]{1,0:T(8,128)S(1)} %slice_select_fusion), channel_id=1, source_target_pairs={{4,6},{3,1},{12,14},{11,9},{20,22},{19,17},{28,30},{27,25}} | collective-permute-start | bytes 1572872 | tf_op jit(solution)/shard_map/ppermute | solution.py:409
  157.8 92.3 %collective-permute-start.36 = (f32[256,2048]{1,0:T(8,128)}, f32[256,2048]{1,0:T(8,128)S(1)}, u32[]{:S(2)}, u32[]{:S(2)}) collective-permute-start(f32[256,2048]{1,0:T(8,128)} %slice_bitcast_fusion), channel_id=1, source_target_pairs={{0,2},{1,3},{2,4},{3,5},{4,6},{5,7},{6,0},{7,1},{8,10},{9,11},{10,... | collective-permute-start | bytes 6291464 | tf_op jit(solution)/shard_map/ppermute | solution.py:378
  161.6 56.2 %collective-permute-start.28 = (f32[768,512]{1,0:T(8,128)S(1)}, f32[768,512]{1,0:T(8,128)S(1)}, u32[]{:S(2)}, u32[]{:S(2)}) collective-permute-start(f32[768,512]{1,0:T(8,128)S(1)} %shard_map.59.refs_2_), channel_id=1, source_target_pairs={{0,1},{1,0},{2,3},{3,2},{4,5},{5,4},{6,7},{7,6},{8,9},{9,8},{10,11... | collective-permute-start | bytes 4718600 | tf_op jit(solution)/shard_map/ppermute | solution.py:370
  214.7 1.2 copy-start.7
  215.8 3.0 copy-start.14
  217.7 1.1 copy-start.11
  218.9 2.2 copy-start.13
  221.0 1.4 copy-start.8
  222.4 1.4 copy-start.12
  250.0 1.2 copy-start.10
  250.1 1.8 copy-start.15
  250.4 13.9 %collective-permute-start.37 = (f32[256,2048]{1,0:T(8,128)S(1)}, f32[256,2048]{1,0:T(8,128)S(1)}, u32[]{:S(2)}, u32[]{:S(2)}) collective-permute-start(f32[256,2048]{1,0:T(8,128)S(1)} %broadcast_select_fusion), channel_id=1, source_target_pairs={{0,1},{1,0},{2,3},{3,2},{4,5},{5,4},{6,7},{7,6},{8,9},{9,8},{10,11... | collective-permute-start | bytes 6291464 | tf_op jit(solution)/shard_map/ppermute | solution.py:370
  251.4 9.5 %collective-permute-start.32 = (f32[128,2048]{1,0:T(8,128)S(1)}, f32[128,2048]{1,0:T(8,128)S(1)}, u32[]{:S(2)}, u32[]{:S(2)}) collective-permute-start(f32[128,2048]{1,0:T(8,128)S(1)} %broadcast_select_fusion.2), channel_id=1, source_target_pairs={{0,1},{1,0},{2,3},{3,2},{4,5},{5,4},{6,7},{7,6},{8,9},{9,8},{10,11... | collective-permute-start | bytes 3145736 | tf_op jit(solution)/shard_map/ppermute | solution.py:370
  251.9 27.0 %collective-permute-start.41 = (f32[128,2048]{1,0:T(8,128)S(1)}, f32[128,2048]{1,0:T(8,128)S(1)}, u32[]{:S(2)}, u32[]{:S(2)}) collective-permute-start(f32[128,2048]{1,0:T(8,128)S(1)} %copy-done.15), channel_id=1, source_target_pairs={{0,2},{1,3},{2,4},{3,5},{4,6},{5,7},{6,0},{7,1},{8,10},{9,11},{10,... | collective-permute-start | bytes 3145736 | tf_op jit(solution)/shard_map/ppermute | solution.py:378
  257.4 24.5 %collective-permute-start.31 = (f32[128,512]{1,0:T(8,128)S(1)}, f32[128,512]{1,0:T(8,128)S(1)}, u32[]{:S(2)}, u32[]{:S(2)}) collective-permute-start(f32[128,512]{1,0:T(8,128)S(1)} %get-tuple-element.86), channel_id=1, source_target_pairs={{0,24},{8,16},{16,8},{24,0},{1,25},{9,17},{17,9},{25,1},{2,26},{10... | collective-permute-start | bytes 786440 | tf_op jit(solution)/shard_map/ppermute | solution.py:430
  260.1 22.6 %collective-permute-start.30 = (f32[128,512]{1,0:T(8,128)S(1)}, f32[128,512]{1,0:T(8,128)S(1)}, u32[]{:S(2)}, u32[]{:S(2)}) collective-permute-start(f32[128,512]{1,0:T(8,128)S(1)} %get-tuple-element.85), channel_id=1, source_target_pairs={{0,16},{8,24},{16,0},{24,8},{1,17},{9,25},{17,1},{25,9},{2,18},{10... | collective-permute-start | bytes 786440 | tf_op jit(solution)/shard_map/ppermute | solution.py:430
  260.9 21.8 %collective-permute-start.29 = (f32[128,512]{1,0:T(8,128)S(1)}, f32[128,512]{1,0:T(8,128)S(1)}, u32[]{:S(2)}, u32[]{:S(2)}) collective-permute-start(f32[128,512]{1,0:T(8,128)S(1)} %get-tuple-element.84), channel_id=1, source_target_pairs={{0,8},{8,0},{16,24},{24,16},{1,9},{9,1},{17,25},{25,17},{2,10},{10... | collective-permute-start | bytes 786440 | tf_op jit(solution)/shard_map/ppermute | solution.py:430
  279.0 21.4 %collective-permute-start.42 = (f32[128,2048]{1,0:T(8,128)S(1)}, f32[128,2048]{1,0:T(8,128)S(1)}, u32[]{:S(2)}, u32[]{:S(2)}) collective-permute-start(f32[128,2048]{1,0:T(8,128)S(1)} %broadcast_select_fusion.1), channel_id=1, source_target_pairs={{0,1},{1,0},{2,3},{3,2},{4,5},{5,4},{6,7},{7,6},{8,9},{9,8},{10,11... | collective-permute-start | bytes 3145736 | tf_op jit(solution)/shard_map/ppermute | solution.py:370
  279.1 6.9 %collective-permute-start.35 = (f32[128,256]{1,0:T(8,128)S(1)}, f32[128,256]{1,0:T(8,128)S(1)}, u32[]{:S(2)}, u32[]{:S(2)}) collective-permute-start(f32[128,256]{1,0:T(8,128)S(1)} %get-tuple-element.92), channel_id=1, source_target_pairs={{0,24},{8,16},{16,8},{24,0},{1,25},{9,17},{17,9},{25,1},{2,26},{10... | collective-permute-start | bytes 393224 | tf_op jit(solution)/shard_map/ppermute | solution.py:430
  281.8 7.9 %collective-permute-start.34 = (f32[128,256]{1,0:T(8,128)S(1)}, f32[128,256]{1,0:T(8,128)S(1)}, u32[]{:S(2)}, u32[]{:S(2)}) collective-permute-start(f32[128,256]{1,0:T(8,128)S(1)} %get-tuple-element.91), channel_id=1, source_target_pairs={{0,16},{8,24},{16,0},{24,8},{1,17},{9,25},{17,1},{25,9},{2,18},{10... | collective-permute-start | bytes 393224 | tf_op jit(solution)/shard_map/ppermute | solution.py:430
  282.7 8.6 %collective-permute-start.33 = (f32[128,256]{1,0:T(8,128)S(1)}, f32[128,256]{1,0:T(8,128)S(1)}, u32[]{:S(2)}, u32[]{:S(2)}) collective-permute-start(f32[128,256]{1,0:T(8,128)S(1)} %get-tuple-element.90), channel_id=1, source_target_pairs={{0,8},{8,0},{16,24},{24,16},{1,9},{9,1},{17,25},{25,17},{2,10},{10... | collective-permute-start | bytes 393224 | tf_op jit(solution)/shard_map/ppermute | solution.py:430
  282.8 12.6 %collective-permute-start.40 = (f32[128,512]{1,0:T(8,128)S(1)}, f32[128,512]{1,0:T(8,128)S(1)}, u32[]{:S(2)}, u32[]{:S(2)}) collective-permute-start(f32[128,512]{1,0:T(8,128)S(1)} %get-tuple-element.99), channel_id=1, source_target_pairs={{0,24},{8,16},{16,8},{24,0},{1,25},{9,17},{17,9},{25,1},{2,26},{10... | collective-permute-start | bytes 786440 | tf_op jit(solution)/shard_map/ppermute | solution.py:430
  286.0 13.9 %collective-permute-start.39 = (f32[128,512]{1,0:T(8,128)S(1)}, f32[128,512]{1,0:T(8,128)S(1)}, u32[]{:S(2)}, u32[]{:S(2)}) collective-permute-start(f32[128,512]{1,0:T(8,128)S(1)} %get-tuple-element.98), channel_id=1, source_target_pairs={{0,16},{8,24},{16,0},{24,8},{1,17},{9,25},{17,1},{25,9},{2,18},{10... | collective-permute-start | bytes 786440 | tf_op jit(solution)/shard_map/ppermute | solution.py:430
  289.8 10.6 %collective-permute-start.38 = (f32[128,512]{1,0:T(8,128)S(1)}, f32[128,512]{1,0:T(8,128)S(1)}, u32[]{:S(2)}, u32[]{:S(2)}) collective-permute-start(f32[128,512]{1,0:T(8,128)S(1)} %get-tuple-element.97), channel_id=1, source_target_pairs={{0,8},{8,0},{16,24},{24,16},{1,9},{9,1},{17,25},{25,17},{2,10},{10... | collective-permute-start | bytes 786440 | tf_op jit(solution)/shard_map/ppermute | solution.py:430
  303.9 7.1 %collective-permute-start.45 = (f32[128,256]{1,0:T(8,128)S(1)}, f32[128,256]{1,0:T(8,128)S(1)}, u32[]{:S(2)}, u32[]{:S(2)}) collective-permute-start(f32[128,256]{1,0:T(8,128)S(1)} %get-tuple-element.106), channel_id=1, source_target_pairs={{0,24},{8,16},{16,8},{24,0},{1,25},{9,17},{17,9},{25,1},{2,26},{10... | collective-permute-start | bytes 393224 | tf_op jit(solution)/shard_map/ppermute | solution.py:430
  305.7 7.0 %collective-permute-start.44 = (f32[128,256]{1,0:T(8,128)S(1)}, f32[128,256]{1,0:T(8,128)S(1)}, u32[]{:S(2)}, u32[]{:S(2)}) collective-permute-start(f32[128,256]{1,0:T(8,128)S(1)} %get-tuple-element.105), channel_id=1, source_target_pairs={{0,16},{8,24},{16,0},{24,8},{1,17},{9,25},{17,1},{25,9},{2,18},{10... | collective-permute-start | bytes 393224 | tf_op jit(solution)/shard_map/ppermute | solution.py:430
  307.0 5.8 %collective-permute-start.43 = (f32[128,256]{1,0:T(8,128)S(1)}, f32[128,256]{1,0:T(8,128)S(1)}, u32[]{:S(2)}, u32[]{:S(2)}) collective-permute-start(f32[128,256]{1,0:T(8,128)S(1)} %get-tuple-element.104), channel_id=1, source_target_pairs={{0,8},{8,0},{16,24},{24,16},{1,9},{9,1},{17,25},{25,17},{2,10},{10... | collective-permute-start | bytes 393224 | tf_op jit(solution)/shard_map/ppermute | solution.py:430
  313.0 0.9 copy-start.16

commit v4 on v3

--- a/solution.py
+++ b/solution.py
@@ -11,9 +11,9 @@
 CHUNKS = 17
 SKEW = 2
 GROUPS = ((0, 9), (9, 14), (14, 17))
-TRAIN_CUTS = (128, 256, 128)
+TRAIN_CUTS = (96, 256, 160)
 MIB = 1024 * 1024
-ANY = pl.BlockSpec(memory_space=pl.ANY)
+HBM = pl.BlockSpec(memory_space=pltpu.HBM)
 SMEM = pl.BlockSpec(memory_space=pltpu.SMEM)
 VMEM = pl.BlockSpec(memory_space=pltpu.VMEM)
 
@@ -33,10 +33,6 @@
     return dot(a[0], b[0], contract) + (dot(a[0], b[1], contract) + dot(a[1], b[0], contract))
 
 
-def after(value, *others):
-    return lax.optimization_barrier((value, *others))[0]
-
-
 def partner(section, k, n_sec):
     if n_sec & (n_sec - 1) == 0:
         return section ^ k
@@ -51,8 +47,58 @@
     return pl.CostEstimate(flops=flops, bytes_accessed=moved, transcendentals=0)
 
 
-def invert_kernel(panel_ref, block_ref, packed_ref):
+def copy_kernel(start, source, *refs):
+    out, sem = refs[-2:]
+    copy = pltpu.make_async_copy(source.at[pl.ds(start, out.shape[0])], out, sem)
+    copy.start()
+    copy.wait()
+
+
+def copied(source, start, length, *earlier):
+    return pl.pallas_call(
+        functools.partial(copy_kernel, start),
+        out_shape=jax.ShapeDtypeStruct((length, source.shape[1]), source.dtype),
+        in_specs=[HBM] * (1 + len(earlier)),
+        out_specs=HBM,
+        scratch_shapes=[pltpu.SemaphoreType.DMA],
+        compiler_params=param(4),
+        cost_estimate=cost(0, 1000),
+    )(source, *earlier)
+
+
+def choose_kernel(start, info, train, far, *refs):
+    out, sem = refs[-2:]
+    own_copy = pltpu.make_async_copy(train.at[pl.ds(start, out.shape[0])], out, sem)
+    far_copy = pltpu.make_async_copy(far, out, sem)
+    pl.when(info[1] == 0)(own_copy.start)
+    pl.when(info[1] != 0)(far_copy.start)
+    own_copy.wait()
+
+
+def chosen(info, train, start, far, *earlier):
+    return pl.pallas_call(
+        functools.partial(choose_kernel, start),
+        out_shape=jax.ShapeDtypeStruct(far.shape, far.dtype),
+        in_specs=[SMEM] + [HBM] * (2 + len(earlier)),
+        out_specs=HBM,
+        scratch_shapes=[pltpu.SemaphoreType.DMA],
+        compiler_params=param(4),
+        cost_estimate=cost(0, 1000),
+    )(info, train, far, *earlier)
+
+
+def corner(value):
+    return value[:8, :128]
+
+
+def invert_kernel(panels, info, slot, packed_ref, block_ref, sem):
     size = block_ref.shape[0]
+    held = 0
+    for j in range(1, panels):
+        held = jnp.where(info[5 + j] == info[3], j, held)
+    copy = pltpu.make_async_copy(slot.at[pl.ds(pl.multiple_of(held * size, size), size)], block_ref, sem)
+    copy.start()
+    copy.wait()
     count = 4
     tile = size // count
     row = lax.broadcasted_iota(jnp.int32, (tile, tile), 0)
@@ -88,21 +134,18 @@
     packed_ref[2 * tile :, 2 * tile :] = whole[mid : 2 * tile, 0 : 2 * tile]
 
 
-def inverted_diagonal(slot, panel):
+def inverted_diagonal(panels, info, slot):
     size = slot.shape[1]
     rows = size // 2 + size // 8
     return pl.pallas_call(
-        invert_kernel,
+        functools.partial(invert_kernel, panels),
         out_shape=jax.ShapeDtypeStruct((rows, size), jnp.float32),
-        grid_spec=pltpu.PrefetchScalarGridSpec(
-            num_scalar_prefetch=1,
-            grid=(1,),
-            in_specs=[pl.BlockSpec((size, size), lambda i, which: (which[0], 0))],
-            out_specs=pl.BlockSpec((rows, size), lambda i, which: (0, 0)),
-        ),
+        in_specs=[SMEM, HBM],
+        out_specs=VMEM,
+        scratch_shapes=[pltpu.VMEM((size, size), jnp.float32), pltpu.SemaphoreType.DMA],
         compiler_params=param(16),
         cost_estimate=cost(0, 1000),
-    )(panel, slot)
+    )(info, slot)
 
 
 class Stream:
@@ -136,7 +179,7 @@
         return found
 
 
-def build_kernel(stream, info, slot, peer, packed, peer_packed, out, sems):
+def build_kernel(stream, info, slot, peer, packed, peer_packed, earlier, out, sems):
     place, me = info[2], info[3]
     pending = []
     for piece, (j, k) in enumerate(stream.pieces):
@@ -156,20 +199,58 @@
         copy.wait()
 
 
-def build_stream(stream, chips, info, slot, peer, packed, peer_packed):
+def build_stream(stream, chips, info, slot, peer, packed, peer_packed, earlier):
     rows = stream.total + SKEW * stream.step * (chips - 1)
     return pl.pallas_call(
         functools.partial(build_kernel, stream),
         out_shape=jax.ShapeDtypeStruct((rows, stream.size), jnp.float32),
-        in_specs=[SMEM, ANY, ANY, ANY, ANY],
-        out_specs=ANY,
+        in_specs=[SMEM] + [HBM] * 5,
+        out_specs=HBM,
         scratch_shapes=[pltpu.SemaphoreType.DMA((len(stream.pieces),))],
         compiler_params=param(4),
         cost_estimate=cost(0, 1000),
-    )(info, slot, peer, packed, peer_packed)
-
-
-def collect_kernel(stream, chips, first, last, info, own, *refs):
+    )(info, slot, peer, packed, peer_packed, earlier)
+
+
+def step_kernel(stream, number, info, own, *refs):
+    out, sems = refs[-2:]
+    unit = stream.packed // 5
+    place = info[2]
+    pending = []
+    for g in range(stream.step // unit):
+        inside = pl.ds(g * unit, unit)
+        copy = pltpu.make_async_copy(
+            own.at[pl.ds(number * stream.step + g * unit, unit)], out.at[inside], sems.at[g]
+        )
+        pending.append(copy)
+        if number < SKEW:
+            copy.start()
+            continue
+        row = number * stream.step + g * unit - place * (SKEW * stream.step)
+        origin = info[5 + stream.panels]
+        for j in range(1, stream.panels):
+            origin = jnp.where(row >= stream.panel_start(j), info[5 + stream.panels + j], origin)
+        passing = pltpu.make_async_copy(refs[0].at[inside], out.at[inside], sems.at[g])
+        pl.when(origin < place)(passing.start)
+        pl.when(origin >= place)(copy.start)
+    for copy in pending:
+        copy.wait()
+
+
+def step_block(stream, number, info, own, got, earlier):
+    operands = ([got[number - SKEW]] if number >= SKEW else []) + earlier
+    return pl.pallas_call(
+        functools.partial(step_kernel, stream, number),
+        out_shape=jax.ShapeDtypeStruct((stream.step, stream.size), jnp.float32),
+        in_specs=[SMEM] + [HBM] * (1 + len(operands)),
+        out_specs=HBM,
+        scratch_shapes=[pltpu.SemaphoreType.DMA((stream.step * 5 // stream.packed,))],
+        compiler_params=param(4),
+        cost_estimate=cost(0, 1000),
+    )(info, own, *operands)
+
+
+def collect_kernel(stream, chips, first, last, info, counts, own, *refs):
     received, out, sems = refs[:-2], refs[-2], refs[-1]
     place = info[2]
     pending = []
@@ -190,54 +271,65 @@
         copy.wait()
 
 
-def collected(stream, chips, first, last, info, own, got):
+def collected(stream, chips, first, last, info, counts, own, got):
     received = [got[s] for s in range(first, last + SKEW * (chips - 2))]
     return pl.pallas_call(
         functools.partial(collect_kernel, stream, chips, first, last),
         out_shape=jax.ShapeDtypeStruct(((last - first) * stream.step, stream.size), jnp.float32),
-        in_specs=[SMEM] + [ANY] * (1 + len(received)),
-        out_specs=ANY,
+        in_specs=[SMEM, SMEM] + [HBM] * (1 + len(received)),
+        out_specs=HBM,
         scratch_shapes=[pltpu.SemaphoreType.DMA(((last - first) * len(stream.pieces),))],
         compiler_params=param(4),
         cost_estimate=cost(0, 1000),
-    )(info, own, *received)
-
-
-def sweep_kernel(stream, n_sec, info, query, *refs):
+    )(info, counts, own, *received)
+
+
+def sweep_kernel(stream, n_sec, info, earlier, query, *refs):
     groups = len(GROUPS)
     own, other = refs[:groups], refs[groups : 2 * groups]
-    out_high, out_low, low_high, low_low, inv_high, inv_low, pending, part_high, part_low = refs[2 * groups : -2]
+    out_high, out_low, done_ref, low_high, low_low, inv_high, inv_low, pending, part_high, part_low = refs[2 * groups : -2]
     arrived, sems = refs[-2:]
+    done_ref[...] = jnp.zeros_like(done_ref)
     place, section = info[2], info[4]
     panels, size, step = stream.panels, stream.size, stream.step
     rows = query.shape[0]
     block = rows // n_sec
     tile = size // 4
 
+    slots = arrived.shape[0]
+    found = stream.cuts([(first * step, last * step) for first, last in GROUPS])
     copies = []
-    for j, group, low, count in stream.cuts([(first * step, last * step) for first, last in GROUPS]):
+
+    def fetch(number):
+        j, group, low, count = found[number]
         inside = pl.ds(low - GROUPS[group][0] * step, count)
-        target = arrived.at[pl.ds(low, count)]
-        number = len(copies)
+        target = arrived.at[number % slots, pl.ds(0, count)]
         own_copy = pltpu.make_async_copy(own[group].at[inside], target, sems.at[number])
         other_copy = pltpu.make_async_copy(other[group].at[inside], target, sems.at[number])
         ahead = info[5 + panels + j] > place
         pl.when(ahead)(other_copy.start)
         pl.when(jnp.logical_not(ahead))(own_copy.start)
-        copies.append((low, count, own_copy))
+        copies.append(own_copy)
+
+    for number in range(slots):
+        fetch(number)
 
     for k in range(n_sec):
         start = pl.multiple_of(partner(section, k, n_sec) * block, block)
         for j in range(panels):
             pending[j, k * block : (k + 1) * block, :] = query[pl.ds(start, block), j * size : (j + 1) * size]
 
-    for low, count, copy in copies:
-        copy.wait()
+    for number, (_, _, low, count) in enumerate(found):
+        copies[number].wait()
 
         @pl.loop(0, count // 64)
         def _(i):
+            inside = pl.ds(pl.multiple_of(i * 64, 64), 64)
             span = pl.ds(pl.multiple_of(low + i * 64, 64), 64)
-            low_high[span, :], low_low[span, :] = parts_of(arrived[span, :])
+            low_high[span, :], low_low[span, :] = parts_of(arrived[number % slots, inside, :])
+
+        if number + slots < len(found):
+            fetch(number + slots)
 
     for j in range(panels):
         s = stream.panel_start(j + 1) - stream.packed
@@ -276,15 +368,15 @@
         out_high[j], out_low[j] = parts_of(answer)
 
 
-def swept(stream, n_sec, info, query, own, other):
+def swept(stream, n_sec, info, earlier, query, own, other):
     rows = query.shape[0]
     panels, size, total = stream.panels, stream.size, stream.total
     out = jax.ShapeDtypeStruct((panels, rows, size), jnp.bfloat16)
     return pl.pallas_call(
         functools.partial(sweep_kernel, stream, n_sec),
-        out_shape=(out, out),
-        in_specs=[SMEM, VMEM] + [ANY] * (len(own) + len(other)),
-        out_specs=(VMEM, VMEM),
+        out_shape=(out, out, jax.ShapeDtypeStruct((8, 128), jnp.float32)),
+        in_specs=[SMEM, HBM, VMEM] + [HBM] * (len(own) + len(other)),
+        out_specs=(VMEM, VMEM, VMEM),
         scratch_shapes=[
             pltpu.VMEM((total, size), jnp.bfloat16),
             pltpu.VMEM((total, size), jnp.bfloat16),
@@ -293,15 +385,15 @@
             pltpu.VMEM((panels, rows, size), jnp.float32),
             pltpu.VMEM((rows, size), jnp.bfloat16),
             pltpu.VMEM((rows, size), jnp.bfloat16),
-            pltpu.VMEM((total, size), jnp.float32),
+            pltpu.VMEM((4, size, size), jnp.float32),
             pltpu.SemaphoreType.DMA((len(stream.pieces) + len(GROUPS),)),
         ],
-        compiler_params=param(46),
-        cost_estimate=cost(0, 1000),
-    )(info, query, *own, *other)
-
-
-def score_kernel(n_sec, scale, first, counts, high, low, *refs):
+        compiler_params=param(40),
+        cost_estimate=cost(0, 1000),
+    )(info, earlier, query, *own, *other)
+
+
+def score_kernel(n_sec, scale, first, counts, earlier, high, low, *refs):
     blocks = len(refs) - n_sec - 3
     trains, outs = refs[:blocks], refs[blocks : blocks + n_sec]
     train_high, train_low, total = refs[-3:]
@@ -327,13 +419,13 @@
         outs[k][...] = total[k * share : (k + 1) * share, :] * factor
 
 
-def scored(n_sec, scale, first, counts, high, low, trains):
+def scored(n_sec, scale, first, counts, earlier, high, low, trains):
     panels, rows, size = high.shape
     cols = sum(t.shape[0] for t in trains)
     return pl.pallas_call(
         functools.partial(score_kernel, n_sec, scale, first),
         out_shape=tuple(jax.ShapeDtypeStruct((rows // n_sec, cols), jnp.float32) for _ in range(n_sec)),
-        in_specs=[SMEM] + [VMEM] * (2 + len(trains)),
+        in_specs=[SMEM, HBM] + [VMEM] * (2 + len(trains)),
         out_specs=tuple(VMEM for _ in range(n_sec)),
         scratch_shapes=[
             pltpu.VMEM((panels, cols, size), jnp.bfloat16),
@@ -342,7 +434,7 @@
         ],
         compiler_params=param(24),
         cost_estimate=cost(0, 1000),
-    )(counts, high, low, *trains)
+    )(counts, earlier, high, low, *trains)
 
 
 def body(query_gradient_stack, train_grads, factor_slots, owner, train_count):
@@ -353,7 +445,6 @@
     n_dp, n_sec = lax.axis_size("dp"), lax.axis_size("section")
     chips = n_dp // 2
     stream = Stream(panels, size)
-    step_rows = stream.step
     me = lax.axis_index("dp")
     section = lax.axis_index("section")
     chip, core = lax.shift_right_logical(me, 1), me & 1
@@ -370,53 +461,39 @@
         return lax.ppermute(value, "dp", swap_pairs)
 
     cuts = [sum(TRAIN_CUTS[:i]) for i in range(len(TRAIN_CUTS) + 1)]
-    train_parts = [train[a:b] for a, b in zip(cuts, cuts[1:])]
-    far = [None] * len(train_parts)
-
-    def send_train(index, *deps):
-        part = after(train_parts[index], *deps) if deps else train_parts[index]
-        far[index] = lax.ppermute(part, "dp", next_chip)
-
-    send_train(0)
-    slot, train_count, owners = lax.optimization_barrier((slot, train_count, owners, train_parts[0]))[:3]
+    first_part, slot = lax.optimization_barrier((train[: cuts[1]], slot))
+    far = [lax.ppermute(first_part, "dp", next_chip)]
+
+    def send_train(index, *earlier):
+        part = copied(train, cuts[index], cuts[index + 1] - cuts[index], *earlier)
+        far.append(lax.ppermute(part, "dp", next_chip))
+        return part
+
+    peer = swapped(slot)
+    packed = inverted_diagonal(panels, info, slot)
+    own_rows = build_stream(stream, chips, info, slot, peer, packed, swapped(packed), corner(far[0]))
     count_2 = lax.ppermute(train_count, "dp", next_chip)
     count_1 = lax.ppermute(train_count, "dp", [(d, (d + 1) % n_dp) for d in range(n_dp)])
     near_counts = jnp.concatenate([count_1, count_2])
 
-    peer = swapped(slot)
-    held = jnp.argmax(owners == me).astype(jnp.int32).reshape(1)
-    packed = inverted_diagonal(slot, held)
-    own_rows = build_stream(stream, chips, info, slot, peer, packed, swapped(packed))
-
-    row = lax.broadcasted_iota(jnp.int32, own_rows.shape[:1] + (1,), 0) - place * (SKEW * step_rows)
-    origin = jnp.broadcast_to(owner_place[0], row.shape)
-    for j in range(1, panels):
-        origin = jnp.where(row >= stream.panel_start(j), owner_place[j], origin)
-    from_before = origin < place
-
     got, own, other = {}, [], []
-    sent = [far[0], near_counts]
-    for number in range(CHUNKS + SKEW * (chips - 2)):
-        span = slice(number * step_rows, (number + 1) * step_rows)
-        if number >= SKEW:
-            block = jnp.where(from_before[span], after(got[number - SKEW], *sent), own_rows[span])
-        else:
-            block = after(own_rows[span], *sent)
+    steps = CHUNKS + SKEW * (chips - 2)
+    for number in range(steps):
+        block = step_block(stream, number, info, own_rows, got, [] if number == 0 else [block])
         pairs = []
         for p in range(chips - 1):
             if 0 <= number - SKEW * p < CHUNKS:
                 pairs += [(2 * p, 2 * p + 2), (2 * (chips - 1 - p) + 1, 2 * (chips - 2 - p) + 1)]
         got[number] = lax.ppermute(block, "dp", pairs)
-        sent = [block]
         for first, last in GROUPS:
             if number == last - 1 + SKEW * (chips - 2):
-                value = collected(stream, chips, first, last, info, own_rows, got)
+                value = collected(stream, chips, first, last, info, near_counts, own_rows, got)
                 own.append(value)
                 other.append(swapped(value))
-    send_train(1, *sent)
-    high, low = swept(stream, n_sec, info, query, own, other)
-    for index in range(2, len(train_parts)):
-        send_train(index, high)
+
+    part = send_train(1, swapped(corner(got[steps - 1]) + corner(got[steps - 2])))
+    high, low, swept_token = swept(stream, n_sec, info, corner(part), query, own, other)
+    send_train(2, swept_token)
 
     scale = (coords * n_sec) ** (-0.5)
 
@@ -430,14 +507,18 @@
             total = total + lax.ppermute(parts[k], "section", pairs)
         return total
 
-    parts = scored(n_sec, scale, 0, train_count, high, low, [train])
+    parts = scored(n_sec, scale, 0, train_count, swept_token, high, low, [train])
     own_scores = summed(parts)
-    near_scores, far_scores = [], []
-    for index, (part, far_part) in enumerate(zip(train_parts, far)):
-        near_part = swapped(jnp.where(first_core, part, after(far_part, high if index < 2 else parts[0])))
+    near_scores, far_scores, earlier = [], [], [corner(own_scores)]
+    for index, far_part in enumerate(far):
+        last = index + 1 == len(far)
+        near_part = swapped(chosen(info, train, cuts[index], far_part, *(earlier if last else [swept_token])))
         length = cuts[index + 1] - cuts[index]
-        parts = scored(n_sec, scale, cuts[index], after(near_counts, parts[0]), high, low, [near_part, far_part])
+        parts = scored(
+            n_sec, scale, cuts[index], near_counts, corner(parts[0]), high, low, [near_part, far_part]
+        )
         both = summed(parts)
+        earlier.append(corner(both))
         near_scores.append(both[:, :length])
         far_scores.append(both[:, length:])
     return jnp.concatenate([own_scores] + near_scores + far_scores, axis=1)[None]

time: 315 us -> 285 us (0.905)
  starting transfers between devices: 155 us -> 101 us
  Pallas kernels: 57.7 us -> 90.2 us
  other arithmetic: 21 us -> 2.21 us
  waiting for transfers between devices: 60.4 us -> 71.4 us
    ppermute x8 -> x9, starting transfers between devices: 60.6 us -> 14.9 us  [swapped(): return lax.ppermute(value, 'dp', swap_pairs)]
    pallas_call x1 -> x27, Pallas kernels: 5.51 us -> 36.2 us  [the longest x21 27.4 us: step_block(): pl.pallas_call(functools.partial(step_kernel, stream, number), out_shape=...]
    select_n x22 -> x0, other arithmetic: 15.4 us -> none  [the longest x19 14.8 us: body(): jnp.where(from_before[span], after(got[number - SKEW], *sent), own_rows[s...]
    ppermute x1, waiting for transfers between devices: 14.4 us -> 1.63 us  [body(): count_2 = lax.ppermute(train_count, 'dp', next_chip)]
    ppermute x3, waiting for transfers between devices: 9.04 us -> 21.3 us  [the longest x1 10.9 us: body(): far = [lax.ppermute(first_part, 'dp', next_chip)]]
    ppermute x1, waiting for transfers between devices: 0.01 us -> 4.92 us  [body(): lax.ppermute(train_count, 'dp', [(d, (d + 1) % n_dp) for d in range(n_dp)])]
    ppermute x12, waiting for transfers between devices: 16.6 us -> 21.3 us  [summed(): total = total + lax.ppermute(parts[k], 'section', pairs)]
    slice x5 -> x12, local copies, waits for them, and re-layouts: 5.42 us -> 2.07 us  [the longest x1 1.18 us: body(): first_part, slot = lax.optimization_barrier((train[:cuts[1]], slot))]
  transfers between devices with their start and end apart: 46 -> 47, of which waited for: 23 -> 24; matrix products, arithmetic and copies ran while one was open for 7% -> 1% of each run, Pallas kernels for 17% -> 27%
where the time goes in v4:
time: 285 us; the launch traced here: 284 us
  starting transfers between devices  101 us (35%)
  Pallas kernels  90.2 us (32%)
  waiting for transfers between devices  71.4 us (25%)
  local copies, waits for them, and re-layouts  17.5 us (6%)
    ppermute x21, starting transfers between devices, body(): got[number] = lax.ppermute(block, 'dp', pairs)  69.4 us
    pallas_call x21, Pallas kernels, step_block(): pl.pallas_call(functools.partial(step_kernel, stream, number), out_shape=...  27.4 us
    pallas_call x1, Pallas kernels, swept(): pl.pallas_call(functools.partial(sweep_kernel, stream, n_sec), out_shape=...  26.7 us
    ppermute x12, waiting for transfers between devices, summed(): total = total + lax.ppermute(parts[k], 'section', pairs)  21.3 us
    pallas_call x4, Pallas kernels, scored(): pl.pallas_call(functools.partial(score_kernel, n_sec, scale, first), out_...  18.4 us
    ppermute x21, waiting for transfers between devices, body(): got[number] = lax.ppermute(block, 'dp', pairs)  17.3 us
    ppermute x9, starting transfers between devices, swapped(): return lax.ppermute(value, 'dp', swap_pairs)  14.9 us
    ppermute x12, starting transfers between devices, summed(): total = total + lax.ppermute(parts[k], 'section', pairs)  14.1 us
  transfers between devices with their start and end apart: 47, of which 24 were waited for; matrix products, arithmetic and copies ran while one was open for 1% of the time, Pallas kernels for 27%

profile of v4, /device:TPU:0, one launch (start us, length us, event | category | flops | bytes accessed | tf_op | source)
XLA Modules:
  0.0 283.9 jit_solution(13964746982330033373)
XLA Ops:
  1.7 2.6 collective-permute-start.2
  5.7 2.2 copy-done.2
  7.9 5.4 %shard_map.55.packed = f32[320,512]{1,0:T(8,128)S(1)} custom-call(s32[13]{0:T(128)S(1)} %concatenate.9.info, f32[2048,512]{1,0:T(8,128)S(1)} %bitcast.20), custom_call_target="tpu_custom_call" | custom-call | bytes 1000 | tf_op jit(solution)/shard_map/pallas_call | solution.py:140
  13.6 10.9 %collective-permute-done.2.far.refs_1_ = f32[96,2048]{1,0:T(8,128)S(1)} collective-permute-done((f32[96,2048]{1,0:T(8,128)S(1)}, f32[96,2048]{1,0:T(8,128)S(1)}, u32[]{:S(2)}, u32[]{:S(2)}) %collective-permute-start.2) | collective-permute-done | bytes 786464 | tf_op jit(solution)/shard_map/ppermute | solution.py:465
  24.5 3.0 %shard_map.56.own = f32[5888,512]{1,0:T(8,128)S(1)} custom-call(s32[13]{0:T(128)S(1)} %concatenate.9.info, f32[2048,512]{1,0:T(8,128)S(1)} %bitcast.21, f32[2048,512]{1,0:T(8,128)} %collective-permute-done.peer, f32[320,512]{1,0:T(8,128)S(1)} %shard_map.55.packed, f32[320,512]{1,0:T(8,128)S(1)} %collective-permute-done.1.peer_packed, f32[8,128]{1,0:T(8,128)S(1)} %slice.72.earlier), custom_call_target="tpu_custom_call" | custom-call | bytes 1000 | tf_op jit(solution)/shard_map/pallas_call | solution.py:204
  28.8 2.3 collective-permute-start.3
  32.3 1.3 collective-permute-start.5
  33.6 4.1 %collective-permute-done.3.refs_0_ = f32[256,512]{1,0:T(8,128)S(1)} collective-permute-done((f32[256,512]{1,0:T(8,128)S(1)}, f32[256,512]{1,0:T(8,128)S(1)}, u32[]{:S(2)}, u32[]{:S(2)}) %collective-permute-start.3) | collective-permute-done | bytes 524320 | tf_op jit(solution)/shard_map/ppermute | solution.py:487
  39.0 4.4 %collective-permute-start.4 = (f32[256,512]{1,0:T(8,128)S(1)}, f32[256,512]{1,0:T(8,128)S(1)}, u32[]{:S(2)}, u32[]{:S(2)}) collective-permute-start(f32[256,512]{1,0:T(8,128)S(1)} %shard_map.59.refs_1_), channel_id=1, source_target_pairs={{0,2},{7,5},{2,4},{5,3},{8,10},{15,13},{10,12},{13,11},{16,18},{23... | collective-permute-start | bytes 1572872 | tf_op jit(solution)/shard_map/ppermute | solution.py:487
  43.5 1.3 shard_map.60.refs_1_
  44.8 4.3 %collective-permute-start.7 = (f32[256,512]{1,0:T(8,128)S(1)}, f32[256,512]{1,0:T(8,128)S(1)}, u32[]{:S(2)}, u32[]{:S(2)}) collective-permute-start(f32[256,512]{1,0:T(8,128)S(1)} %shard_map.60.refs_1_), channel_id=1, source_target_pairs={{0,2},{7,5},{2,4},{5,3},{8,10},{15,13},{10,12},{13,11},{16,18},{23... | collective-permute-start | bytes 1572872 | tf_op jit(solution)/shard_map/ppermute | solution.py:487
  51.4 4.4 %collective-permute-start.6 = (f32[256,512]{1,0:T(8,128)S(1)}, f32[256,512]{1,0:T(8,128)S(1)}, u32[]{:S(2)}, u32[]{:S(2)}) collective-permute-start(f32[256,512]{1,0:T(8,128)S(1)} %shard_map.61.refs_1_), channel_id=1, source_target_pairs={{0,2},{7,5},{2,4},{5,3},{4,6},{3,1},{8,10},{15,13},{10,12},{13,11}... | collective-permute-start | bytes 1572872 | tf_op jit(solution)/shard_map/ppermute | solution.py:487
  55.8 1.3 shard_map.62.refs_1_
  57.2 4.3 %collective-permute-start.9 = (f32[256,512]{1,0:T(8,128)S(1)}, f32[256,512]{1,0:T(8,128)S(1)}, u32[]{:S(2)}, u32[]{:S(2)}) collective-permute-start(f32[256,512]{1,0:T(8,128)S(1)} %shard_map.62.refs_1_), channel_id=1, source_target_pairs={{0,2},{7,5},{2,4},{5,3},{4,6},{3,1},{8,10},{15,13},{10,12},{13,11}... | collective-permute-start | bytes 1572872 | tf_op jit(solution)/shard_map/ppermute | solution.py:487
  63.8 4.4 %collective-permute-start.8 = (f32[256,512]{1,0:T(8,128)S(1)}, f32[256,512]{1,0:T(8,128)S(1)}, u32[]{:S(2)}, u32[]{:S(2)}) collective-permute-start(f32[256,512]{1,0:T(8,128)S(1)} %shard_map.63.refs_1_), channel_id=1, source_target_pairs={{0,2},{7,5},{2,4},{5,3},{4,6},{3,1},{8,10},{15,13},{10,12},{13,11}... | collective-permute-start | bytes 1572872 | tf_op jit(solution)/shard_map/ppermute | solution.py:487
  68.2 1.3 shard_map.64.refs_1_
  69.6 4.3 %collective-permute-start.11 = (f32[256,512]{1,0:T(8,128)S(1)}, f32[256,512]{1,0:T(8,128)S(1)}, u32[]{:S(2)}, u32[]{:S(2)}) collective-permute-start(f32[256,512]{1,0:T(8,128)S(1)} %shard_map.64.refs_1_), channel_id=1, source_target_pairs={{0,2},{7,5},{2,4},{5,3},{4,6},{3,1},{8,10},{15,13},{10,12},{13,11}... | collective-permute-start | bytes 1572872 | tf_op jit(solution)/shard_map/ppermute | solution.py:487
  76.2 4.4 %collective-permute-start.10 = (f32[256,512]{1,0:T(8,128)S(1)}, f32[256,512]{1,0:T(8,128)S(1)}, u32[]{:S(2)}, u32[]{:S(2)}) collective-permute-start(f32[256,512]{1,0:T(8,128)S(1)} %shard_map.65.refs_1_), channel_id=1, source_target_pairs={{0,2},{7,5},{2,4},{5,3},{4,6},{3,1},{8,10},{15,13},{10,12},{13,11}... | collective-permute-start | bytes 1572872 | tf_op jit(solution)/shard_map/ppermute | solution.py:487
  80.6 1.3 shard_map.66.refs_1_
  82.0 4.3 %collective-permute-start.13 = (f32[256,512]{1,0:T(8,128)S(1)}, f32[256,512]{1,0:T(8,128)S(1)}, u32[]{:S(2)}, u32[]{:S(2)}) collective-permute-start(f32[256,512]{1,0:T(8,128)S(1)} %shard_map.66.refs_1_), channel_id=1, source_target_pairs={{0,2},{7,5},{2,4},{5,3},{4,6},{3,1},{8,10},{15,13},{10,12},{13,11}... | collective-permute-start | bytes 1572872 | tf_op jit(solution)/shard_map/ppermute | solution.py:487
  88.6 4.4 %collective-permute-start.12 = (f32[256,512]{1,0:T(8,128)S(1)}, f32[256,512]{1,0:T(8,128)S(1)}, u32[]{:S(2)}, u32[]{:S(2)}) collective-permute-start(f32[256,512]{1,0:T(8,128)S(1)} %shard_map.67.refs_1_), channel_id=1, source_target_pairs={{0,2},{7,5},{2,4},{5,3},{4,6},{3,1},{8,10},{15,13},{10,12},{13,11}... | collective-permute-start | bytes 1572872 | tf_op jit(solution)/shard_map/ppermute | solution.py:487
  93.0 1.3 shard_map.68.refs_1_
  94.3 4.3 %collective-permute-start.15 = (f32[256,512]{1,0:T(8,128)S(1)}, f32[256,512]{1,0:T(8,128)S(1)}, u32[]{:S(2)}, u32[]{:S(2)}) collective-permute-start(f32[256,512]{1,0:T(8,128)S(1)} %shard_map.68.refs_1_), channel_id=1, source_target_pairs={{0,2},{7,5},{2,4},{5,3},{4,6},{3,1},{8,10},{15,13},{10,12},{13,11}... | collective-permute-start | bytes 1572872 | tf_op jit(solution)/shard_map/ppermute | solution.py:487
  101.0 4.4 %collective-permute-start.14 = (f32[256,512]{1,0:T(8,128)S(1)}, f32[256,512]{1,0:T(8,128)S(1)}, u32[]{:S(2)}, u32[]{:S(2)}) collective-permute-start(f32[256,512]{1,0:T(8,128)S(1)} %shard_map.69.refs_1_), channel_id=1, source_target_pairs={{0,2},{7,5},{2,4},{5,3},{4,6},{3,1},{8,10},{15,13},{10,12},{13,11}... | collective-permute-start | bytes 1572872 | tf_op jit(solution)/shard_map/ppermute | solution.py:487
  105.5 4.9 %collective-permute-done.25 = s32[1]{0:T(128)} collective-permute-done((s32[1]{0:T(128)}, s32[1]{0:T(128)}, u32[]{:S(2)}, u32[]{:S(2)}) %collective-permute-start.25) | collective-permute-done | bytes 36 | tf_op jit(solution)/shard_map/ppermute | solution.py:476
  110.5 1.6 collective-permute-done.26
  113.4 2.2 shard_map.79.refs_0_
  115.7 1.3 shard_map.70.refs_1_
  117.8 4.5 %collective-permute-start.17 = (f32[256,512]{1,0:T(8,128)S(1)}, f32[256,512]{1,0:T(8,128)S(1)}, u32[]{:S(2)}, u32[]{:S(2)}) collective-permute-start(f32[256,512]{1,0:T(8,128)S(1)} %shard_map.70.refs_1_), channel_id=1, source_target_pairs={{0,2},{7,5},{2,4},{5,3},{4,6},{3,1},{8,10},{15,13},{10,12},{13,11}... | collective-permute-start | bytes 1572872 | tf_op jit(solution)/shard_map/ppermute | solution.py:487
  123.6 1.9 collective-permute-start.16
  125.6 3.4 %collective-permute-done.17.refs_0_.refs_4_ = f32[256,512]{1,0:T(8,128)S(1)} collective-permute-done((f32[256,512]{1,0:T(8,128)S(1)}, f32[256,512]{1,0:T(8,128)S(1)}, u32[]{:S(2)}, u32[]{:S(2)}) %collective-permute-start.17) | collective-permute-done | bytes 524320 | tf_op jit(solution)/shard_map/ppermute | solution.py:487
  130.3 4.4 %collective-permute-start.19 = (f32[256,512]{1,0:T(8,128)S(1)}, f32[256,512]{1,0:T(8,128)S(1)}, u32[]{:S(2)}, u32[]{:S(2)}) collective-permute-start(f32[256,512]{1,0:T(8,128)S(1)} %shard_map.72.refs_1_), channel_id=1, source_target_pairs={{0,2},{7,5},{2,4},{5,3},{4,6},{3,1},{8,10},{15,13},{10,12},{13,11}... | collective-permute-start | bytes 1572872 | tf_op jit(solution)/shard_map/ppermute | solution.py:487
  136.0 4.3 %collective-permute-start.18 = (f32[256,512]{1,0:T(8,128)S(1)}, f32[256,512]{1,0:T(8,128)S(1)}, u32[]{:S(2)}, u32[]{:S(2)}) collective-permute-start(f32[256,512]{1,0:T(8,128)S(1)} %shard_map.73.refs_1_), channel_id=1, source_target_pairs={{0,2},{7,5},{2,4},{5,3},{4,6},{3,1},{8,10},{15,13},{10,12},{13,11}... | collective-permute-start | bytes 1572872 | tf_op jit(solution)/shard_map/ppermute | solution.py:487
  143.4 3.6 %collective-permute-done.18.refs_0_.refs_7_.refs_2_ = f32[256,512]{1,0:T(8,128)S(1)} collective-permute-done((f32[256,512]{1,0:T(8,128)S(1)}, f32[256,512]{1,0:T(8,128)S(1)}, u32[]{:S(2)}, u32[]{:S(2)}) %collective-permute-start.18) | collective-permute-done | bytes 524320 | tf_op jit(solution)/shard_map/ppermute | solution.py:487
  153.1 2.2 shard_map.80.refs_1_
  155.3 6.6 %collective-permute-start.28 = (f32[1280,512]{1,0:T(8,128)S(1)}, f32[1280,512]{1,0:T(8,128)S(1)}, u32[]{:S(2)}, u32[]{:S(2)}) collective-permute-start(f32[1280,512]{1,0:T(8,128)S(1)} %shard_map.80.refs_1_), channel_id=1, source_target_pairs={{0,1},{1,0},{2,3},{3,2},{4,5},{5,4},{6,7},{7,6},{8,9},{9,8},{10,11... | collective-permute-start | bytes 7864328 | tf_op jit(solution)/shard_map/ppermute | solution.py:461
  161.9 6.3 %collective-permute-start.24 = (f32[8,128]{1,0:T(8,128)S(1)}, f32[8,128]{1,0:T(8,128)S(1)}, u32[]{:S(2)}, u32[]{:S(2)}) collective-permute-start(f32[8,128]{1,0:T(8,128)S(1)} %slice_add_fusion), channel_id=1, source_target_pairs={{0,1},{1,0},{2,3},{3,2},{4,5},{5,4},{6,7},{7,6},{8,9},{9,8},{10,11... | collective-permute-start | bytes 12296 | tf_op jit(solution)/shard_map/ppermute | solution.py:461
  169.1 1.3 shard_map.78
  170.5 1.4 shard_map.81.refs_2_
  176.5 1.5 copy-done.5
  178.0 2.2 copy-done.9
  180.2 1.4 copy-done.4
  181.6 1.7 copy-done.6
  183.4 1.4 copy-done.8
  184.8 26.7 %shard_map.82 = (bf16[4,512,512]{2,1,0:T(8,128)(2,1)S(1)}, bf16[4,512,512]{2,1,0:T(8,128)(2,1)S(1)}, f32[8,128]{1,0:T(8,128)S(1)}) custom-call(s32[13]{0:T(128)S(1)} %concatenate.9.info, f32[8,128]{1,0:T(8,128)S(1)} %slice.75.earlier, f32[512,2048]{1,0:T(8,128)} %bitcast.22, f32[2304,512]{1,0:T(8,128)} %copy-done.1, f32[1280,512]{1,0:T(8,128)S(1)} %shard_map.80.refs_1_, ...), custom_call_target="tpu_custom_call" | custom-call | bytes 1000 | tf_op jit(solution)/shard_map/pallas_call | solution.py:375
  211.5 10.4 %collective-permute-done.37.far.refs_1_ = f32[256,2048]{1,0:T(8,128)S(1)} collective-permute-done((f32[256,2048]{1,0:T(8,128)}, f32[256,2048]{1,0:T(8,128)S(1)}, u32[]{:S(2)}, u32[]{:S(2)}) %collective-permute-start.37) | collective-permute-done | bytes 2097184 | tf_op jit(solution)/shard_map/ppermute | solution.py:469
  224.7 4.8 %shard_map.83 = (f32[128,512]{1,0:T(8,128)S(1)}, f32[128,512]{1,0:T(8,128)S(1)}, f32[128,512]{1,0:T(8,128)S(1)}, f32[128,512]{1,0:T(8,128)S(1)}) custom-call(s32[1]{0:T(128)S(6)} %copy.6.counts, f32[8,128]{1,0:T(8,128)S(1)} %get-tuple-element.28.earlier.refs_0_, bf16[4,512,512]{2,1,0:T(8,128)(2,1)S(1)} %get-tuple-element.29.high, ...), custom_call_target="tpu_custom_call" | custom-call | bytes 1000 | tf_op jit(solution)/shard_map/pallas_call | solution.py:425
  229.4 1.6 collective-permute-start.30
  231.0 1.5 collective-permute-start.31
  233.0 3.2 %shard_map.85 = (f32[128,192]{1,0:T(8,128)S(1)}, f32[128,192]{1,0:T(8,128)S(1)}, f32[128,192]{1,0:T(8,128)S(1)}, f32[128,192]{1,0:T(8,128)S(1)}) custom-call(s32[2]{0:T(128)S(1)} %pad_add_fusion.counts, f32[8,128]{1,0:T(8,128)S(1)} %slice.60.earlier, bf16[4,512,512]{2,1,0:T(8,128)(2,1)S(1)} %get-tuple-element.29.high, ...), custom_call_target="tpu_custom_call" | custom-call | bytes 1000 | tf_op jit(solution)/shard_map/pallas_call | solution.py:425
  236.2 2.5 collective-permute-done.30
  238.7 1.5 collective-permute-start.34
  240.2 1.5 collective-permute-start.35
  241.7 5.5 %shard_map.87 = (f32[128,512]{1,0:T(8,128)S(1)}, f32[128,512]{1,0:T(8,128)S(1)}, f32[128,512]{1,0:T(8,128)S(1)}, f32[128,512]{1,0:T(8,128)S(1)}) custom-call(s32[2]{0:T(128)S(1)} %pad_add_fusion.counts, f32[8,128]{1,0:T(8,128)S(1)} %slice.62.earlier, bf16[4,512,512]{2,1,0:T(8,128)(2,1)S(1)} %get-tuple-element.29.high, ...), custom_call_target="tpu_custom_call" | custom-call | bytes 1000 | tf_op jit(solution)/shard_map/pallas_call | solution.py:425
  247.7 1.5 collective-permute-start.39
  249.2 1.5 collective-permute-start.40
  251.3 3.4 %collective-permute-done.36 = f32[128,192]{1,0:T(8,128)S(1)} collective-permute-done((f32[128,192]{1,0:T(8,128)S(1)}, f32[128,192]{1,0:T(8,128)S(1)}, u32[]{:S(2)}, u32[]{:S(2)}) %collective-permute-start.36) | collective-permute-done | bytes 98336 | tf_op jit(solution)/shard_map/ppermute | solution.py:507
  254.7 4.0 %collective-permute-done.39 = f32[128,512]{1,0:T(8,128)S(1)} collective-permute-done((f32[128,512]{1,0:T(8,128)S(1)}, f32[128,512]{1,0:T(8,128)S(1)}, u32[]{:S(2)}, u32[]{:S(2)}) %collective-permute-start.39) | collective-permute-done | bytes 262176 | tf_op jit(solution)/shard_map/ppermute | solution.py:507
  259.7 2.9 %collective-permute-done.41 = f32[128,512]{1,0:T(8,128)S(1)} collective-permute-done((f32[128,512]{1,0:T(8,128)S(1)}, f32[128,512]{1,0:T(8,128)S(1)}, u32[]{:S(2)}, u32[]{:S(2)}) %collective-permute-start.41) | collective-permute-done | bytes 262176 | tf_op jit(solution)/shard_map/ppermute | solution.py:507
  263.5 2.9 %collective-permute-done.43.refs_0_ = f32[160,2048]{1,0:T(8,128)S(1)} collective-permute-done((f32[160,2048]{1,0:T(8,128)S(1)}, f32[160,2048]{1,0:T(8,128)S(1)}, u32[]{:S(2)}, u32[]{:S(2)}) %collective-permute-start.43) | collective-permute-done | bytes 1310752 | tf_op jit(solution)/shard_map/ppermute | solution.py:461
  266.4 5.0 %shard_map.90 = (f32[128,320]{1,0:T(8,128)S(1)}, f32[128,320]{1,0:T(8,128)S(1)}, f32[128,320]{1,0:T(8,128)S(1)}, f32[128,320]{1,0:T(8,128)S(1)}) custom-call(s32[2]{0:T(128)S(1)} %pad_add_fusion.counts, f32[8,128]{1,0:T(8,128)S(1)} %slice.64.earlier, bf16[4,512,512]{2,1,0:T(8,128)(2,1)S(1)} %get-tuple-element.29.high, ...), custom_call_target="tpu_custom_call" | custom-call | bytes 1000 | tf_op jit(solution)/shard_map/pallas_call | solution.py:425
  272.6 2.4 collective-permute-start.46
  275.0 4.2 %collective-permute-done.44 = f32[128,320]{1,0:T(8,128)S(1)} collective-permute-done((f32[128,320]{1,0:T(8,128)S(1)}, f32[128,320]{1,0:T(8,128)S(1)}, u32[]{:S(2)}, u32[]{:S(2)}) %collective-permute-start.44) | collective-permute-done | bytes 163872 | tf_op jit(solution)/shard_map/ppermute | solution.py:507
  279.3 3.4 %collective-permute-done.46 = f32[128,320]{1,0:T(8,128)S(1)} collective-permute-done((f32[128,320]{1,0:T(8,128)S(1)}, f32[128,320]{1,0:T(8,128)S(1)}, u32[]{:S(2)}, u32[]{:S(2)}) %collective-permute-start.46) | collective-permute-done | bytes 163872 | tf_op jit(solution)/shard_map/ppermute | solution.py:507
  (107 shorter events, 47.8 us)
Async XLA Ops:
  1.2 23.3 %collective-permute-start = (f32[2048,512]{1,0:T(8,128)}, f32[2048,512]{1,0:T(8,128)}, u32[]{:S(2)}, u32[]{:S(2)}) collective-permute-start(f32[2048,512]{1,0:T(8,128)} %bitcast.19), channel_id=1, source_target_pairs={{0,1},{1,0},{2,3},{3,2},{4,5},{5,4},{6,7},{7,6},{8,9},{9,8},{10,11... | collective-permute-start | bytes 12582920 | tf_op jit(solution)/shard_map/ppermute | solution.py:461
  1.7 22.8 %collective-permute-start.2 = (f32[96,2048]{1,0:T(8,128)S(1)}, f32[96,2048]{1,0:T(8,128)S(1)}, u32[]{:S(2)}, u32[]{:S(2)}) collective-permute-start(f32[96,2048]{1,0:T(8,128)S(1)} %slice_bitcast_fusion), channel_id=1, source_target_pairs={{0,2},{1,3},{2,4},{3,5},{4,6},{5,7},{6,0},{7,1},{8,10},{9,11},{10,... | collective-permute-start | bytes 2359304 | tf_op jit(solution)/shard_map/ppermute | solution.py:465
  5.7 2.2 copy-start.2
  13.4 11.2 %collective-permute-start.1 = (f32[320,512]{1,0:T(8,128)S(1)}, f32[320,512]{1,0:T(8,128)S(1)}, u32[]{:S(2)}, u32[]{:S(2)}) collective-permute-start(f32[320,512]{1,0:T(8,128)S(1)} %shard_map.55.packed), channel_id=1, source_target_pairs={{0,1},{1,0},{2,3},{3,2},{4,5},{5,4},{6,7},{7,6},{8,9},{9,8},{10,11... | collective-permute-start | bytes 1966088 | tf_op jit(solution)/shard_map/ppermute | solution.py:461
  28.8 8.9 %collective-permute-start.3 = (f32[256,512]{1,0:T(8,128)S(1)}, f32[256,512]{1,0:T(8,128)S(1)}, u32[]{:S(2)}, u32[]{:S(2)}) collective-permute-start(f32[256,512]{1,0:T(8,128)S(1)} %shard_map.57.refs_0_), channel_id=1, source_target_pairs={{0,2},{7,5},{8,10},{15,13},{16,18},{23,21},{24,26},{31,29}} | collective-permute-start | bytes 1572872 | tf_op jit(solution)/shard_map/ppermute | solution.py:487
  32.3 11.1 %collective-permute-start.5 = (f32[256,512]{1,0:T(8,128)S(1)}, f32[256,512]{1,0:T(8,128)S(1)}, u32[]{:S(2)}, u32[]{:S(2)}) collective-permute-start(f32[256,512]{1,0:T(8,128)S(1)} %shard_map.58.refs_1_), channel_id=1, source_target_pairs={{0,2},{7,5},{8,10},{15,13},{16,18},{23,21},{24,26},{31,29}} | collective-permute-start | bytes 1572872 | tf_op jit(solution)/shard_map/ppermute | solution.py:487
  39.0 11.1 %collective-permute-start.4 = (f32[256,512]{1,0:T(8,128)S(1)}, f32[256,512]{1,0:T(8,128)S(1)}, u32[]{:S(2)}, u32[]{:S(2)}) collective-permute-start(f32[256,512]{1,0:T(8,128)S(1)} %shard_map.59.refs_1_), channel_id=1, source_target_pairs={{0,2},{7,5},{2,4},{5,3},{8,10},{15,13},{10,12},{13,11},{16,18},{23... | collective-permute-start | bytes 1572872 | tf_op jit(solution)/shard_map/ppermute | solution.py:487
  44.8 11.1 %collective-permute-start.7 = (f32[256,512]{1,0:T(8,128)S(1)}, f32[256,512]{1,0:T(8,128)S(1)}, u32[]{:S(2)}, u32[]{:S(2)}) collective-permute-start(f32[256,512]{1,0:T(8,128)S(1)} %shard_map.60.refs_1_), channel_id=1, source_target_pairs={{0,2},{7,5},{2,4},{5,3},{8,10},{15,13},{10,12},{13,11},{16,18},{23... | collective-permute-start | bytes 1572872 | tf_op jit(solution)/shard_map/ppermute | solution.py:487
  51.4 11.1 %collective-permute-start.6 = (f32[256,512]{1,0:T(8,128)S(1)}, f32[256,512]{1,0:T(8,128)S(1)}, u32[]{:S(2)}, u32[]{:S(2)}) collective-permute-start(f32[256,512]{1,0:T(8,128)S(1)} %shard_map.61.refs_1_), channel_id=1, source_target_pairs={{0,2},{7,5},{2,4},{5,3},{4,6},{3,1},{8,10},{15,13},{10,12},{13,11}... | collective-permute-start | bytes 1572872 | tf_op jit(solution)/shard_map/ppermute | solution.py:487
  57.2 11.1 %collective-permute-start.9 = (f32[256,512]{1,0:T(8,128)S(1)}, f32[256,512]{1,0:T(8,128)S(1)}, u32[]{:S(2)}, u32[]{:S(2)}) collective-permute-start(f32[256,512]{1,0:T(8,128)S(1)} %shard_map.62.refs_1_), channel_id=1, source_target_pairs={{0,2},{7,5},{2,4},{5,3},{4,6},{3,1},{8,10},{15,13},{10,12},{13,11}... | collective-permute-start | bytes 1572872 | tf_op jit(solution)/shard_map/ppermute | solution.py:487
  63.8 11.1 %collective-permute-start.8 = (f32[256,512]{1,0:T(8,128)S(1)}, f32[256,512]{1,0:T(8,128)S(1)}, u32[]{:S(2)}, u32[]{:S(2)}) collective-permute-start(f32[256,512]{1,0:T(8,128)S(1)} %shard_map.63.refs_1_), channel_id=1, source_target_pairs={{0,2},{7,5},{2,4},{5,3},{4,6},{3,1},{8,10},{15,13},{10,12},{13,11}... | collective-permute-start | bytes 1572872 | tf_op jit(solution)/shard_map/ppermute | solution.py:487
  69.6 11.1 %collective-permute-start.11 = (f32[256,512]{1,0:T(8,128)S(1)}, f32[256,512]{1,0:T(8,128)S(1)}, u32[]{:S(2)}, u32[]{:S(2)}) collective-permute-start(f32[256,512]{1,0:T(8,128)S(1)} %shard_map.64.refs_1_), channel_id=1, source_target_pairs={{0,2},{7,5},{2,4},{5,3},{4,6},{3,1},{8,10},{15,13},{10,12},{13,11}... | collective-permute-start | bytes 1572872 | tf_op jit(solution)/shard_map/ppermute | solution.py:487
  76.2 11.1 %collective-permute-start.10 = (f32[256,512]{1,0:T(8,128)S(1)}, f32[256,512]{1,0:T(8,128)S(1)}, u32[]{:S(2)}, u32[]{:S(2)}) collective-permute-start(f32[256,512]{1,0:T(8,128)S(1)} %shard_map.65.refs_1_), channel_id=1, source_target_pairs={{0,2},{7,5},{2,4},{5,3},{4,6},{3,1},{8,10},{15,13},{10,12},{13,11}... | collective-permute-start | bytes 1572872 | tf_op jit(solution)/shard_map/ppermute | solution.py:487
  82.0 11.1 %collective-permute-start.13 = (f32[256,512]{1,0:T(8,128)S(1)}, f32[256,512]{1,0:T(8,128)S(1)}, u32[]{:S(2)}, u32[]{:S(2)}) collective-permute-start(f32[256,512]{1,0:T(8,128)S(1)} %shard_map.66.refs_1_), channel_id=1, source_target_pairs={{0,2},{7,5},{2,4},{5,3},{4,6},{3,1},{8,10},{15,13},{10,12},{13,11}... | collective-permute-start | bytes 1572872 | tf_op jit(solution)/shard_map/ppermute | solution.py:487
  88.6 11.1 %collective-permute-start.12 = (f32[256,512]{1,0:T(8,128)S(1)}, f32[256,512]{1,0:T(8,128)S(1)}, u32[]{:S(2)}, u32[]{:S(2)}) collective-permute-start(f32[256,512]{1,0:T(8,128)S(1)} %shard_map.67.refs_1_), channel_id=1, source_target_pairs={{0,2},{7,5},{2,4},{5,3},{4,6},{3,1},{8,10},{15,13},{10,12},{13,11}... | collective-permute-start | bytes 1572872 | tf_op jit(solution)/shard_map/ppermute | solution.py:487
  94.3 19.0 %collective-permute-start.15 = (f32[256,512]{1,0:T(8,128)S(1)}, f32[256,512]{1,0:T(8,128)S(1)}, u32[]{:S(2)}, u32[]{:S(2)}) collective-permute-start(f32[256,512]{1,0:T(8,128)S(1)} %shard_map.68.refs_1_), channel_id=1, source_target_pairs={{0,2},{7,5},{2,4},{5,3},{4,6},{3,1},{8,10},{15,13},{10,12},{13,11}... | collective-permute-start | bytes 1572872 | tf_op jit(solution)/shard_map/ppermute | solution.py:487
  101.0 12.4 %collective-permute-start.14 = (f32[256,512]{1,0:T(8,128)S(1)}, f32[256,512]{1,0:T(8,128)S(1)}, u32[]{:S(2)}, u32[]{:S(2)}) collective-permute-start(f32[256,512]{1,0:T(8,128)S(1)} %shard_map.69.refs_1_), channel_id=1, source_target_pairs={{0,2},{7,5},{2,4},{5,3},{4,6},{3,1},{8,10},{15,13},{10,12},{13,11}... | collective-permute-start | bytes 1572872 | tf_op jit(solution)/shard_map/ppermute | solution.py:487
  105.4 5.1 %collective-permute-start.25 = (s32[1]{0:T(128)}, s32[1]{0:T(128)}, u32[]{:S(2)}, u32[]{:S(2)}) collective-permute-start(s32[1]{0:T(128)} %param.9), channel_id=1, source_target_pairs={{0,1},{1,2},{2,3},{3,4},{4,5},{5,6},{6,7},{7,0},{8,9},{9,10},{10,1... | collective-permute-start | bytes 20 | tf_op jit(solution)/shard_map/ppermute | solution.py:476
  105.5 6.6 %collective-permute-start.26 = (s32[1]{0:T(128)}, s32[1]{0:T(128)}, u32[]{:S(2)}, u32[]{:S(2)}) collective-permute-start(s32[1]{0:T(128)} %param.9), channel_id=1, source_target_pairs={{0,2},{1,3},{2,4},{3,5},{4,6},{5,7},{6,0},{7,1},{8,10},{9,11},{10,... | collective-permute-start | bytes 20 | tf_op jit(solution)/shard_map/ppermute | solution.py:475
  115.6 2.2 copy-start.1
  115.6 62.4 %collective-permute-start.27 = (f32[2304,512]{1,0:T(8,128)S(1)}, f32[2304,512]{1,0:T(8,128)S(1)}, u32[]{:S(2)}, u32[]{:S(2)}) collective-permute-start(f32[2304,512]{1,0:T(8,128)S(1)} %shard_map.79.refs_0_), channel_id=1, source_target_pairs={{0,1},{1,0},{2,3},{3,2},{4,5},{5,4},{6,7},{7,6},{8,9},{9,8},{10,11... | collective-permute-start | bytes 14155784 | tf_op jit(solution)/shard_map/ppermute | solution.py:461
  117.8 11.2 %collective-permute-start.17 = (f32[256,512]{1,0:T(8,128)S(1)}, f32[256,512]{1,0:T(8,128)S(1)}, u32[]{:S(2)}, u32[]{:S(2)}) collective-permute-start(f32[256,512]{1,0:T(8,128)S(1)} %shard_map.70.refs_1_), channel_id=1, source_target_pairs={{0,2},{7,5},{2,4},{5,3},{4,6},{3,1},{8,10},{15,13},{10,12},{13,11}... | collective-permute-start | bytes 1572872 | tf_op jit(solution)/shard_map/ppermute | solution.py:487
  123.6 11.1 %collective-permute-start.16 = (f32[256,512]{1,0:T(8,128)S(1)}, f32[256,512]{1,0:T(8,128)S(1)}, u32[]{:S(2)}, u32[]{:S(2)}) collective-permute-start(f32[256,512]{1,0:T(8,128)S(1)} %shard_map.71.refs_1_), channel_id=1, source_target_pairs={{0,2},{7,5},{2,4},{5,3},{4,6},{3,1},{8,10},{15,13},{10,12},{13,11}... | collective-permute-start | bytes 1572872 | tf_op jit(solution)/shard_map/ppermute | solution.py:487
  130.3 11.1 %collective-permute-start.19 = (f32[256,512]{1,0:T(8,128)S(1)}, f32[256,512]{1,0:T(8,128)S(1)}, u32[]{:S(2)}, u32[]{:S(2)}) collective-permute-start(f32[256,512]{1,0:T(8,128)S(1)} %shard_map.72.refs_1_), channel_id=1, source_target_pairs={{0,2},{7,5},{2,4},{5,3},{4,6},{3,1},{8,10},{15,13},{10,12},{13,11}... | collective-permute-start | bytes 1572872 | tf_op jit(solution)/shard_map/ppermute | solution.py:487
  136.0 10.9 %collective-permute-start.18 = (f32[256,512]{1,0:T(8,128)S(1)}, f32[256,512]{1,0:T(8,128)S(1)}, u32[]{:S(2)}, u32[]{:S(2)}) collective-permute-start(f32[256,512]{1,0:T(8,128)S(1)} %shard_map.73.refs_1_), channel_id=1, source_target_pairs={{0,2},{7,5},{2,4},{5,3},{4,6},{3,1},{8,10},{15,13},{10,12},{13,11}... | collective-permute-start | bytes 1572872 | tf_op jit(solution)/shard_map/ppermute | solution.py:487
  142.7 6.3 %collective-permute-start.21 = (f32[256,512]{1,0:T(8,128)S(1)}, f32[256,512]{1,0:T(8,128)S(1)}, u32[]{:S(2)}, u32[]{:S(2)}) collective-permute-start(f32[256,512]{1,0:T(8,128)S(1)} %shard_map.74.refs_1_), channel_id=1, source_target_pairs={{2,4},{5,3},{4,6},{3,1},{10,12},{13,11},{12,14},{11,9},{18,20},{21... | collective-permute-start | bytes 1572872 | tf_op jit(solution)/shard_map/ppermute | solution.py:487
  148.3 2.7 collective-permute-start.20
  150.3 11.6 %collective-permute-start.23 = (f32[256,512]{1,0:T(8,128)S(1)}, f32[256,512]{1,0:T(8,128)S(1)}, u32[]{:S(2)}, u32[]{:S(2)}) collective-permute-start(f32[256,512]{1,0:T(8,128)S(1)} %shard_map.76.refs_1_), channel_id=1, source_target_pairs={{4,6},{3,1},{12,14},{11,9},{20,22},{19,17},{28,30},{27,25}} | collective-permute-start | bytes 1572872 | tf_op jit(solution)/shard_map/ppermute | solution.py:487
  152.4 9.5 %collective-permute-start.22 = (f32[256,512]{1,0:T(8,128)S(1)}, f32[256,512]{1,0:T(8,128)S(1)}, u32[]{:S(2)}, u32[]{:S(2)}) collective-permute-start(f32[256,512]{1,0:T(8,128)S(1)} %shard_map.77), channel_id=1, source_target_pairs={{4,6},{3,1},{12,14},{11,9},{20,22},{19,17},{28,30},{27,25}} | collective-permute-start | bytes 1572872 | tf_op jit(solution)/shard_map/ppermute | solution.py:487
  153.1 16.0 %copy-start = (f32[1,512,2048]{2,1,0:T(8,128)S(1)}, f32[1,512,2048]{2,1,0:T(8,128)}, u32[]{:S(2)}) copy-start(f32[1,512,2048]{2,1,0:T(8,128)} %param.6) | copy-start | bytes 12582916
  155.3 21.2 %collective-permute-start.28 = (f32[1280,512]{1,0:T(8,128)S(1)}, f32[1280,512]{1,0:T(8,128)S(1)}, u32[]{:S(2)}, u32[]{:S(2)}) collective-permute-start(f32[1280,512]{1,0:T(8,128)S(1)} %shard_map.80.refs_1_), channel_id=1, source_target_pairs={{0,1},{1,0},{2,3},{3,2},{4,5},{5,4},{6,7},{7,6},{8,9},{9,8},{10,11... | collective-permute-start | bytes 7864328 | tf_op jit(solution)/shard_map/ppermute | solution.py:461
  161.9 7.2 %collective-permute-start.24 = (f32[8,128]{1,0:T(8,128)S(1)}, f32[8,128]{1,0:T(8,128)S(1)}, u32[]{:S(2)}, u32[]{:S(2)}) collective-permute-start(f32[8,128]{1,0:T(8,128)S(1)} %slice_add_fusion), channel_id=1, source_target_pairs={{0,1},{1,0},{2,3},{3,2},{4,5},{5,4},{6,7},{7,6},{8,9},{9,8},{10,11... | collective-permute-start | bytes 12296 | tf_op jit(solution)/shard_map/ppermute | solution.py:461
  170.4 51.5 %collective-permute-start.37 = (f32[256,2048]{1,0:T(8,128)}, f32[256,2048]{1,0:T(8,128)S(1)}, u32[]{:S(2)}, u32[]{:S(2)}) collective-permute-start(f32[256,2048]{1,0:T(8,128)} %shard_map.78), channel_id=1, source_target_pairs={{0,2},{1,3},{2,4},{3,5},{4,6},{5,7},{6,0},{7,1},{8,10},{9,11},{10,... | collective-permute-start | bytes 6291464 | tf_op jit(solution)/shard_map/ppermute | solution.py:469
  171.8 3.5 %collective-permute-start.29 = (f32[768,512]{1,0:T(8,128)S(1)}, f32[768,512]{1,0:T(8,128)S(1)}, u32[]{:S(2)}, u32[]{:S(2)}) collective-permute-start(f32[768,512]{1,0:T(8,128)S(1)} %shard_map.81.refs_2_), channel_id=1, source_target_pairs={{0,1},{1,0},{2,3},{3,2},{4,5},{5,4},{6,7},{7,6},{8,9},{9,8},{10,11... | collective-permute-start | bytes 4718600 | tf_op jit(solution)/shard_map/ppermute | solution.py:461
  172.2 1.2 copy-start.3
  175.3 1.2 copy-start.7
  176.5 1.5 copy-start.5
  178.0 2.2 copy-start.9
  180.2 1.4 copy-start.4
  181.6 1.7 copy-start.6
  183.4 1.4 copy-start.8
  222.6 17.6 %collective-permute-start.38 = (f32[256,2048]{1,0:T(8,128)S(1)}, f32[256,2048]{1,0:T(8,128)S(1)}, u32[]{:S(2)}, u32[]{:S(2)}) collective-permute-start(f32[256,2048]{1,0:T(8,128)S(1)} %shard_map.86), channel_id=1, source_target_pairs={{0,1},{1,0},{2,3},{3,2},{4,5},{5,4},{6,7},{7,6},{8,9},{9,8},{10,11... | collective-permute-start | bytes 6291464 | tf_op jit(solution)/shard_map/ppermute | solution.py:461
  223.3 9.2 %collective-permute-start.33 = (f32[96,2048]{1,0:T(8,128)S(1)}, f32[96,2048]{1,0:T(8,128)S(1)}, u32[]{:S(2)}, u32[]{:S(2)}) collective-permute-start(f32[96,2048]{1,0:T(8,128)S(1)} %shard_map.84), channel_id=1, source_target_pairs={{0,1},{1,0},{2,3},{3,2},{4,5},{5,4},{6,7},{7,6},{8,9},{9,8},{10,11... | collective-permute-start | bytes 2359304 | tf_op jit(solution)/shard_map/ppermute | solution.py:461
  223.9 38.7 %collective-permute-start.42 = (f32[160,2048]{1,0:T(8,128)S(1)}, f32[160,2048]{1,0:T(8,128)S(1)}, u32[]{:S(2)}, u32[]{:S(2)}) collective-permute-start(f32[160,2048]{1,0:T(8,128)S(1)} %shard_map.88), channel_id=1, source_target_pairs={{0,2},{1,3},{2,4},{3,5},{4,6},{5,7},{6,0},{7,1},{8,10},{9,11},{10,... | collective-permute-start | bytes 3932168 | tf_op jit(solution)/shard_map/ppermute | solution.py:469
  229.4 9.2 %collective-permute-start.30 = (f32[128,512]{1,0:T(8,128)S(1)}, f32[128,512]{1,0:T(8,128)S(1)}, u32[]{:S(2)}, u32[]{:S(2)}) collective-permute-start(f32[128,512]{1,0:T(8,128)S(1)} %get-tuple-element.32), channel_id=1, source_target_pairs={{0,8},{8,0},{16,24},{24,16},{1,9},{9,1},{17,25},{25,17},{2,10},{10... | collective-permute-start | bytes 786440 | tf_op jit(solution)/shard_map/ppermute | solution.py:507
  231.0 16.2 %collective-permute-start.31 = (f32[128,512]{1,0:T(8,128)S(1)}, f32[128,512]{1,0:T(8,128)S(1)}, u32[]{:S(2)}, u32[]{:S(2)}) collective-permute-start(f32[128,512]{1,0:T(8,128)S(1)} %get-tuple-element.33), channel_id=1, source_target_pairs={{0,16},{8,24},{16,0},{24,8},{1,17},{9,25},{17,1},{25,9},{2,18},{10... | collective-permute-start | bytes 786440 | tf_op jit(solution)/shard_map/ppermute | solution.py:507
  232.5 15.2 %collective-permute-start.32 = (f32[128,512]{1,0:T(8,128)S(1)}, f32[128,512]{1,0:T(8,128)S(1)}, u32[]{:S(2)}, u32[]{:S(2)}) collective-permute-start(f32[128,512]{1,0:T(8,128)S(1)} %get-tuple-element.34), channel_id=1, source_target_pairs={{0,24},{8,16},{16,8},{24,0},{1,25},{9,17},{17,9},{25,1},{2,26},{10... | collective-permute-start | bytes 786440 | tf_op jit(solution)/shard_map/ppermute | solution.py:507
  238.7 10.6 %collective-permute-start.34 = (f32[128,192]{1,0:T(8,128)S(1)}, f32[128,192]{1,0:T(8,128)S(1)}, u32[]{:S(2)}, u32[]{:S(2)}) collective-permute-start(f32[128,192]{1,0:T(8,128)S(1)} %get-tuple-element.36), channel_id=1, source_target_pairs={{0,8},{8,0},{16,24},{24,16},{1,9},{9,1},{17,25},{25,17},{2,10},{10... | collective-permute-start | bytes 294920 | tf_op jit(solution)/shard_map/ppermute | solution.py:507
  240.2 10.6 %collective-permute-start.35 = (f32[128,192]{1,0:T(8,128)S(1)}, f32[128,192]{1,0:T(8,128)S(1)}, u32[]{:S(2)}, u32[]{:S(2)}) collective-permute-start(f32[128,192]{1,0:T(8,128)S(1)} %get-tuple-element.37), channel_id=1, source_target_pairs={{0,16},{8,24},{16,0},{24,8},{1,17},{9,25},{17,1},{25,9},{2,18},{10... | collective-permute-start | bytes 294920 | tf_op jit(solution)/shard_map/ppermute | solution.py:507
  247.2 7.5 %collective-permute-start.36 = (f32[128,192]{1,0:T(8,128)S(1)}, f32[128,192]{1,0:T(8,128)S(1)}, u32[]{:S(2)}, u32[]{:S(2)}) collective-permute-start(f32[128,192]{1,0:T(8,128)S(1)} %get-tuple-element.38), channel_id=1, source_target_pairs={{0,24},{8,16},{16,8},{24,0},{1,25},{9,17},{17,9},{25,1},{2,26},{10... | collective-permute-start | bytes 294920 | tf_op jit(solution)/shard_map/ppermute | solution.py:507
  247.7 11.0 %collective-permute-start.39 = (f32[128,512]{1,0:T(8,128)S(1)}, f32[128,512]{1,0:T(8,128)S(1)}, u32[]{:S(2)}, u32[]{:S(2)}) collective-permute-start(f32[128,512]{1,0:T(8,128)S(1)} %get-tuple-element.40), channel_id=1, source_target_pairs={{0,8},{8,0},{16,24},{24,16},{1,9},{9,1},{17,25},{25,17},{2,10},{10... | collective-permute-start | bytes 786440 | tf_op jit(solution)/shard_map/ppermute | solution.py:507
  249.2 10.4 %collective-permute-start.40 = (f32[128,512]{1,0:T(8,128)S(1)}, f32[128,512]{1,0:T(8,128)S(1)}, u32[]{:S(2)}, u32[]{:S(2)}) collective-permute-start(f32[128,512]{1,0:T(8,128)S(1)} %get-tuple-element.41), channel_id=1, source_target_pairs={{0,16},{8,24},{16,0},{24,8},{1,17},{9,25},{17,1},{25,9},{2,18},{10... | collective-permute-start | bytes 786440 | tf_op jit(solution)/shard_map/ppermute | solution.py:507
  250.8 11.7 %collective-permute-start.41 = (f32[128,512]{1,0:T(8,128)S(1)}, f32[128,512]{1,0:T(8,128)S(1)}, u32[]{:S(2)}, u32[]{:S(2)}) collective-permute-start(f32[128,512]{1,0:T(8,128)S(1)} %get-tuple-element.42), channel_id=1, source_target_pairs={{0,24},{8,16},{16,8},{24,0},{1,25},{9,17},{17,9},{25,1},{2,26},{10... | collective-permute-start | bytes 786440 | tf_op jit(solution)/shard_map/ppermute | solution.py:507
  263.3 3.1 %collective-permute-start.43 = (f32[160,2048]{1,0:T(8,128)S(1)}, f32[160,2048]{1,0:T(8,128)S(1)}, u32[]{:S(2)}, u32[]{:S(2)}) collective-permute-start(f32[160,2048]{1,0:T(8,128)S(1)} %shard_map.89), channel_id=1, source_target_pairs={{0,1},{1,0},{2,3},{3,2},{4,5},{5,4},{6,7},{7,6},{8,9},{9,8},{10,11... | collective-permute-start | bytes 3932168 | tf_op jit(solution)/shard_map/ppermute | solution.py:461
  271.4 7.8 %collective-permute-start.44 = (f32[128,320]{1,0:T(8,128)S(1)}, f32[128,320]{1,0:T(8,128)S(1)}, u32[]{:S(2)}, u32[]{:S(2)}) collective-permute-start(f32[128,320]{1,0:T(8,128)S(1)} %get-tuple-element.44), channel_id=1, source_target_pairs={{0,8},{8,0},{16,24},{24,16},{1,9},{9,1},{17,25},{25,17},{2,10},{10... | collective-permute-start | bytes 491528 | tf_op jit(solution)/shard_map/ppermute | solution.py:507
  271.8 7.5 %collective-permute-start.45 = (f32[128,320]{1,0:T(8,128)S(1)}, f32[128,320]{1,0:T(8,128)S(1)}, u32[]{:S(2)}, u32[]{:S(2)}) collective-permute-start(f32[128,320]{1,0:T(8,128)S(1)} %get-tuple-element.45), channel_id=1, source_target_pairs={{0,16},{8,24},{16,0},{24,8},{1,17},{9,25},{17,1},{25,9},{2,18},{10... | collective-permute-start | bytes 491528 | tf_op jit(solution)/shard_map/ppermute | solution.py:507
  272.6 10.1 %collective-permute-start.46 = (f32[128,320]{1,0:T(8,128)S(1)}, f32[128,320]{1,0:T(8,128)S(1)}, u32[]{:S(2)}, u32[]{:S(2)}) collective-permute-start(f32[128,320]{1,0:T(8,128)S(1)} %get-tuple-element.46), channel_id=1, source_target_pairs={{0,24},{8,16},{16,8},{24,0},{1,25},{9,17},{17,9},{25,1},{2,26},{10... | collective-permute-start | bytes 491528 | tf_op jit(solution)/shard_map/ppermute | solution.py:507

commit v5 on v4

--- a/solution.py
+++ b/solution.py
@@ -11,7 +11,7 @@
 CHUNKS = 17
 SKEW = 2
 GROUPS = ((0, 9), (9, 14), (14, 17))
-TRAIN_CUTS = (96, 256, 160)
+TRAIN_CUTS = (96, 320, 96)
 MIB = 1024 * 1024
 HBM = pl.BlockSpec(memory_space=pltpu.HBM)
 SMEM = pl.BlockSpec(memory_space=pltpu.SMEM)
@@ -47,23 +47,19 @@
     return pl.CostEstimate(flops=flops, bytes_accessed=moved, transcendentals=0)
 
 
-def copy_kernel(start, source, *refs):
-    out, sem = refs[-2:]
-    copy = pltpu.make_async_copy(source.at[pl.ds(start, out.shape[0])], out, sem)
-    copy.start()
-    copy.wait()
-
-
-def copied(source, start, length, *earlier):
-    return pl.pallas_call(
-        functools.partial(copy_kernel, start),
-        out_shape=jax.ShapeDtypeStruct((length, source.shape[1]), source.dtype),
+def order_kernel(*refs):
+    del refs
+
+
+def ordered(value, *earlier):
+    return pl.pallas_call(
+        order_kernel,
+        out_shape=jax.ShapeDtypeStruct(value.shape, value.dtype),
         in_specs=[HBM] * (1 + len(earlier)),
         out_specs=HBM,
-        scratch_shapes=[pltpu.SemaphoreType.DMA],
-        compiler_params=param(4),
-        cost_estimate=cost(0, 1000),
-    )(source, *earlier)
+        input_output_aliases={0: 0},
+        cost_estimate=cost(0, 1000),
+    )(value, *earlier)
 
 
 def choose_kernel(start, info, train, far, *refs):
@@ -179,7 +175,7 @@
         return found
 
 
-def build_kernel(stream, info, slot, peer, packed, peer_packed, earlier, out, sems):
+def build_kernel(stream, info, slot, peer, packed, peer_packed, out, sems):
     place, me = info[2], info[3]
     pending = []
     for piece, (j, k) in enumerate(stream.pieces):
@@ -199,20 +195,21 @@
         copy.wait()
 
 
-def build_stream(stream, chips, info, slot, peer, packed, peer_packed, earlier):
+def build_stream(stream, chips, info, slot, peer, packed, peer_packed):
     rows = stream.total + SKEW * stream.step * (chips - 1)
     return pl.pallas_call(
         functools.partial(build_kernel, stream),
         out_shape=jax.ShapeDtypeStruct((rows, stream.size), jnp.float32),
-        in_specs=[SMEM] + [HBM] * 5,
+        in_specs=[SMEM] + [HBM] * 4,
         out_specs=HBM,
         scratch_shapes=[pltpu.SemaphoreType.DMA((len(stream.pieces),))],
         compiler_params=param(4),
         cost_estimate=cost(0, 1000),
-    )(info, slot, peer, packed, peer_packed, earlier)
-
-
-def step_kernel(stream, number, info, own, *refs):
+    )(info, slot, peer, packed, peer_packed)
+
+
+def step_kernel(stream, number, info, counts, own, *refs):
+    del counts
     out, sems = refs[-2:]
     unit = stream.packed // 5
     place = info[2]
@@ -237,20 +234,20 @@
         copy.wait()
 
 
-def step_block(stream, number, info, own, got, earlier):
+def step_block(stream, number, info, counts, own, got, earlier):
     operands = ([got[number - SKEW]] if number >= SKEW else []) + earlier
     return pl.pallas_call(
         functools.partial(step_kernel, stream, number),
         out_shape=jax.ShapeDtypeStruct((stream.step, stream.size), jnp.float32),
-        in_specs=[SMEM] + [HBM] * (1 + len(operands)),
+        in_specs=[SMEM, SMEM] + [HBM] * (1 + len(operands)),
         out_specs=HBM,
         scratch_shapes=[pltpu.SemaphoreType.DMA((stream.step * 5 // stream.packed,))],
         compiler_params=param(4),
         cost_estimate=cost(0, 1000),
-    )(info, own, *operands)
-
-
-def collect_kernel(stream, chips, first, last, info, counts, own, *refs):
+    )(info, counts, own, *operands)
+
+
+def collect_kernel(stream, chips, first, last, info, own, *refs):
     received, out, sems = refs[:-2], refs[-2], refs[-1]
     place = info[2]
     pending = []
@@ -271,17 +268,17 @@
         copy.wait()
 
 
-def collected(stream, chips, first, last, info, counts, own, got):
+def collected(stream, chips, first, last, info, own, got):
     received = [got[s] for s in range(first, last + SKEW * (chips - 2))]
     return pl.pallas_call(
         functools.partial(collect_kernel, stream, chips, first, last),
         out_shape=jax.ShapeDtypeStruct(((last - first) * stream.step, stream.size), jnp.float32),
-        in_specs=[SMEM, SMEM] + [HBM] * (1 + len(received)),
+        in_specs=[SMEM] + [HBM] * (1 + len(received)),
         out_specs=HBM,
         scratch_shapes=[pltpu.SemaphoreType.DMA(((last - first) * len(stream.pieces),))],
         compiler_params=param(4),
         cost_estimate=cost(0, 1000),
-    )(info, counts, own, *received)
+    )(info, own, *received)
 
 
 def sweep_kernel(stream, n_sec, info, earlier, query, *refs):
@@ -388,7 +385,7 @@
             pltpu.VMEM((4, size, size), jnp.float32),
             pltpu.SemaphoreType.DMA((len(stream.pieces) + len(GROUPS),)),
         ],
-        compiler_params=param(40),
+        compiler_params=param(32),
         cost_estimate=cost(0, 1000),
     )(info, earlier, query, *own, *other)
 
@@ -465,13 +462,13 @@
     far = [lax.ppermute(first_part, "dp", next_chip)]
 
     def send_train(index, *earlier):
-        part = copied(train, cuts[index], cuts[index + 1] - cuts[index], *earlier)
+        part = ordered(train[cuts[index] : cuts[index + 1]], *earlier)
         far.append(lax.ppermute(part, "dp", next_chip))
         return part
 
     peer = swapped(slot)
     packed = inverted_diagonal(panels, info, slot)
-    own_rows = build_stream(stream, chips, info, slot, peer, packed, swapped(packed), corner(far[0]))
+    own_rows = build_stream(stream, chips, info, slot, peer, packed, swapped(packed))
     count_2 = lax.ppermute(train_count, "dp", next_chip)
     count_1 = lax.ppermute(train_count, "dp", [(d, (d + 1) % n_dp) for d in range(n_dp)])
     near_counts = jnp.concatenate([count_1, count_2])
@@ -479,7 +476,11 @@
     got, own, other = {}, [], []
     steps = CHUNKS + SKEW * (chips - 2)
     for number in range(steps):
-        block = step_block(stream, number, info, own_rows, got, [] if number == 0 else [block])
+        earlier = [corner(far[0])] if number == 0 else [block]
+        for index, (first, last) in enumerate(GROUPS[:-1]):
+            if number == last + 2 + SKEW * (chips - 2):
+                earlier.append(corner(other[index]))
+        block = step_block(stream, number, info, near_counts, own_rows, got, earlier)
         pairs = []
         for p in range(chips - 1):
             if 0 <= number - SKEW * p < CHUNKS:
@@ -487,13 +488,12 @@
         got[number] = lax.ppermute(block, "dp", pairs)
         for first, last in GROUPS:
             if number == last - 1 + SKEW * (chips - 2):
-                value = collected(stream, chips, first, last, info, near_counts, own_rows, got)
+                value = collected(stream, chips, first, last, info, own_rows, got)
                 own.append(value)
                 other.append(swapped(value))
 
-    part = send_train(1, swapped(corner(got[steps - 1]) + corner(got[steps - 2])))
+    part = send_train(1, corner(other[-1]))
     high, low, swept_token = swept(stream, n_sec, info, corner(part), query, own, other)
-    send_train(2, swept_token)
 
     scale = (coords * n_sec) ** (-0.5)
 
@@ -510,9 +510,11 @@
     parts = scored(n_sec, scale, 0, train_count, swept_token, high, low, [train])
     own_scores = summed(parts)
     near_scores, far_scores, earlier = [], [], [corner(own_scores)]
-    for index, far_part in enumerate(far):
-        last = index + 1 == len(far)
-        near_part = swapped(chosen(info, train, cuts[index], far_part, *(earlier if last else [swept_token])))
+    for index in range(len(cuts) - 1):
+        if index == 1:
+            earlier.append(corner(send_train(2, corner(parts[0]))))
+        far_part = far[index]
+        near_part = swapped(chosen(info, train, cuts[index], far_part, *(earlier if index else [swept_token])))
         length = cuts[index + 1] - cuts[index]
         parts = scored(
             n_sec, scale, cuts[index], near_counts, corner(parts[0]), high, low, [near_part, far_part]

time: 285 us -> 303 us (1.063)
  starting transfers between devices: 101 us -> 113 us
  local copies, waits for them, and re-layouts: 17.5 us -> 27.3 us
    ppermute x1, waiting for transfers between devices: 10.9 us -> 0.01 us  [body(): far = [lax.ppermute(first_part, 'dp', next_chip)]]
    ppermute x2, waiting for transfers between devices: 10.4 us -> 0.01 us  [send_train(): far.append(lax.ppermute(part, 'dp', next_chip))]
    ppermute x12, waiting for transfers between devices: 21.3 us -> 29.7 us  [summed(): total = total + lax.ppermute(parts[k], 'section', pairs)]
    ppermute x9 -> x8, starting transfers between devices: 14.9 us -> 21.8 us  [swapped(): return lax.ppermute(value, 'dp', swap_pairs)]
    ppermute x21, waiting for transfers between devices: 17.3 us -> 23.9 us  [body(): got[number] = lax.ppermute(block, 'dp', pairs)]
    unnamed x20 -> x48, local copies, waits for them, and re-layouts: 13.6 us -> 19 us
    ppermute x1, waiting for transfers between devices: 4.92 us -> 10.3 us  [body(): lax.ppermute(train_count, 'dp', [(d, (d + 1) % n_dp) for d in range(n_dp)])]
    ppermute x2, starting transfers between devices: 0.12 us -> 3.62 us  [send_train(): far.append(lax.ppermute(part, 'dp', next_chip))]
  transfers between devices with their start and end apart: 47 -> 46, of which waited for: 24 -> 24; matrix products, arithmetic and copies ran while one was open for 1% -> 2% of each run, Pallas kernels for 27% -> 24%
where the time goes in v5:
time: 303 us; the launch traced here: 300 us
  starting transfers between devices  113 us (37%)
  Pallas kernels  88.4 us (29%)
  waiting for transfers between devices  68.9 us (23%)
  local copies, waits for them, and re-layouts  27.3 us (9%)
    ppermute x21, starting transfers between devices, body(): got[number] = lax.ppermute(block, 'dp', pairs)  68.6 us
    ppermute x12, waiting for transfers between devices, summed(): total = total + lax.ppermute(parts[k], 'section', pairs)  29.7 us
    pallas_call x21, Pallas kernels, step_block(): pl.pallas_call(functools.partial(step_kernel, stream, number), out_shape=...  27.5 us
    pallas_call x1, Pallas kernels, swept(): pl.pallas_call(functools.partial(sweep_kernel, stream, n_sec), out_shape=...  24.5 us
    ppermute x21, waiting for transfers between devices, body(): got[number] = lax.ppermute(block, 'dp', pairs)  23.9 us
    ppermute x8, starting transfers between devices, swapped(): return lax.ppermute(value, 'dp', swap_pairs)  21.8 us
    pallas_call x4, Pallas kernels, scored(): pl.pallas_call(functools.partial(score_kernel, n_sec, scale, first), out_...  19.9 us
    unnamed x48, local copies, waits for them, and re-layouts  19 us
  transfers between devices with their start and end apart: 46, of which 24 were waited for; matrix products, arithmetic and copies ran while one was open for 2% of the time, Pallas kernels for 24%

profile of v5, /device:TPU:0, one launch (start us, length us, event | category | flops | bytes accessed | tf_op | source)
XLA Modules:
  0.0 300.4 jit_solution(15377015761505753901)
XLA Ops:
  0.0 2.4 slice_bitcast_fusion.1
  2.8 2.6 collective-permute-start.4
  5.5 2.2 copy-done.8
  7.7 5.4 %shard_map.55.packed = f32[320,512]{1,0:T(8,128)S(1)} custom-call(s32[13]{0:T(128)S(1)} %concatenate.9.info, f32[2048,512]{1,0:T(8,128)S(1)} %bitcast.22), custom_call_target="tpu_custom_call" | custom-call | bytes 1000 | tf_op jit(solution)/shard_map/pallas_call | solution.py:136
  13.7 1.6 collective-permute-start.3
  15.3 10.3 %collective-permute-done.2 = s32[1]{0:T(128)} collective-permute-done((s32[1]{0:T(128)}, s32[1]{0:T(128)}, u32[]{:S(2)}, u32[]{:S(2)}) %collective-permute-start.2) | collective-permute-done | bytes 36 | tf_op jit(solution)/shard_map/ppermute | solution.py:473
  27.1 3.6 %shard_map.56.own = f32[5888,512]{1,0:T(8,128)S(1)} custom-call(s32[13]{0:T(128)S(1)} %concatenate.9.info, f32[2048,512]{1,0:T(8,128)S(1)} %bitcast.23, f32[2048,512]{1,0:T(8,128)} %collective-permute-done.peer, f32[320,512]{1,0:T(8,128)S(1)} %shard_map.55.packed, f32[320,512]{1,0:T(8,128)S(1)} %collective-permute-done.1.peer_packed), custom_call_target="tpu_custom_call" | custom-call | bytes 1000 | tf_op jit(solution)/shard_map/pallas_call | solution.py:200
  32.0 1.3 collective-permute-start.5
  34.6 1.3 collective-permute-start.7
  35.9 4.0 %collective-permute-done.5.refs_0_ = f32[256,512]{1,0:T(8,128)S(1)} collective-permute-done((f32[256,512]{1,0:T(8,128)S(1)}, f32[256,512]{1,0:T(8,128)S(1)}, u32[]{:S(2)}, u32[]{:S(2)}) %collective-permute-start.5) | collective-permute-done | bytes 524320 | tf_op jit(solution)/shard_map/ppermute | solution.py:488
  41.3 4.4 %collective-permute-start.6 = (f32[256,512]{1,0:T(8,128)S(1)}, f32[256,512]{1,0:T(8,128)S(1)}, u32[]{:S(2)}, u32[]{:S(2)}) collective-permute-start(f32[256,512]{1,0:T(8,128)S(1)} %shard_map.59.refs_1_), channel_id=1, source_target_pairs={{0,2},{7,5},{2,4},{5,3},{8,10},{15,13},{10,12},{13,11},{16,18},{23... | collective-permute-start | bytes 1572872 | tf_op jit(solution)/shard_map/ppermute | solution.py:488
  45.7 1.3 shard_map.60.refs_1_
  47.0 4.3 %collective-permute-start.9 = (f32[256,512]{1,0:T(8,128)S(1)}, f32[256,512]{1,0:T(8,128)S(1)}, u32[]{:S(2)}, u32[]{:S(2)}) collective-permute-start(f32[256,512]{1,0:T(8,128)S(1)} %shard_map.60.refs_1_), channel_id=1, source_target_pairs={{0,2},{7,5},{2,4},{5,3},{8,10},{15,13},{10,12},{13,11},{16,18},{23... | collective-permute-start | bytes 1572872 | tf_op jit(solution)/shard_map/ppermute | solution.py:488
  53.7 4.4 %collective-permute-start.8 = (f32[256,512]{1,0:T(8,128)S(1)}, f32[256,512]{1,0:T(8,128)S(1)}, u32[]{:S(2)}, u32[]{:S(2)}) collective-permute-start(f32[256,512]{1,0:T(8,128)S(1)} %shard_map.61.refs_1_), channel_id=1, source_target_pairs={{0,2},{7,5},{2,4},{5,3},{4,6},{3,1},{8,10},{15,13},{10,12},{13,11}... | collective-permute-start | bytes 1572872 | tf_op jit(solution)/shard_map/ppermute | solution.py:488
  58.1 1.3 shard_map.62.refs_1_
  59.4 4.3 %collective-permute-start.11 = (f32[256,512]{1,0:T(8,128)S(1)}, f32[256,512]{1,0:T(8,128)S(1)}, u32[]{:S(2)}, u32[]{:S(2)}) collective-permute-start(f32[256,512]{1,0:T(8,128)S(1)} %shard_map.62.refs_1_), channel_id=1, source_target_pairs={{0,2},{7,5},{2,4},{5,3},{4,6},{3,1},{8,10},{15,13},{10,12},{13,11}... | collective-permute-start | bytes 1572872 | tf_op jit(solution)/shard_map/ppermute | solution.py:488
  66.1 4.4 %collective-permute-start.10 = (f32[256,512]{1,0:T(8,128)S(1)}, f32[256,512]{1,0:T(8,128)S(1)}, u32[]{:S(2)}, u32[]{:S(2)}) collective-permute-start(f32[256,512]{1,0:T(8,128)S(1)} %shard_map.63.refs_1_), channel_id=1, source_target_pairs={{0,2},{7,5},{2,4},{5,3},{4,6},{3,1},{8,10},{15,13},{10,12},{13,11}... | collective-permute-start | bytes 1572872 | tf_op jit(solution)/shard_map/ppermute | solution.py:488
  70.5 1.3 shard_map.64.refs_1_
  71.8 4.3 %collective-permute-start.13 = (f32[256,512]{1,0:T(8,128)S(1)}, f32[256,512]{1,0:T(8,128)S(1)}, u32[]{:S(2)}, u32[]{:S(2)}) collective-permute-start(f32[256,512]{1,0:T(8,128)S(1)} %shard_map.64.refs_1_), channel_id=1, source_target_pairs={{0,2},{7,5},{2,4},{5,3},{4,6},{3,1},{8,10},{15,13},{10,12},{13,11}... | collective-permute-start | bytes 1572872 | tf_op jit(solution)/shard_map/ppermute | solution.py:488
  78.5 4.4 %collective-permute-start.12 = (f32[256,512]{1,0:T(8,128)S(1)}, f32[256,512]{1,0:T(8,128)S(1)}, u32[]{:S(2)}, u32[]{:S(2)}) collective-permute-start(f32[256,512]{1,0:T(8,128)S(1)} %shard_map.65.refs_1_), channel_id=1, source_target_pairs={{0,2},{7,5},{2,4},{5,3},{4,6},{3,1},{8,10},{15,13},{10,12},{13,11}... | collective-permute-start | bytes 1572872 | tf_op jit(solution)/shard_map/ppermute | solution.py:488
  84.2 4.3 %collective-permute-start.15 = (f32[256,512]{1,0:T(8,128)S(1)}, f32[256,512]{1,0:T(8,128)S(1)}, u32[]{:S(2)}, u32[]{:S(2)}) collective-permute-start(f32[256,512]{1,0:T(8,128)S(1)} %shard_map.66.refs_1_), channel_id=1, source_target_pairs={{0,2},{7,5},{2,4},{5,3},{4,6},{3,1},{8,10},{15,13},{10,12},{13,11}... | collective-permute-start | bytes 1572872 | tf_op jit(solution)/shard_map/ppermute | solution.py:488
  90.8 4.4 %collective-permute-start.14 = (f32[256,512]{1,0:T(8,128)S(1)}, f32[256,512]{1,0:T(8,128)S(1)}, u32[]{:S(2)}, u32[]{:S(2)}) collective-permute-start(f32[256,512]{1,0:T(8,128)S(1)} %shard_map.67.refs_1_), channel_id=1, source_target_pairs={{0,2},{7,5},{2,4},{5,3},{4,6},{3,1},{8,10},{15,13},{10,12},{13,11}... | collective-permute-start | bytes 1572872 | tf_op jit(solution)/shard_map/ppermute | solution.py:488
  96.6 4.3 %collective-permute-start.17 = (f32[256,512]{1,0:T(8,128)S(1)}, f32[256,512]{1,0:T(8,128)S(1)}, u32[]{:S(2)}, u32[]{:S(2)}) collective-permute-start(f32[256,512]{1,0:T(8,128)S(1)} %shard_map.68.refs_1_), channel_id=1, source_target_pairs={{0,2},{7,5},{2,4},{5,3},{4,6},{3,1},{8,10},{15,13},{10,12},{13,11}... | collective-permute-start | bytes 1572872 | tf_op jit(solution)/shard_map/ppermute | solution.py:488
  103.2 4.4 %collective-permute-start.16 = (f32[256,512]{1,0:T(8,128)S(1)}, f32[256,512]{1,0:T(8,128)S(1)}, u32[]{:S(2)}, u32[]{:S(2)}) collective-permute-start(f32[256,512]{1,0:T(8,128)S(1)} %shard_map.69.refs_1_), channel_id=1, source_target_pairs={{0,2},{7,5},{2,4},{5,3},{4,6},{3,1},{8,10},{15,13},{10,12},{13,11}... | collective-permute-start | bytes 1572872 | tf_op jit(solution)/shard_map/ppermute | solution.py:488
  107.7 6.6 %collective-permute-done.16.refs_0_.refs_12_.refs_3_ = f32[256,512]{1,0:T(8,128)S(1)} collective-permute-done((f32[256,512]{1,0:T(8,128)S(1)}, f32[256,512]{1,0:T(8,128)S(1)}, u32[]{:S(2)}, u32[]{:S(2)}) %collective-permute-start.16) | collective-permute-done | bytes 524320 | tf_op jit(solution)/shard_map/ppermute | solution.py:488
  114.3 2.2 shard_map.72.refs_0_
  118.7 4.4 %collective-permute-start.19 = (f32[256,512]{1,0:T(8,128)S(1)}, f32[256,512]{1,0:T(8,128)S(1)}, u32[]{:S(2)}, u32[]{:S(2)}) collective-permute-start(f32[256,512]{1,0:T(8,128)S(1)} %shard_map.70.refs_1_), channel_id=1, source_target_pairs={{0,2},{7,5},{2,4},{5,3},{4,6},{3,1},{8,10},{15,13},{10,12},{13,11}... | collective-permute-start | bytes 1572872 | tf_op jit(solution)/shard_map/ppermute | solution.py:488
  124.5 1.9 collective-permute-start.18
  126.4 3.4 %collective-permute-done.19.refs_0_.refs_4_ = f32[256,512]{1,0:T(8,128)S(1)} collective-permute-done((f32[256,512]{1,0:T(8,128)S(1)}, f32[256,512]{1,0:T(8,128)S(1)}, u32[]{:S(2)}, u32[]{:S(2)}) %collective-permute-start.19) | collective-permute-done | bytes 524320 | tf_op jit(solution)/shard_map/ppermute | solution.py:488
  131.1 4.4 %collective-permute-start.21 = (f32[256,512]{1,0:T(8,128)S(1)}, f32[256,512]{1,0:T(8,128)S(1)}, u32[]{:S(2)}, u32[]{:S(2)}) collective-permute-start(f32[256,512]{1,0:T(8,128)S(1)} %shard_map.73.refs_1_), channel_id=1, source_target_pairs={{0,2},{7,5},{2,4},{5,3},{4,6},{3,1},{8,10},{15,13},{10,12},{13,11}... | collective-permute-start | bytes 1572872 | tf_op jit(solution)/shard_map/ppermute | solution.py:488
  136.9 4.3 %collective-permute-start.22 = (f32[256,512]{1,0:T(8,128)S(1)}, f32[256,512]{1,0:T(8,128)S(1)}, u32[]{:S(2)}, u32[]{:S(2)}) collective-permute-start(f32[256,512]{1,0:T(8,128)S(1)} %shard_map.74.refs_1_), channel_id=1, source_target_pairs={{0,2},{7,5},{2,4},{5,3},{4,6},{3,1},{8,10},{15,13},{10,12},{13,11}... | collective-permute-start | bytes 1572872 | tf_op jit(solution)/shard_map/ppermute | solution.py:488
  144.2 3.6 %collective-permute-done.22.refs_0_.refs_7_.refs_2_ = f32[256,512]{1,0:T(8,128)S(1)} collective-permute-done((f32[256,512]{1,0:T(8,128)S(1)}, f32[256,512]{1,0:T(8,128)S(1)}, u32[]{:S(2)}, u32[]{:S(2)}) %collective-permute-start.22) | collective-permute-done | bytes 524320 | tf_op jit(solution)/shard_map/ppermute | solution.py:488
  147.8 2.0 shard_map.78.refs_1_
  149.8 4.5 %collective-permute-start.26 = (f32[1280,512]{1,0:T(8,128)S(1)}, f32[1280,512]{1,0:T(8,128)S(1)}, u32[]{:S(2)}, u32[]{:S(2)}) collective-permute-start(f32[1280,512]{1,0:T(8,128)S(1)} %shard_map.78.refs_1_), channel_id=1, source_target_pairs={{0,1},{1,0},{2,3},{3,2},{4,5},{5,4},{6,7},{7,6},{8,9},{9,8},{10,11... | collective-permute-start | bytes 7864328 | tf_op jit(solution)/shard_map/ppermute | solution.py:458
  158.8 1.4 copy-done.14
  162.5 1.4 shard_map.80.refs_2_
  163.9 16.0 %collective-permute-start.28 = (f32[768,512]{1,0:T(8,128)S(1)}, f32[768,512]{1,0:T(8,128)S(1)}, u32[]{:S(2)}, u32[]{:S(2)}) collective-permute-start(f32[768,512]{1,0:T(8,128)S(1)} %shard_map.80.refs_2_), channel_id=1, source_target_pairs={{0,1},{1,0},{2,3},{3,2},{4,5},{5,4},{6,7},{7,6},{8,9},{9,8},{10,11... | collective-permute-start | bytes 4718600 | tf_op jit(solution)/shard_map/ppermute | solution.py:458
  179.9 1.8 slice_bitcast_fusion.refs_0_
  185.4 2.3 copy-done.7
  187.7 1.7 copy-done.10
  189.5 1.4 copy-done.12
  190.9 2.2 copy-done.13
  193.1 1.7 copy-done.15
  194.8 1.4 copy-done.17
  196.2 24.5 %shard_map.82 = (bf16[4,512,512]{2,1,0:T(8,128)(2,1)S(1)}, bf16[4,512,512]{2,1,0:T(8,128)(2,1)S(1)}, f32[8,128]{1,0:T(8,128)S(1)}) custom-call(s32[13]{0:T(128)S(1)} %concatenate.9.info, f32[8,128]{1,0:T(8,128)S(1)} %slice.101.earlier, f32[512,2048]{1,0:T(8,128)S(1)} %bitcast.24, f32[2304,512]{1,0:T(8,128)S(1)} %copy-done.7, f32[1280,512]{1,0:T(8,128)S(1)} %copy-done.10, ...), custom_call_target="tpu_custom_call" | custom-call | bytes 1000 | tf_op jit(solution)/shard_map/pallas_call | solution.py:372
  222.4 4.8 %shard_map.83 = (f32[128,512]{1,0:T(8,128)S(1)}, f32[128,512]{1,0:T(8,128)S(1)}, f32[128,512]{1,0:T(8,128)S(1)}, f32[128,512]{1,0:T(8,128)S(1)}) custom-call(s32[1]{0:T(128)S(6)} %copy.10.counts, f32[8,128]{1,0:T(8,128)S(1)} %get-tuple-element.28.earlier.refs_0_, bf16[4,512,512]{2,1,0:T(8,128)(2,1)S(1)} %get-tuple-element.29.high, ...), custom_call_target="tpu_custom_call" | custom-call | bytes 1000 | tf_op jit(solution)/shard_map/pallas_call | solution.py:422
  227.2 1.9 collective-permute-start.29
  230.7 3.2 %shard_map.85 = (f32[128,192]{1,0:T(8,128)S(1)}, f32[128,192]{1,0:T(8,128)S(1)}, f32[128,192]{1,0:T(8,128)S(1)}, f32[128,192]{1,0:T(8,128)S(1)}) custom-call(s32[2]{0:T(128)S(1)} %pad_add_fusion.counts, f32[8,128]{1,0:T(8,128)S(1)} %slice.82.earlier, bf16[4,512,512]{2,1,0:T(8,128)(2,1)S(1)} %get-tuple-element.29.high, ...), custom_call_target="tpu_custom_call" | custom-call | bytes 1000 | tf_op jit(solution)/shard_map/pallas_call | solution.py:422
  233.9 1.9 collective-permute-start.33
  236.3 1.9 collective-permute-start.34
  238.2 5.4 %collective-permute-done.30 = f32[128,512]{1,0:T(8,128)S(1)} collective-permute-done((f32[128,512]{1,0:T(8,128)S(1)}, f32[128,512]{1,0:T(8,128)S(1)}, u32[]{:S(2)}, u32[]{:S(2)}) %collective-permute-start.30) | collective-permute-done | bytes 262176 | tf_op jit(solution)/shard_map/ppermute | solution.py:507
  245.1 2.2 collective-permute-done.34
  247.3 2.1 collective-permute-done.35
  249.6 2.2 copy-done.2
  252.9 3.6 %collective-permute-start.41 = (f32[96,2048]{1,0:T(8,128)S(1)}, f32[96,2048]{1,0:T(8,128)S(1)}, u32[]{:S(2)}, u32[]{:S(2)}) collective-permute-start(f32[96,2048]{1,0:T(8,128)S(1)} %copy-done.20), channel_id=1, source_target_pairs={{0,2},{1,3},{2,4},{3,5},{4,6},{5,7},{6,0},{7,1},{8,10},{9,11},{10,... | collective-permute-start | bytes 2359304 | tf_op jit(solution)/shard_map/ppermute | solution.py:466
  257.5 8.7 %shard_map.88 = (f32[128,640]{1,0:T(8,128)S(1)}, f32[128,640]{1,0:T(8,128)S(1)}, f32[128,640]{1,0:T(8,128)S(1)}, f32[128,640]{1,0:T(8,128)S(1)}) custom-call(s32[2]{0:T(128)S(1)} %pad_add_fusion.counts, f32[8,128]{1,0:T(8,128)S(1)} %copy-done.18, bf16[4,512,512]{2,1,0:T(8,128)(2,1)S(1)} %get-tuple-element.29.high, bf16[4,512,512]{2,1,0:T(8,128)(2,1)S(1)} %copy-done.5, ...), custom_call_target="tpu_custom_call" | custom-call | bytes 1000 | tf_op jit(solution)/shard_map/pallas_call | solution.py:422
  268.0 1.7 collective-permute-start.40
  269.7 7.1 %collective-permute-done.38 = f32[128,640]{1,0:T(8,128)S(1)} collective-permute-done((f32[128,640]{1,0:T(8,128)S(1)}, f32[128,640]{1,0:T(8,128)S(1)}, u32[]{:S(2)}, u32[]{:S(2)}) %collective-permute-start.38) | collective-permute-done | bytes 327712 | tf_op jit(solution)/shard_map/ppermute | solution.py:507
  276.8 7.3 %collective-permute-done.39 = f32[128,640]{1,0:T(8,128)S(1)} collective-permute-done((f32[128,640]{1,0:T(8,128)S(1)}, f32[128,640]{1,0:T(8,128)S(1)}, u32[]{:S(2)}, u32[]{:S(2)}) %collective-permute-start.39) | collective-permute-done | bytes 327712 | tf_op jit(solution)/shard_map/ppermute | solution.py:507
  285.1 2.2 collective-permute-done.42.refs_0_
  287.3 3.2 %shard_map.90 = (f32[128,192]{1,0:T(8,128)S(1)}, f32[128,192]{1,0:T(8,128)S(1)}, f32[128,192]{1,0:T(8,128)S(1)}, f32[128,192]{1,0:T(8,128)S(1)}) custom-call(s32[2]{0:T(128)S(1)} %pad_add_fusion.counts, f32[8,128]{1,0:T(8,128)S(1)} %slice.91.earlier, bf16[4,512,512]{2,1,0:T(8,128)(2,1)S(1)} %get-tuple-element.29.high, bf16[4,512,512]{2,1,0:T(8,128)(2,1)S(1)} %copy-done.5, ...), custom_call_target="tpu_custom_call" | custom-call | bytes 1000 | tf_op jit(solution)/shard_map/pallas_call | solution.py:422
  292.3 1.8 collective-permute-start.45
  294.1 2.7 collective-permute-done.43
  296.9 2.4 collective-permute-done.44
  (137 shorter events, 53.0 us)
Async XLA Ops:
  0.0 5.4 %copy-start.23 = (s32[1,4]{1,0:T(1,128)S(1)}, s32[1,4]{1,0:T(1,128)}, u32[]{:S(2)}) copy-start(s32[1,4]{1,0:T(1,128)} %param.8) | copy-start | bytes 52
  2.4 24.7 %collective-permute-start = (f32[2048,512]{1,0:T(8,128)}, f32[2048,512]{1,0:T(8,128)}, u32[]{:S(2)}, u32[]{:S(2)}) collective-permute-start(f32[2048,512]{1,0:T(8,128)} %bitcast.21), channel_id=1, source_target_pairs={{0,1},{1,0},{2,3},{3,2},{4,5},{5,4},{6,7},{7,6},{8,9},{9,8},{10,11... | collective-permute-start | bytes 12582920 | tf_op jit(solution)/shard_map/ppermute | solution.py:458
  2.8 24.2 %collective-permute-start.4 = (f32[96,2048]{1,0:T(8,128)S(1)}, f32[96,2048]{1,0:T(8,128)S(1)}, u32[]{:S(2)}, u32[]{:S(2)}) collective-permute-start(f32[96,2048]{1,0:T(8,128)S(1)} %get-tuple-element.27), channel_id=1, source_target_pairs={{0,2},{1,3},{2,4},{3,5},{4,6},{5,7},{6,0},{7,1},{8,10},{9,11},{10,... | collective-permute-start | bytes 2359304 | tf_op jit(solution)/shard_map/ppermute | solution.py:462
  5.5 2.2 copy-start.8
  13.1 14.0 %collective-permute-start.1 = (f32[320,512]{1,0:T(8,128)S(1)}, f32[320,512]{1,0:T(8,128)S(1)}, u32[]{:S(2)}, u32[]{:S(2)}) collective-permute-start(f32[320,512]{1,0:T(8,128)S(1)} %shard_map.55.packed), channel_id=1, source_target_pairs={{0,1},{1,0},{2,3},{3,2},{4,5},{5,4},{6,7},{7,6},{8,9},{9,8},{10,11... | collective-permute-start | bytes 1966088 | tf_op jit(solution)/shard_map/ppermute | solution.py:458
  13.4 12.1 %collective-permute-start.2 = (s32[1]{0:T(128)}, s32[1]{0:T(128)}, u32[]{:S(2)}, u32[]{:S(2)}) collective-permute-start(s32[1]{0:T(128)} %param.9), channel_id=1, source_target_pairs={{0,1},{1,2},{2,3},{3,4},{4,5},{5,6},{6,7},{7,0},{8,9},{9,10},{10,1... | collective-permute-start | bytes 20 | tf_op jit(solution)/shard_map/ppermute | solution.py:473
  13.7 12.1 %collective-permute-start.3 = (s32[1]{0:T(128)}, s32[1]{0:T(128)}, u32[]{:S(2)}, u32[]{:S(2)}) collective-permute-start(s32[1]{0:T(128)} %param.9), channel_id=1, source_target_pairs={{0,2},{1,3},{2,4},{3,5},{4,6},{5,7},{6,0},{7,1},{8,10},{9,11},{10,... | collective-permute-start | bytes 20 | tf_op jit(solution)/shard_map/ppermute | solution.py:472
  32.0 8.0 %collective-permute-start.5 = (f32[256,512]{1,0:T(8,128)S(1)}, f32[256,512]{1,0:T(8,128)S(1)}, u32[]{:S(2)}, u32[]{:S(2)}) collective-permute-start(f32[256,512]{1,0:T(8,128)S(1)} %shard_map.57.refs_0_), channel_id=1, source_target_pairs={{0,2},{7,5},{8,10},{15,13},{16,18},{23,21},{24,26},{31,29}} | collective-permute-start | bytes 1572872 | tf_op jit(solution)/shard_map/ppermute | solution.py:488
  34.6 11.1 %collective-permute-start.7 = (f32[256,512]{1,0:T(8,128)S(1)}, f32[256,512]{1,0:T(8,128)S(1)}, u32[]{:S(2)}, u32[]{:S(2)}) collective-permute-start(f32[256,512]{1,0:T(8,128)S(1)} %shard_map.58.refs_1_), channel_id=1, source_target_pairs={{0,2},{7,5},{8,10},{15,13},{16,18},{23,21},{24,26},{31,29}} | collective-permute-start | bytes 1572872 | tf_op jit(solution)/shard_map/ppermute | solution.py:488
  41.3 11.1 %collective-permute-start.6 = (f32[256,512]{1,0:T(8,128)S(1)}, f32[256,512]{1,0:T(8,128)S(1)}, u32[]{:S(2)}, u32[]{:S(2)}) collective-permute-start(f32[256,512]{1,0:T(8,128)S(1)} %shard_map.59.refs_1_), channel_id=1, source_target_pairs={{0,2},{7,5},{2,4},{5,3},{8,10},{15,13},{10,12},{13,11},{16,18},{23... | collective-permute-start | bytes 1572872 | tf_op jit(solution)/shard_map/ppermute | solution.py:488
  47.0 11.1 %collective-permute-start.9 = (f32[256,512]{1,0:T(8,128)S(1)}, f32[256,512]{1,0:T(8,128)S(1)}, u32[]{:S(2)}, u32[]{:S(2)}) collective-permute-start(f32[256,512]{1,0:T(8,128)S(1)} %shard_map.60.refs_1_), channel_id=1, source_target_pairs={{0,2},{7,5},{2,4},{5,3},{8,10},{15,13},{10,12},{13,11},{16,18},{23... | collective-permute-start | bytes 1572872 | tf_op jit(solution)/shard_map/ppermute | solution.py:488
  53.7 11.1 %collective-permute-start.8 = (f32[256,512]{1,0:T(8,128)S(1)}, f32[256,512]{1,0:T(8,128)S(1)}, u32[]{:S(2)}, u32[]{:S(2)}) collective-permute-start(f32[256,512]{1,0:T(8,128)S(1)} %shard_map.61.refs_1_), channel_id=1, source_target_pairs={{0,2},{7,5},{2,4},{5,3},{4,6},{3,1},{8,10},{15,13},{10,12},{13,11}... | collective-permute-start | bytes 1572872 | tf_op jit(solution)/shard_map/ppermute | solution.py:488
  59.4 11.1 %collective-permute-start.11 = (f32[256,512]{1,0:T(8,128)S(1)}, f32[256,512]{1,0:T(8,128)S(1)}, u32[]{:S(2)}, u32[]{:S(2)}) collective-permute-start(f32[256,512]{1,0:T(8,128)S(1)} %shard_map.62.refs_1_), channel_id=1, source_target_pairs={{0,2},{7,5},{2,4},{5,3},{4,6},{3,1},{8,10},{15,13},{10,12},{13,11}... | collective-permute-start | bytes 1572872 | tf_op jit(solution)/shard_map/ppermute | solution.py:488
  66.1 11.1 %collective-permute-start.10 = (f32[256,512]{1,0:T(8,128)S(1)}, f32[256,512]{1,0:T(8,128)S(1)}, u32[]{:S(2)}, u32[]{:S(2)}) collective-permute-start(f32[256,512]{1,0:T(8,128)S(1)} %shard_map.63.refs_1_), channel_id=1, source_target_pairs={{0,2},{7,5},{2,4},{5,3},{4,6},{3,1},{8,10},{15,13},{10,12},{13,11}... | collective-permute-start | bytes 1572872 | tf_op jit(solution)/shard_map/ppermute | solution.py:488
  71.8 11.1 %collective-permute-start.13 = (f32[256,512]{1,0:T(8,128)S(1)}, f32[256,512]{1,0:T(8,128)S(1)}, u32[]{:S(2)}, u32[]{:S(2)}) collective-permute-start(f32[256,512]{1,0:T(8,128)S(1)} %shard_map.64.refs_1_), channel_id=1, source_target_pairs={{0,2},{7,5},{2,4},{5,3},{4,6},{3,1},{8,10},{15,13},{10,12},{13,11}... | collective-permute-start | bytes 1572872 | tf_op jit(solution)/shard_map/ppermute | solution.py:488
  78.5 11.1 %collective-permute-start.12 = (f32[256,512]{1,0:T(8,128)S(1)}, f32[256,512]{1,0:T(8,128)S(1)}, u32[]{:S(2)}, u32[]{:S(2)}) collective-permute-start(f32[256,512]{1,0:T(8,128)S(1)} %shard_map.65.refs_1_), channel_id=1, source_target_pairs={{0,2},{7,5},{2,4},{5,3},{4,6},{3,1},{8,10},{15,13},{10,12},{13,11}... | collective-permute-start | bytes 1572872 | tf_op jit(solution)/shard_map/ppermute | solution.py:488
  84.2 11.1 %collective-permute-start.15 = (f32[256,512]{1,0:T(8,128)S(1)}, f32[256,512]{1,0:T(8,128)S(1)}, u32[]{:S(2)}, u32[]{:S(2)}) collective-permute-start(f32[256,512]{1,0:T(8,128)S(1)} %shard_map.66.refs_1_), channel_id=1, source_target_pairs={{0,2},{7,5},{2,4},{5,3},{4,6},{3,1},{8,10},{15,13},{10,12},{13,11}... | collective-permute-start | bytes 1572872 | tf_op jit(solution)/shard_map/ppermute | solution.py:488
  90.8 11.1 %collective-permute-start.14 = (f32[256,512]{1,0:T(8,128)S(1)}, f32[256,512]{1,0:T(8,128)S(1)}, u32[]{:S(2)}, u32[]{:S(2)}) collective-permute-start(f32[256,512]{1,0:T(8,128)S(1)} %shard_map.67.refs_1_), channel_id=1, source_target_pairs={{0,2},{7,5},{2,4},{5,3},{4,6},{3,1},{8,10},{15,13},{10,12},{13,11}... | collective-permute-start | bytes 1572872 | tf_op jit(solution)/shard_map/ppermute | solution.py:488
  96.6 11.1 %collective-permute-start.17 = (f32[256,512]{1,0:T(8,128)S(1)}, f32[256,512]{1,0:T(8,128)S(1)}, u32[]{:S(2)}, u32[]{:S(2)}) collective-permute-start(f32[256,512]{1,0:T(8,128)S(1)} %shard_map.68.refs_1_), channel_id=1, source_target_pairs={{0,2},{7,5},{2,4},{5,3},{4,6},{3,1},{8,10},{15,13},{10,12},{13,11}... | collective-permute-start | bytes 1572872 | tf_op jit(solution)/shard_map/ppermute | solution.py:488
  103.2 11.1 %collective-permute-start.16 = (f32[256,512]{1,0:T(8,128)S(1)}, f32[256,512]{1,0:T(8,128)S(1)}, u32[]{:S(2)}, u32[]{:S(2)}) collective-permute-start(f32[256,512]{1,0:T(8,128)S(1)} %shard_map.69.refs_1_), channel_id=1, source_target_pairs={{0,2},{7,5},{2,4},{5,3},{4,6},{3,1},{8,10},{15,13},{10,12},{13,11}... | collective-permute-start | bytes 1572872 | tf_op jit(solution)/shard_map/ppermute | solution.py:488
  116.6 2.2 copy-start.6
  116.6 9.8 %collective-permute-start.20 = (f32[2304,512]{1,0:T(8,128)S(1)}, f32[2304,512]{1,0:T(8,128)S(1)}, u32[]{:S(2)}, u32[]{:S(2)}) collective-permute-start(f32[2304,512]{1,0:T(8,128)S(1)} %shard_map.72.refs_0_), channel_id=1, source_target_pairs={{0,1},{1,0},{2,3},{3,2},{4,5},{5,4},{6,7},{7,6},{8,9},{9,8},{10,11... | collective-permute-start | bytes 14155784 | tf_op jit(solution)/shard_map/ppermute | solution.py:458
  118.7 11.1 %collective-permute-start.19 = (f32[256,512]{1,0:T(8,128)S(1)}, f32[256,512]{1,0:T(8,128)S(1)}, u32[]{:S(2)}, u32[]{:S(2)}) collective-permute-start(f32[256,512]{1,0:T(8,128)S(1)} %shard_map.70.refs_1_), channel_id=1, source_target_pairs={{0,2},{7,5},{2,4},{5,3},{4,6},{3,1},{8,10},{15,13},{10,12},{13,11}... | collective-permute-start | bytes 1572872 | tf_op jit(solution)/shard_map/ppermute | solution.py:488
  124.5 11.1 %collective-permute-start.18 = (f32[256,512]{1,0:T(8,128)S(1)}, f32[256,512]{1,0:T(8,128)S(1)}, u32[]{:S(2)}, u32[]{:S(2)}) collective-permute-start(f32[256,512]{1,0:T(8,128)S(1)} %shard_map.71.refs_1_), channel_id=1, source_target_pairs={{0,2},{7,5},{2,4},{5,3},{4,6},{3,1},{8,10},{15,13},{10,12},{13,11}... | collective-permute-start | bytes 1572872 | tf_op jit(solution)/shard_map/ppermute | solution.py:488
  126.4 4.7 %copy-start.19 = (f32[2304,512]{1,0:T(8,128)}, f32[2304,512]{1,0:T(8,128)S(1)}, u32[]{:S(2)}) copy-start(f32[2304,512]{1,0:T(8,128)S(1)} %collective-permute-done.20.refs_3_) | copy-start | bytes 14155780
  131.1 11.1 %collective-permute-start.21 = (f32[256,512]{1,0:T(8,128)S(1)}, f32[256,512]{1,0:T(8,128)S(1)}, u32[]{:S(2)}, u32[]{:S(2)}) collective-permute-start(f32[256,512]{1,0:T(8,128)S(1)} %shard_map.73.refs_1_), channel_id=1, source_target_pairs={{0,2},{7,5},{2,4},{5,3},{4,6},{3,1},{8,10},{15,13},{10,12},{13,11}... | collective-permute-start | bytes 1572872 | tf_op jit(solution)/shard_map/ppermute | solution.py:488
  136.9 10.9 %collective-permute-start.22 = (f32[256,512]{1,0:T(8,128)S(1)}, f32[256,512]{1,0:T(8,128)S(1)}, u32[]{:S(2)}, u32[]{:S(2)}) collective-permute-start(f32[256,512]{1,0:T(8,128)S(1)} %shard_map.74.refs_1_), channel_id=1, source_target_pairs={{0,2},{7,5},{2,4},{5,3},{4,6},{3,1},{8,10},{15,13},{10,12},{13,11}... | collective-permute-start | bytes 1572872 | tf_op jit(solution)/shard_map/ppermute | solution.py:488
  143.5 4.3 %collective-permute-start.23 = (f32[256,512]{1,0:T(8,128)S(1)}, f32[256,512]{1,0:T(8,128)S(1)}, u32[]{:S(2)}, u32[]{:S(2)}) collective-permute-start(f32[256,512]{1,0:T(8,128)S(1)} %shard_map.75.refs_1_), channel_id=1, source_target_pairs={{2,4},{5,3},{4,6},{3,1},{10,12},{13,11},{12,14},{11,9},{18,20},{21... | collective-permute-start | bytes 1572872 | tf_op jit(solution)/shard_map/ppermute | solution.py:488
  149.8 5.8 %copy-start.9 = (f32[1280,512]{1,0:T(8,128)}, f32[1280,512]{1,0:T(8,128)S(1)}, u32[]{:S(2)}) copy-start(f32[1280,512]{1,0:T(8,128)S(1)} %shard_map.78.refs_1_) | copy-start | bytes 7864324
  149.8 9.0 %collective-permute-start.26 = (f32[1280,512]{1,0:T(8,128)S(1)}, f32[1280,512]{1,0:T(8,128)S(1)}, u32[]{:S(2)}, u32[]{:S(2)}) collective-permute-start(f32[1280,512]{1,0:T(8,128)S(1)} %shard_map.78.refs_1_), channel_id=1, source_target_pairs={{0,1},{1,0},{2,3},{3,2},{4,5},{5,4},{6,7},{7,6},{8,9},{9,8},{10,11... | collective-permute-start | bytes 7864328 | tf_op jit(solution)/shard_map/ppermute | solution.py:458
  155.6 4.7 %collective-permute-start.24 = (f32[256,512]{1,0:T(8,128)S(1)}, f32[256,512]{1,0:T(8,128)S(1)}, u32[]{:S(2)}, u32[]{:S(2)}) collective-permute-start(f32[256,512]{1,0:T(8,128)S(1)} %shard_map.76.refs_1_), channel_id=1, source_target_pairs={{2,4},{5,3},{4,6},{3,1},{10,12},{13,11},{12,14},{11,9},{18,20},{21... | collective-permute-start | bytes 1572872 | tf_op jit(solution)/shard_map/ppermute | solution.py:488
  157.8 4.6 %collective-permute-start.25 = (f32[256,512]{1,0:T(8,128)S(1)}, f32[256,512]{1,0:T(8,128)S(1)}, u32[]{:S(2)}, u32[]{:S(2)}) collective-permute-start(f32[256,512]{1,0:T(8,128)S(1)} %shard_map.77.refs_1_), channel_id=1, source_target_pairs={{4,6},{3,1},{12,14},{11,9},{20,22},{19,17},{28,30},{27,25}} | collective-permute-start | bytes 1572872 | tf_op jit(solution)/shard_map/ppermute | solution.py:488
  161.6 18.2 %copy-start = (f32[1,512,2048]{2,1,0:T(8,128)S(1)}, f32[1,512,2048]{2,1,0:T(8,128)}, u32[]{:S(2)}) copy-start(f32[1,512,2048]{2,1,0:T(8,128)} %param.6) | copy-start | bytes 12582916
  161.6 0.8 collective-permute-start.27
  163.9 17.8 %copy-start.11 = (f32[768,512]{1,0:T(8,128)}, f32[768,512]{1,0:T(8,128)S(1)}, u32[]{:S(2)}) copy-start(f32[768,512]{1,0:T(8,128)S(1)} %shard_map.80.refs_2_) | copy-start | bytes 4718596
  163.9 19.0 %collective-permute-start.28 = (f32[768,512]{1,0:T(8,128)S(1)}, f32[768,512]{1,0:T(8,128)S(1)}, u32[]{:S(2)}, u32[]{:S(2)}) collective-permute-start(f32[768,512]{1,0:T(8,128)S(1)} %shard_map.80.refs_2_), channel_id=1, source_target_pairs={{0,1},{1,0},{2,3},{3,2},{4,5},{5,4},{6,7},{7,6},{8,9},{9,8},{10,11... | collective-permute-start | bytes 4718600 | tf_op jit(solution)/shard_map/ppermute | solution.py:458
  184.7 64.9 %collective-permute-start.36 = (f32[320,2048]{1,0:T(8,128)}, f32[320,2048]{1,0:T(8,128)}, u32[]{:S(2)}, u32[]{:S(2)}) collective-permute-start(f32[320,2048]{1,0:T(8,128)} %shard_map.81), channel_id=1, source_target_pairs={{0,2},{1,3},{2,4},{3,5},{4,6},{5,7},{6,0},{7,1},{8,10},{9,11},{10,... | collective-permute-start | bytes 7864328 | tf_op jit(solution)/shard_map/ppermute | solution.py:466
  185.4 2.3 copy-start.7
  187.7 1.7 copy-start.10
  190.9 2.2 copy-start.13
  193.1 1.7 copy-start.15
  196.2 24.5 %copy-start.1 = (f32[1,512,2048]{2,1,0:T(8,128)S(1)}, f32[1,512,2048]{2,1,0:T(8,128)}, u32[]{:S(2)}) copy-start(f32[1,512,2048]{2,1,0:T(8,128)} %param.6) | copy-start | bytes 12582916
  220.7 10.0 %copy-start.4 = (bf16[4,512,512]{2,1,0:T(8,128)(2,1)}, bf16[4,512,512]{2,1,0:T(8,128)(2,1)S(1)}, u32[]{:S(2)}) copy-start(bf16[4,512,512]{2,1,0:T(8,128)(2,1)S(1)} %get-tuple-element.30.low) | copy-start | bytes 6291460
  221.3 9.4 %collective-permute-start.32 = (f32[96,2048]{1,0:T(8,128)S(1)}, f32[96,2048]{1,0:T(8,128)S(1)}, u32[]{:S(2)}, u32[]{:S(2)}) collective-permute-start(f32[96,2048]{1,0:T(8,128)S(1)} %shard_map.84), channel_id=1, source_target_pairs={{0,1},{1,0},{2,3},{3,2},{4,5},{5,4},{6,7},{7,6},{8,9},{9,8},{10,11... | collective-permute-start | bytes 2359304 | tf_op jit(solution)/shard_map/ppermute | solution.py:458
  227.2 9.1 %collective-permute-start.29 = (f32[128,512]{1,0:T(8,128)S(1)}, f32[128,512]{1,0:T(8,128)S(1)}, u32[]{:S(2)}, u32[]{:S(2)}) collective-permute-start(f32[128,512]{1,0:T(8,128)S(1)} %get-tuple-element.32), channel_id=1, source_target_pairs={{0,8},{8,0},{16,24},{24,16},{1,9},{9,1},{17,25},{25,17},{2,10},{10... | collective-permute-start | bytes 786440 | tf_op jit(solution)/shard_map/ppermute | solution.py:507
  229.1 14.5 %collective-permute-start.30 = (f32[128,512]{1,0:T(8,128)S(1)}, f32[128,512]{1,0:T(8,128)S(1)}, u32[]{:S(2)}, u32[]{:S(2)}) collective-permute-start(f32[128,512]{1,0:T(8,128)S(1)} %get-tuple-element.33), channel_id=1, source_target_pairs={{0,16},{8,24},{16,0},{24,8},{1,17},{9,25},{17,1},{25,9},{2,18},{10... | collective-permute-start | bytes 786440 | tf_op jit(solution)/shard_map/ppermute | solution.py:507
  229.9 13.7 %collective-permute-start.31 = (f32[128,512]{1,0:T(8,128)S(1)}, f32[128,512]{1,0:T(8,128)S(1)}, u32[]{:S(2)}, u32[]{:S(2)}) collective-permute-start(f32[128,512]{1,0:T(8,128)S(1)} %get-tuple-element.34), channel_id=1, source_target_pairs={{0,24},{8,16},{16,8},{24,0},{1,25},{9,17},{17,9},{25,1},{2,26},{10... | collective-permute-start | bytes 786440 | tf_op jit(solution)/shard_map/ppermute | solution.py:507
  233.9 11.2 %collective-permute-start.33 = (f32[128,192]{1,0:T(8,128)S(1)}, f32[128,192]{1,0:T(8,128)S(1)}, u32[]{:S(2)}, u32[]{:S(2)}) collective-permute-start(f32[128,192]{1,0:T(8,128)S(1)} %get-tuple-element.36), channel_id=1, source_target_pairs={{0,8},{8,0},{16,24},{24,16},{1,9},{9,1},{17,25},{25,17},{2,10},{10... | collective-permute-start | bytes 294920 | tf_op jit(solution)/shard_map/ppermute | solution.py:507
  236.3 11.0 %collective-permute-start.34 = (f32[128,192]{1,0:T(8,128)S(1)}, f32[128,192]{1,0:T(8,128)S(1)}, u32[]{:S(2)}, u32[]{:S(2)}) collective-permute-start(f32[128,192]{1,0:T(8,128)S(1)} %get-tuple-element.37), channel_id=1, source_target_pairs={{0,16},{8,24},{16,0},{24,8},{1,17},{9,25},{17,1},{25,9},{2,18},{10... | collective-permute-start | bytes 294920 | tf_op jit(solution)/shard_map/ppermute | solution.py:507
  243.6 5.9 %collective-permute-start.35 = (f32[128,192]{1,0:T(8,128)S(1)}, f32[128,192]{1,0:T(8,128)S(1)}, u32[]{:S(2)}, u32[]{:S(2)}) collective-permute-start(f32[128,192]{1,0:T(8,128)S(1)} %get-tuple-element.38), channel_id=1, source_target_pairs={{0,24},{8,16},{16,8},{24,0},{1,25},{9,17},{17,9},{25,1},{2,26},{10... | collective-permute-start | bytes 294920 | tf_op jit(solution)/shard_map/ppermute | solution.py:507
  249.5 2.2 copy-start.2
  251.7 5.7 %copy-start.5 = (bf16[4,512,512]{2,1,0:T(8,128)(2,1)S(1)}, bf16[4,512,512]{2,1,0:T(8,128)(2,1)}, u32[]{:S(2)}) copy-start(bf16[4,512,512]{2,1,0:T(8,128)(2,1)} %copy-done.4) | copy-start | bytes 6291460
  251.7 5.7 %copy-start.18 = (f32[8,128]{1,0:T(8,128)S(1)}, f32[8,128]{1,0:T(8,128)}, u32[]{:S(2)}) copy-start(f32[8,128]{1,0:T(8,128)} %slice.84.refs_1_.earlier) | copy-start | bytes 12292
  252.5 5.0 %collective-permute-start.37 = (f32[320,2048]{1,0:T(8,128)S(1)}, f32[320,2048]{1,0:T(8,128)S(1)}, u32[]{:S(2)}, u32[]{:S(2)}) collective-permute-start(f32[320,2048]{1,0:T(8,128)S(1)} %shard_map.87), channel_id=1, source_target_pairs={{0,1},{1,0},{2,3},{3,2},{4,5},{5,4},{6,7},{7,6},{8,9},{9,8},{10,11... | collective-permute-start | bytes 7864328 | tf_op jit(solution)/shard_map/ppermute | solution.py:458
  252.9 31.4 %collective-permute-start.41 = (f32[96,2048]{1,0:T(8,128)S(1)}, f32[96,2048]{1,0:T(8,128)S(1)}, u32[]{:S(2)}, u32[]{:S(2)}) collective-permute-start(f32[96,2048]{1,0:T(8,128)S(1)} %copy-done.20), channel_id=1, source_target_pairs={{0,2},{1,3},{2,4},{3,5},{4,6},{5,7},{6,0},{7,1},{8,10},{9,11},{10,... | collective-permute-start | bytes 2359304 | tf_op jit(solution)/shard_map/ppermute | solution.py:466
  257.5 26.8 %copy-start.3 = (f32[1,512,2048]{2,1,0:T(8,128)S(1)}, f32[1,512,2048]{2,1,0:T(8,128)}, u32[]{:S(2)}) copy-start(f32[1,512,2048]{2,1,0:T(8,128)} %param.6) | copy-start | bytes 12582916
  266.2 10.6 %collective-permute-start.38 = (f32[128,640]{1,0:T(8,128)S(1)}, f32[128,640]{1,0:T(8,128)S(1)}, u32[]{:S(2)}, u32[]{:S(2)}) collective-permute-start(f32[128,640]{1,0:T(8,128)S(1)} %get-tuple-element.40), channel_id=1, source_target_pairs={{0,8},{8,0},{16,24},{24,16},{1,9},{9,1},{17,25},{25,17},{2,10},{10... | collective-permute-start | bytes 983048 | tf_op jit(solution)/shard_map/ppermute | solution.py:507
  267.4 16.7 %collective-permute-start.39 = (f32[128,640]{1,0:T(8,128)S(1)}, f32[128,640]{1,0:T(8,128)S(1)}, u32[]{:S(2)}, u32[]{:S(2)}) collective-permute-start(f32[128,640]{1,0:T(8,128)S(1)} %get-tuple-element.41), channel_id=1, source_target_pairs={{0,16},{8,24},{16,0},{24,8},{1,17},{9,25},{17,1},{25,9},{2,18},{10... | collective-permute-start | bytes 983048 | tf_op jit(solution)/shard_map/ppermute | solution.py:507
  268.0 16.1 %collective-permute-start.40 = (f32[128,640]{1,0:T(8,128)S(1)}, f32[128,640]{1,0:T(8,128)S(1)}, u32[]{:S(2)}, u32[]{:S(2)}) collective-permute-start(f32[128,640]{1,0:T(8,128)S(1)} %get-tuple-element.42), channel_id=1, source_target_pairs={{0,24},{8,16},{16,8},{24,0},{1,25},{9,17},{17,9},{25,1},{2,26},{10... | collective-permute-start | bytes 983048 | tf_op jit(solution)/shard_map/ppermute | solution.py:507
  284.9 2.4 collective-permute-start.42
  285.1 14.3 %copy-start.22 = (f32[128,512]{1,0:T(8,128)S(1)}, f32[128,512]{1,0:T(8,128)}, u32[]{:S(2)}) copy-start(f32[128,512]{1,0:T(8,128)} %copy-done.21) | copy-start | bytes 786436
  290.5 6.4 %collective-permute-start.43 = (f32[128,192]{1,0:T(8,128)S(1)}, f32[128,192]{1,0:T(8,128)S(1)}, u32[]{:S(2)}, u32[]{:S(2)}) collective-permute-start(f32[128,192]{1,0:T(8,128)S(1)} %get-tuple-element.44), channel_id=1, source_target_pairs={{0,8},{8,0},{16,24},{24,16},{1,9},{9,1},{17,25},{25,17},{2,10},{10... | collective-permute-start | bytes 294920 | tf_op jit(solution)/shard_map/ppermute | solution.py:507
  291.2 8.1 %collective-permute-start.44 = (f32[128,192]{1,0:T(8,128)S(1)}, f32[128,192]{1,0:T(8,128)S(1)}, u32[]{:S(2)}, u32[]{:S(2)}) collective-permute-start(f32[128,192]{1,0:T(8,128)S(1)} %get-tuple-element.45), channel_id=1, source_target_pairs={{0,16},{8,24},{16,0},{24,8},{1,17},{9,25},{17,1},{25,9},{2,18},{10... | collective-permute-start | bytes 294920 | tf_op jit(solution)/shard_map/ppermute | solution.py:507
  292.3 7.0 %collective-permute-start.45 = (f32[128,192]{1,0:T(8,128)S(1)}, f32[128,192]{1,0:T(8,128)S(1)}, u32[]{:S(2)}, u32[]{:S(2)}) collective-permute-start(f32[128,192]{1,0:T(8,128)S(1)} %get-tuple-element.46), channel_id=1, source_target_pairs={{0,24},{8,16},{16,8},{24,0},{1,25},{9,17},{17,9},{25,1},{2,26},{10... | collective-permute-start | bytes 294920 | tf_op jit(solution)/shard_map/ppermute | solution.py:507
  (6 other events, 7.3 us)

commit v6 on v5

--- a/solution.py
+++ b/solution.py
@@ -10,8 +10,8 @@
 HIGHEST = lax.Precision.HIGHEST
 CHUNKS = 17
 SKEW = 2
-GROUPS = ((0, 9), (9, 14), (14, 17))
-TRAIN_CUTS = (96, 320, 96)
+GROUPS = ((0, 4), (4, 8), (8, 12), (12, 17))
+TRAIN_CUTS = (96, 256, 96, 64)
 MIB = 1024 * 1024
 HBM = pl.BlockSpec(memory_space=pltpu.HBM)
 SMEM = pl.BlockSpec(memory_space=pltpu.SMEM)
@@ -268,17 +268,17 @@
         copy.wait()
 
 
-def collected(stream, chips, first, last, info, own, got):
+def collected(stream, chips, first, last, info, own, got, earlier):
     received = [got[s] for s in range(first, last + SKEW * (chips - 2))]
     return pl.pallas_call(
         functools.partial(collect_kernel, stream, chips, first, last),
         out_shape=jax.ShapeDtypeStruct(((last - first) * stream.step, stream.size), jnp.float32),
-        in_specs=[SMEM] + [HBM] * (1 + len(received)),
+        in_specs=[SMEM] + [HBM] * (1 + len(received) + len(earlier)),
         out_specs=HBM,
         scratch_shapes=[pltpu.SemaphoreType.DMA(((last - first) * len(stream.pieces),))],
         compiler_params=param(4),
         cost_estimate=cost(0, 1000),
-    )(info, own, *received)
+    )(info, own, *received, *earlier)
 
 
 def sweep_kernel(stream, n_sec, info, earlier, query, *refs):
@@ -390,39 +390,40 @@
     )(info, earlier, query, *own, *other)
 
 
-def score_kernel(n_sec, scale, first, counts, earlier, high, low, *refs):
-    blocks = len(refs) - n_sec - 3
-    trains, outs = refs[:blocks], refs[blocks : blocks + n_sec]
+def score_kernel(n_sec, scale, blocks, counts, earlier, high, low, *refs):
+    trains, outs = refs[: len(blocks)], refs[len(blocks) : len(blocks) + n_sec]
     train_high, train_low, total = refs[-3:]
     panels, rows, size = high.shape
-    length = trains[0].shape[0]
-    for b, train in enumerate(trains):
+    cols = total.shape[1]
+    col = lax.broadcasted_iota(jnp.int32, (1, cols), 1)
+    start, limit = 0, None
+    for (length, which, first), train in zip(blocks, trains):
         for p in range(panels):
-            span = slice(b * length, (b + 1) * length)
+            span = slice(start, start + length)
             train_high[p, span, :], train_low[p, span, :] = parts_of(train[:, p * size : (p + 1) * size])
+        bound = jnp.full_like(col, counts[which] - first + start)
+        limit = bound if limit is None else jnp.where(col >= start, bound, limit)
+        start += length
     total[...] = jnp.zeros_like(total)
 
     @pl.loop(0, panels)
     def _(p):
         total[...] += dot_parts((high[p], low[p]), (train_high[p], train_low[p]), 1)
 
-    col = lax.broadcasted_iota(jnp.int32, (1, blocks * length), 1)
-    limit = jnp.full_like(col, counts[0] - first)
-    for b in range(1, blocks):
-        limit = jnp.where(col >= b * length, counts[b] - first + b * length, limit)
     factor = jnp.where(col < limit, scale, 0.0).astype(jnp.float32)
     share = rows // n_sec
     for k in range(n_sec):
         outs[k][...] = total[k * share : (k + 1) * share, :] * factor
 
 
-def scored(n_sec, scale, first, counts, earlier, high, low, trains):
+def scored(n_sec, scale, counts, earlier, high, low, runs):
     panels, rows, size = high.shape
-    cols = sum(t.shape[0] for t in trains)
-    return pl.pallas_call(
-        functools.partial(score_kernel, n_sec, scale, first),
+    blocks = [(train.shape[0], which, first) for train, which, first in runs]
+    cols = sum(length for length, _, _ in blocks)
+    return pl.pallas_call(
+        functools.partial(score_kernel, n_sec, scale, blocks),
         out_shape=tuple(jax.ShapeDtypeStruct((rows // n_sec, cols), jnp.float32) for _ in range(n_sec)),
-        in_specs=[SMEM, HBM] + [VMEM] * (2 + len(trains)),
+        in_specs=[SMEM, HBM] + [VMEM] * (2 + len(runs)),
         out_specs=tuple(VMEM for _ in range(n_sec)),
         scratch_shapes=[
             pltpu.VMEM((panels, cols, size), jnp.bfloat16),
@@ -431,7 +432,7 @@
         ],
         compiler_params=param(24),
         cost_estimate=cost(0, 1000),
-    )(counts, earlier, high, low, *trains)
+    )(counts, earlier, high, low, *[train for train, _, _ in runs])
 
 
 def body(query_gradient_stack, train_grads, factor_slots, owner, train_count):
@@ -471,16 +472,13 @@
     own_rows = build_stream(stream, chips, info, slot, peer, packed, swapped(packed))
     count_2 = lax.ppermute(train_count, "dp", next_chip)
     count_1 = lax.ppermute(train_count, "dp", [(d, (d + 1) % n_dp) for d in range(n_dp)])
-    near_counts = jnp.concatenate([count_1, count_2])
+    counts = jnp.concatenate([train_count, count_1, count_2])
 
     got, own, other = {}, [], []
     steps = CHUNKS + SKEW * (chips - 2)
     for number in range(steps):
         earlier = [corner(far[0])] if number == 0 else [block]
-        for index, (first, last) in enumerate(GROUPS[:-1]):
-            if number == last + 2 + SKEW * (chips - 2):
-                earlier.append(corner(other[index]))
-        block = step_block(stream, number, info, near_counts, own_rows, got, earlier)
+        block = step_block(stream, number, info, counts, own_rows, got, earlier)
         pairs = []
         for p in range(chips - 1):
             if 0 <= number - SKEW * p < CHUNKS:
@@ -488,12 +486,15 @@
         got[number] = lax.ppermute(block, "dp", pairs)
         for first, last in GROUPS:
             if number == last - 1 + SKEW * (chips - 2):
-                value = collected(stream, chips, first, last, info, own_rows, got)
+                before = [corner(rows_before) for rows_before in other[:2]] if last == CHUNKS else []
+                value = collected(stream, chips, first, last, info, own_rows, got, before)
                 own.append(value)
                 other.append(swapped(value))
 
-    part = send_train(1, corner(other[-1]))
-    high, low, swept_token = swept(stream, n_sec, info, corner(part), query, own, other)
+    token = corner(other[-1])
+    for index in range(1, len(cuts) - 1):
+        token = corner(send_train(index, token))
+    high, low, swept_token = swept(stream, n_sec, info, token, query, own, other)
 
     scale = (coords * n_sec) ** (-0.5)
 
@@ -507,20 +508,21 @@
             total = total + lax.ppermute(parts[k], "section", pairs)
         return total
 
-    parts = scored(n_sec, scale, 0, train_count, swept_token, high, low, [train])
-    own_scores = summed(parts)
-    near_scores, far_scores, earlier = [], [], [corner(own_scores)]
+    def near_rows(index, *earlier):
+        return swapped(chosen(info, train, cuts[index], far[index], *earlier))
+
+    runs = [(train, 0, 0), (near_rows(0, swept_token), 1, 0), (far[0], 2, 0)]
+    near_scores, far_scores, summed_corners, earlier = [], [], [], [swept_token]
     for index in range(len(cuts) - 1):
-        if index == 1:
-            earlier.append(corner(send_train(2, corner(parts[0]))))
-        far_part = far[index]
-        near_part = swapped(chosen(info, train, cuts[index], far_part, *(earlier if index else [swept_token])))
+        if index:
+            runs = [(near_rows(index, *earlier), 1, cuts[index]), (far[index], 2, cuts[index])]
+        parts = scored(n_sec, scale, counts, earlier[0], high, low, runs)
+        both = summed(parts)
+        summed_corners.append(corner(both))
+        earlier = [corner(parts[0])] + (summed_corners if index else [])
         length = cuts[index + 1] - cuts[index]
-        parts = scored(
-            n_sec, scale, cuts[index], near_counts, corner(parts[0]), high, low, [near_part, far_part]
-        )
-        both = summed(parts)
-        earlier.append(corner(both))
+        if index == 0:
+            own_scores, both = both[:, :rows], both[:, rows:]
         near_scores.append(both[:, :length])
         far_scores.append(both[:, length:])
     return jnp.concatenate([own_scores] + near_scores + far_scores, axis=1)[None]

time: 303 us -> 289 us (0.954)
  waiting for transfers between devices: 68.9 us -> 56.6 us
  Pallas kernels: 88.4 us -> 92.3 us
    ppermute x21, waiting for transfers between devices: 23.9 us -> 15 us  [body(): got[number] = lax.ppermute(block, 'dp', pairs)]
    ppermute x12, waiting for transfers between devices: 29.7 us -> 25.3 us  [summed(): total = total + lax.ppermute(parts[k], 'section', pairs)]
    unnamed x48 -> x36, local copies, waits for them, and re-layouts: 19 us -> 14.8 us
    ppermute x8 -> x10, starting transfers between devices: 21.8 us -> 18.8 us  [swapped(): return lax.ppermute(value, 'dp', swap_pairs)]
    pallas_call x3 -> x4, Pallas kernels: 5.58 us -> 6.72 us  [collected(): pl.pallas_call(functools.partial(collect_kernel, stream, chips, first, la...]
  transfers between devices with their start and end apart: 46 -> 49, of which waited for: 24 -> 26; matrix products, arithmetic and copies ran while one was open for 2% -> 3% of each run, Pallas kernels for 24% -> 28%
where the time goes in v6:
time: 289 us; the launch traced here: 287 us
  starting transfers between devices  110 us (38%)
  Pallas kernels  92.3 us (32%)
  waiting for transfers between devices  56.6 us (20%)
  local copies, waits for them, and re-layouts  25.9 us (9%)
    ppermute x21, starting transfers between devices, body(): got[number] = lax.ppermute(block, 'dp', pairs)  68.7 us
    pallas_call x21, Pallas kernels, step_block(): pl.pallas_call(functools.partial(step_kernel, stream, number), out_shape=...  27.5 us
    pallas_call x1, Pallas kernels, swept(): pl.pallas_call(functools.partial(sweep_kernel, stream, n_sec), out_shape=...  26.7 us
    ppermute x12, waiting for transfers between devices, summed(): total = total + lax.ppermute(parts[k], 'section', pairs)  25.3 us
    pallas_call x4, Pallas kernels, scored(): pl.pallas_call(functools.partial(score_kernel, n_sec, scale, blocks), out...  19.9 us
    ppermute x10, starting transfers between devices, swapped(): return lax.ppermute(value, 'dp', swap_pairs)  18.8 us
    ppermute x12, starting transfers between devices, summed(): total = total + lax.ppermute(parts[k], 'section', pairs)  15 us
    ppermute x21, waiting for transfers between devices, body(): got[number] = lax.ppermute(block, 'dp', pairs)  15 us
  transfers between devices with their start and end apart: 49, of which 26 were waited for; matrix products, arithmetic and copies ran while one was open for 3% of the time, Pallas kernels for 28%

profile of v6, /device:TPU:0, one launch (start us, length us, event | category | flops | bytes accessed | tf_op | source)
XLA Modules:
  0.0 287.4 jit_solution(13512519097115348792)
XLA Ops:
  0.0 2.4 slice_bitcast_fusion.1
  2.8 2.6 collective-permute-start.4
  5.5 2.2 copy-done.2
  7.7 5.4 %shard_map.55.packed = f32[320,512]{1,0:T(8,128)S(1)} custom-call(s32[13]{0:T(128)S(1)} %concatenate.11.info, f32[2048,512]{1,0:T(8,128)S(1)} %bitcast.25), custom_call_target="tpu_custom_call" | custom-call | bytes 1000 | tf_op jit(solution)/shard_map/pallas_call | solution.py:136
  13.7 1.6 collective-permute-start.1
  16.0 9.6 %collective-permute-done = s32[1]{0:T(128)} collective-permute-done((s32[1]{0:T(128)}, s32[1]{0:T(128)}, u32[]{:S(2)}, u32[]{:S(2)}) %collective-permute-start) | collective-permute-done | bytes 36 | tf_op jit(solution)/shard_map/ppermute | solution.py:474
  25.8 1.3 pad_add_fusion.counts
  27.2 3.5 %shard_map.56.own = f32[5888,512]{1,0:T(8,128)S(1)} custom-call(s32[13]{0:T(128)S(1)} %concatenate.11.info, f32[2048,512]{1,0:T(8,128)S(1)} %bitcast.26, f32[2048,512]{1,0:T(8,128)} %collective-permute-done.2.peer, f32[320,512]{1,0:T(8,128)S(1)} %shard_map.55.packed, f32[320,512]{1,0:T(8,128)S(1)} %collective-permute-done.3.peer_packed), custom_call_target="tpu_custom_call" | custom-call | bytes 1000 | tf_op jit(solution)/shard_map/pallas_call | solution.py:200
  32.0 1.7 collective-permute-start.5
  34.9 1.3 collective-permute-start.7
  36.3 4.0 %collective-permute-done.5.refs_0_ = f32[256,512]{1,0:T(8,128)S(1)} collective-permute-done((f32[256,512]{1,0:T(8,128)S(1)}, f32[256,512]{1,0:T(8,128)S(1)}, u32[]{:S(2)}, u32[]{:S(2)}) %collective-permute-start.5) | collective-permute-done | bytes 524320 | tf_op jit(solution)/shard_map/ppermute | solution.py:486
  41.6 4.4 %collective-permute-start.6 = (f32[256,512]{1,0:T(8,128)S(1)}, f32[256,512]{1,0:T(8,128)S(1)}, u32[]{:S(2)}, u32[]{:S(2)}) collective-permute-start(f32[256,512]{1,0:T(8,128)S(1)} %shard_map.59.refs_1_), channel_id=1, source_target_pairs={{0,2},{7,5},{2,4},{5,3},{8,10},{15,13},{10,12},{13,11},{16,18},{23... | collective-permute-start | bytes 1572872 | tf_op jit(solution)/shard_map/ppermute | solution.py:486
  46.1 1.3 shard_map.60.refs_1_
  47.4 4.3 %collective-permute-start.9 = (f32[256,512]{1,0:T(8,128)S(1)}, f32[256,512]{1,0:T(8,128)S(1)}, u32[]{:S(2)}, u32[]{:S(2)}) collective-permute-start(f32[256,512]{1,0:T(8,128)S(1)} %shard_map.60.refs_1_), channel_id=1, source_target_pairs={{0,2},{7,5},{2,4},{5,3},{8,10},{15,13},{10,12},{13,11},{16,18},{23... | collective-permute-start | bytes 1572872 | tf_op jit(solution)/shard_map/ppermute | solution.py:486
  54.0 4.4 %collective-permute-start.8 = (f32[256,512]{1,0:T(8,128)S(1)}, f32[256,512]{1,0:T(8,128)S(1)}, u32[]{:S(2)}, u32[]{:S(2)}) collective-permute-start(f32[256,512]{1,0:T(8,128)S(1)} %shard_map.61.refs_1_), channel_id=1, source_target_pairs={{0,2},{7,5},{2,4},{5,3},{4,6},{3,1},{8,10},{15,13},{10,12},{13,11}... | collective-permute-start | bytes 1572872 | tf_op jit(solution)/shard_map/ppermute | solution.py:486
  58.5 1.3 shard_map.62.refs_1_
  59.8 4.3 %collective-permute-start.11 = (f32[256,512]{1,0:T(8,128)S(1)}, f32[256,512]{1,0:T(8,128)S(1)}, u32[]{:S(2)}, u32[]{:S(2)}) collective-permute-start(f32[256,512]{1,0:T(8,128)S(1)} %shard_map.62.refs_1_), channel_id=1, source_target_pairs={{0,2},{7,5},{2,4},{5,3},{4,6},{3,1},{8,10},{15,13},{10,12},{13,11}... | collective-permute-start | bytes 1572872 | tf_op jit(solution)/shard_map/ppermute | solution.py:486
  66.4 4.4 %collective-permute-start.10 = (f32[256,512]{1,0:T(8,128)S(1)}, f32[256,512]{1,0:T(8,128)S(1)}, u32[]{:S(2)}, u32[]{:S(2)}) collective-permute-start(f32[256,512]{1,0:T(8,128)S(1)} %shard_map.63.refs_1_), channel_id=1, source_target_pairs={{0,2},{7,5},{2,4},{5,3},{4,6},{3,1},{8,10},{15,13},{10,12},{13,11}... | collective-permute-start | bytes 1572872 | tf_op jit(solution)/shard_map/ppermute | solution.py:486
  72.2 4.3 %collective-permute-start.13 = (f32[256,512]{1,0:T(8,128)S(1)}, f32[256,512]{1,0:T(8,128)S(1)}, u32[]{:S(2)}, u32[]{:S(2)}) collective-permute-start(f32[256,512]{1,0:T(8,128)S(1)} %shard_map.64.refs_1_), channel_id=1, source_target_pairs={{0,2},{7,5},{2,4},{5,3},{4,6},{3,1},{8,10},{15,13},{10,12},{13,11}... | collective-permute-start | bytes 1572872 | tf_op jit(solution)/shard_map/ppermute | solution.py:486
  78.8 4.4 %collective-permute-start.12 = (f32[256,512]{1,0:T(8,128)S(1)}, f32[256,512]{1,0:T(8,128)S(1)}, u32[]{:S(2)}, u32[]{:S(2)}) collective-permute-start(f32[256,512]{1,0:T(8,128)S(1)} %shard_map.65.refs_1_), channel_id=1, source_target_pairs={{0,2},{7,5},{2,4},{5,3},{4,6},{3,1},{8,10},{15,13},{10,12},{13,11}... | collective-permute-start | bytes 1572872 | tf_op jit(solution)/shard_map/ppermute | solution.py:486
  84.6 4.3 %collective-permute-start.15 = (f32[256,512]{1,0:T(8,128)S(1)}, f32[256,512]{1,0:T(8,128)S(1)}, u32[]{:S(2)}, u32[]{:S(2)}) collective-permute-start(f32[256,512]{1,0:T(8,128)S(1)} %shard_map.66.refs_1_), channel_id=1, source_target_pairs={{0,2},{7,5},{2,4},{5,3},{4,6},{3,1},{8,10},{15,13},{10,12},{13,11}... | collective-permute-start | bytes 1572872 | tf_op jit(solution)/shard_map/ppermute | solution.py:486
  91.2 4.4 %collective-permute-start.14 = (f32[256,512]{1,0:T(8,128)S(1)}, f32[256,512]{1,0:T(8,128)S(1)}, u32[]{:S(2)}, u32[]{:S(2)}) collective-permute-start(f32[256,512]{1,0:T(8,128)S(1)} %shard_map.67.refs_1_), channel_id=1, source_target_pairs={{0,2},{7,5},{2,4},{5,3},{4,6},{3,1},{8,10},{15,13},{10,12},{13,11}... | collective-permute-start | bytes 1572872 | tf_op jit(solution)/shard_map/ppermute | solution.py:486
  97.0 4.3 %collective-permute-start.17 = (f32[256,512]{1,0:T(8,128)S(1)}, f32[256,512]{1,0:T(8,128)S(1)}, u32[]{:S(2)}, u32[]{:S(2)}) collective-permute-start(f32[256,512]{1,0:T(8,128)S(1)} %shard_map.68.refs_1_), channel_id=1, source_target_pairs={{0,2},{7,5},{2,4},{5,3},{4,6},{3,1},{8,10},{15,13},{10,12},{13,11}... | collective-permute-start | bytes 1572872 | tf_op jit(solution)/shard_map/ppermute | solution.py:486
  103.6 4.4 %collective-permute-start.16 = (f32[256,512]{1,0:T(8,128)S(1)}, f32[256,512]{1,0:T(8,128)S(1)}, u32[]{:S(2)}, u32[]{:S(2)}) collective-permute-start(f32[256,512]{1,0:T(8,128)S(1)} %shard_map.69.refs_1_), channel_id=1, source_target_pairs={{0,2},{7,5},{2,4},{5,3},{4,6},{3,1},{8,10},{15,13},{10,12},{13,11}... | collective-permute-start | bytes 1572872 | tf_op jit(solution)/shard_map/ppermute | solution.py:486
  109.4 4.3 %collective-permute-start.18 = (f32[256,512]{1,0:T(8,128)S(1)}, f32[256,512]{1,0:T(8,128)S(1)}, u32[]{:S(2)}, u32[]{:S(2)}) collective-permute-start(f32[256,512]{1,0:T(8,128)S(1)} %shard_map.70.refs_1_), channel_id=1, source_target_pairs={{0,2},{7,5},{2,4},{5,3},{4,6},{3,1},{8,10},{15,13},{10,12},{13,11}... | collective-permute-start | bytes 1572872 | tf_op jit(solution)/shard_map/ppermute | solution.py:486
  116.0 4.4 %collective-permute-start.19 = (f32[256,512]{1,0:T(8,128)S(1)}, f32[256,512]{1,0:T(8,128)S(1)}, u32[]{:S(2)}, u32[]{:S(2)}) collective-permute-start(f32[256,512]{1,0:T(8,128)S(1)} %shard_map.71.refs_1_), channel_id=1, source_target_pairs={{0,2},{7,5},{2,4},{5,3},{4,6},{3,1},{8,10},{15,13},{10,12},{13,11}... | collective-permute-start | bytes 1572872 | tf_op jit(solution)/shard_map/ppermute | solution.py:486
  121.7 1.5 shard_map.79.refs_1_
  125.1 1.9 collective-permute-start.20
  128.4 4.4 %collective-permute-start.21 = (f32[256,512]{1,0:T(8,128)S(1)}, f32[256,512]{1,0:T(8,128)S(1)}, u32[]{:S(2)}, u32[]{:S(2)}) collective-permute-start(f32[256,512]{1,0:T(8,128)S(1)} %shard_map.73.refs_1_), channel_id=1, source_target_pairs={{0,2},{7,5},{2,4},{5,3},{4,6},{3,1},{8,10},{15,13},{10,12},{13,11}... | collective-permute-start | bytes 1572872 | tf_op jit(solution)/shard_map/ppermute | solution.py:486
  135.7 3.8 %collective-permute-done.21.refs_0_.refs_4_ = f32[256,512]{1,0:T(8,128)S(1)} collective-permute-done((f32[256,512]{1,0:T(8,128)S(1)}, f32[256,512]{1,0:T(8,128)S(1)}, u32[]{:S(2)}, u32[]{:S(2)}) %collective-permute-start.21) | collective-permute-done | bytes 524320 | tf_op jit(solution)/shard_map/ppermute | solution.py:486
  146.9 1.4 copy-done.12
  148.3 1.9 shard_map.80.refs_3_
  150.2 14.9 %collective-permute-start.28 = (f32[1280,512]{1,0:T(8,128)S(1)}, f32[1280,512]{1,0:T(8,128)S(1)}, u32[]{:S(2)}, u32[]{:S(2)}) collective-permute-start(f32[1280,512]{1,0:T(8,128)S(1)} %shard_map.80.refs_3_), channel_id=1, source_target_pairs={{0,1},{1,0},{2,3},{3,2},{4,5},{5,4},{6,7},{7,6},{8,9},{9,8},{10,11... | collective-permute-start | bytes 7864328 | tf_op jit(solution)/shard_map/ppermute | solution.py:459
  165.1 2.2 shard_map.84.refs_2_
  167.4 1.6 slice_bitcast_fusion.refs_0_
  170.2 1.5 copy-done.8
  171.7 1.9 slice_bitcast_fusion.3.refs_0_
  176.8 1.6 copy-done.5
  178.4 1.6 copy-done.7
  179.9 1.7 copy-done.9
  181.7 1.6 copy-done.11
  183.3 1.6 copy-done.13
  184.9 26.7 %shard_map.85 = (bf16[4,512,512]{2,1,0:T(8,128)(2,1)S(1)}, bf16[4,512,512]{2,1,0:T(8,128)(2,1)S(1)}, f32[8,128]{1,0:T(8,128)S(1)}) custom-call(s32[13]{0:T(128)S(1)} %concatenate.11.info, f32[8,128]{1,0:T(8,128)S(1)} %slice.127.earlier, f32[512,2048]{1,0:T(8,128)} %bitcast.27, f32[1024,512]{1,0:T(8,128)S(1)} %copy-done.5, f32[1024,512]{1,0:T(8,128)S(1)} %copy-done.7, ...), custom_call_target="tpu_custom_call" | custom-call | bytes 1000 | tf_op jit(solution)/shard_map/pallas_call | solution.py:372
  212.6 1.9 collective-permute-done.30.refs_1_
  214.6 7.2 %shard_map.87 = (f32[128,704]{1,0:T(8,128)S(1)}, f32[128,704]{1,0:T(8,128)S(1)}, f32[128,704]{1,0:T(8,128)S(1)}, f32[128,704]{1,0:T(8,128)S(1)}) custom-call(s32[3]{0:T(128)S(1)} %pad_add_fusion.counts, f32[8,128]{1,0:T(8,128)S(1)} %get-tuple-element.28.refs_0_.earlier, bf16[4,512,512]{2,1,0:T(8,128)(2,1)S(1)} %get-tuple-element.29.high, ...), custom_call_target="tpu_custom_call" | custom-call | bytes 1000 | tf_op jit(solution)/shard_map/pallas_call | solution.py:423
  222.6 1.9 collective-permute-start.35
  224.4 1.5 collective-permute-start.31
  229.2 6.5 %shard_map.89 = (f32[128,512]{1,0:T(8,128)S(1)}, f32[128,512]{1,0:T(8,128)S(1)}, f32[128,512]{1,0:T(8,128)S(1)}, f32[128,512]{1,0:T(8,128)S(1)}) custom-call(s32[3]{0:T(128)S(1)} %pad_add_fusion.counts, f32[8,128]{1,0:T(8,128)S(1)} %slice.108.refs_0_.earlier, bf16[4,512,512]{2,1,0:T(8,128)(2,1)S(1)} %get-tuple-element.29.high, ...), custom_call_target="tpu_custom_call" | custom-call | bytes 1000 | tf_op jit(solution)/shard_map/pallas_call | solution.py:423
  235.7 1.6 collective-permute-start.36
  238.5 6.1 %collective-permute-done.32 = f32[128,704]{1,0:T(8,128)S(1)} collective-permute-done((f32[128,704]{1,0:T(8,128)S(1)}, f32[128,704]{1,0:T(8,128)S(1)}, u32[]{:S(2)}, u32[]{:S(2)}) %collective-permute-start.32) | collective-permute-done | bytes 360480 | tf_op jit(solution)/shard_map/ppermute | solution.py:508
  244.7 1.6 collective-permute-start.38
  246.4 4.1 %collective-permute-done.36 = f32[128,512]{1,0:T(8,128)S(1)} collective-permute-done((f32[128,512]{1,0:T(8,128)S(1)}, f32[128,512]{1,0:T(8,128)S(1)}, u32[]{:S(2)}, u32[]{:S(2)}) %collective-permute-start.36) | collective-permute-done | bytes 262176 | tf_op jit(solution)/shard_map/ppermute | solution.py:508
  250.5 5.9 %collective-permute-done.37 = f32[128,512]{1,0:T(8,128)S(1)} collective-permute-done((f32[128,512]{1,0:T(8,128)S(1)}, f32[128,512]{1,0:T(8,128)S(1)}, u32[]{:S(2)}, u32[]{:S(2)}) %collective-permute-start.37) | collective-permute-done | bytes 262176 | tf_op jit(solution)/shard_map/ppermute | solution.py:508
  257.5 1.3 collective-permute-start.44
  259.5 3.2 %shard_map.91 = (f32[128,192]{1,0:T(8,128)S(1)}, f32[128,192]{1,0:T(8,128)S(1)}, f32[128,192]{1,0:T(8,128)S(1)}, f32[128,192]{1,0:T(8,128)S(1)}) custom-call(s32[3]{0:T(128)S(1)} %pad_add_fusion.counts, f32[8,128]{1,0:T(8,128)S(1)} %slice.110.refs_0_.earlier, bf16[4,512,512]{2,1,0:T(8,128)(2,1)S(1)} %get-tuple-element.29.high, ...), custom_call_target="tpu_custom_call" | custom-call | bytes 1000 | tf_op jit(solution)/shard_map/pallas_call | solution.py:423
  264.8 1.4 collective-permute-start.43
  266.2 2.9 collective-permute-done.41
  269.1 1.3 collective-permute-done.42
  270.4 1.3 collective-permute-done.43
  271.8 1.6 collective-permute-done.44.far.refs_1_
  274.2 1.8 collective-permute-done.45.refs_0_
  276.0 3.0 %shard_map.93 = (f32[128,128]{1,0:T(8,128)S(1)}, f32[128,128]{1,0:T(8,128)S(1)}, f32[128,128]{1,0:T(8,128)S(1)}, f32[128,128]{1,0:T(8,128)S(1)}) custom-call(s32[3]{0:T(128)S(1)} %pad_add_fusion.counts, f32[8,128]{1,0:T(8,128)S(1)} %slice.114.refs_0_.earlier, bf16[4,512,512]{2,1,0:T(8,128)(2,1)S(1)} %get-tuple-element.29.high, ...), custom_call_target="tpu_custom_call" | custom-call | bytes 1000 | tf_op jit(solution)/shard_map/pallas_call | solution.py:423
  281.1 1.4 collective-permute-start.48
  284.2 2.0 collective-permute-done.48
  (139 shorter events, 59.9 us)
Async XLA Ops:
  0.0 5.4 %copy-start.17 = (s32[1,4]{1,0:T(1,128)S(1)}, s32[1,4]{1,0:T(1,128)}, u32[]{:S(2)}) copy-start(s32[1,4]{1,0:T(1,128)} %param.8) | copy-start | bytes 52
  2.4 24.8 %collective-permute-start.2 = (f32[2048,512]{1,0:T(8,128)}, f32[2048,512]{1,0:T(8,128)}, u32[]{:S(2)}, u32[]{:S(2)}) collective-permute-start(f32[2048,512]{1,0:T(8,128)} %bitcast.24), channel_id=1, source_target_pairs={{0,1},{1,0},{2,3},{3,2},{4,5},{5,4},{6,7},{7,6},{8,9},{9,8},{10,11... | collective-permute-start | bytes 12582920 | tf_op jit(solution)/shard_map/ppermute | solution.py:459
  2.8 24.3 %collective-permute-start.4 = (f32[96,2048]{1,0:T(8,128)S(1)}, f32[96,2048]{1,0:T(8,128)S(1)}, u32[]{:S(2)}, u32[]{:S(2)}) collective-permute-start(f32[96,2048]{1,0:T(8,128)S(1)} %get-tuple-element.27), channel_id=1, source_target_pairs={{0,2},{1,3},{2,4},{3,5},{4,6},{5,7},{6,0},{7,1},{8,10},{9,11},{10,... | collective-permute-start | bytes 2359304 | tf_op jit(solution)/shard_map/ppermute | solution.py:463
  5.5 2.2 copy-start.2
  7.7 19.5 %copy-start.3 = (f32[1,1,2048,512]{3,2,1,0:T(8,128)S(1)}, f32[1,1,2048,512]{3,2,1,0:T(8,128)}, u32[]{:S(2)}) copy-start(f32[1,1,2048,512]{3,2,1,0:T(8,128)} %param.7) | copy-start | bytes 12582916
  13.1 14.0 %collective-permute-start.3 = (f32[320,512]{1,0:T(8,128)S(1)}, f32[320,512]{1,0:T(8,128)S(1)}, u32[]{:S(2)}, u32[]{:S(2)}) collective-permute-start(f32[320,512]{1,0:T(8,128)S(1)} %shard_map.55.packed), channel_id=1, source_target_pairs={{0,1},{1,0},{2,3},{3,2},{4,5},{5,4},{6,7},{7,6},{8,9},{9,8},{10,11... | collective-permute-start | bytes 1966088 | tf_op jit(solution)/shard_map/ppermute | solution.py:459
  13.4 12.1 %collective-permute-start = (s32[1]{0:T(128)}, s32[1]{0:T(128)}, u32[]{:S(2)}, u32[]{:S(2)}) collective-permute-start(s32[1]{0:T(128)} %param.9), channel_id=1, source_target_pairs={{0,1},{1,2},{2,3},{3,4},{4,5},{5,6},{6,7},{7,0},{8,9},{9,10},{10,1... | collective-permute-start | bytes 20 | tf_op jit(solution)/shard_map/ppermute | solution.py:474
  13.7 12.1 %collective-permute-start.1 = (s32[1]{0:T(128)}, s32[1]{0:T(128)}, u32[]{:S(2)}, u32[]{:S(2)}) collective-permute-start(s32[1]{0:T(128)} %param.9), channel_id=1, source_target_pairs={{0,2},{1,3},{2,4},{3,5},{4,6},{5,7},{6,0},{7,1},{8,10},{9,11},{10,... | collective-permute-start | bytes 20 | tf_op jit(solution)/shard_map/ppermute | solution.py:473
  32.0 8.3 %collective-permute-start.5 = (f32[256,512]{1,0:T(8,128)S(1)}, f32[256,512]{1,0:T(8,128)S(1)}, u32[]{:S(2)}, u32[]{:S(2)}) collective-permute-start(f32[256,512]{1,0:T(8,128)S(1)} %shard_map.57.refs_0_), channel_id=1, source_target_pairs={{0,2},{7,5},{8,10},{15,13},{16,18},{23,21},{24,26},{31,29}} | collective-permute-start | bytes 1572872 | tf_op jit(solution)/shard_map/ppermute | solution.py:486
  34.9 11.1 %collective-permute-start.7 = (f32[256,512]{1,0:T(8,128)S(1)}, f32[256,512]{1,0:T(8,128)S(1)}, u32[]{:S(2)}, u32[]{:S(2)}) collective-permute-start(f32[256,512]{1,0:T(8,128)S(1)} %shard_map.58.refs_1_), channel_id=1, source_target_pairs={{0,2},{7,5},{8,10},{15,13},{16,18},{23,21},{24,26},{31,29}} | collective-permute-start | bytes 1572872 | tf_op jit(solution)/shard_map/ppermute | solution.py:486
  41.6 11.1 %collective-permute-start.6 = (f32[256,512]{1,0:T(8,128)S(1)}, f32[256,512]{1,0:T(8,128)S(1)}, u32[]{:S(2)}, u32[]{:S(2)}) collective-permute-start(f32[256,512]{1,0:T(8,128)S(1)} %shard_map.59.refs_1_), channel_id=1, source_target_pairs={{0,2},{7,5},{2,4},{5,3},{8,10},{15,13},{10,12},{13,11},{16,18},{23... | collective-permute-start | bytes 1572872 | tf_op jit(solution)/shard_map/ppermute | solution.py:486
  47.4 11.1 %collective-permute-start.9 = (f32[256,512]{1,0:T(8,128)S(1)}, f32[256,512]{1,0:T(8,128)S(1)}, u32[]{:S(2)}, u32[]{:S(2)}) collective-permute-start(f32[256,512]{1,0:T(8,128)S(1)} %shard_map.60.refs_1_), channel_id=1, source_target_pairs={{0,2},{7,5},{2,4},{5,3},{8,10},{15,13},{10,12},{13,11},{16,18},{23... | collective-permute-start | bytes 1572872 | tf_op jit(solution)/shard_map/ppermute | solution.py:486
  54.0 11.1 %collective-permute-start.8 = (f32[256,512]{1,0:T(8,128)S(1)}, f32[256,512]{1,0:T(8,128)S(1)}, u32[]{:S(2)}, u32[]{:S(2)}) collective-permute-start(f32[256,512]{1,0:T(8,128)S(1)} %shard_map.61.refs_1_), channel_id=1, source_target_pairs={{0,2},{7,5},{2,4},{5,3},{4,6},{3,1},{8,10},{15,13},{10,12},{13,11}... | collective-permute-start | bytes 1572872 | tf_op jit(solution)/shard_map/ppermute | solution.py:486
  59.8 11.1 %collective-permute-start.11 = (f32[256,512]{1,0:T(8,128)S(1)}, f32[256,512]{1,0:T(8,128)S(1)}, u32[]{:S(2)}, u32[]{:S(2)}) collective-permute-start(f32[256,512]{1,0:T(8,128)S(1)} %shard_map.62.refs_1_), channel_id=1, source_target_pairs={{0,2},{7,5},{2,4},{5,3},{4,6},{3,1},{8,10},{15,13},{10,12},{13,11}... | collective-permute-start | bytes 1572872 | tf_op jit(solution)/shard_map/ppermute | solution.py:486
  66.4 11.1 %collective-permute-start.10 = (f32[256,512]{1,0:T(8,128)S(1)}, f32[256,512]{1,0:T(8,128)S(1)}, u32[]{:S(2)}, u32[]{:S(2)}) collective-permute-start(f32[256,512]{1,0:T(8,128)S(1)} %shard_map.63.refs_1_), channel_id=1, source_target_pairs={{0,2},{7,5},{2,4},{5,3},{4,6},{3,1},{8,10},{15,13},{10,12},{13,11}... | collective-permute-start | bytes 1572872 | tf_op jit(solution)/shard_map/ppermute | solution.py:486
  72.2 11.1 %collective-permute-start.13 = (f32[256,512]{1,0:T(8,128)S(1)}, f32[256,512]{1,0:T(8,128)S(1)}, u32[]{:S(2)}, u32[]{:S(2)}) collective-permute-start(f32[256,512]{1,0:T(8,128)S(1)} %shard_map.64.refs_1_), channel_id=1, source_target_pairs={{0,2},{7,5},{2,4},{5,3},{4,6},{3,1},{8,10},{15,13},{10,12},{13,11}... | collective-permute-start | bytes 1572872 | tf_op jit(solution)/shard_map/ppermute | solution.py:486
  78.8 11.1 %collective-permute-start.12 = (f32[256,512]{1,0:T(8,128)S(1)}, f32[256,512]{1,0:T(8,128)S(1)}, u32[]{:S(2)}, u32[]{:S(2)}) collective-permute-start(f32[256,512]{1,0:T(8,128)S(1)} %shard_map.65.refs_1_), channel_id=1, source_target_pairs={{0,2},{7,5},{2,4},{5,3},{4,6},{3,1},{8,10},{15,13},{10,12},{13,11}... | collective-permute-start | bytes 1572872 | tf_op jit(solution)/shard_map/ppermute | solution.py:486
  84.6 11.1 %collective-permute-start.15 = (f32[256,512]{1,0:T(8,128)S(1)}, f32[256,512]{1,0:T(8,128)S(1)}, u32[]{:S(2)}, u32[]{:S(2)}) collective-permute-start(f32[256,512]{1,0:T(8,128)S(1)} %shard_map.66.refs_1_), channel_id=1, source_target_pairs={{0,2},{7,5},{2,4},{5,3},{4,6},{3,1},{8,10},{15,13},{10,12},{13,11}... | collective-permute-start | bytes 1572872 | tf_op jit(solution)/shard_map/ppermute | solution.py:486
  91.2 11.1 %collective-permute-start.14 = (f32[256,512]{1,0:T(8,128)S(1)}, f32[256,512]{1,0:T(8,128)S(1)}, u32[]{:S(2)}, u32[]{:S(2)}) collective-permute-start(f32[256,512]{1,0:T(8,128)S(1)} %shard_map.67.refs_1_), channel_id=1, source_target_pairs={{0,2},{7,5},{2,4},{5,3},{4,6},{3,1},{8,10},{15,13},{10,12},{13,11}... | collective-permute-start | bytes 1572872 | tf_op jit(solution)/shard_map/ppermute | solution.py:486
  97.0 11.1 %collective-permute-start.17 = (f32[256,512]{1,0:T(8,128)S(1)}, f32[256,512]{1,0:T(8,128)S(1)}, u32[]{:S(2)}, u32[]{:S(2)}) collective-permute-start(f32[256,512]{1,0:T(8,128)S(1)} %shard_map.68.refs_1_), channel_id=1, source_target_pairs={{0,2},{7,5},{2,4},{5,3},{4,6},{3,1},{8,10},{15,13},{10,12},{13,11}... | collective-permute-start | bytes 1572872 | tf_op jit(solution)/shard_map/ppermute | solution.py:486
  103.6 11.1 %collective-permute-start.16 = (f32[256,512]{1,0:T(8,128)S(1)}, f32[256,512]{1,0:T(8,128)S(1)}, u32[]{:S(2)}, u32[]{:S(2)}) collective-permute-start(f32[256,512]{1,0:T(8,128)S(1)} %shard_map.69.refs_1_), channel_id=1, source_target_pairs={{0,2},{7,5},{2,4},{5,3},{4,6},{3,1},{8,10},{15,13},{10,12},{13,11}... | collective-permute-start | bytes 1572872 | tf_op jit(solution)/shard_map/ppermute | solution.py:486
  109.4 14.4 %collective-permute-start.18 = (f32[256,512]{1,0:T(8,128)S(1)}, f32[256,512]{1,0:T(8,128)S(1)}, u32[]{:S(2)}, u32[]{:S(2)}) collective-permute-start(f32[256,512]{1,0:T(8,128)S(1)} %shard_map.70.refs_1_), channel_id=1, source_target_pairs={{0,2},{7,5},{2,4},{5,3},{4,6},{3,1},{8,10},{15,13},{10,12},{13,11}... | collective-permute-start | bytes 1572872 | tf_op jit(solution)/shard_map/ppermute | solution.py:486
  116.0 11.1 %collective-permute-start.19 = (f32[256,512]{1,0:T(8,128)S(1)}, f32[256,512]{1,0:T(8,128)S(1)}, u32[]{:S(2)}, u32[]{:S(2)}) collective-permute-start(f32[256,512]{1,0:T(8,128)S(1)} %shard_map.71.refs_1_), channel_id=1, source_target_pairs={{0,2},{7,5},{2,4},{5,3},{4,6},{3,1},{8,10},{15,13},{10,12},{13,11}... | collective-permute-start | bytes 1572872 | tf_op jit(solution)/shard_map/ppermute | solution.py:486
  121.6 1.6 copy-start.4
  121.6 24.0 %collective-permute-start.26 = (f32[1024,512]{1,0:T(8,128)S(1)}, f32[1024,512]{1,0:T(8,128)S(1)}, u32[]{:S(2)}, u32[]{:S(2)}) collective-permute-start(f32[1024,512]{1,0:T(8,128)S(1)} %shard_map.78.refs_0_), channel_id=1, source_target_pairs={{0,1},{1,0},{2,3},{3,2},{4,5},{5,4},{6,7},{7,6},{8,9},{9,8},{10,11... | collective-permute-start | bytes 6291464 | tf_op jit(solution)/shard_map/ppermute | solution.py:459
  123.2 1.9 copy-start.6
  123.2 23.7 %collective-permute-start.27 = (f32[1024,512]{1,0:T(8,128)S(1)}, f32[1024,512]{1,0:T(8,128)S(1)}, u32[]{:S(2)}, u32[]{:S(2)}) collective-permute-start(f32[1024,512]{1,0:T(8,128)S(1)} %shard_map.79.refs_1_), channel_id=1, source_target_pairs={{0,1},{1,0},{2,3},{3,2},{4,5},{5,4},{6,7},{7,6},{8,9},{9,8},{10,11... | collective-permute-start | bytes 6291464 | tf_op jit(solution)/shard_map/ppermute | solution.py:459
  125.1 8.6 %collective-permute-start.20 = (f32[256,512]{1,0:T(8,128)S(1)}, f32[256,512]{1,0:T(8,128)S(1)}, u32[]{:S(2)}, u32[]{:S(2)}) collective-permute-start(f32[256,512]{1,0:T(8,128)S(1)} %shard_map.72.refs_1_), channel_id=1, source_target_pairs={{0,2},{7,5},{2,4},{5,3},{4,6},{3,1},{8,10},{15,13},{10,12},{13,11}... | collective-permute-start | bytes 1572872 | tf_op jit(solution)/shard_map/ppermute | solution.py:486
  128.4 11.1 %collective-permute-start.21 = (f32[256,512]{1,0:T(8,128)S(1)}, f32[256,512]{1,0:T(8,128)S(1)}, u32[]{:S(2)}, u32[]{:S(2)}) collective-permute-start(f32[256,512]{1,0:T(8,128)S(1)} %shard_map.73.refs_1_), channel_id=1, source_target_pairs={{0,2},{7,5},{2,4},{5,3},{4,6},{3,1},{8,10},{15,13},{10,12},{13,11}... | collective-permute-start | bytes 1572872 | tf_op jit(solution)/shard_map/ppermute | solution.py:486
  135.0 6.5 %collective-permute-start.22 = (f32[256,512]{1,0:T(8,128)S(1)}, f32[256,512]{1,0:T(8,128)S(1)}, u32[]{:S(2)}, u32[]{:S(2)}) collective-permute-start(f32[256,512]{1,0:T(8,128)S(1)} %shard_map.74.refs_1_), channel_id=1, source_target_pairs={{2,4},{5,3},{4,6},{3,1},{10,12},{13,11},{12,14},{11,9},{18,20},{21... | collective-permute-start | bytes 1572872 | tf_op jit(solution)/shard_map/ppermute | solution.py:486
  140.8 2.7 collective-permute-start.23
  142.8 5.5 %collective-permute-start.24 = (f32[256,512]{1,0:T(8,128)S(1)}, f32[256,512]{1,0:T(8,128)S(1)}, u32[]{:S(2)}, u32[]{:S(2)}) collective-permute-start(f32[256,512]{1,0:T(8,128)S(1)} %shard_map.76.refs_1_), channel_id=1, source_target_pairs={{4,6},{3,1},{12,14},{11,9},{20,22},{19,17},{28,30},{27,25}} | collective-permute-start | bytes 1572872 | tf_op jit(solution)/shard_map/ppermute | solution.py:486
  144.9 3.4 %collective-permute-start.25 = (f32[256,512]{1,0:T(8,128)S(1)}, f32[256,512]{1,0:T(8,128)S(1)}, u32[]{:S(2)}, u32[]{:S(2)}) collective-permute-start(f32[256,512]{1,0:T(8,128)S(1)} %shard_map.77), channel_id=1, source_target_pairs={{4,6},{3,1},{12,14},{11,9},{20,22},{19,17},{28,30},{27,25}} | collective-permute-start | bytes 1572872 | tf_op jit(solution)/shard_map/ppermute | solution.py:486
  150.2 17.2 %copy-start = (f32[1,512,2048]{2,1,0:T(8,128)S(1)}, f32[1,512,2048]{2,1,0:T(8,128)}, u32[]{:S(2)}) copy-start(f32[1,512,2048]{2,1,0:T(8,128)} %param.6) | copy-start | bytes 12582916
  150.2 19.4 %collective-permute-start.28 = (f32[1280,512]{1,0:T(8,128)S(1)}, f32[1280,512]{1,0:T(8,128)S(1)}, u32[]{:S(2)}, u32[]{:S(2)}) collective-permute-start(f32[1280,512]{1,0:T(8,128)S(1)} %shard_map.80.refs_3_), channel_id=1, source_target_pairs={{0,1},{1,0},{2,3},{3,2},{4,5},{5,4},{6,7},{7,6},{8,9},{9,8},{10,11... | collective-permute-start | bytes 7864328 | tf_op jit(solution)/shard_map/ppermute | solution.py:459
  167.3 9.4 %collective-permute-start.29 = (f32[1024,512]{1,0:T(8,128)}, f32[1024,512]{1,0:T(8,128)}, u32[]{:S(2)}, u32[]{:S(2)}) collective-permute-start(f32[1024,512]{1,0:T(8,128)} %shard_map.84.refs_2_), channel_id=1, source_target_pairs={{0,1},{1,0},{2,3},{3,2},{4,5},{5,4},{6,7},{7,6},{8,9},{9,8},{10,11... | collective-permute-start | bytes 6291464 | tf_op jit(solution)/shard_map/ppermute | solution.py:459
  171.7 50.1 %collective-permute-start.34 = (f32[256,2048]{1,0:T(8,128)}, f32[256,2048]{1,0:T(8,128)}, u32[]{:S(2)}, u32[]{:S(2)}) collective-permute-start(f32[256,2048]{1,0:T(8,128)} %shard_map.81), channel_id=1, source_target_pairs={{0,2},{1,3},{2,4},{3,5},{4,6},{5,7},{6,0},{7,1},{8,10},{9,11},{10,... | collective-permute-start | bytes 6291464 | tf_op jit(solution)/shard_map/ppermute | solution.py:467
  176.8 1.6 copy-start.5
  178.4 1.6 copy-start.7
  179.9 1.7 copy-start.9
  181.7 1.6 copy-start.11
  183.3 1.6 copy-start.13
  184.9 26.7 %copy-start.1 = (f32[1,512,2048]{2,1,0:T(8,128)S(1)}, f32[1,512,2048]{2,1,0:T(8,128)}, u32[]{:S(2)}) copy-start(f32[1,512,2048]{2,1,0:T(8,128)} %param.6) | copy-start | bytes 12582916
  212.2 2.4 collective-permute-start.30
  221.8 6.1 %copy-start.14 = (f32[96,2048]{1,0:T(8,128)S(1)}, f32[96,2048]{1,0:T(8,128)}, u32[]{:S(2)}) copy-start(f32[96,2048]{1,0:T(8,128)} %shard_map.82) | copy-start | bytes 2359300
  222.6 6.6 %collective-permute-start.35 = (f32[256,2048]{1,0:T(8,128)S(1)}, f32[256,2048]{1,0:T(8,128)S(1)}, u32[]{:S(2)}, u32[]{:S(2)}) collective-permute-start(f32[256,2048]{1,0:T(8,128)S(1)} %shard_map.88), channel_id=1, source_target_pairs={{0,1},{1,0},{2,3},{3,2},{4,5},{5,4},{6,7},{7,6},{8,9},{9,8},{10,11... | collective-permute-start | bytes 6291464 | tf_op jit(solution)/shard_map/ppermute | solution.py:459
  224.4 12.9 %collective-permute-start.31 = (f32[128,704]{1,0:T(8,128)S(1)}, f32[128,704]{1,0:T(8,128)S(1)}, u32[]{:S(2)}, u32[]{:S(2)}) collective-permute-start(f32[128,704]{1,0:T(8,128)S(1)} %get-tuple-element.32), channel_id=1, source_target_pairs={{0,8},{8,0},{16,24},{24,16},{1,9},{9,1},{17,25},{25,17},{2,10},{10... | collective-permute-start | bytes 1081352 | tf_op jit(solution)/shard_map/ppermute | solution.py:508
  225.9 18.8 %collective-permute-start.32 = (f32[128,704]{1,0:T(8,128)S(1)}, f32[128,704]{1,0:T(8,128)S(1)}, u32[]{:S(2)}, u32[]{:S(2)}) collective-permute-start(f32[128,704]{1,0:T(8,128)S(1)} %get-tuple-element.33), channel_id=1, source_target_pairs={{0,16},{8,24},{16,0},{24,8},{1,17},{9,25},{17,1},{25,9},{2,18},{10... | collective-permute-start | bytes 1081352 | tf_op jit(solution)/shard_map/ppermute | solution.py:508
  227.1 19.2 %collective-permute-start.33 = (f32[128,704]{1,0:T(8,128)S(1)}, f32[128,704]{1,0:T(8,128)S(1)}, u32[]{:S(2)}, u32[]{:S(2)}) collective-permute-start(f32[128,704]{1,0:T(8,128)S(1)} %get-tuple-element.34), channel_id=1, source_target_pairs={{0,24},{8,16},{16,8},{24,0},{1,25},{9,17},{17,9},{25,1},{2,26},{10... | collective-permute-start | bytes 1081352 | tf_op jit(solution)/shard_map/ppermute | solution.py:508
  227.9 28.6 %collective-permute-start.39 = (f32[96,2048]{1,0:T(8,128)S(1)}, f32[96,2048]{1,0:T(8,128)S(1)}, u32[]{:S(2)}, u32[]{:S(2)}) collective-permute-start(f32[96,2048]{1,0:T(8,128)S(1)} %copy-done.14), channel_id=1, source_target_pairs={{0,2},{1,3},{2,4},{3,5},{4,6},{5,7},{6,0},{7,1},{8,10},{9,11},{10,... | collective-permute-start | bytes 2359304 | tf_op jit(solution)/shard_map/ppermute | solution.py:467
  235.7 14.8 %collective-permute-start.36 = (f32[128,512]{1,0:T(8,128)S(1)}, f32[128,512]{1,0:T(8,128)S(1)}, u32[]{:S(2)}, u32[]{:S(2)}) collective-permute-start(f32[128,512]{1,0:T(8,128)S(1)} %get-tuple-element.36), channel_id=1, source_target_pairs={{0,8},{8,0},{16,24},{24,16},{1,9},{9,1},{17,25},{25,17},{2,10},{10... | collective-permute-start | bytes 786440 | tf_op jit(solution)/shard_map/ppermute | solution.py:508
  237.3 19.0 %collective-permute-start.37 = (f32[128,512]{1,0:T(8,128)S(1)}, f32[128,512]{1,0:T(8,128)S(1)}, u32[]{:S(2)}, u32[]{:S(2)}) collective-permute-start(f32[128,512]{1,0:T(8,128)S(1)} %get-tuple-element.37), channel_id=1, source_target_pairs={{0,16},{8,24},{16,0},{24,8},{1,17},{9,25},{17,1},{25,9},{2,18},{10... | collective-permute-start | bytes 786440 | tf_op jit(solution)/shard_map/ppermute | solution.py:508
  244.7 11.7 %collective-permute-start.38 = (f32[128,512]{1,0:T(8,128)S(1)}, f32[128,512]{1,0:T(8,128)S(1)}, u32[]{:S(2)}, u32[]{:S(2)}) collective-permute-start(f32[128,512]{1,0:T(8,128)S(1)} %get-tuple-element.38), channel_id=1, source_target_pairs={{0,24},{8,16},{16,8},{24,0},{1,25},{9,17},{17,9},{25,1},{2,26},{10... | collective-permute-start | bytes 786440 | tf_op jit(solution)/shard_map/ppermute | solution.py:508
  246.4 27.7 %copy-start.16 = (f32[128,704]{1,0:T(8,128)}, f32[128,704]{1,0:T(8,128)S(1)}, u32[]{:S(2)}) copy-start(f32[128,704]{1,0:T(8,128)S(1)} %add_add_fusion) | copy-start | bytes 1081348
  257.1 2.4 collective-permute-start.40
  257.5 15.9 %collective-permute-start.44 = (f32[64,2048]{1,0:T(8,128)S(1)}, f32[64,2048]{1,0:T(8,128)S(1)}, u32[]{:S(2)}, u32[]{:S(2)}) collective-permute-start(f32[64,2048]{1,0:T(8,128)S(1)} %copy-done.15), channel_id=1, source_target_pairs={{0,2},{1,3},{2,4},{3,5},{4,6},{5,7},{6,0},{7,1},{8,10},{9,11},{10,... | collective-permute-start | bytes 1572872 | tf_op jit(solution)/shard_map/ppermute | solution.py:467
  262.7 6.4 %collective-permute-start.41 = (f32[128,192]{1,0:T(8,128)S(1)}, f32[128,192]{1,0:T(8,128)S(1)}, u32[]{:S(2)}, u32[]{:S(2)}) collective-permute-start(f32[128,192]{1,0:T(8,128)S(1)} %get-tuple-element.40), channel_id=1, source_target_pairs={{0,8},{8,0},{16,24},{24,16},{1,9},{9,1},{17,25},{25,17},{2,10},{10... | collective-permute-start | bytes 294920 | tf_op jit(solution)/shard_map/ppermute | solution.py:508
  263.7 6.7 %collective-permute-start.42 = (f32[128,192]{1,0:T(8,128)S(1)}, f32[128,192]{1,0:T(8,128)S(1)}, u32[]{:S(2)}, u32[]{:S(2)}) collective-permute-start(f32[128,192]{1,0:T(8,128)S(1)} %get-tuple-element.41), channel_id=1, source_target_pairs={{0,16},{8,24},{16,0},{24,8},{1,17},{9,25},{17,1},{25,9},{2,18},{10... | collective-permute-start | bytes 294920 | tf_op jit(solution)/shard_map/ppermute | solution.py:508
  264.8 7.0 %collective-permute-start.43 = (f32[128,192]{1,0:T(8,128)S(1)}, f32[128,192]{1,0:T(8,128)S(1)}, u32[]{:S(2)}, u32[]{:S(2)}) collective-permute-start(f32[128,192]{1,0:T(8,128)S(1)} %get-tuple-element.42), channel_id=1, source_target_pairs={{0,24},{8,16},{16,8},{24,0},{1,25},{9,17},{17,9},{25,1},{2,26},{10... | collective-permute-start | bytes 294920 | tf_op jit(solution)/shard_map/ppermute | solution.py:508
  274.0 2.0 collective-permute-start.45
  274.2 12.1 %slice-start = ((f32[128,704]{1,0:T(8,128)}), f32[128,608]{1,0:T(8,128)S(1)}, s32[]{:S(2)}) async-start(f32[128,704]{1,0:T(8,128)} %copy-done.16), calls=%async_computation | async-start | bytes 655360 | tf_op jit(solution)/shard_map/slice | solution.py:525
  279.0 4.3 %collective-permute-start.46 = (f32[128,128]{1,0:T(8,128)S(1)}, f32[128,128]{1,0:T(8,128)S(1)}, u32[]{:S(2)}, u32[]{:S(2)}) collective-permute-start(f32[128,128]{1,0:T(8,128)S(1)} %get-tuple-element.44), channel_id=1, source_target_pairs={{0,8},{8,0},{16,24},{24,16},{1,9},{9,1},{17,25},{25,17},{2,10},{10... | collective-permute-start | bytes 196616 | tf_op jit(solution)/shard_map/ppermute | solution.py:508
  280.0 4.3 %collective-permute-start.47 = (f32[128,128]{1,0:T(8,128)S(1)}, f32[128,128]{1,0:T(8,128)S(1)}, u32[]{:S(2)}, u32[]{:S(2)}) collective-permute-start(f32[128,128]{1,0:T(8,128)S(1)} %get-tuple-element.45), channel_id=1, source_target_pairs={{0,16},{8,24},{16,0},{24,8},{1,17},{9,25},{17,1},{25,9},{2,18},{10... | collective-permute-start | bytes 196616 | tf_op jit(solution)/shard_map/ppermute | solution.py:508
  281.1 5.2 %collective-permute-start.48 = (f32[128,128]{1,0:T(8,128)S(1)}, f32[128,128]{1,0:T(8,128)S(1)}, u32[]{:S(2)}, u32[]{:S(2)}) collective-permute-start(f32[128,128]{1,0:T(8,128)S(1)} %get-tuple-element.46), channel_id=1, source_target_pairs={{0,24},{8,16},{16,8},{24,0},{1,25},{9,17},{17,9},{25,1},{2,26},{10... | collective-permute-start | bytes 196616 | tf_op jit(solution)/shard_map/ppermute | solution.py:508
  (4 other events, 5.2 us)

commit v7 on v6

--- a/solution.py
+++ b/solution.py
@@ -272,7 +272,7 @@
     received = [got[s] for s in range(first, last + SKEW * (chips - 2))]
     return pl.pallas_call(
         functools.partial(collect_kernel, stream, chips, first, last),
-        out_shape=jax.ShapeDtypeStruct(((last - first) * stream.step, stream.size), jnp.float32),
+        out_shape=pltpu.HBM(((last - first) * stream.step, stream.size), jnp.float32),
         in_specs=[SMEM] + [HBM] * (1 + len(received) + len(earlier)),
         out_specs=HBM,
         scratch_shapes=[pltpu.SemaphoreType.DMA(((last - first) * len(stream.pieces),))],
@@ -387,7 +387,7 @@
         ],
         compiler_params=param(32),
         cost_estimate=cost(0, 1000),
-    )(info, earlier, query, *own, *other)
+    )(info, earlier, query, *[pltpu.with_memory_space_constraint(x, pltpu.HBM) for x in (*own, *other)])
 
 
 def score_kernel(n_sec, scale, blocks, counts, earlier, high, low, *refs):
@@ -491,10 +491,10 @@
                 own.append(value)
                 other.append(swapped(value))
 
-    token = corner(other[-1])
-    for index in range(1, len(cuts) - 1):
-        token = corner(send_train(index, token))
-    high, low, swept_token = swept(stream, n_sec, info, token, query, own, other)
+    part = send_train(1, corner(other[-1]))
+    high, low, swept_token = swept(stream, n_sec, info, corner(part), query, own, other)
+    for index in range(2, len(cuts) - 1):
+        send_train(index, swept_token)
 
     scale = (coords * n_sec) ** (-0.5)
 

time: 289 us -> 293 us (1.014)
  waiting for transfers between devices: 56.6 us -> 62.6 us
  Pallas kernels: 92.3 us -> 98 us
  local copies, waits for them, and re-layouts: 25.9 us -> 21.6 us
  starting transfers between devices: 110 us -> 106 us
    ppermute x3, waiting for transfers between devices: 1.59 us -> 7.98 us  [send_train(): far.append(lax.ppermute(part, 'dp', next_chip))]
    ppermute x12, waiting for transfers between devices: 25.3 us -> 21 us  [summed(): total = total + lax.ppermute(parts[k], 'section', pairs)]
    unnamed x36 -> x38, local copies, waits for them, and re-layouts: 14.8 us -> 14.2 us
  transfers between devices with their start and end apart: 49 -> 49, of which waited for: 26 -> 28; matrix products, arithmetic and copies ran while one was open for 3% -> 2% of each run, Pallas kernels for 28% -> 29%
where the time goes in v7:
time: 293 us; the launch traced here: 292 us
  starting transfers between devices  106 us (36%)
  Pallas kernels  98 us (33%)
  waiting for transfers between devices  62.6 us (21%)
  local copies, waits for them, and re-layouts  21.6 us (7%)
    ppermute x21, starting transfers between devices, body(): got[number] = lax.ppermute(block, 'dp', pairs)  66.7 us
    pallas_call x21, Pallas kernels, step_block(): pl.pallas_call(functools.partial(step_kernel, stream, number), out_shape=...  27.5 us
    pallas_call x1, Pallas kernels, swept(): pl.pallas_call(functools.partial(sweep_kernel, stream, n_sec), out_shape=...  26.3 us
    pallas_call x4, Pallas kernels, scored(): pl.pallas_call(functools.partial(score_kernel, n_sec, scale, blocks), out...  21.6 us
    ppermute x12, waiting for transfers between devices, summed(): total = total + lax.ppermute(parts[k], 'section', pairs)  21 us
    ppermute x10, starting transfers between devices, swapped(): return lax.ppermute(value, 'dp', swap_pairs)  18 us
    ppermute x12, starting transfers between devices, summed(): total = total + lax.ppermute(parts[k], 'section', pairs)  16.6 us
    ppermute x21, waiting for transfers between devices, body(): got[number] = lax.ppermute(block, 'dp', pairs)  16.6 us
  transfers between devices with their start and end apart: 49, of which 28 were waited for; matrix products, arithmetic and copies ran while one was open for 2% of the time, Pallas kernels for 29%

profile of v7, /device:TPU:0, one launch (start us, length us, event | category | flops | bytes accessed | tf_op | source)
XLA Modules:
  0.0 292.2 jit_solution(5136409684553439219)
XLA Ops:
  0.0 2.4 slice_bitcast_fusion.1
  2.8 2.6 collective-permute-start.4
  5.5 2.2 copy-done.7
  7.7 5.4 %shard_map.55.packed = f32[320,512]{1,0:T(8,128)S(1)} custom-call(s32[13]{0:T(128)S(1)} %concatenate.11.info, f32[2048,512]{1,0:T(8,128)S(1)} %bitcast.25), custom_call_target="tpu_custom_call" | custom-call | bytes 1000 | tf_op jit(solution)/shard_map/pallas_call | solution.py:136
  13.7 1.6 collective-permute-start.1
  16.0 9.6 %collective-permute-done = s32[1]{0:T(128)} collective-permute-done((s32[1]{0:T(128)}, s32[1]{0:T(128)}, u32[]{:S(2)}, u32[]{:S(2)}) %collective-permute-start) | collective-permute-done | bytes 36 | tf_op jit(solution)/shard_map/ppermute | solution.py:474
  27.1 3.2 %shard_map.56.own = f32[5888,512]{1,0:T(8,128)S(1)} custom-call(s32[13]{0:T(128)S(1)} %concatenate.11.info, f32[2048,512]{1,0:T(8,128)S(1)} %bitcast.26, f32[2048,512]{1,0:T(8,128)} %collective-permute-done.2.peer, f32[320,512]{1,0:T(8,128)S(1)} %shard_map.55.packed, f32[320,512]{1,0:T(8,128)S(1)} %collective-permute-done.3.peer_packed), custom_call_target="tpu_custom_call" | custom-call | bytes 1000 | tf_op jit(solution)/shard_map/pallas_call | solution.py:200
  31.6 1.4 collective-permute-start.5
  34.3 1.3 collective-permute-start.7
  35.6 4.0 %collective-permute-done.5.refs_0_ = f32[256,512]{1,0:T(8,128)S(1)} collective-permute-done((f32[256,512]{1,0:T(8,128)S(1)}, f32[256,512]{1,0:T(8,128)S(1)}, u32[]{:S(2)}, u32[]{:S(2)}) %collective-permute-start.5) | collective-permute-done | bytes 524320 | tf_op jit(solution)/shard_map/ppermute | solution.py:486
  41.0 4.4 %collective-permute-start.6 = (f32[256,512]{1,0:T(8,128)S(1)}, f32[256,512]{1,0:T(8,128)S(1)}, u32[]{:S(2)}, u32[]{:S(2)}) collective-permute-start(f32[256,512]{1,0:T(8,128)S(1)} %shard_map.59.refs_1_), channel_id=1, source_target_pairs={{0,2},{7,5},{2,4},{5,3},{8,10},{15,13},{10,12},{13,11},{16,18},{23... | collective-permute-start | bytes 1572872 | tf_op jit(solution)/shard_map/ppermute | solution.py:486
  45.4 1.3 shard_map.60.refs_1_
  46.7 4.3 %collective-permute-start.9 = (f32[256,512]{1,0:T(8,128)S(1)}, f32[256,512]{1,0:T(8,128)S(1)}, u32[]{:S(2)}, u32[]{:S(2)}) collective-permute-start(f32[256,512]{1,0:T(8,128)S(1)} %shard_map.60.refs_1_), channel_id=1, source_target_pairs={{0,2},{7,5},{2,4},{5,3},{8,10},{15,13},{10,12},{13,11},{16,18},{23... | collective-permute-start | bytes 1572872 | tf_op jit(solution)/shard_map/ppermute | solution.py:486
  53.4 4.4 %collective-permute-start.8 = (f32[256,512]{1,0:T(8,128)S(1)}, f32[256,512]{1,0:T(8,128)S(1)}, u32[]{:S(2)}, u32[]{:S(2)}) collective-permute-start(f32[256,512]{1,0:T(8,128)S(1)} %shard_map.61.refs_1_), channel_id=1, source_target_pairs={{0,2},{7,5},{2,4},{5,3},{4,6},{3,1},{8,10},{15,13},{10,12},{13,11}... | collective-permute-start | bytes 1572872 | tf_op jit(solution)/shard_map/ppermute | solution.py:486
  59.1 4.3 %collective-permute-start.11 = (f32[256,512]{1,0:T(8,128)S(1)}, f32[256,512]{1,0:T(8,128)S(1)}, u32[]{:S(2)}, u32[]{:S(2)}) collective-permute-start(f32[256,512]{1,0:T(8,128)S(1)} %shard_map.62.refs_1_), channel_id=1, source_target_pairs={{0,2},{7,5},{2,4},{5,3},{4,6},{3,1},{8,10},{15,13},{10,12},{13,11}... | collective-permute-start | bytes 1572872 | tf_op jit(solution)/shard_map/ppermute | solution.py:486
  65.8 4.4 %collective-permute-start.10 = (f32[256,512]{1,0:T(8,128)S(1)}, f32[256,512]{1,0:T(8,128)S(1)}, u32[]{:S(2)}, u32[]{:S(2)}) collective-permute-start(f32[256,512]{1,0:T(8,128)S(1)} %shard_map.63.refs_1_), channel_id=1, source_target_pairs={{0,2},{7,5},{2,4},{5,3},{4,6},{3,1},{8,10},{15,13},{10,12},{13,11}... | collective-permute-start | bytes 1572872 | tf_op jit(solution)/shard_map/ppermute | solution.py:486
  71.5 4.3 %collective-permute-start.13 = (f32[256,512]{1,0:T(8,128)S(1)}, f32[256,512]{1,0:T(8,128)S(1)}, u32[]{:S(2)}, u32[]{:S(2)}) collective-permute-start(f32[256,512]{1,0:T(8,128)S(1)} %shard_map.64.refs_1_), channel_id=1, source_target_pairs={{0,2},{7,5},{2,4},{5,3},{4,6},{3,1},{8,10},{15,13},{10,12},{13,11}... | collective-permute-start | bytes 1572872 | tf_op jit(solution)/shard_map/ppermute | solution.py:486
  78.2 4.4 %collective-permute-start.12 = (f32[256,512]{1,0:T(8,128)S(1)}, f32[256,512]{1,0:T(8,128)S(1)}, u32[]{:S(2)}, u32[]{:S(2)}) collective-permute-start(f32[256,512]{1,0:T(8,128)S(1)} %shard_map.65.refs_1_), channel_id=1, source_target_pairs={{0,2},{7,5},{2,4},{5,3},{4,6},{3,1},{8,10},{15,13},{10,12},{13,11}... | collective-permute-start | bytes 1572872 | tf_op jit(solution)/shard_map/ppermute | solution.py:486
  83.9 4.3 %collective-permute-start.15 = (f32[256,512]{1,0:T(8,128)S(1)}, f32[256,512]{1,0:T(8,128)S(1)}, u32[]{:S(2)}, u32[]{:S(2)}) collective-permute-start(f32[256,512]{1,0:T(8,128)S(1)} %shard_map.66.refs_1_), channel_id=1, source_target_pairs={{0,2},{7,5},{2,4},{5,3},{4,6},{3,1},{8,10},{15,13},{10,12},{13,11}... | collective-permute-start | bytes 1572872 | tf_op jit(solution)/shard_map/ppermute | solution.py:486
  90.6 4.4 %collective-permute-start.14 = (f32[256,512]{1,0:T(8,128)S(1)}, f32[256,512]{1,0:T(8,128)S(1)}, u32[]{:S(2)}, u32[]{:S(2)}) collective-permute-start(f32[256,512]{1,0:T(8,128)S(1)} %shard_map.67.refs_1_), channel_id=1, source_target_pairs={{0,2},{7,5},{2,4},{5,3},{4,6},{3,1},{8,10},{15,13},{10,12},{13,11}... | collective-permute-start | bytes 1572872 | tf_op jit(solution)/shard_map/ppermute | solution.py:486
  96.3 4.3 %collective-permute-start.17 = (f32[256,512]{1,0:T(8,128)S(1)}, f32[256,512]{1,0:T(8,128)S(1)}, u32[]{:S(2)}, u32[]{:S(2)}) collective-permute-start(f32[256,512]{1,0:T(8,128)S(1)} %shard_map.68.refs_1_), channel_id=1, source_target_pairs={{0,2},{7,5},{2,4},{5,3},{4,6},{3,1},{8,10},{15,13},{10,12},{13,11}... | collective-permute-start | bytes 1572872 | tf_op jit(solution)/shard_map/ppermute | solution.py:486
  103.0 4.4 %collective-permute-start.16 = (f32[256,512]{1,0:T(8,128)S(1)}, f32[256,512]{1,0:T(8,128)S(1)}, u32[]{:S(2)}, u32[]{:S(2)}) collective-permute-start(f32[256,512]{1,0:T(8,128)S(1)} %shard_map.69.refs_1_), channel_id=1, source_target_pairs={{0,2},{7,5},{2,4},{5,3},{4,6},{3,1},{8,10},{15,13},{10,12},{13,11}... | collective-permute-start | bytes 1572872 | tf_op jit(solution)/shard_map/ppermute | solution.py:486
  108.7 4.3 %collective-permute-start.18 = (f32[256,512]{1,0:T(8,128)S(1)}, f32[256,512]{1,0:T(8,128)S(1)}, u32[]{:S(2)}, u32[]{:S(2)}) collective-permute-start(f32[256,512]{1,0:T(8,128)S(1)} %shard_map.70.refs_1_), channel_id=1, source_target_pairs={{0,2},{7,5},{2,4},{5,3},{4,6},{3,1},{8,10},{15,13},{10,12},{13,11}... | collective-permute-start | bytes 1572872 | tf_op jit(solution)/shard_map/ppermute | solution.py:486
  115.4 4.4 %collective-permute-start.19 = (f32[256,512]{1,0:T(8,128)S(1)}, f32[256,512]{1,0:T(8,128)S(1)}, u32[]{:S(2)}, u32[]{:S(2)}) collective-permute-start(f32[256,512]{1,0:T(8,128)S(1)} %shard_map.71.refs_1_), channel_id=1, source_target_pairs={{0,2},{7,5},{2,4},{5,3},{4,6},{3,1},{8,10},{15,13},{10,12},{13,11}... | collective-permute-start | bytes 1572872 | tf_op jit(solution)/shard_map/ppermute | solution.py:486
  119.8 2.2 shard_map.78.refs_0_
  122.1 2.3 shard_map.79.refs_1_
  126.3 1.9 collective-permute-start.20
  129.6 2.6 collective-permute-start.21
  132.2 2.7 collective-permute-done.20.refs_0_.refs_3_.refs_7_
  136.9 3.6 %collective-permute-done.21.refs_0_.refs_4_ = f32[256,512]{1,0:T(8,128)S(1)} collective-permute-done((f32[256,512]{1,0:T(8,128)S(1)}, f32[256,512]{1,0:T(8,128)S(1)}, u32[]{:S(2)}, u32[]{:S(2)}) %collective-permute-start.21) | collective-permute-done | bytes 524320 | tf_op jit(solution)/shard_map/ppermute | solution.py:486
  148.5 2.5 shard_map.80.refs_3_
  151.0 15.9 %collective-permute-start.28 = (f32[1280,512]{1,0:T(8,128)}, f32[1280,512]{1,0:T(8,128)S(1)}, u32[]{:S(2)}, u32[]{:S(2)}) collective-permute-start(f32[1280,512]{1,0:T(8,128)} %shard_map.80.refs_3_), channel_id=1, source_target_pairs={{0,1},{1,0},{2,3},{3,2},{4,5},{5,4},{6,7},{7,6},{8,9},{9,8},{10,11... | collective-permute-start | bytes 7864328 | tf_op jit(solution)/shard_map/ppermute | solution.py:459
  166.9 2.2 shard_map.82.refs_2_
  169.2 1.5 slice_bitcast_fusion.refs_0_
  171.7 1.5 copy-done.12
  174.7 1.3 copy-done.15
  176.0 2.2 copy-done.10
  178.2 26.3 %shard_map.83 = (bf16[4,512,512]{2,1,0:T(8,128)(2,1)S(1)}, bf16[4,512,512]{2,1,0:T(8,128)(2,1)S(1)}, f32[8,128]{1,0:T(8,128)S(1)}) custom-call(s32[13]{0:T(128)S(1)} %concatenate.11.info, f32[8,128]{1,0:T(8,128)S(1)} %slice.117.earlier, f32[512,2048]{1,0:T(8,128)S(1)} %bitcast.27, f32[1024,512]{1,0:T(8,128)} %shard_map.78.refs_0_, ...), custom_call_target="tpu_custom_call" | custom-call | bytes 1000 | tf_op jit(solution)/shard_map/pallas_call | solution.py:372
  205.6 1.9 collective-permute-done.30.refs_1_
  207.6 8.1 %shard_map.85 = (f32[128,704]{1,0:T(8,128)S(1)}, f32[128,704]{1,0:T(8,128)}, f32[128,704]{1,0:T(8,128)}, f32[128,704]{1,0:T(8,128)}) custom-call(s32[3]{0:T(128)S(1)} %pad_add_fusion.counts, f32[8,128]{1,0:T(8,128)S(1)} %get-tuple-element.28.refs_0_.earlier.refs_1_, bf16[4,512,512]{2,1,0:T(8,128)(2,1)S(1)} %get-tuple-element.29.high, ...), custom_call_target="tpu_custom_call" | custom-call | bytes 1000 | tf_op jit(solution)/shard_map/pallas_call | solution.py:423
  215.7 8.0 %collective-permute-done.34.far.refs_1_ = f32[256,2048]{1,0:T(8,128)S(1)} collective-permute-done((f32[256,2048]{1,0:T(8,128)}, f32[256,2048]{1,0:T(8,128)S(1)}, u32[]{:S(2)}, u32[]{:S(2)}) %collective-permute-start.34) | collective-permute-done | bytes 2097184 | tf_op jit(solution)/shard_map/ppermute | solution.py:467
  223.7 2.1 shard_map.86
  225.9 1.8 collective-permute-start.31
  227.7 1.5 collective-permute-start.32
  230.4 1.6 copy-done.5
  232.0 1.6 copy-done.9
  233.5 6.7 %shard_map.87 = (f32[128,512]{1,0:T(8,128)S(1)}, f32[128,512]{1,0:T(8,128)S(1)}, f32[128,512]{1,0:T(8,128)S(1)}, f32[128,512]{1,0:T(8,128)S(1)}) custom-call(s32[3]{0:T(128)S(1)} %pad_add_fusion.counts, f32[8,128]{1,0:T(8,128)S(1)} %slice.96.refs_0_.earlier, bf16[4,512,512]{2,1,0:T(8,128)(2,1)S(1)} %get-tuple-element.29.high, ...), custom_call_target="tpu_custom_call" | custom-call | bytes 1000 | tf_op jit(solution)/shard_map/pallas_call | solution.py:423
  240.2 1.8 collective-permute-start.36
  242.1 1.5 collective-permute-start.37
  243.6 3.8 %collective-permute-done.32 = f32[128,704]{1,0:T(8,128)} collective-permute-done((f32[128,704]{1,0:T(8,128)}, f32[128,704]{1,0:T(8,128)}, u32[]{:S(2)}, u32[]{:S(2)}) %collective-permute-start.32) | collective-permute-done | bytes 360480 | tf_op jit(solution)/shard_map/ppermute | solution.py:508
  247.5 2.5 collective-permute-start.38
  249.9 1.3 add_add_fusion
  252.2 5.7 %collective-permute-done.37 = f32[128,512]{1,0:T(8,128)S(1)} collective-permute-done((f32[128,512]{1,0:T(8,128)S(1)}, f32[128,512]{1,0:T(8,128)S(1)}, u32[]{:S(2)}, u32[]{:S(2)}) %collective-permute-start.37) | collective-permute-done | bytes 262176 | tf_op jit(solution)/shard_map/ppermute | solution.py:508
  259.0 1.4 shard_map.89
  261.4 1.8 collective-permute-done.40.refs_0_
  263.2 1.6 copy-done.6
  264.7 3.8 %shard_map.90 = (f32[128,192]{1,0:T(8,128)S(1)}, f32[128,192]{1,0:T(8,128)S(1)}, f32[128,192]{1,0:T(8,128)S(1)}, f32[128,192]{1,0:T(8,128)S(1)}) custom-call(s32[3]{0:T(128)S(1)} %pad_add_fusion.counts, f32[8,128]{1,0:T(8,128)S(1)} %slice.98.refs_0_.earlier, bf16[4,512,512]{2,1,0:T(8,128)(2,1)S(1)} %get-tuple-element.29.high, ...), custom_call_target="tpu_custom_call" | custom-call | bytes 1000 | tf_op jit(solution)/shard_map/pallas_call | solution.py:423
  272.1 2.8 collective-permute-done.41
  274.9 1.6 collective-permute-done.42
  276.5 1.3 collective-permute-done.43
  279.0 1.5 collective-permute-done.45.refs_0_
  280.5 3.0 %shard_map.93 = (f32[128,128]{1,0:T(8,128)S(1)}, f32[128,128]{1,0:T(8,128)S(1)}, f32[128,128]{1,0:T(8,128)S(1)}, f32[128,128]{1,0:T(8,128)S(1)}) custom-call(s32[3]{0:T(128)S(1)} %pad_add_fusion.counts, f32[8,128]{1,0:T(8,128)S(1)} %slice.104.refs_0_.earlier, bf16[4,512,512]{2,1,0:T(8,128)(2,1)S(1)} %get-tuple-element.29.high, ...), custom_call_target="tpu_custom_call" | custom-call | bytes 1000 | tf_op jit(solution)/shard_map/pallas_call | solution.py:423
  284.5 1.3 collective-permute-start.47
  288.8 2.2 collective-permute-done.48
  (139 shorter events, 57.9 us)
Async XLA Ops:
  0.0 5.4 %copy-start.18 = (s32[1,4]{1,0:T(1,128)S(1)}, s32[1,4]{1,0:T(1,128)}, u32[]{:S(2)}) copy-start(s32[1,4]{1,0:T(1,128)} %param.8) | copy-start | bytes 52
  2.4 24.7 %collective-permute-start.2 = (f32[2048,512]{1,0:T(8,128)}, f32[2048,512]{1,0:T(8,128)}, u32[]{:S(2)}, u32[]{:S(2)}) collective-permute-start(f32[2048,512]{1,0:T(8,128)} %bitcast.24), channel_id=1, source_target_pairs={{0,1},{1,0},{2,3},{3,2},{4,5},{5,4},{6,7},{7,6},{8,9},{9,8},{10,11... | collective-permute-start | bytes 12582920 | tf_op jit(solution)/shard_map/ppermute | solution.py:459
  2.8 24.2 %collective-permute-start.4 = (f32[96,2048]{1,0:T(8,128)S(1)}, f32[96,2048]{1,0:T(8,128)S(1)}, u32[]{:S(2)}, u32[]{:S(2)}) collective-permute-start(f32[96,2048]{1,0:T(8,128)S(1)} %get-tuple-element.27), channel_id=1, source_target_pairs={{0,2},{1,3},{2,4},{3,5},{4,6},{5,7},{6,0},{7,1},{8,10},{9,11},{10,... | collective-permute-start | bytes 2359304 | tf_op jit(solution)/shard_map/ppermute | solution.py:463
  5.5 2.2 copy-start.7
  13.1 14.0 %collective-permute-start.3 = (f32[320,512]{1,0:T(8,128)S(1)}, f32[320,512]{1,0:T(8,128)S(1)}, u32[]{:S(2)}, u32[]{:S(2)}) collective-permute-start(f32[320,512]{1,0:T(8,128)S(1)} %shard_map.55.packed), channel_id=1, source_target_pairs={{0,1},{1,0},{2,3},{3,2},{4,5},{5,4},{6,7},{7,6},{8,9},{9,8},{10,11... | collective-permute-start | bytes 1966088 | tf_op jit(solution)/shard_map/ppermute | solution.py:459
  13.4 12.1 %collective-permute-start = (s32[1]{0:T(128)}, s32[1]{0:T(128)}, u32[]{:S(2)}, u32[]{:S(2)}) collective-permute-start(s32[1]{0:T(128)} %param.9), channel_id=1, source_target_pairs={{0,1},{1,2},{2,3},{3,4},{4,5},{5,6},{6,7},{7,0},{8,9},{9,10},{10,1... | collective-permute-start | bytes 20 | tf_op jit(solution)/shard_map/ppermute | solution.py:474
  13.7 12.1 %collective-permute-start.1 = (s32[1]{0:T(128)}, s32[1]{0:T(128)}, u32[]{:S(2)}, u32[]{:S(2)}) collective-permute-start(s32[1]{0:T(128)} %param.9), channel_id=1, source_target_pairs={{0,2},{1,3},{2,4},{3,5},{4,6},{5,7},{6,0},{7,1},{8,10},{9,11},{10,... | collective-permute-start | bytes 20 | tf_op jit(solution)/shard_map/ppermute | solution.py:473
  31.6 8.1 %collective-permute-start.5 = (f32[256,512]{1,0:T(8,128)S(1)}, f32[256,512]{1,0:T(8,128)S(1)}, u32[]{:S(2)}, u32[]{:S(2)}) collective-permute-start(f32[256,512]{1,0:T(8,128)S(1)} %shard_map.57.refs_0_), channel_id=1, source_target_pairs={{0,2},{7,5},{8,10},{15,13},{16,18},{23,21},{24,26},{31,29}} | collective-permute-start | bytes 1572872 | tf_op jit(solution)/shard_map/ppermute | solution.py:486
  34.3 11.1 %collective-permute-start.7 = (f32[256,512]{1,0:T(8,128)S(1)}, f32[256,512]{1,0:T(8,128)S(1)}, u32[]{:S(2)}, u32[]{:S(2)}) collective-permute-start(f32[256,512]{1,0:T(8,128)S(1)} %shard_map.58.refs_1_), channel_id=1, source_target_pairs={{0,2},{7,5},{8,10},{15,13},{16,18},{23,21},{24,26},{31,29}} | collective-permute-start | bytes 1572872 | tf_op jit(solution)/shard_map/ppermute | solution.py:486
  41.0 11.1 %collective-permute-start.6 = (f32[256,512]{1,0:T(8,128)S(1)}, f32[256,512]{1,0:T(8,128)S(1)}, u32[]{:S(2)}, u32[]{:S(2)}) collective-permute-start(f32[256,512]{1,0:T(8,128)S(1)} %shard_map.59.refs_1_), channel_id=1, source_target_pairs={{0,2},{7,5},{2,4},{5,3},{8,10},{15,13},{10,12},{13,11},{16,18},{23... | collective-permute-start | bytes 1572872 | tf_op jit(solution)/shard_map/ppermute | solution.py:486
  46.7 11.1 %collective-permute-start.9 = (f32[256,512]{1,0:T(8,128)S(1)}, f32[256,512]{1,0:T(8,128)S(1)}, u32[]{:S(2)}, u32[]{:S(2)}) collective-permute-start(f32[256,512]{1,0:T(8,128)S(1)} %shard_map.60.refs_1_), channel_id=1, source_target_pairs={{0,2},{7,5},{2,4},{5,3},{8,10},{15,13},{10,12},{13,11},{16,18},{23... | collective-permute-start | bytes 1572872 | tf_op jit(solution)/shard_map/ppermute | solution.py:486
  53.4 11.1 %collective-permute-start.8 = (f32[256,512]{1,0:T(8,128)S(1)}, f32[256,512]{1,0:T(8,128)S(1)}, u32[]{:S(2)}, u32[]{:S(2)}) collective-permute-start(f32[256,512]{1,0:T(8,128)S(1)} %shard_map.61.refs_1_), channel_id=1, source_target_pairs={{0,2},{7,5},{2,4},{5,3},{4,6},{3,1},{8,10},{15,13},{10,12},{13,11}... | collective-permute-start | bytes 1572872 | tf_op jit(solution)/shard_map/ppermute | solution.py:486
  59.1 11.1 %collective-permute-start.11 = (f32[256,512]{1,0:T(8,128)S(1)}, f32[256,512]{1,0:T(8,128)S(1)}, u32[]{:S(2)}, u32[]{:S(2)}) collective-permute-start(f32[256,512]{1,0:T(8,128)S(1)} %shard_map.62.refs_1_), channel_id=1, source_target_pairs={{0,2},{7,5},{2,4},{5,3},{4,6},{3,1},{8,10},{15,13},{10,12},{13,11}... | collective-permute-start | bytes 1572872 | tf_op jit(solution)/shard_map/ppermute | solution.py:486
  65.8 11.1 %collective-permute-start.10 = (f32[256,512]{1,0:T(8,128)S(1)}, f32[256,512]{1,0:T(8,128)S(1)}, u32[]{:S(2)}, u32[]{:S(2)}) collective-permute-start(f32[256,512]{1,0:T(8,128)S(1)} %shard_map.63.refs_1_), channel_id=1, source_target_pairs={{0,2},{7,5},{2,4},{5,3},{4,6},{3,1},{8,10},{15,13},{10,12},{13,11}... | collective-permute-start | bytes 1572872 | tf_op jit(solution)/shard_map/ppermute | solution.py:486
  71.5 11.1 %collective-permute-start.13 = (f32[256,512]{1,0:T(8,128)S(1)}, f32[256,512]{1,0:T(8,128)S(1)}, u32[]{:S(2)}, u32[]{:S(2)}) collective-permute-start(f32[256,512]{1,0:T(8,128)S(1)} %shard_map.64.refs_1_), channel_id=1, source_target_pairs={{0,2},{7,5},{2,4},{5,3},{4,6},{3,1},{8,10},{15,13},{10,12},{13,11}... | collective-permute-start | bytes 1572872 | tf_op jit(solution)/shard_map/ppermute | solution.py:486
  78.2 11.1 %collective-permute-start.12 = (f32[256,512]{1,0:T(8,128)S(1)}, f32[256,512]{1,0:T(8,128)S(1)}, u32[]{:S(2)}, u32[]{:S(2)}) collective-permute-start(f32[256,512]{1,0:T(8,128)S(1)} %shard_map.65.refs_1_), channel_id=1, source_target_pairs={{0,2},{7,5},{2,4},{5,3},{4,6},{3,1},{8,10},{15,13},{10,12},{13,11}... | collective-permute-start | bytes 1572872 | tf_op jit(solution)/shard_map/ppermute | solution.py:486
  83.9 11.1 %collective-permute-start.15 = (f32[256,512]{1,0:T(8,128)S(1)}, f32[256,512]{1,0:T(8,128)S(1)}, u32[]{:S(2)}, u32[]{:S(2)}) collective-permute-start(f32[256,512]{1,0:T(8,128)S(1)} %shard_map.66.refs_1_), channel_id=1, source_target_pairs={{0,2},{7,5},{2,4},{5,3},{4,6},{3,1},{8,10},{15,13},{10,12},{13,11}... | collective-permute-start | bytes 1572872 | tf_op jit(solution)/shard_map/ppermute | solution.py:486
  90.6 11.1 %collective-permute-start.14 = (f32[256,512]{1,0:T(8,128)S(1)}, f32[256,512]{1,0:T(8,128)S(1)}, u32[]{:S(2)}, u32[]{:S(2)}) collective-permute-start(f32[256,512]{1,0:T(8,128)S(1)} %shard_map.67.refs_1_), channel_id=1, source_target_pairs={{0,2},{7,5},{2,4},{5,3},{4,6},{3,1},{8,10},{15,13},{10,12},{13,11}... | collective-permute-start | bytes 1572872 | tf_op jit(solution)/shard_map/ppermute | solution.py:486
  96.3 11.1 %collective-permute-start.17 = (f32[256,512]{1,0:T(8,128)S(1)}, f32[256,512]{1,0:T(8,128)S(1)}, u32[]{:S(2)}, u32[]{:S(2)}) collective-permute-start(f32[256,512]{1,0:T(8,128)S(1)} %shard_map.68.refs_1_), channel_id=1, source_target_pairs={{0,2},{7,5},{2,4},{5,3},{4,6},{3,1},{8,10},{15,13},{10,12},{13,11}... | collective-permute-start | bytes 1572872 | tf_op jit(solution)/shard_map/ppermute | solution.py:486
  103.0 11.1 %collective-permute-start.16 = (f32[256,512]{1,0:T(8,128)S(1)}, f32[256,512]{1,0:T(8,128)S(1)}, u32[]{:S(2)}, u32[]{:S(2)}) collective-permute-start(f32[256,512]{1,0:T(8,128)S(1)} %shard_map.69.refs_1_), channel_id=1, source_target_pairs={{0,2},{7,5},{2,4},{5,3},{4,6},{3,1},{8,10},{15,13},{10,12},{13,11}... | collective-permute-start | bytes 1572872 | tf_op jit(solution)/shard_map/ppermute | solution.py:486
  108.7 16.3 %collective-permute-start.18 = (f32[256,512]{1,0:T(8,128)S(1)}, f32[256,512]{1,0:T(8,128)S(1)}, u32[]{:S(2)}, u32[]{:S(2)}) collective-permute-start(f32[256,512]{1,0:T(8,128)S(1)} %shard_map.70.refs_1_), channel_id=1, source_target_pairs={{0,2},{7,5},{2,4},{5,3},{4,6},{3,1},{8,10},{15,13},{10,12},{13,11}... | collective-permute-start | bytes 1572872 | tf_op jit(solution)/shard_map/ppermute | solution.py:486
  115.4 12.9 %collective-permute-start.19 = (f32[256,512]{1,0:T(8,128)S(1)}, f32[256,512]{1,0:T(8,128)S(1)}, u32[]{:S(2)}, u32[]{:S(2)}) collective-permute-start(f32[256,512]{1,0:T(8,128)S(1)} %shard_map.71.refs_1_), channel_id=1, source_target_pairs={{0,2},{7,5},{2,4},{5,3},{4,6},{3,1},{8,10},{15,13},{10,12},{13,11}... | collective-permute-start | bytes 1572872 | tf_op jit(solution)/shard_map/ppermute | solution.py:486
  122.0 24.5 %collective-permute-start.26 = (f32[1024,512]{1,0:T(8,128)}, f32[1024,512]{1,0:T(8,128)S(1)}, u32[]{:S(2)}, u32[]{:S(2)}) collective-permute-start(f32[1024,512]{1,0:T(8,128)} %shard_map.78.refs_0_), channel_id=1, source_target_pairs={{0,1},{1,0},{2,3},{3,2},{4,5},{5,4},{6,7},{7,6},{8,9},{9,8},{10,11... | collective-permute-start | bytes 6291464 | tf_op jit(solution)/shard_map/ppermute | solution.py:459
  124.4 22.2 %collective-permute-start.27 = (f32[1024,512]{1,0:T(8,128)}, f32[1024,512]{1,0:T(8,128)S(1)}, u32[]{:S(2)}, u32[]{:S(2)}) collective-permute-start(f32[1024,512]{1,0:T(8,128)} %shard_map.79.refs_1_), channel_id=1, source_target_pairs={{0,1},{1,0},{2,3},{3,2},{4,5},{5,4},{6,7},{7,6},{8,9},{9,8},{10,11... | collective-permute-start | bytes 6291464 | tf_op jit(solution)/shard_map/ppermute | solution.py:459
  126.3 8.6 %collective-permute-start.20 = (f32[256,512]{1,0:T(8,128)S(1)}, f32[256,512]{1,0:T(8,128)S(1)}, u32[]{:S(2)}, u32[]{:S(2)}) collective-permute-start(f32[256,512]{1,0:T(8,128)S(1)} %shard_map.72.refs_1_), channel_id=1, source_target_pairs={{0,2},{7,5},{2,4},{5,3},{4,6},{3,1},{8,10},{15,13},{10,12},{13,11}... | collective-permute-start | bytes 1572872 | tf_op jit(solution)/shard_map/ppermute | solution.py:486
  129.6 10.9 %collective-permute-start.21 = (f32[256,512]{1,0:T(8,128)S(1)}, f32[256,512]{1,0:T(8,128)S(1)}, u32[]{:S(2)}, u32[]{:S(2)}) collective-permute-start(f32[256,512]{1,0:T(8,128)S(1)} %shard_map.73.refs_1_), channel_id=1, source_target_pairs={{0,2},{7,5},{2,4},{5,3},{4,6},{3,1},{8,10},{15,13},{10,12},{13,11}... | collective-permute-start | bytes 1572872 | tf_op jit(solution)/shard_map/ppermute | solution.py:486
  136.2 6.3 %collective-permute-start.22 = (f32[256,512]{1,0:T(8,128)S(1)}, f32[256,512]{1,0:T(8,128)S(1)}, u32[]{:S(2)}, u32[]{:S(2)}) collective-permute-start(f32[256,512]{1,0:T(8,128)S(1)} %shard_map.74.refs_1_), channel_id=1, source_target_pairs={{2,4},{5,3},{4,6},{3,1},{10,12},{13,11},{12,14},{11,9},{18,20},{21... | collective-permute-start | bytes 1572872 | tf_op jit(solution)/shard_map/ppermute | solution.py:486
  141.8 2.7 collective-permute-start.23
  143.8 2.8 collective-permute-start.24
  145.9 0.8 collective-permute-start.25
  146.6 1.9 copy-start.14
  151.0 18.3 %copy-start = (f32[1,512,2048]{2,1,0:T(8,128)S(1)}, f32[1,512,2048]{2,1,0:T(8,128)}, u32[]{:S(2)}) copy-start(f32[1,512,2048]{2,1,0:T(8,128)} %param.6) | copy-start | bytes 12582916
  151.0 20.7 %collective-permute-start.28 = (f32[1280,512]{1,0:T(8,128)}, f32[1280,512]{1,0:T(8,128)S(1)}, u32[]{:S(2)}, u32[]{:S(2)}) collective-permute-start(f32[1280,512]{1,0:T(8,128)} %shard_map.80.refs_3_), channel_id=1, source_target_pairs={{0,1},{1,0},{2,3},{3,2},{4,5},{5,4},{6,7},{7,6},{8,9},{9,8},{10,11... | collective-permute-start | bytes 7864328 | tf_op jit(solution)/shard_map/ppermute | solution.py:459
  169.2 5.5 %collective-permute-start.29 = (f32[1024,512]{1,0:T(8,128)}, f32[1024,512]{1,0:T(8,128)S(1)}, u32[]{:S(2)}, u32[]{:S(2)}) collective-permute-start(f32[1024,512]{1,0:T(8,128)} %shard_map.82.refs_2_), channel_id=1, source_target_pairs={{0,1},{1,0},{2,3},{3,2},{4,5},{5,4},{6,7},{7,6},{8,9},{9,8},{10,11... | collective-permute-start | bytes 6291464 | tf_op jit(solution)/shard_map/ppermute | solution.py:459
  173.8 49.9 %collective-permute-start.34 = (f32[256,2048]{1,0:T(8,128)}, f32[256,2048]{1,0:T(8,128)S(1)}, u32[]{:S(2)}, u32[]{:S(2)}) collective-permute-start(f32[256,2048]{1,0:T(8,128)} %shard_map.81), channel_id=1, source_target_pairs={{0,2},{1,3},{2,4},{3,5},{4,6},{5,7},{6,0},{7,1},{8,10},{9,11},{10,... | collective-permute-start | bytes 6291464 | tf_op jit(solution)/shard_map/ppermute | solution.py:467
  176.0 2.2 copy-start.10
  178.2 26.4 %copy-start.1 = (f32[1,512,2048]{2,1,0:T(8,128)S(1)}, f32[1,512,2048]{2,1,0:T(8,128)}, u32[]{:S(2)}) copy-start(f32[1,512,2048]{2,1,0:T(8,128)} %param.6) | copy-start | bytes 12582916
  204.5 3.0 %copy-start.4 = (bf16[4,512,512]{2,1,0:T(8,128)(2,1)}, bf16[4,512,512]{2,1,0:T(8,128)(2,1)S(1)}, u32[]{:S(2)}) copy-start(bf16[4,512,512]{2,1,0:T(8,128)(2,1)S(1)} %get-tuple-element.30.low) | copy-start | bytes 6291460
  204.5 3.0 %copy-start.11 = (f32[8,128]{1,0:T(8,128)}, f32[8,128]{1,0:T(8,128)S(1)}, u32[]{:S(2)}) copy-start(f32[8,128]{1,0:T(8,128)S(1)} %get-tuple-element.28.refs_0_.earlier.refs_1_) | copy-start | bytes 12292
  205.2 2.4 collective-permute-start.30
  223.7 2.1 copy-start.8
  225.8 4.6 %collective-permute-start.35 = (f32[256,2048]{1,0:T(8,128)}, f32[256,2048]{1,0:T(8,128)}, u32[]{:S(2)}, u32[]{:S(2)}) collective-permute-start(f32[256,2048]{1,0:T(8,128)} %shard_map.86), channel_id=1, source_target_pairs={{0,1},{1,0},{2,3},{3,2},{4,5},{5,4},{6,7},{7,6},{8,9},{9,8},{10,11... | collective-permute-start | bytes 6291464 | tf_op jit(solution)/shard_map/ppermute | solution.py:459
  225.9 16.2 %collective-permute-start.31 = (f32[128,704]{1,0:T(8,128)}, f32[128,704]{1,0:T(8,128)}, u32[]{:S(2)}, u32[]{:S(2)}) collective-permute-start(f32[128,704]{1,0:T(8,128)} %get-tuple-element.32), channel_id=1, source_target_pairs={{0,8},{8,0},{16,24},{24,16},{1,9},{9,1},{17,25},{25,17},{2,10},{10... | collective-permute-start | bytes 1081352 | tf_op jit(solution)/shard_map/ppermute | solution.py:508
  227.7 19.7 %collective-permute-start.32 = (f32[128,704]{1,0:T(8,128)}, f32[128,704]{1,0:T(8,128)}, u32[]{:S(2)}, u32[]{:S(2)}) collective-permute-start(f32[128,704]{1,0:T(8,128)} %get-tuple-element.33), channel_id=1, source_target_pairs={{0,16},{8,24},{16,0},{24,8},{1,17},{9,25},{17,1},{25,9},{2,18},{10... | collective-permute-start | bytes 1081352 | tf_op jit(solution)/shard_map/ppermute | solution.py:508
  229.2 20.7 %collective-permute-start.33 = (f32[128,704]{1,0:T(8,128)}, f32[128,704]{1,0:T(8,128)}, u32[]{:S(2)}, u32[]{:S(2)}) collective-permute-start(f32[128,704]{1,0:T(8,128)} %get-tuple-element.34), channel_id=1, source_target_pairs={{0,24},{8,16},{16,8},{24,0},{1,25},{9,17},{17,9},{25,1},{2,26},{10... | collective-permute-start | bytes 1081352 | tf_op jit(solution)/shard_map/ppermute | solution.py:508
  229.5 29.5 %collective-permute-start.39 = (f32[96,2048]{1,0:T(8,128)}, f32[96,2048]{1,0:T(8,128)S(1)}, u32[]{:S(2)}, u32[]{:S(2)}) collective-permute-start(f32[96,2048]{1,0:T(8,128)} %shard_map.88), channel_id=1, source_target_pairs={{0,2},{1,3},{2,4},{3,5},{4,6},{5,7},{6,0},{7,1},{8,10},{9,11},{10,... | collective-permute-start | bytes 2359304 | tf_op jit(solution)/shard_map/ppermute | solution.py:467
  230.4 1.6 copy-start.5
  233.5 25.5 %copy-start.2 = (f32[1,512,2048]{2,1,0:T(8,128)S(1)}, f32[1,512,2048]{2,1,0:T(8,128)}, u32[]{:S(2)}) copy-start(f32[1,512,2048]{2,1,0:T(8,128)} %param.6) | copy-start | bytes 12582916
  240.2 11.9 %collective-permute-start.36 = (f32[128,512]{1,0:T(8,128)S(1)}, f32[128,512]{1,0:T(8,128)S(1)}, u32[]{:S(2)}, u32[]{:S(2)}) collective-permute-start(f32[128,512]{1,0:T(8,128)S(1)} %get-tuple-element.36), channel_id=1, source_target_pairs={{0,8},{8,0},{16,24},{24,16},{1,9},{9,1},{17,25},{25,17},{2,10},{10... | collective-permute-start | bytes 786440 | tf_op jit(solution)/shard_map/ppermute | solution.py:508
  242.1 15.7 %collective-permute-start.37 = (f32[128,512]{1,0:T(8,128)S(1)}, f32[128,512]{1,0:T(8,128)S(1)}, u32[]{:S(2)}, u32[]{:S(2)}) collective-permute-start(f32[128,512]{1,0:T(8,128)S(1)} %get-tuple-element.37), channel_id=1, source_target_pairs={{0,16},{8,24},{16,0},{24,8},{1,17},{9,25},{17,1},{25,9},{2,18},{10... | collective-permute-start | bytes 786440 | tf_op jit(solution)/shard_map/ppermute | solution.py:508
  247.5 11.4 %collective-permute-start.38 = (f32[128,512]{1,0:T(8,128)S(1)}, f32[128,512]{1,0:T(8,128)S(1)}, u32[]{:S(2)}, u32[]{:S(2)}) collective-permute-start(f32[128,512]{1,0:T(8,128)S(1)} %get-tuple-element.38), channel_id=1, source_target_pairs={{0,24},{8,16},{16,8},{24,0},{1,25},{9,17},{17,9},{25,1},{2,26},{10... | collective-permute-start | bytes 786440 | tf_op jit(solution)/shard_map/ppermute | solution.py:508
  251.3 9.2 %copy-start.16 = (f32[128,704]{1,0:T(8,128)}, f32[128,704]{1,0:T(8,128)S(1)}, u32[]{:S(2)}) copy-start(f32[128,704]{1,0:T(8,128)S(1)} %add_add_fusion) | copy-start | bytes 1081348
  260.5 2.7 collective-permute-start.40
  261.4 16.5 %copy-start.3 = (f32[1,512,2048]{2,1,0:T(8,128)S(1)}, f32[1,512,2048]{2,1,0:T(8,128)}, u32[]{:S(2)}) copy-start(f32[1,512,2048]{2,1,0:T(8,128)} %param.6) | copy-start | bytes 12582916
  261.4 16.5 %collective-permute-start.44 = (f32[64,2048]{1,0:T(8,128)}, f32[64,2048]{1,0:T(8,128)S(1)}, u32[]{:S(2)}, u32[]{:S(2)}) collective-permute-start(f32[64,2048]{1,0:T(8,128)} %shard_map.91), channel_id=1, source_target_pairs={{0,2},{1,3},{2,4},{3,5},{4,6},{5,7},{6,0},{7,1},{8,10},{9,11},{10,... | collective-permute-start | bytes 1572872 | tf_op jit(solution)/shard_map/ppermute | solution.py:467
  263.2 1.6 copy-start.6
  268.6 6.3 %collective-permute-start.41 = (f32[128,192]{1,0:T(8,128)S(1)}, f32[128,192]{1,0:T(8,128)S(1)}, u32[]{:S(2)}, u32[]{:S(2)}) collective-permute-start(f32[128,192]{1,0:T(8,128)S(1)} %get-tuple-element.40), channel_id=1, source_target_pairs={{0,8},{8,0},{16,24},{24,16},{1,9},{9,1},{17,25},{25,17},{2,10},{10... | collective-permute-start | bytes 294920 | tf_op jit(solution)/shard_map/ppermute | solution.py:508
  269.8 6.7 %collective-permute-start.42 = (f32[128,192]{1,0:T(8,128)S(1)}, f32[128,192]{1,0:T(8,128)S(1)}, u32[]{:S(2)}, u32[]{:S(2)}) collective-permute-start(f32[128,192]{1,0:T(8,128)S(1)} %get-tuple-element.41), channel_id=1, source_target_pairs={{0,16},{8,24},{16,0},{24,8},{1,17},{9,25},{17,1},{25,9},{2,18},{10... | collective-permute-start | bytes 294920 | tf_op jit(solution)/shard_map/ppermute | solution.py:508
  270.9 7.0 %collective-permute-start.43 = (f32[128,192]{1,0:T(8,128)S(1)}, f32[128,192]{1,0:T(8,128)S(1)}, u32[]{:S(2)}, u32[]{:S(2)}) collective-permute-start(f32[128,192]{1,0:T(8,128)S(1)} %get-tuple-element.42), channel_id=1, source_target_pairs={{0,24},{8,16},{16,8},{24,0},{1,25},{9,17},{17,9},{25,1},{2,26},{10... | collective-permute-start | bytes 294920 | tf_op jit(solution)/shard_map/ppermute | solution.py:508
  278.5 2.0 collective-permute-start.45
  279.0 12.1 %slice-start = ((f32[128,704]{1,0:T(8,128)}), f32[128,608]{1,0:T(8,128)S(1)}, s32[]{:S(2)}) async-start(f32[128,704]{1,0:T(8,128)} %copy-done.16), calls=%async_computation | async-start | bytes 655360 | tf_op jit(solution)/shard_map/slice | solution.py:525
  283.5 4.3 %collective-permute-start.46 = (f32[128,128]{1,0:T(8,128)S(1)}, f32[128,128]{1,0:T(8,128)S(1)}, u32[]{:S(2)}, u32[]{:S(2)}) collective-permute-start(f32[128,128]{1,0:T(8,128)S(1)} %get-tuple-element.44), channel_id=1, source_target_pairs={{0,8},{8,0},{16,24},{24,16},{1,9},{9,1},{17,25},{25,17},{2,10},{10... | collective-permute-start | bytes 196616 | tf_op jit(solution)/shard_map/ppermute | solution.py:508
  284.5 4.3 %collective-permute-start.47 = (f32[128,128]{1,0:T(8,128)S(1)}, f32[128,128]{1,0:T(8,128)S(1)}, u32[]{:S(2)}, u32[]{:S(2)}) collective-permute-start(f32[128,128]{1,0:T(8,128)S(1)} %get-tuple-element.45), channel_id=1, source_target_pairs={{0,16},{8,24},{16,0},{24,8},{1,17},{9,25},{17,1},{25,9},{2,18},{10... | collective-permute-start | bytes 196616 | tf_op jit(solution)/shard_map/ppermute | solution.py:508
  285.8 5.2 %collective-permute-start.48 = (f32[128,128]{1,0:T(8,128)S(1)}, f32[128,128]{1,0:T(8,128)S(1)}, u32[]{:S(2)}, u32[]{:S(2)}) collective-permute-start(f32[128,128]{1,0:T(8,128)S(1)} %get-tuple-element.46), channel_id=1, source_target_pairs={{0,24},{8,16},{16,8},{24,0},{1,25},{9,17},{17,9},{25,1},{2,26},{10... | collective-permute-start | bytes 196616 | tf_op jit(solution)/shard_map/ppermute | solution.py:508
  (5 other events, 6.7 us)

commit v8 on v7

--- a/solution.py
+++ b/solution.py
@@ -11,7 +11,7 @@
 CHUNKS = 17
 SKEW = 2
 GROUPS = ((0, 4), (4, 8), (8, 12), (12, 17))
-TRAIN_CUTS = (96, 256, 96, 64)
+TRAIN_CUTS = (96, 256, 160)
 MIB = 1024 * 1024
 HBM = pl.BlockSpec(memory_space=pltpu.HBM)
 SMEM = pl.BlockSpec(memory_space=pltpu.SMEM)

time: 293 us -> 283 us (0.966)
  starting transfers between devices: 106 us -> 101 us
  Pallas kernels: 98 us -> 93.9 us
    ppermute x12 -> x9, starting transfers between devices: 16.6 us -> 11.7 us  [summed(): total = total + lax.ppermute(parts[k], 'section', pairs)]
    pallas_call x4 -> x3, Pallas kernels: 21.6 us -> 18.9 us  [scored(): pl.pallas_call(functools.partial(score_kernel, n_sec, scale, blocks), out...]
    ppermute x12 -> x9, waiting for transfers between devices: 21 us -> 22.9 us  [summed(): total = total + lax.ppermute(parts[k], 'section', pairs)]
    ppermute x10 -> x9, waiting for transfers between devices: 7.16 us -> 5.94 us  [swapped(): return lax.ppermute(value, 'dp', swap_pairs)]
    ppermute x10 -> x9, starting transfers between devices: 18 us -> 17.2 us  [swapped(): return lax.ppermute(value, 'dp', swap_pairs)]
    ppermute x3 -> x2, waiting for transfers between devices: 7.98 us -> 8.07 us  [send_train(): far.append(lax.ppermute(part, 'dp', next_chip))]
  transfers between devices with their start and end apart: 49 -> 44, of which waited for: 28 -> 22; matrix products, arithmetic and copies ran while one was open for 2% -> 2% of each run, Pallas kernels for 29% -> 28%
where the time goes in v8:
time: 283 us; the launch traced here: 282 us
  starting transfers between devices  101 us (36%)
  Pallas kernels  93.9 us (33%)
  waiting for transfers between devices  61.8 us (22%)
  local copies, waits for them, and re-layouts  21.8 us (8%)
    ppermute x21, starting transfers between devices, body(): got[number] = lax.ppermute(block, 'dp', pairs)  67.2 us
    pallas_call x21, Pallas kernels, step_block(): pl.pallas_call(functools.partial(step_kernel, stream, number), out_shape=...  27.5 us
    pallas_call x1, Pallas kernels, swept(): pl.pallas_call(functools.partial(sweep_kernel, stream, n_sec), out_shape=...  26.3 us
    ppermute x9, waiting for transfers between devices, summed(): total = total + lax.ppermute(parts[k], 'section', pairs)  22.9 us
    pallas_call x3, Pallas kernels, scored(): pl.pallas_call(functools.partial(score_kernel, n_sec, scale, blocks), out...  18.9 us
    ppermute x9, starting transfers between devices, swapped(): return lax.ppermute(value, 'dp', swap_pairs)  17.2 us
    ppermute x21, waiting for transfers between devices, body(): got[number] = lax.ppermute(block, 'dp', pairs)  16.5 us
    unnamed x38, local copies, waits for them, and re-layouts  14.6 us
  transfers between devices with their start and end apart: 44, of which 22 were waited for; matrix products, arithmetic and copies ran while one was open for 2% of the time, Pallas kernels for 28%

profile of v8, /device:TPU:0, one launch (start us, length us, event | category | flops | bytes accessed | tf_op | source)
XLA Modules:
  0.0 281.8 jit_solution(3255567164990400362)
XLA Ops:
  1.7 2.6 collective-permute-start.4
  5.7 2.2 copy-done.5
  7.9 5.4 %shard_map.55.packed = f32[320,512]{1,0:T(8,128)S(1)} custom-call(s32[13]{0:T(128)S(1)} %concatenate.11.info, f32[2048,512]{1,0:T(8,128)S(1)} %bitcast.22), custom_call_target="tpu_custom_call" | custom-call | bytes 1000 | tf_op jit(solution)/shard_map/pallas_call | solution.py:136
  13.9 1.6 collective-permute-start.1
  16.2 8.2 %collective-permute-done = s32[1]{0:T(128)} collective-permute-done((s32[1]{0:T(128)}, s32[1]{0:T(128)}, u32[]{:S(2)}, u32[]{:S(2)}) %collective-permute-start) | collective-permute-done | bytes 36 | tf_op jit(solution)/shard_map/ppermute | solution.py:474
  24.5 1.3 pad_add_fusion.counts
  25.9 3.2 %shard_map.56.own = f32[5888,512]{1,0:T(8,128)S(1)} custom-call(s32[13]{0:T(128)S(1)} %concatenate.11.info, f32[2048,512]{1,0:T(8,128)S(1)} %bitcast.23, f32[2048,512]{1,0:T(8,128)} %collective-permute-done.2.peer, f32[320,512]{1,0:T(8,128)S(1)} %shard_map.55.packed, f32[320,512]{1,0:T(8,128)S(1)} %collective-permute-done.3.peer_packed), custom_call_target="tpu_custom_call" | custom-call | bytes 1000 | tf_op jit(solution)/shard_map/pallas_call | solution.py:200
  30.4 2.0 collective-permute-start.5
  33.6 1.3 collective-permute-start.7
  35.0 4.0 %collective-permute-done.5.refs_0_ = f32[256,512]{1,0:T(8,128)S(1)} collective-permute-done((f32[256,512]{1,0:T(8,128)S(1)}, f32[256,512]{1,0:T(8,128)S(1)}, u32[]{:S(2)}, u32[]{:S(2)}) %collective-permute-start.5) | collective-permute-done | bytes 524320 | tf_op jit(solution)/shard_map/ppermute | solution.py:486
  40.3 4.4 %collective-permute-start.6 = (f32[256,512]{1,0:T(8,128)S(1)}, f32[256,512]{1,0:T(8,128)S(1)}, u32[]{:S(2)}, u32[]{:S(2)}) collective-permute-start(f32[256,512]{1,0:T(8,128)S(1)} %shard_map.59.refs_1_), channel_id=1, source_target_pairs={{0,2},{7,5},{2,4},{5,3},{8,10},{15,13},{10,12},{13,11},{16,18},{23... | collective-permute-start | bytes 1572872 | tf_op jit(solution)/shard_map/ppermute | solution.py:486
  44.8 1.3 shard_map.60.refs_1_
  46.1 4.3 %collective-permute-start.9 = (f32[256,512]{1,0:T(8,128)S(1)}, f32[256,512]{1,0:T(8,128)S(1)}, u32[]{:S(2)}, u32[]{:S(2)}) collective-permute-start(f32[256,512]{1,0:T(8,128)S(1)} %shard_map.60.refs_1_), channel_id=1, source_target_pairs={{0,2},{7,5},{2,4},{5,3},{8,10},{15,13},{10,12},{13,11},{16,18},{23... | collective-permute-start | bytes 1572872 | tf_op jit(solution)/shard_map/ppermute | solution.py:486
  52.7 4.4 %collective-permute-start.8 = (f32[256,512]{1,0:T(8,128)S(1)}, f32[256,512]{1,0:T(8,128)S(1)}, u32[]{:S(2)}, u32[]{:S(2)}) collective-permute-start(f32[256,512]{1,0:T(8,128)S(1)} %shard_map.61.refs_1_), channel_id=1, source_target_pairs={{0,2},{7,5},{2,4},{5,3},{4,6},{3,1},{8,10},{15,13},{10,12},{13,11}... | collective-permute-start | bytes 1572872 | tf_op jit(solution)/shard_map/ppermute | solution.py:486
  57.2 1.3 shard_map.62.refs_1_
  58.5 4.3 %collective-permute-start.11 = (f32[256,512]{1,0:T(8,128)S(1)}, f32[256,512]{1,0:T(8,128)S(1)}, u32[]{:S(2)}, u32[]{:S(2)}) collective-permute-start(f32[256,512]{1,0:T(8,128)S(1)} %shard_map.62.refs_1_), channel_id=1, source_target_pairs={{0,2},{7,5},{2,4},{5,3},{4,6},{3,1},{8,10},{15,13},{10,12},{13,11}... | collective-permute-start | bytes 1572872 | tf_op jit(solution)/shard_map/ppermute | solution.py:486
  65.1 4.4 %collective-permute-start.10 = (f32[256,512]{1,0:T(8,128)S(1)}, f32[256,512]{1,0:T(8,128)S(1)}, u32[]{:S(2)}, u32[]{:S(2)}) collective-permute-start(f32[256,512]{1,0:T(8,128)S(1)} %shard_map.63.refs_1_), channel_id=1, source_target_pairs={{0,2},{7,5},{2,4},{5,3},{4,6},{3,1},{8,10},{15,13},{10,12},{13,11}... | collective-permute-start | bytes 1572872 | tf_op jit(solution)/shard_map/ppermute | solution.py:486
  69.6 1.3 shard_map.64.refs_1_
  70.9 4.3 %collective-permute-start.13 = (f32[256,512]{1,0:T(8,128)S(1)}, f32[256,512]{1,0:T(8,128)S(1)}, u32[]{:S(2)}, u32[]{:S(2)}) collective-permute-start(f32[256,512]{1,0:T(8,128)S(1)} %shard_map.64.refs_1_), channel_id=1, source_target_pairs={{0,2},{7,5},{2,4},{5,3},{4,6},{3,1},{8,10},{15,13},{10,12},{13,11}... | collective-permute-start | bytes 1572872 | tf_op jit(solution)/shard_map/ppermute | solution.py:486
  77.5 4.4 %collective-permute-start.12 = (f32[256,512]{1,0:T(8,128)S(1)}, f32[256,512]{1,0:T(8,128)S(1)}, u32[]{:S(2)}, u32[]{:S(2)}) collective-permute-start(f32[256,512]{1,0:T(8,128)S(1)} %shard_map.65.refs_1_), channel_id=1, source_target_pairs={{0,2},{7,5},{2,4},{5,3},{4,6},{3,1},{8,10},{15,13},{10,12},{13,11}... | collective-permute-start | bytes 1572872 | tf_op jit(solution)/shard_map/ppermute | solution.py:486
  82.0 1.3 shard_map.66.refs_1_
  83.3 4.3 %collective-permute-start.15 = (f32[256,512]{1,0:T(8,128)S(1)}, f32[256,512]{1,0:T(8,128)S(1)}, u32[]{:S(2)}, u32[]{:S(2)}) collective-permute-start(f32[256,512]{1,0:T(8,128)S(1)} %shard_map.66.refs_1_), channel_id=1, source_target_pairs={{0,2},{7,5},{2,4},{5,3},{4,6},{3,1},{8,10},{15,13},{10,12},{13,11}... | collective-permute-start | bytes 1572872 | tf_op jit(solution)/shard_map/ppermute | solution.py:486
  89.9 4.4 %collective-permute-start.14 = (f32[256,512]{1,0:T(8,128)S(1)}, f32[256,512]{1,0:T(8,128)S(1)}, u32[]{:S(2)}, u32[]{:S(2)}) collective-permute-start(f32[256,512]{1,0:T(8,128)S(1)} %shard_map.67.refs_1_), channel_id=1, source_target_pairs={{0,2},{7,5},{2,4},{5,3},{4,6},{3,1},{8,10},{15,13},{10,12},{13,11}... | collective-permute-start | bytes 1572872 | tf_op jit(solution)/shard_map/ppermute | solution.py:486
  94.4 1.3 shard_map.68.refs_1_
  95.7 4.3 %collective-permute-start.17 = (f32[256,512]{1,0:T(8,128)S(1)}, f32[256,512]{1,0:T(8,128)S(1)}, u32[]{:S(2)}, u32[]{:S(2)}) collective-permute-start(f32[256,512]{1,0:T(8,128)S(1)} %shard_map.68.refs_1_), channel_id=1, source_target_pairs={{0,2},{7,5},{2,4},{5,3},{4,6},{3,1},{8,10},{15,13},{10,12},{13,11}... | collective-permute-start | bytes 1572872 | tf_op jit(solution)/shard_map/ppermute | solution.py:486
  102.3 4.4 %collective-permute-start.16 = (f32[256,512]{1,0:T(8,128)S(1)}, f32[256,512]{1,0:T(8,128)S(1)}, u32[]{:S(2)}, u32[]{:S(2)}) collective-permute-start(f32[256,512]{1,0:T(8,128)S(1)} %shard_map.69.refs_1_), channel_id=1, source_target_pairs={{0,2},{7,5},{2,4},{5,3},{4,6},{3,1},{8,10},{15,13},{10,12},{13,11}... | collective-permute-start | bytes 1572872 | tf_op jit(solution)/shard_map/ppermute | solution.py:486
  106.8 1.3 shard_map.70.refs_1_
  108.1 4.3 %collective-permute-start.18 = (f32[256,512]{1,0:T(8,128)S(1)}, f32[256,512]{1,0:T(8,128)S(1)}, u32[]{:S(2)}, u32[]{:S(2)}) collective-permute-start(f32[256,512]{1,0:T(8,128)S(1)} %shard_map.70.refs_1_), channel_id=1, source_target_pairs={{0,2},{7,5},{2,4},{5,3},{4,6},{3,1},{8,10},{15,13},{10,12},{13,11}... | collective-permute-start | bytes 1572872 | tf_op jit(solution)/shard_map/ppermute | solution.py:486
  114.7 4.4 %collective-permute-start.19 = (f32[256,512]{1,0:T(8,128)S(1)}, f32[256,512]{1,0:T(8,128)S(1)}, u32[]{:S(2)}, u32[]{:S(2)}) collective-permute-start(f32[256,512]{1,0:T(8,128)S(1)} %shard_map.71.refs_1_), channel_id=1, source_target_pairs={{0,2},{7,5},{2,4},{5,3},{4,6},{3,1},{8,10},{15,13},{10,12},{13,11}... | collective-permute-start | bytes 1572872 | tf_op jit(solution)/shard_map/ppermute | solution.py:486
  119.1 2.3 shard_map.78.refs_0_
  121.5 2.3 shard_map.79.refs_1_
  125.6 1.9 collective-permute-start.20
  127.6 1.3 shard_map.73.refs_1_
  128.9 2.6 collective-permute-start.21
  131.5 2.7 collective-permute-done.20.refs_0_.refs_3_.refs_7_
  136.2 3.6 %collective-permute-done.21.refs_0_.refs_4_ = f32[256,512]{1,0:T(8,128)S(1)} collective-permute-done((f32[256,512]{1,0:T(8,128)S(1)}, f32[256,512]{1,0:T(8,128)S(1)}, u32[]{:S(2)}, u32[]{:S(2)}) %collective-permute-start.21) | collective-permute-done | bytes 524320 | tf_op jit(solution)/shard_map/ppermute | solution.py:486
  141.9 1.3 shard_map.76.refs_1_
  146.0 1.3 copy-done.15
  148.6 2.5 shard_map.80.refs_3_
  151.1 15.2 %collective-permute-start.28 = (f32[1280,512]{1,0:T(8,128)}, f32[1280,512]{1,0:T(8,128)S(1)}, u32[]{:S(2)}, u32[]{:S(2)}) collective-permute-start(f32[1280,512]{1,0:T(8,128)} %shard_map.80.refs_3_), channel_id=1, source_target_pairs={{0,1},{1,0},{2,3},{3,2},{4,5},{5,4},{6,7},{7,6},{8,9},{9,8},{10,11... | collective-permute-start | bytes 7864328 | tf_op jit(solution)/shard_map/ppermute | solution.py:459
  166.2 2.2 shard_map.82.refs_2_
  168.6 1.5 slice_bitcast_fusion.refs_0_
  171.0 1.5 copy-done.14
  174.0 1.4 copy-done.17
  175.3 2.2 copy-done.8
  177.5 26.3 %shard_map.83 = (bf16[4,512,512]{2,1,0:T(8,128)(2,1)S(1)}, bf16[4,512,512]{2,1,0:T(8,128)(2,1)S(1)}, f32[8,128]{1,0:T(8,128)S(1)}) custom-call(s32[13]{0:T(128)S(1)} %concatenate.11.info, f32[8,128]{1,0:T(8,128)S(1)} %slice.93.earlier, f32[512,2048]{1,0:T(8,128)S(1)} %bitcast.24, f32[1024,512]{1,0:T(8,128)} %shard_map.78.refs_0_, ...), custom_call_target="tpu_custom_call" | custom-call | bytes 1000 | tf_op jit(solution)/shard_map/pallas_call | solution.py:372
  205.0 1.9 collective-permute-done.30.refs_1_
  206.9 7.2 %shard_map.85 = (f32[128,704]{1,0:T(8,128)S(1)}, f32[128,704]{1,0:T(8,128)S(1)}, f32[128,704]{1,0:T(8,128)S(1)}, f32[128,704]{1,0:T(8,128)S(1)}) custom-call(s32[3]{0:T(128)S(1)} %pad_add_fusion.counts, f32[8,128]{1,0:T(8,128)S(1)} %get-tuple-element.24.refs_0_.earlier.refs_1_, bf16[4,512,512]{2,1,0:T(8,128)(2,1)S(1)} %get-tuple-element.25.high, ...), custom_call_target="tpu_custom_call" | custom-call | bytes 1000 | tf_op jit(solution)/shard_map/pallas_call | solution.py:423
  215.6 7.4 %collective-permute-done.34.far.refs_1_ = f32[256,2048]{1,0:T(8,128)S(1)} collective-permute-done((f32[256,2048]{1,0:T(8,128)}, f32[256,2048]{1,0:T(8,128)S(1)}, u32[]{:S(2)}, u32[]{:S(2)}) %collective-permute-start.34) | collective-permute-done | bytes 2097184 | tf_op jit(solution)/shard_map/ppermute | solution.py:467
  223.0 2.1 shard_map.86
  227.6 1.8 collective-permute-start.32
  229.9 1.6 copy-done.4
  231.5 1.6 copy-done.7
  233.1 6.7 %shard_map.87 = (f32[128,512]{1,0:T(8,128)S(1)}, f32[128,512]{1,0:T(8,128)S(1)}, f32[128,512]{1,0:T(8,128)S(1)}, f32[128,512]{1,0:T(8,128)S(1)}) custom-call(s32[3]{0:T(128)S(1)} %pad_add_fusion.counts, f32[8,128]{1,0:T(8,128)S(1)} %slice.78.refs_0_.earlier, bf16[4,512,512]{2,1,0:T(8,128)(2,1)S(1)} %get-tuple-element.25.high, ...), custom_call_target="tpu_custom_call" | custom-call | bytes 1000 | tf_op jit(solution)/shard_map/pallas_call | solution.py:423
  241.0 1.9 collective-permute-start.37
  242.8 4.8 %collective-permute-done.32 = f32[128,704]{1,0:T(8,128)S(1)} collective-permute-done((f32[128,704]{1,0:T(8,128)}, f32[128,704]{1,0:T(8,128)S(1)}, u32[]{:S(2)}, u32[]{:S(2)}) %collective-permute-start.32) | collective-permute-done | bytes 360480 | tf_op jit(solution)/shard_map/ppermute | solution.py:508
  247.6 1.6 collective-permute-start.38
  249.3 3.3 %collective-permute-done.36 = f32[128,512]{1,0:T(8,128)S(1)} collective-permute-done((f32[128,512]{1,0:T(8,128)S(1)}, f32[128,512]{1,0:T(8,128)S(1)}, u32[]{:S(2)}, u32[]{:S(2)}) %collective-permute-start.36) | collective-permute-done | bytes 262176 | tf_op jit(solution)/shard_map/ppermute | solution.py:508
  252.6 6.1 %collective-permute-done.37 = f32[128,512]{1,0:T(8,128)S(1)} collective-permute-done((f32[128,512]{1,0:T(8,128)S(1)}, f32[128,512]{1,0:T(8,128)S(1)}, u32[]{:S(2)}, u32[]{:S(2)}) %collective-permute-start.37) | collective-permute-done | bytes 262176 | tf_op jit(solution)/shard_map/ppermute | solution.py:508
  260.4 2.9 %collective-permute-done.40.refs_0_ = f32[160,2048]{1,0:T(8,128)S(1)} collective-permute-done((f32[160,2048]{1,0:T(8,128)S(1)}, f32[160,2048]{1,0:T(8,128)S(1)}, u32[]{:S(2)}, u32[]{:S(2)}) %collective-permute-start.40) | collective-permute-done | bytes 1310752 | tf_op jit(solution)/shard_map/ppermute | solution.py:459
  263.3 5.0 %shard_map.90 = (f32[128,320]{1,0:T(8,128)S(1)}, f32[128,320]{1,0:T(8,128)S(1)}, f32[128,320]{1,0:T(8,128)S(1)}, f32[128,320]{1,0:T(8,128)S(1)}) custom-call(s32[3]{0:T(128)S(1)} %pad_add_fusion.counts, f32[8,128]{1,0:T(8,128)S(1)} %slice.80.refs_0_.earlier, bf16[4,512,512]{2,1,0:T(8,128)(2,1)S(1)} %get-tuple-element.25.high, ...), custom_call_target="tpu_custom_call" | custom-call | bytes 1000 | tf_op jit(solution)/shard_map/pallas_call | solution.py:423
  269.6 1.8 collective-permute-start.42
  271.9 4.2 %collective-permute-done.41 = f32[128,320]{1,0:T(8,128)S(1)} collective-permute-done((f32[128,320]{1,0:T(8,128)S(1)}, f32[128,320]{1,0:T(8,128)S(1)}, u32[]{:S(2)}, u32[]{:S(2)}) %collective-permute-start.41) | collective-permute-done | bytes 163872 | tf_op jit(solution)/shard_map/ppermute | solution.py:508
  276.2 4.4 %collective-permute-done.42 = f32[128,320]{1,0:T(8,128)S(1)} collective-permute-done((f32[128,320]{1,0:T(8,128)S(1)}, f32[128,320]{1,0:T(8,128)S(1)}, u32[]{:S(2)}, u32[]{:S(2)}) %collective-permute-start.42) | collective-permute-done | bytes 163872 | tf_op jit(solution)/shard_map/ppermute | solution.py:508
  (122 shorter events, 45.6 us)
Async XLA Ops:
  1.2 24.7 %collective-permute-start.2 = (f32[2048,512]{1,0:T(8,128)}, f32[2048,512]{1,0:T(8,128)}, u32[]{:S(2)}, u32[]{:S(2)}) collective-permute-start(f32[2048,512]{1,0:T(8,128)} %bitcast.21), channel_id=1, source_target_pairs={{0,1},{1,0},{2,3},{3,2},{4,5},{5,4},{6,7},{7,6},{8,9},{9,8},{10,11... | collective-permute-start | bytes 12582920 | tf_op jit(solution)/shard_map/ppermute | solution.py:459
  1.7 24.2 %collective-permute-start.4 = (f32[96,2048]{1,0:T(8,128)S(1)}, f32[96,2048]{1,0:T(8,128)S(1)}, u32[]{:S(2)}, u32[]{:S(2)}) collective-permute-start(f32[96,2048]{1,0:T(8,128)S(1)} %slice_bitcast_fusion.2), channel_id=1, source_target_pairs={{0,2},{1,3},{2,4},{3,5},{4,6},{5,7},{6,0},{7,1},{8,10},{9,11},{10,... | collective-permute-start | bytes 2359304 | tf_op jit(solution)/shard_map/ppermute | solution.py:463
  5.7 2.2 copy-start.5
  13.4 12.5 %collective-permute-start.3 = (f32[320,512]{1,0:T(8,128)S(1)}, f32[320,512]{1,0:T(8,128)S(1)}, u32[]{:S(2)}, u32[]{:S(2)}) collective-permute-start(f32[320,512]{1,0:T(8,128)S(1)} %shard_map.55.packed), channel_id=1, source_target_pairs={{0,1},{1,0},{2,3},{3,2},{4,5},{5,4},{6,7},{7,6},{8,9},{9,8},{10,11... | collective-permute-start | bytes 1966088 | tf_op jit(solution)/shard_map/ppermute | solution.py:459
  13.6 10.8 %collective-permute-start = (s32[1]{0:T(128)}, s32[1]{0:T(128)}, u32[]{:S(2)}, u32[]{:S(2)}) collective-permute-start(s32[1]{0:T(128)} %param.9), channel_id=1, source_target_pairs={{0,1},{1,2},{2,3},{3,4},{4,5},{5,6},{6,7},{7,0},{8,9},{9,10},{10,1... | collective-permute-start | bytes 20 | tf_op jit(solution)/shard_map/ppermute | solution.py:474
  13.9 10.6 %collective-permute-start.1 = (s32[1]{0:T(128)}, s32[1]{0:T(128)}, u32[]{:S(2)}, u32[]{:S(2)}) collective-permute-start(s32[1]{0:T(128)} %param.9), channel_id=1, source_target_pairs={{0,2},{1,3},{2,4},{3,5},{4,6},{5,7},{6,0},{7,1},{8,10},{9,11},{10,... | collective-permute-start | bytes 20 | tf_op jit(solution)/shard_map/ppermute | solution.py:473
  30.4 8.7 %collective-permute-start.5 = (f32[256,512]{1,0:T(8,128)S(1)}, f32[256,512]{1,0:T(8,128)S(1)}, u32[]{:S(2)}, u32[]{:S(2)}) collective-permute-start(f32[256,512]{1,0:T(8,128)S(1)} %shard_map.57.refs_0_), channel_id=1, source_target_pairs={{0,2},{7,5},{8,10},{15,13},{16,18},{23,21},{24,26},{31,29}} | collective-permute-start | bytes 1572872 | tf_op jit(solution)/shard_map/ppermute | solution.py:486
  33.6 11.1 %collective-permute-start.7 = (f32[256,512]{1,0:T(8,128)S(1)}, f32[256,512]{1,0:T(8,128)S(1)}, u32[]{:S(2)}, u32[]{:S(2)}) collective-permute-start(f32[256,512]{1,0:T(8,128)S(1)} %shard_map.58.refs_1_), channel_id=1, source_target_pairs={{0,2},{7,5},{8,10},{15,13},{16,18},{23,21},{24,26},{31,29}} | collective-permute-start | bytes 1572872 | tf_op jit(solution)/shard_map/ppermute | solution.py:486
  40.3 11.1 %collective-permute-start.6 = (f32[256,512]{1,0:T(8,128)S(1)}, f32[256,512]{1,0:T(8,128)S(1)}, u32[]{:S(2)}, u32[]{:S(2)}) collective-permute-start(f32[256,512]{1,0:T(8,128)S(1)} %shard_map.59.refs_1_), channel_id=1, source_target_pairs={{0,2},{7,5},{2,4},{5,3},{8,10},{15,13},{10,12},{13,11},{16,18},{23... | collective-permute-start | bytes 1572872 | tf_op jit(solution)/shard_map/ppermute | solution.py:486
  46.1 11.1 %collective-permute-start.9 = (f32[256,512]{1,0:T(8,128)S(1)}, f32[256,512]{1,0:T(8,128)S(1)}, u32[]{:S(2)}, u32[]{:S(2)}) collective-permute-start(f32[256,512]{1,0:T(8,128)S(1)} %shard_map.60.refs_1_), channel_id=1, source_target_pairs={{0,2},{7,5},{2,4},{5,3},{8,10},{15,13},{10,12},{13,11},{16,18},{23... | collective-permute-start | bytes 1572872 | tf_op jit(solution)/shard_map/ppermute | solution.py:486
  52.7 11.1 %collective-permute-start.8 = (f32[256,512]{1,0:T(8,128)S(1)}, f32[256,512]{1,0:T(8,128)S(1)}, u32[]{:S(2)}, u32[]{:S(2)}) collective-permute-start(f32[256,512]{1,0:T(8,128)S(1)} %shard_map.61.refs_1_), channel_id=1, source_target_pairs={{0,2},{7,5},{2,4},{5,3},{4,6},{3,1},{8,10},{15,13},{10,12},{13,11}... | collective-permute-start | bytes 1572872 | tf_op jit(solution)/shard_map/ppermute | solution.py:486
  58.5 11.1 %collective-permute-start.11 = (f32[256,512]{1,0:T(8,128)S(1)}, f32[256,512]{1,0:T(8,128)S(1)}, u32[]{:S(2)}, u32[]{:S(2)}) collective-permute-start(f32[256,512]{1,0:T(8,128)S(1)} %shard_map.62.refs_1_), channel_id=1, source_target_pairs={{0,2},{7,5},{2,4},{5,3},{4,6},{3,1},{8,10},{15,13},{10,12},{13,11}... | collective-permute-start | bytes 1572872 | tf_op jit(solution)/shard_map/ppermute | solution.py:486
  65.1 11.1 %collective-permute-start.10 = (f32[256,512]{1,0:T(8,128)S(1)}, f32[256,512]{1,0:T(8,128)S(1)}, u32[]{:S(2)}, u32[]{:S(2)}) collective-permute-start(f32[256,512]{1,0:T(8,128)S(1)} %shard_map.63.refs_1_), channel_id=1, source_target_pairs={{0,2},{7,5},{2,4},{5,3},{4,6},{3,1},{8,10},{15,13},{10,12},{13,11}... | collective-permute-start | bytes 1572872 | tf_op jit(solution)/shard_map/ppermute | solution.py:486
  70.9 11.1 %collective-permute-start.13 = (f32[256,512]{1,0:T(8,128)S(1)}, f32[256,512]{1,0:T(8,128)S(1)}, u32[]{:S(2)}, u32[]{:S(2)}) collective-permute-start(f32[256,512]{1,0:T(8,128)S(1)} %shard_map.64.refs_1_), channel_id=1, source_target_pairs={{0,2},{7,5},{2,4},{5,3},{4,6},{3,1},{8,10},{15,13},{10,12},{13,11}... | collective-permute-start | bytes 1572872 | tf_op jit(solution)/shard_map/ppermute | solution.py:486
  77.5 11.1 %collective-permute-start.12 = (f32[256,512]{1,0:T(8,128)S(1)}, f32[256,512]{1,0:T(8,128)S(1)}, u32[]{:S(2)}, u32[]{:S(2)}) collective-permute-start(f32[256,512]{1,0:T(8,128)S(1)} %shard_map.65.refs_1_), channel_id=1, source_target_pairs={{0,2},{7,5},{2,4},{5,3},{4,6},{3,1},{8,10},{15,13},{10,12},{13,11}... | collective-permute-start | bytes 1572872 | tf_op jit(solution)/shard_map/ppermute | solution.py:486
  83.3 11.1 %collective-permute-start.15 = (f32[256,512]{1,0:T(8,128)S(1)}, f32[256,512]{1,0:T(8,128)S(1)}, u32[]{:S(2)}, u32[]{:S(2)}) collective-permute-start(f32[256,512]{1,0:T(8,128)S(1)} %shard_map.66.refs_1_), channel_id=1, source_target_pairs={{0,2},{7,5},{2,4},{5,3},{4,6},{3,1},{8,10},{15,13},{10,12},{13,11}... | collective-permute-start | bytes 1572872 | tf_op jit(solution)/shard_map/ppermute | solution.py:486
  89.9 11.1 %collective-permute-start.14 = (f32[256,512]{1,0:T(8,128)S(1)}, f32[256,512]{1,0:T(8,128)S(1)}, u32[]{:S(2)}, u32[]{:S(2)}) collective-permute-start(f32[256,512]{1,0:T(8,128)S(1)} %shard_map.67.refs_1_), channel_id=1, source_target_pairs={{0,2},{7,5},{2,4},{5,3},{4,6},{3,1},{8,10},{15,13},{10,12},{13,11}... | collective-permute-start | bytes 1572872 | tf_op jit(solution)/shard_map/ppermute | solution.py:486
  95.7 11.1 %collective-permute-start.17 = (f32[256,512]{1,0:T(8,128)S(1)}, f32[256,512]{1,0:T(8,128)S(1)}, u32[]{:S(2)}, u32[]{:S(2)}) collective-permute-start(f32[256,512]{1,0:T(8,128)S(1)} %shard_map.68.refs_1_), channel_id=1, source_target_pairs={{0,2},{7,5},{2,4},{5,3},{4,6},{3,1},{8,10},{15,13},{10,12},{13,11}... | collective-permute-start | bytes 1572872 | tf_op jit(solution)/shard_map/ppermute | solution.py:486
  102.3 11.1 %collective-permute-start.16 = (f32[256,512]{1,0:T(8,128)S(1)}, f32[256,512]{1,0:T(8,128)S(1)}, u32[]{:S(2)}, u32[]{:S(2)}) collective-permute-start(f32[256,512]{1,0:T(8,128)S(1)} %shard_map.69.refs_1_), channel_id=1, source_target_pairs={{0,2},{7,5},{2,4},{5,3},{4,6},{3,1},{8,10},{15,13},{10,12},{13,11}... | collective-permute-start | bytes 1572872 | tf_op jit(solution)/shard_map/ppermute | solution.py:486
  108.1 16.2 %collective-permute-start.18 = (f32[256,512]{1,0:T(8,128)S(1)}, f32[256,512]{1,0:T(8,128)S(1)}, u32[]{:S(2)}, u32[]{:S(2)}) collective-permute-start(f32[256,512]{1,0:T(8,128)S(1)} %shard_map.70.refs_1_), channel_id=1, source_target_pairs={{0,2},{7,5},{2,4},{5,3},{4,6},{3,1},{8,10},{15,13},{10,12},{13,11}... | collective-permute-start | bytes 1572872 | tf_op jit(solution)/shard_map/ppermute | solution.py:486
  114.7 12.9 %collective-permute-start.19 = (f32[256,512]{1,0:T(8,128)S(1)}, f32[256,512]{1,0:T(8,128)S(1)}, u32[]{:S(2)}, u32[]{:S(2)}) collective-permute-start(f32[256,512]{1,0:T(8,128)S(1)} %shard_map.71.refs_1_), channel_id=1, source_target_pairs={{0,2},{7,5},{2,4},{5,3},{4,6},{3,1},{8,10},{15,13},{10,12},{13,11}... | collective-permute-start | bytes 1572872 | tf_op jit(solution)/shard_map/ppermute | solution.py:486
  121.4 24.5 %collective-permute-start.26 = (f32[1024,512]{1,0:T(8,128)}, f32[1024,512]{1,0:T(8,128)S(1)}, u32[]{:S(2)}, u32[]{:S(2)}) collective-permute-start(f32[1024,512]{1,0:T(8,128)} %shard_map.78.refs_0_), channel_id=1, source_target_pairs={{0,1},{1,0},{2,3},{3,2},{4,5},{5,4},{6,7},{7,6},{8,9},{9,8},{10,11... | collective-permute-start | bytes 6291464 | tf_op jit(solution)/shard_map/ppermute | solution.py:459
  123.8 23.5 %collective-permute-start.27 = (f32[1024,512]{1,0:T(8,128)}, f32[1024,512]{1,0:T(8,128)S(1)}, u32[]{:S(2)}, u32[]{:S(2)}) collective-permute-start(f32[1024,512]{1,0:T(8,128)} %shard_map.79.refs_1_), channel_id=1, source_target_pairs={{0,1},{1,0},{2,3},{3,2},{4,5},{5,4},{6,7},{7,6},{8,9},{9,8},{10,11... | collective-permute-start | bytes 6291464 | tf_op jit(solution)/shard_map/ppermute | solution.py:459
  125.6 8.6 %collective-permute-start.20 = (f32[256,512]{1,0:T(8,128)S(1)}, f32[256,512]{1,0:T(8,128)S(1)}, u32[]{:S(2)}, u32[]{:S(2)}) collective-permute-start(f32[256,512]{1,0:T(8,128)S(1)} %shard_map.72.refs_1_), channel_id=1, source_target_pairs={{0,2},{7,5},{2,4},{5,3},{4,6},{3,1},{8,10},{15,13},{10,12},{13,11}... | collective-permute-start | bytes 1572872 | tf_op jit(solution)/shard_map/ppermute | solution.py:486
  128.9 10.9 %collective-permute-start.21 = (f32[256,512]{1,0:T(8,128)S(1)}, f32[256,512]{1,0:T(8,128)S(1)}, u32[]{:S(2)}, u32[]{:S(2)}) collective-permute-start(f32[256,512]{1,0:T(8,128)S(1)} %shard_map.73.refs_1_), channel_id=1, source_target_pairs={{0,2},{7,5},{2,4},{5,3},{4,6},{3,1},{8,10},{15,13},{10,12},{13,11}... | collective-permute-start | bytes 1572872 | tf_op jit(solution)/shard_map/ppermute | solution.py:486
  135.5 6.3 %collective-permute-start.22 = (f32[256,512]{1,0:T(8,128)S(1)}, f32[256,512]{1,0:T(8,128)S(1)}, u32[]{:S(2)}, u32[]{:S(2)}) collective-permute-start(f32[256,512]{1,0:T(8,128)S(1)} %shard_map.74.refs_1_), channel_id=1, source_target_pairs={{2,4},{5,3},{4,6},{3,1},{10,12},{13,11},{12,14},{11,9},{18,20},{21... | collective-permute-start | bytes 1572872 | tf_op jit(solution)/shard_map/ppermute | solution.py:486
  141.2 2.7 collective-permute-start.23
  143.2 4.1 %collective-permute-start.24 = (f32[256,512]{1,0:T(8,128)S(1)}, f32[256,512]{1,0:T(8,128)S(1)}, u32[]{:S(2)}, u32[]{:S(2)}) collective-permute-start(f32[256,512]{1,0:T(8,128)S(1)} %shard_map.76.refs_1_), channel_id=1, source_target_pairs={{4,6},{3,1},{12,14},{11,9},{20,22},{19,17},{28,30},{27,25}} | collective-permute-start | bytes 1572872 | tf_op jit(solution)/shard_map/ppermute | solution.py:486
  145.2 2.1 collective-permute-start.25
  145.9 1.3 copy-start.15
  147.3 1.3 copy-start.16
  151.1 17.5 %copy-start = (f32[1,512,2048]{2,1,0:T(8,128)S(1)}, f32[1,512,2048]{2,1,0:T(8,128)}, u32[]{:S(2)}) copy-start(f32[1,512,2048]{2,1,0:T(8,128)} %param.6) | copy-start | bytes 12582916
  151.1 19.9 %collective-permute-start.28 = (f32[1280,512]{1,0:T(8,128)}, f32[1280,512]{1,0:T(8,128)S(1)}, u32[]{:S(2)}, u32[]{:S(2)}) collective-permute-start(f32[1280,512]{1,0:T(8,128)} %shard_map.80.refs_3_), channel_id=1, source_target_pairs={{0,1},{1,0},{2,3},{3,2},{4,5},{5,4},{6,7},{7,6},{8,9},{9,8},{10,11... | collective-permute-start | bytes 7864328 | tf_op jit(solution)/shard_map/ppermute | solution.py:459
  168.5 5.5 %collective-permute-start.29 = (f32[1024,512]{1,0:T(8,128)}, f32[1024,512]{1,0:T(8,128)S(1)}, u32[]{:S(2)}, u32[]{:S(2)}) collective-permute-start(f32[1024,512]{1,0:T(8,128)} %shard_map.82.refs_2_), channel_id=1, source_target_pairs={{0,1},{1,0},{2,3},{3,2},{4,5},{5,4},{6,7},{7,6},{8,9},{9,8},{10,11... | collective-permute-start | bytes 6291464 | tf_op jit(solution)/shard_map/ppermute | solution.py:459
  171.0 1.5 copy-start.14
  173.1 49.9 %collective-permute-start.34 = (f32[256,2048]{1,0:T(8,128)}, f32[256,2048]{1,0:T(8,128)S(1)}, u32[]{:S(2)}, u32[]{:S(2)}) collective-permute-start(f32[256,2048]{1,0:T(8,128)} %shard_map.81), channel_id=1, source_target_pairs={{0,2},{1,3},{2,4},{3,5},{4,6},{5,7},{6,0},{7,1},{8,10},{9,11},{10,... | collective-permute-start | bytes 6291464 | tf_op jit(solution)/shard_map/ppermute | solution.py:467
  174.0 1.4 copy-start.17
  175.3 2.2 copy-start.8
  177.5 26.3 %copy-start.1 = (f32[1,512,2048]{2,1,0:T(8,128)S(1)}, f32[1,512,2048]{2,1,0:T(8,128)}, u32[]{:S(2)}) copy-start(f32[1,512,2048]{2,1,0:T(8,128)} %param.6) | copy-start | bytes 12582916
  203.9 3.0 %copy-start.3 = (bf16[4,512,512]{2,1,0:T(8,128)(2,1)}, bf16[4,512,512]{2,1,0:T(8,128)(2,1)S(1)}, u32[]{:S(2)}) copy-start(bf16[4,512,512]{2,1,0:T(8,128)(2,1)S(1)} %get-tuple-element.26.low) | copy-start | bytes 6291460
  203.9 3.0 %copy-start.9 = (f32[8,128]{1,0:T(8,128)}, f32[8,128]{1,0:T(8,128)S(1)}, u32[]{:S(2)}) copy-start(f32[8,128]{1,0:T(8,128)S(1)} %get-tuple-element.24.refs_0_.earlier.refs_1_) | copy-start | bytes 12292
  204.5 2.4 collective-permute-start.30
  214.1 0.8 copy-start.12
  214.9 0.7 copy-start.13
  215.6 9.5 %copy-start.10 = (f32[128,704]{1,0:T(8,128)}, f32[128,704]{1,0:T(8,128)S(1)}, u32[]{:S(2)}) copy-start(f32[128,704]{1,0:T(8,128)S(1)} %get-tuple-element.30) | copy-start | bytes 1081348
  223.0 2.1 copy-start.6
  225.1 4.8 %collective-permute-start.35 = (f32[256,2048]{1,0:T(8,128)}, f32[256,2048]{1,0:T(8,128)}, u32[]{:S(2)}, u32[]{:S(2)}) collective-permute-start(f32[256,2048]{1,0:T(8,128)} %shard_map.86), channel_id=1, source_target_pairs={{0,1},{1,0},{2,3},{3,2},{4,5},{5,4},{6,7},{7,6},{8,9},{9,8},{10,11... | collective-permute-start | bytes 6291464 | tf_op jit(solution)/shard_map/ppermute | solution.py:459
  225.2 4.2 %copy-start.11 = (f32[128,704]{1,0:T(8,128)S(1)}, f32[128,704]{1,0:T(8,128)}, u32[]{:S(2)}) copy-start(f32[128,704]{1,0:T(8,128)} %copy-done.10) | copy-start | bytes 1081348
  226.4 33.2 %collective-permute-start.39 = (f32[160,2048]{1,0:T(8,128)}, f32[160,2048]{1,0:T(8,128)S(1)}, u32[]{:S(2)}, u32[]{:S(2)}) collective-permute-start(f32[160,2048]{1,0:T(8,128)} %shard_map.88), channel_id=1, source_target_pairs={{0,2},{1,3},{2,4},{3,5},{4,6},{5,7},{6,0},{7,1},{8,10},{9,11},{10,... | collective-permute-start | bytes 3932168 | tf_op jit(solution)/shard_map/ppermute | solution.py:467
  226.4 14.6 %collective-permute-start.31 = (f32[128,704]{1,0:T(8,128)}, f32[128,704]{1,0:T(8,128)S(1)}, u32[]{:S(2)}, u32[]{:S(2)}) collective-permute-start(f32[128,704]{1,0:T(8,128)} %copy-done.13), channel_id=1, source_target_pairs={{0,8},{8,0},{16,24},{24,16},{1,9},{9,1},{17,25},{25,17},{2,10},{10... | collective-permute-start | bytes 1081352 | tf_op jit(solution)/shard_map/ppermute | solution.py:508
  227.6 20.1 %collective-permute-start.32 = (f32[128,704]{1,0:T(8,128)}, f32[128,704]{1,0:T(8,128)S(1)}, u32[]{:S(2)}, u32[]{:S(2)}) collective-permute-start(f32[128,704]{1,0:T(8,128)} %copy-done.12), channel_id=1, source_target_pairs={{0,16},{8,24},{16,0},{24,8},{1,17},{9,25},{17,1},{25,9},{2,18},{10... | collective-permute-start | bytes 1081352 | tf_op jit(solution)/shard_map/ppermute | solution.py:508
  229.4 19.8 %collective-permute-start.33 = (f32[128,704]{1,0:T(8,128)S(1)}, f32[128,704]{1,0:T(8,128)S(1)}, u32[]{:S(2)}, u32[]{:S(2)}) collective-permute-start(f32[128,704]{1,0:T(8,128)S(1)} %copy-done.11), channel_id=1, source_target_pairs={{0,24},{8,16},{16,8},{24,0},{1,25},{9,17},{17,9},{25,1},{2,26},{10... | collective-permute-start | bytes 1081352 | tf_op jit(solution)/shard_map/ppermute | solution.py:508
  229.9 1.6 copy-start.4
  231.5 1.6 copy-start.7
  233.1 26.5 %copy-start.2 = (f32[1,512,2048]{2,1,0:T(8,128)S(1)}, f32[1,512,2048]{2,1,0:T(8,128)}, u32[]{:S(2)}) copy-start(f32[1,512,2048]{2,1,0:T(8,128)} %param.6) | copy-start | bytes 12582916
  239.8 12.8 %collective-permute-start.36 = (f32[128,512]{1,0:T(8,128)S(1)}, f32[128,512]{1,0:T(8,128)S(1)}, u32[]{:S(2)}, u32[]{:S(2)}) collective-permute-start(f32[128,512]{1,0:T(8,128)S(1)} %get-tuple-element.32), channel_id=1, source_target_pairs={{0,8},{8,0},{16,24},{24,16},{1,9},{9,1},{17,25},{25,17},{2,10},{10... | collective-permute-start | bytes 786440 | tf_op jit(solution)/shard_map/ppermute | solution.py:508
  241.0 17.8 %collective-permute-start.37 = (f32[128,512]{1,0:T(8,128)S(1)}, f32[128,512]{1,0:T(8,128)S(1)}, u32[]{:S(2)}, u32[]{:S(2)}) collective-permute-start(f32[128,512]{1,0:T(8,128)S(1)} %get-tuple-element.33), channel_id=1, source_target_pairs={{0,16},{8,24},{16,0},{24,8},{1,17},{9,25},{17,1},{25,9},{2,18},{10... | collective-permute-start | bytes 786440 | tf_op jit(solution)/shard_map/ppermute | solution.py:508
  247.6 11.1 %collective-permute-start.38 = (f32[128,512]{1,0:T(8,128)S(1)}, f32[128,512]{1,0:T(8,128)S(1)}, u32[]{:S(2)}, u32[]{:S(2)}) collective-permute-start(f32[128,512]{1,0:T(8,128)S(1)} %get-tuple-element.34), channel_id=1, source_target_pairs={{0,24},{8,16},{16,8},{24,0},{1,25},{9,17},{17,9},{25,1},{2,26},{10... | collective-permute-start | bytes 786440 | tf_op jit(solution)/shard_map/ppermute | solution.py:508
  249.3 11.0 %copy-start.18 = (f32[128,704]{1,0:T(8,128)}, f32[128,704]{1,0:T(8,128)S(1)}, u32[]{:S(2)}) copy-start(f32[128,704]{1,0:T(8,128)S(1)} %add_add_fusion) | copy-start | bytes 1081348
  260.2 3.1 %collective-permute-start.40 = (f32[160,2048]{1,0:T(8,128)S(1)}, f32[160,2048]{1,0:T(8,128)S(1)}, u32[]{:S(2)}, u32[]{:S(2)}) collective-permute-start(f32[160,2048]{1,0:T(8,128)S(1)} %shard_map.89), channel_id=1, source_target_pairs={{0,1},{1,0},{2,3},{3,2},{4,5},{5,4},{6,7},{7,6},{8,9},{9,8},{10,11... | collective-permute-start | bytes 3932168 | tf_op jit(solution)/shard_map/ppermute | solution.py:459
  268.3 12.4 %slice-start = ((f32[128,704]{1,0:T(8,128)}), f32[128,608]{1,0:T(8,128)S(1)}, s32[]{:S(2)}) async-start(f32[128,704]{1,0:T(8,128)} %copy-done.18), calls=%async_computation | async-start | bytes 655360 | tf_op jit(solution)/shard_map/slice | solution.py:525
  268.4 7.8 %collective-permute-start.41 = (f32[128,320]{1,0:T(8,128)S(1)}, f32[128,320]{1,0:T(8,128)S(1)}, u32[]{:S(2)}, u32[]{:S(2)}) collective-permute-start(f32[128,320]{1,0:T(8,128)S(1)} %get-tuple-element.36), channel_id=1, source_target_pairs={{0,8},{8,0},{16,24},{24,16},{1,9},{9,1},{17,25},{25,17},{2,10},{10... | collective-permute-start | bytes 491528 | tf_op jit(solution)/shard_map/ppermute | solution.py:508
  269.6 11.0 %collective-permute-start.42 = (f32[128,320]{1,0:T(8,128)S(1)}, f32[128,320]{1,0:T(8,128)S(1)}, u32[]{:S(2)}, u32[]{:S(2)}) collective-permute-start(f32[128,320]{1,0:T(8,128)S(1)} %get-tuple-element.37), channel_id=1, source_target_pairs={{0,16},{8,24},{16,0},{24,8},{1,17},{9,25},{17,1},{25,9},{2,18},{10... | collective-permute-start | bytes 491528 | tf_op jit(solution)/shard_map/ppermute | solution.py:508
  271.4 9.1 %collective-permute-start.43 = (f32[128,320]{1,0:T(8,128)S(1)}, f32[128,320]{1,0:T(8,128)S(1)}, u32[]{:S(2)}, u32[]{:S(2)}) collective-permute-start(f32[128,320]{1,0:T(8,128)S(1)} %get-tuple-element.38), channel_id=1, source_target_pairs={{0,24},{8,16},{16,8},{24,0},{1,25},{9,17},{17,9},{25,1},{2,26},{10... | collective-permute-start | bytes 491528 | tf_op jit(solution)/shard_map/ppermute | solution.py:508

commit v9 on v8

--- a/solution.py
+++ b/solution.py
@@ -11,7 +11,7 @@
 CHUNKS = 17
 SKEW = 2
 GROUPS = ((0, 4), (4, 8), (8, 12), (12, 17))
-TRAIN_CUTS = (96, 256, 160)
+TRAIN_CUTS = (112, 256, 144)
 MIB = 1024 * 1024
 HBM = pl.BlockSpec(memory_space=pltpu.HBM)
 SMEM = pl.BlockSpec(memory_space=pltpu.SMEM)

time: 283 us -> 285 us (level)
  waiting for transfers between devices: 61.8 us -> 65 us
    unnamed x38 -> x40, local copies, waits for them, and re-layouts: 14.6 us -> 12.3 us
where the time goes in v9:
time: 285 us; the launch traced here: 284 us
  starting transfers between devices  102 us (36%)
  Pallas kernels  94 us (33%)
  waiting for transfers between devices  65 us (23%)
  local copies, waits for them, and re-layouts  19.4 us (7%)
    ppermute x21, starting transfers between devices, body(): got[number] = lax.ppermute(block, 'dp', pairs)  66.9 us
    pallas_call x21, Pallas kernels, step_block(): pl.pallas_call(functools.partial(step_kernel, stream, number), out_shape=...  27.5 us
    pallas_call x1, Pallas kernels, swept(): pl.pallas_call(functools.partial(sweep_kernel, stream, n_sec), out_shape=...  26.3 us
    ppermute x9, waiting for transfers between devices, summed(): total = total + lax.ppermute(parts[k], 'section', pairs)  22.7 us
    pallas_call x3, Pallas kernels, scored(): pl.pallas_call(functools.partial(score_kernel, n_sec, scale, blocks), out...  18.9 us
    ppermute x9, starting transfers between devices, swapped(): return lax.ppermute(value, 'dp', swap_pairs)  17.9 us
    ppermute x21, waiting for transfers between devices, body(): got[number] = lax.ppermute(block, 'dp', pairs)  16.5 us
    ppermute x9, starting transfers between devices, summed(): total = total + lax.ppermute(parts[k], 'section', pairs)  12.6 us
  transfers between devices with their start and end apart: 44, of which 22 were waited for; matrix products, arithmetic and copies ran while one was open for 2% of the time, Pallas kernels for 28%

profile of v9, /device:TPU:0, one launch (start us, length us, event | category | flops | bytes accessed | tf_op | source)
XLA Modules:
  0.0 284.2 jit_solution(12896115880954687309)
XLA Ops:
  1.8 2.6 collective-permute-start.4
  5.8 2.2 copy-done.5
  8.0 5.4 %shard_map.55.packed = f32[320,512]{1,0:T(8,128)S(1)} custom-call(s32[13]{0:T(128)S(1)} %concatenate.11.info, f32[2048,512]{1,0:T(8,128)S(1)} %bitcast.22), custom_call_target="tpu_custom_call" | custom-call | bytes 1000 | tf_op jit(solution)/shard_map/pallas_call | solution.py:136
  14.0 1.6 collective-permute-start.1
  16.3 10.8 %collective-permute-done = s32[1]{0:T(128)} collective-permute-done((s32[1]{0:T(128)}, s32[1]{0:T(128)}, u32[]{:S(2)}, u32[]{:S(2)}) %collective-permute-start) | collective-permute-done | bytes 36 | tf_op jit(solution)/shard_map/ppermute | solution.py:474
  27.6 1.3 pad_add_fusion.counts
  28.9 3.0 %shard_map.56.own = f32[5888,512]{1,0:T(8,128)S(1)} custom-call(s32[13]{0:T(128)S(1)} %concatenate.11.info, f32[2048,512]{1,0:T(8,128)S(1)} %bitcast.23, f32[2048,512]{1,0:T(8,128)} %collective-permute-done.2.peer, f32[320,512]{1,0:T(8,128)S(1)} %shard_map.55.packed, f32[320,512]{1,0:T(8,128)S(1)} %collective-permute-done.3.peer_packed), custom_call_target="tpu_custom_call" | custom-call | bytes 1000 | tf_op jit(solution)/shard_map/pallas_call | solution.py:200
  33.2 1.6 collective-permute-start.5
  36.1 1.3 collective-permute-start.7
  37.4 4.0 %collective-permute-done.5.refs_0_ = f32[256,512]{1,0:T(8,128)S(1)} collective-permute-done((f32[256,512]{1,0:T(8,128)S(1)}, f32[256,512]{1,0:T(8,128)S(1)}, u32[]{:S(2)}, u32[]{:S(2)}) %collective-permute-start.5) | collective-permute-done | bytes 524320 | tf_op jit(solution)/shard_map/ppermute | solution.py:486
  42.8 4.4 %collective-permute-start.6 = (f32[256,512]{1,0:T(8,128)S(1)}, f32[256,512]{1,0:T(8,128)S(1)}, u32[]{:S(2)}, u32[]{:S(2)}) collective-permute-start(f32[256,512]{1,0:T(8,128)S(1)} %shard_map.59.refs_1_), channel_id=1, source_target_pairs={{0,2},{7,5},{2,4},{5,3},{8,10},{15,13},{10,12},{13,11},{16,18},{23... | collective-permute-start | bytes 1572872 | tf_op jit(solution)/shard_map/ppermute | solution.py:486
  47.2 1.3 shard_map.60.refs_1_
  48.6 4.3 %collective-permute-start.9 = (f32[256,512]{1,0:T(8,128)S(1)}, f32[256,512]{1,0:T(8,128)S(1)}, u32[]{:S(2)}, u32[]{:S(2)}) collective-permute-start(f32[256,512]{1,0:T(8,128)S(1)} %shard_map.60.refs_1_), channel_id=1, source_target_pairs={{0,2},{7,5},{2,4},{5,3},{8,10},{15,13},{10,12},{13,11},{16,18},{23... | collective-permute-start | bytes 1572872 | tf_op jit(solution)/shard_map/ppermute | solution.py:486
  55.2 4.4 %collective-permute-start.8 = (f32[256,512]{1,0:T(8,128)S(1)}, f32[256,512]{1,0:T(8,128)S(1)}, u32[]{:S(2)}, u32[]{:S(2)}) collective-permute-start(f32[256,512]{1,0:T(8,128)S(1)} %shard_map.61.refs_1_), channel_id=1, source_target_pairs={{0,2},{7,5},{2,4},{5,3},{4,6},{3,1},{8,10},{15,13},{10,12},{13,11}... | collective-permute-start | bytes 1572872 | tf_op jit(solution)/shard_map/ppermute | solution.py:486
  59.6 1.3 shard_map.62.refs_1_
  61.0 4.3 %collective-permute-start.11 = (f32[256,512]{1,0:T(8,128)S(1)}, f32[256,512]{1,0:T(8,128)S(1)}, u32[]{:S(2)}, u32[]{:S(2)}) collective-permute-start(f32[256,512]{1,0:T(8,128)S(1)} %shard_map.62.refs_1_), channel_id=1, source_target_pairs={{0,2},{7,5},{2,4},{5,3},{4,6},{3,1},{8,10},{15,13},{10,12},{13,11}... | collective-permute-start | bytes 1572872 | tf_op jit(solution)/shard_map/ppermute | solution.py:486
  67.6 4.4 %collective-permute-start.10 = (f32[256,512]{1,0:T(8,128)S(1)}, f32[256,512]{1,0:T(8,128)S(1)}, u32[]{:S(2)}, u32[]{:S(2)}) collective-permute-start(f32[256,512]{1,0:T(8,128)S(1)} %shard_map.63.refs_1_), channel_id=1, source_target_pairs={{0,2},{7,5},{2,4},{5,3},{4,6},{3,1},{8,10},{15,13},{10,12},{13,11}... | collective-permute-start | bytes 1572872 | tf_op jit(solution)/shard_map/ppermute | solution.py:486
  72.0 1.3 shard_map.64.refs_1_
  73.3 4.3 %collective-permute-start.13 = (f32[256,512]{1,0:T(8,128)S(1)}, f32[256,512]{1,0:T(8,128)S(1)}, u32[]{:S(2)}, u32[]{:S(2)}) collective-permute-start(f32[256,512]{1,0:T(8,128)S(1)} %shard_map.64.refs_1_), channel_id=1, source_target_pairs={{0,2},{7,5},{2,4},{5,3},{4,6},{3,1},{8,10},{15,13},{10,12},{13,11}... | collective-permute-start | bytes 1572872 | tf_op jit(solution)/shard_map/ppermute | solution.py:486
  80.0 4.4 %collective-permute-start.12 = (f32[256,512]{1,0:T(8,128)S(1)}, f32[256,512]{1,0:T(8,128)S(1)}, u32[]{:S(2)}, u32[]{:S(2)}) collective-permute-start(f32[256,512]{1,0:T(8,128)S(1)} %shard_map.65.refs_1_), channel_id=1, source_target_pairs={{0,2},{7,5},{2,4},{5,3},{4,6},{3,1},{8,10},{15,13},{10,12},{13,11}... | collective-permute-start | bytes 1572872 | tf_op jit(solution)/shard_map/ppermute | solution.py:486
  84.4 1.3 shard_map.66.refs_1_
  85.7 4.3 %collective-permute-start.15 = (f32[256,512]{1,0:T(8,128)S(1)}, f32[256,512]{1,0:T(8,128)S(1)}, u32[]{:S(2)}, u32[]{:S(2)}) collective-permute-start(f32[256,512]{1,0:T(8,128)S(1)} %shard_map.66.refs_1_), channel_id=1, source_target_pairs={{0,2},{7,5},{2,4},{5,3},{4,6},{3,1},{8,10},{15,13},{10,12},{13,11}... | collective-permute-start | bytes 1572872 | tf_op jit(solution)/shard_map/ppermute | solution.py:486
  92.4 4.4 %collective-permute-start.14 = (f32[256,512]{1,0:T(8,128)S(1)}, f32[256,512]{1,0:T(8,128)S(1)}, u32[]{:S(2)}, u32[]{:S(2)}) collective-permute-start(f32[256,512]{1,0:T(8,128)S(1)} %shard_map.67.refs_1_), channel_id=1, source_target_pairs={{0,2},{7,5},{2,4},{5,3},{4,6},{3,1},{8,10},{15,13},{10,12},{13,11}... | collective-permute-start | bytes 1572872 | tf_op jit(solution)/shard_map/ppermute | solution.py:486
  96.8 1.3 shard_map.68.refs_1_
  98.1 4.3 %collective-permute-start.17 = (f32[256,512]{1,0:T(8,128)S(1)}, f32[256,512]{1,0:T(8,128)S(1)}, u32[]{:S(2)}, u32[]{:S(2)}) collective-permute-start(f32[256,512]{1,0:T(8,128)S(1)} %shard_map.68.refs_1_), channel_id=1, source_target_pairs={{0,2},{7,5},{2,4},{5,3},{4,6},{3,1},{8,10},{15,13},{10,12},{13,11}... | collective-permute-start | bytes 1572872 | tf_op jit(solution)/shard_map/ppermute | solution.py:486
  104.8 4.4 %collective-permute-start.16 = (f32[256,512]{1,0:T(8,128)S(1)}, f32[256,512]{1,0:T(8,128)S(1)}, u32[]{:S(2)}, u32[]{:S(2)}) collective-permute-start(f32[256,512]{1,0:T(8,128)S(1)} %shard_map.69.refs_1_), channel_id=1, source_target_pairs={{0,2},{7,5},{2,4},{5,3},{4,6},{3,1},{8,10},{15,13},{10,12},{13,11}... | collective-permute-start | bytes 1572872 | tf_op jit(solution)/shard_map/ppermute | solution.py:486
  109.2 1.3 shard_map.70.refs_1_
  110.5 4.3 %collective-permute-start.18 = (f32[256,512]{1,0:T(8,128)S(1)}, f32[256,512]{1,0:T(8,128)S(1)}, u32[]{:S(2)}, u32[]{:S(2)}) collective-permute-start(f32[256,512]{1,0:T(8,128)S(1)} %shard_map.70.refs_1_), channel_id=1, source_target_pairs={{0,2},{7,5},{2,4},{5,3},{4,6},{3,1},{8,10},{15,13},{10,12},{13,11}... | collective-permute-start | bytes 1572872 | tf_op jit(solution)/shard_map/ppermute | solution.py:486
  117.2 4.4 %collective-permute-start.19 = (f32[256,512]{1,0:T(8,128)S(1)}, f32[256,512]{1,0:T(8,128)S(1)}, u32[]{:S(2)}, u32[]{:S(2)}) collective-permute-start(f32[256,512]{1,0:T(8,128)S(1)} %shard_map.71.refs_1_), channel_id=1, source_target_pairs={{0,2},{7,5},{2,4},{5,3},{4,6},{3,1},{8,10},{15,13},{10,12},{13,11}... | collective-permute-start | bytes 1572872 | tf_op jit(solution)/shard_map/ppermute | solution.py:486
  121.6 2.3 shard_map.78.refs_0_
  124.0 2.3 shard_map.79.refs_1_
  128.1 1.9 collective-permute-start.20
  131.4 2.6 collective-permute-start.21
  134.0 2.7 collective-permute-done.20.refs_0_.refs_3_.refs_7_
  138.7 3.6 %collective-permute-done.21.refs_0_.refs_4_ = f32[256,512]{1,0:T(8,128)S(1)} collective-permute-done((f32[256,512]{1,0:T(8,128)S(1)}, f32[256,512]{1,0:T(8,128)S(1)}, u32[]{:S(2)}, u32[]{:S(2)}) %collective-permute-start.21) | collective-permute-done | bytes 524320 | tf_op jit(solution)/shard_map/ppermute | solution.py:486
  150.3 2.5 shard_map.80.refs_3_
  152.8 15.9 %collective-permute-start.28 = (f32[1280,512]{1,0:T(8,128)}, f32[1280,512]{1,0:T(8,128)S(1)}, u32[]{:S(2)}, u32[]{:S(2)}) collective-permute-start(f32[1280,512]{1,0:T(8,128)} %shard_map.80.refs_3_), channel_id=1, source_target_pairs={{0,1},{1,0},{2,3},{3,2},{4,5},{5,4},{6,7},{7,6},{8,9},{9,8},{10,11... | collective-permute-start | bytes 7864328 | tf_op jit(solution)/shard_map/ppermute | solution.py:459
  168.7 2.2 shard_map.82.refs_2_
  171.0 1.4 slice_bitcast_fusion.refs_0_
  173.5 1.5 copy-done.15
  176.5 1.3 copy-done.18
  177.8 2.2 copy-done.8
  180.0 26.3 %shard_map.83 = (bf16[4,512,512]{2,1,0:T(8,128)(2,1)S(1)}, bf16[4,512,512]{2,1,0:T(8,128)(2,1)S(1)}, f32[8,128]{1,0:T(8,128)S(1)}) custom-call(s32[13]{0:T(128)S(1)} %concatenate.11.info, f32[8,128]{1,0:T(8,128)S(1)} %slice.93.earlier, f32[512,2048]{1,0:T(8,128)S(1)} %bitcast.24, f32[1024,512]{1,0:T(8,128)} %shard_map.78.refs_0_, ...), custom_call_target="tpu_custom_call" | custom-call | bytes 1000 | tf_op jit(solution)/shard_map/pallas_call | solution.py:372
  207.6 2.1 collective-permute-done.30.refs_1_
  209.7 7.3 %shard_map.85 = (f32[128,736]{1,0:T(8,128)S(1)}, f32[128,736]{1,0:T(8,128)S(1)}, f32[128,736]{1,0:T(8,128)S(1)}, f32[128,736]{1,0:T(8,128)S(1)}) custom-call(s32[3]{0:T(128)S(1)} %pad_add_fusion.counts, f32[8,128]{1,0:T(8,128)S(1)} %get-tuple-element.24.refs_0_.earlier.refs_1_, bf16[4,512,512]{2,1,0:T(8,128)(2,1)S(1)} %get-tuple-element.25.high, ...), custom_call_target="tpu_custom_call" | custom-call | bytes 1000 | tf_op jit(solution)/shard_map/pallas_call | solution.py:423
  217.0 8.4 %collective-permute-done.34.far.refs_1_ = f32[256,2048]{1,0:T(8,128)S(1)} collective-permute-done((f32[256,2048]{1,0:T(8,128)}, f32[256,2048]{1,0:T(8,128)S(1)}, u32[]{:S(2)}, u32[]{:S(2)}) %collective-permute-start.34) | collective-permute-done | bytes 2097184 | tf_op jit(solution)/shard_map/ppermute | solution.py:467
  225.5 2.1 shard_map.86
  228.8 1.7 collective-permute-start.31
  230.5 1.8 collective-permute-start.32
  232.4 1.6 copy-done.4
  234.0 1.6 copy-done.7
  235.6 6.7 %shard_map.87 = (f32[128,512]{1,0:T(8,128)S(1)}, f32[128,512]{1,0:T(8,128)S(1)}, f32[128,512]{1,0:T(8,128)S(1)}, f32[128,512]{1,0:T(8,128)S(1)}) custom-call(s32[3]{0:T(128)S(1)} %pad_add_fusion.counts, f32[8,128]{1,0:T(8,128)S(1)} %slice.78.refs_0_.earlier, bf16[4,512,512]{2,1,0:T(8,128)(2,1)S(1)} %get-tuple-element.25.high, ...), custom_call_target="tpu_custom_call" | custom-call | bytes 1000 | tf_op jit(solution)/shard_map/pallas_call | solution.py:423
  242.3 1.7 collective-permute-start.36
  243.9 1.9 collective-permute-start.37
  245.8 4.5 %collective-permute-done.32 = f32[128,736]{1,0:T(8,128)S(1)} collective-permute-done((f32[128,736]{1,0:T(8,128)S(1)}, f32[128,736]{1,0:T(8,128)S(1)}, u32[]{:S(2)}, u32[]{:S(2)}) %collective-permute-start.32) | collective-permute-done | bytes 376864 | tf_op jit(solution)/shard_map/ppermute | solution.py:508
  250.3 2.0 collective-permute-start.38
  252.3 2.7 collective-permute-done.36
  255.0 5.7 %collective-permute-done.37 = f32[128,512]{1,0:T(8,128)S(1)} collective-permute-done((f32[128,512]{1,0:T(8,128)S(1)}, f32[128,512]{1,0:T(8,128)S(1)}, u32[]{:S(2)}, u32[]{:S(2)}) %collective-permute-start.37) | collective-permute-done | bytes 262176 | tf_op jit(solution)/shard_map/ppermute | solution.py:508
  262.8 2.7 collective-permute-done.40.refs_0_
  265.6 4.9 %shard_map.90 = (f32[128,288]{1,0:T(8,128)S(1)}, f32[128,288]{1,0:T(8,128)S(1)}, f32[128,288]{1,0:T(8,128)S(1)}, f32[128,288]{1,0:T(8,128)S(1)}) custom-call(s32[3]{0:T(128)S(1)} %pad_add_fusion.counts, f32[8,128]{1,0:T(8,128)S(1)} %slice.80.refs_0_.earlier, bf16[4,512,512]{2,1,0:T(8,128)(2,1)S(1)} %get-tuple-element.25.high, ...), custom_call_target="tpu_custom_call" | custom-call | bytes 1000 | tf_op jit(solution)/shard_map/pallas_call | solution.py:423
  270.5 1.6 collective-permute-start.41
  272.6 1.4 collective-permute-start.43
  274.1 4.2 %collective-permute-done.41 = f32[128,288]{1,0:T(8,128)S(1)} collective-permute-done((f32[128,288]{1,0:T(8,128)S(1)}, f32[128,288]{1,0:T(8,128)S(1)}, u32[]{:S(2)}, u32[]{:S(2)}) %collective-permute-start.41) | collective-permute-done | bytes 147488 | tf_op jit(solution)/shard_map/ppermute | solution.py:508
  278.3 4.6 %collective-permute-done.42 = f32[128,288]{1,0:T(8,128)S(1)} collective-permute-done((f32[128,288]{1,0:T(8,128)S(1)}, f32[128,288]{1,0:T(8,128)S(1)}, u32[]{:S(2)}, u32[]{:S(2)}) %collective-permute-start.42) | collective-permute-done | bytes 147488 | tf_op jit(solution)/shard_map/ppermute | solution.py:508
  (124 shorter events, 44.3 us)
Async XLA Ops:
  1.2 27.7 %collective-permute-start.2 = (f32[2048,512]{1,0:T(8,128)}, f32[2048,512]{1,0:T(8,128)}, u32[]{:S(2)}, u32[]{:S(2)}) collective-permute-start(f32[2048,512]{1,0:T(8,128)} %bitcast.21), channel_id=1, source_target_pairs={{0,1},{1,0},{2,3},{3,2},{4,5},{5,4},{6,7},{7,6},{8,9},{9,8},{10,11... | collective-permute-start | bytes 12582920 | tf_op jit(solution)/shard_map/ppermute | solution.py:459
  1.8 27.1 %collective-permute-start.4 = (f32[112,2048]{1,0:T(8,128)S(1)}, f32[112,2048]{1,0:T(8,128)S(1)}, u32[]{:S(2)}, u32[]{:S(2)}) collective-permute-start(f32[112,2048]{1,0:T(8,128)S(1)} %slice_bitcast_fusion.2), channel_id=1, source_target_pairs={{0,2},{1,3},{2,4},{3,5},{4,6},{5,7},{6,0},{7,1},{8,10},{9,11},{10,... | collective-permute-start | bytes 2752520 | tf_op jit(solution)/shard_map/ppermute | solution.py:463
  5.8 2.2 copy-start.5
  13.4 15.5 %collective-permute-start.3 = (f32[320,512]{1,0:T(8,128)S(1)}, f32[320,512]{1,0:T(8,128)S(1)}, u32[]{:S(2)}, u32[]{:S(2)}) collective-permute-start(f32[320,512]{1,0:T(8,128)S(1)} %shard_map.55.packed), channel_id=1, source_target_pairs={{0,1},{1,0},{2,3},{3,2},{4,5},{5,4},{6,7},{7,6},{8,9},{9,8},{10,11... | collective-permute-start | bytes 1966088 | tf_op jit(solution)/shard_map/ppermute | solution.py:459
  13.6 13.4 %collective-permute-start = (s32[1]{0:T(128)}, s32[1]{0:T(128)}, u32[]{:S(2)}, u32[]{:S(2)}) collective-permute-start(s32[1]{0:T(128)} %param.9), channel_id=1, source_target_pairs={{0,1},{1,2},{2,3},{3,4},{4,5},{5,6},{6,7},{7,0},{8,9},{9,10},{10,1... | collective-permute-start | bytes 20 | tf_op jit(solution)/shard_map/ppermute | solution.py:474
  14.0 13.6 %collective-permute-start.1 = (s32[1]{0:T(128)}, s32[1]{0:T(128)}, u32[]{:S(2)}, u32[]{:S(2)}) collective-permute-start(s32[1]{0:T(128)} %param.9), channel_id=1, source_target_pairs={{0,2},{1,3},{2,4},{3,5},{4,6},{5,7},{6,0},{7,1},{8,10},{9,11},{10,... | collective-permute-start | bytes 20 | tf_op jit(solution)/shard_map/ppermute | solution.py:473
  33.2 8.3 %collective-permute-start.5 = (f32[256,512]{1,0:T(8,128)S(1)}, f32[256,512]{1,0:T(8,128)S(1)}, u32[]{:S(2)}, u32[]{:S(2)}) collective-permute-start(f32[256,512]{1,0:T(8,128)S(1)} %shard_map.57.refs_0_), channel_id=1, source_target_pairs={{0,2},{7,5},{8,10},{15,13},{16,18},{23,21},{24,26},{31,29}} | collective-permute-start | bytes 1572872 | tf_op jit(solution)/shard_map/ppermute | solution.py:486
  36.1 11.1 %collective-permute-start.7 = (f32[256,512]{1,0:T(8,128)S(1)}, f32[256,512]{1,0:T(8,128)S(1)}, u32[]{:S(2)}, u32[]{:S(2)}) collective-permute-start(f32[256,512]{1,0:T(8,128)S(1)} %shard_map.58.refs_1_), channel_id=1, source_target_pairs={{0,2},{7,5},{8,10},{15,13},{16,18},{23,21},{24,26},{31,29}} | collective-permute-start | bytes 1572872 | tf_op jit(solution)/shard_map/ppermute | solution.py:486
  42.8 11.1 %collective-permute-start.6 = (f32[256,512]{1,0:T(8,128)S(1)}, f32[256,512]{1,0:T(8,128)S(1)}, u32[]{:S(2)}, u32[]{:S(2)}) collective-permute-start(f32[256,512]{1,0:T(8,128)S(1)} %shard_map.59.refs_1_), channel_id=1, source_target_pairs={{0,2},{7,5},{2,4},{5,3},{8,10},{15,13},{10,12},{13,11},{16,18},{23... | collective-permute-start | bytes 1572872 | tf_op jit(solution)/shard_map/ppermute | solution.py:486
  48.6 11.1 %collective-permute-start.9 = (f32[256,512]{1,0:T(8,128)S(1)}, f32[256,512]{1,0:T(8,128)S(1)}, u32[]{:S(2)}, u32[]{:S(2)}) collective-permute-start(f32[256,512]{1,0:T(8,128)S(1)} %shard_map.60.refs_1_), channel_id=1, source_target_pairs={{0,2},{7,5},{2,4},{5,3},{8,10},{15,13},{10,12},{13,11},{16,18},{23... | collective-permute-start | bytes 1572872 | tf_op jit(solution)/shard_map/ppermute | solution.py:486
  55.2 11.1 %collective-permute-start.8 = (f32[256,512]{1,0:T(8,128)S(1)}, f32[256,512]{1,0:T(8,128)S(1)}, u32[]{:S(2)}, u32[]{:S(2)}) collective-permute-start(f32[256,512]{1,0:T(8,128)S(1)} %shard_map.61.refs_1_), channel_id=1, source_target_pairs={{0,2},{7,5},{2,4},{5,3},{4,6},{3,1},{8,10},{15,13},{10,12},{13,11}... | collective-permute-start | bytes 1572872 | tf_op jit(solution)/shard_map/ppermute | solution.py:486
  61.0 11.1 %collective-permute-start.11 = (f32[256,512]{1,0:T(8,128)S(1)}, f32[256,512]{1,0:T(8,128)S(1)}, u32[]{:S(2)}, u32[]{:S(2)}) collective-permute-start(f32[256,512]{1,0:T(8,128)S(1)} %shard_map.62.refs_1_), channel_id=1, source_target_pairs={{0,2},{7,5},{2,4},{5,3},{4,6},{3,1},{8,10},{15,13},{10,12},{13,11}... | collective-permute-start | bytes 1572872 | tf_op jit(solution)/shard_map/ppermute | solution.py:486
  67.6 11.1 %collective-permute-start.10 = (f32[256,512]{1,0:T(8,128)S(1)}, f32[256,512]{1,0:T(8,128)S(1)}, u32[]{:S(2)}, u32[]{:S(2)}) collective-permute-start(f32[256,512]{1,0:T(8,128)S(1)} %shard_map.63.refs_1_), channel_id=1, source_target_pairs={{0,2},{7,5},{2,4},{5,3},{4,6},{3,1},{8,10},{15,13},{10,12},{13,11}... | collective-permute-start | bytes 1572872 | tf_op jit(solution)/shard_map/ppermute | solution.py:486
  73.3 11.1 %collective-permute-start.13 = (f32[256,512]{1,0:T(8,128)S(1)}, f32[256,512]{1,0:T(8,128)S(1)}, u32[]{:S(2)}, u32[]{:S(2)}) collective-permute-start(f32[256,512]{1,0:T(8,128)S(1)} %shard_map.64.refs_1_), channel_id=1, source_target_pairs={{0,2},{7,5},{2,4},{5,3},{4,6},{3,1},{8,10},{15,13},{10,12},{13,11}... | collective-permute-start | bytes 1572872 | tf_op jit(solution)/shard_map/ppermute | solution.py:486
  80.0 11.1 %collective-permute-start.12 = (f32[256,512]{1,0:T(8,128)S(1)}, f32[256,512]{1,0:T(8,128)S(1)}, u32[]{:S(2)}, u32[]{:S(2)}) collective-permute-start(f32[256,512]{1,0:T(8,128)S(1)} %shard_map.65.refs_1_), channel_id=1, source_target_pairs={{0,2},{7,5},{2,4},{5,3},{4,6},{3,1},{8,10},{15,13},{10,12},{13,11}... | collective-permute-start | bytes 1572872 | tf_op jit(solution)/shard_map/ppermute | solution.py:486
  85.7 11.1 %collective-permute-start.15 = (f32[256,512]{1,0:T(8,128)S(1)}, f32[256,512]{1,0:T(8,128)S(1)}, u32[]{:S(2)}, u32[]{:S(2)}) collective-permute-start(f32[256,512]{1,0:T(8,128)S(1)} %shard_map.66.refs_1_), channel_id=1, source_target_pairs={{0,2},{7,5},{2,4},{5,3},{4,6},{3,1},{8,10},{15,13},{10,12},{13,11}... | collective-permute-start | bytes 1572872 | tf_op jit(solution)/shard_map/ppermute | solution.py:486
  92.4 11.1 %collective-permute-start.14 = (f32[256,512]{1,0:T(8,128)S(1)}, f32[256,512]{1,0:T(8,128)S(1)}, u32[]{:S(2)}, u32[]{:S(2)}) collective-permute-start(f32[256,512]{1,0:T(8,128)S(1)} %shard_map.67.refs_1_), channel_id=1, source_target_pairs={{0,2},{7,5},{2,4},{5,3},{4,6},{3,1},{8,10},{15,13},{10,12},{13,11}... | collective-permute-start | bytes 1572872 | tf_op jit(solution)/shard_map/ppermute | solution.py:486
  98.1 11.1 %collective-permute-start.17 = (f32[256,512]{1,0:T(8,128)S(1)}, f32[256,512]{1,0:T(8,128)S(1)}, u32[]{:S(2)}, u32[]{:S(2)}) collective-permute-start(f32[256,512]{1,0:T(8,128)S(1)} %shard_map.68.refs_1_), channel_id=1, source_target_pairs={{0,2},{7,5},{2,4},{5,3},{4,6},{3,1},{8,10},{15,13},{10,12},{13,11}... | collective-permute-start | bytes 1572872 | tf_op jit(solution)/shard_map/ppermute | solution.py:486
  104.8 11.1 %collective-permute-start.16 = (f32[256,512]{1,0:T(8,128)S(1)}, f32[256,512]{1,0:T(8,128)S(1)}, u32[]{:S(2)}, u32[]{:S(2)}) collective-permute-start(f32[256,512]{1,0:T(8,128)S(1)} %shard_map.69.refs_1_), channel_id=1, source_target_pairs={{0,2},{7,5},{2,4},{5,3},{4,6},{3,1},{8,10},{15,13},{10,12},{13,11}... | collective-permute-start | bytes 1572872 | tf_op jit(solution)/shard_map/ppermute | solution.py:486
  110.5 16.2 %collective-permute-start.18 = (f32[256,512]{1,0:T(8,128)S(1)}, f32[256,512]{1,0:T(8,128)S(1)}, u32[]{:S(2)}, u32[]{:S(2)}) collective-permute-start(f32[256,512]{1,0:T(8,128)S(1)} %shard_map.70.refs_1_), channel_id=1, source_target_pairs={{0,2},{7,5},{2,4},{5,3},{4,6},{3,1},{8,10},{15,13},{10,12},{13,11}... | collective-permute-start | bytes 1572872 | tf_op jit(solution)/shard_map/ppermute | solution.py:486
  117.2 12.9 %collective-permute-start.19 = (f32[256,512]{1,0:T(8,128)S(1)}, f32[256,512]{1,0:T(8,128)S(1)}, u32[]{:S(2)}, u32[]{:S(2)}) collective-permute-start(f32[256,512]{1,0:T(8,128)S(1)} %shard_map.71.refs_1_), channel_id=1, source_target_pairs={{0,2},{7,5},{2,4},{5,3},{4,6},{3,1},{8,10},{15,13},{10,12},{13,11}... | collective-permute-start | bytes 1572872 | tf_op jit(solution)/shard_map/ppermute | solution.py:486
  123.9 24.5 %collective-permute-start.26 = (f32[1024,512]{1,0:T(8,128)}, f32[1024,512]{1,0:T(8,128)S(1)}, u32[]{:S(2)}, u32[]{:S(2)}) collective-permute-start(f32[1024,512]{1,0:T(8,128)} %shard_map.78.refs_0_), channel_id=1, source_target_pairs={{0,1},{1,0},{2,3},{3,2},{4,5},{5,4},{6,7},{7,6},{8,9},{9,8},{10,11... | collective-permute-start | bytes 6291464 | tf_op jit(solution)/shard_map/ppermute | solution.py:459
  126.2 22.2 %collective-permute-start.27 = (f32[1024,512]{1,0:T(8,128)}, f32[1024,512]{1,0:T(8,128)S(1)}, u32[]{:S(2)}, u32[]{:S(2)}) collective-permute-start(f32[1024,512]{1,0:T(8,128)} %shard_map.79.refs_1_), channel_id=1, source_target_pairs={{0,1},{1,0},{2,3},{3,2},{4,5},{5,4},{6,7},{7,6},{8,9},{9,8},{10,11... | collective-permute-start | bytes 6291464 | tf_op jit(solution)/shard_map/ppermute | solution.py:459
  128.1 8.6 %collective-permute-start.20 = (f32[256,512]{1,0:T(8,128)S(1)}, f32[256,512]{1,0:T(8,128)S(1)}, u32[]{:S(2)}, u32[]{:S(2)}) collective-permute-start(f32[256,512]{1,0:T(8,128)S(1)} %shard_map.72.refs_1_), channel_id=1, source_target_pairs={{0,2},{7,5},{2,4},{5,3},{4,6},{3,1},{8,10},{15,13},{10,12},{13,11}... | collective-permute-start | bytes 1572872 | tf_op jit(solution)/shard_map/ppermute | solution.py:486
  131.4 10.9 %collective-permute-start.21 = (f32[256,512]{1,0:T(8,128)S(1)}, f32[256,512]{1,0:T(8,128)S(1)}, u32[]{:S(2)}, u32[]{:S(2)}) collective-permute-start(f32[256,512]{1,0:T(8,128)S(1)} %shard_map.73.refs_1_), channel_id=1, source_target_pairs={{0,2},{7,5},{2,4},{5,3},{4,6},{3,1},{8,10},{15,13},{10,12},{13,11}... | collective-permute-start | bytes 1572872 | tf_op jit(solution)/shard_map/ppermute | solution.py:486
  138.0 6.3 %collective-permute-start.22 = (f32[256,512]{1,0:T(8,128)S(1)}, f32[256,512]{1,0:T(8,128)S(1)}, u32[]{:S(2)}, u32[]{:S(2)}) collective-permute-start(f32[256,512]{1,0:T(8,128)S(1)} %shard_map.74.refs_1_), channel_id=1, source_target_pairs={{2,4},{5,3},{4,6},{3,1},{10,12},{13,11},{12,14},{11,9},{18,20},{21... | collective-permute-start | bytes 1572872 | tf_op jit(solution)/shard_map/ppermute | solution.py:486
  143.6 2.7 collective-permute-start.23
  145.6 2.8 collective-permute-start.24
  147.7 0.8 collective-permute-start.25
  148.4 1.9 copy-start.17
  152.8 18.2 %copy-start = (f32[1,512,2048]{2,1,0:T(8,128)S(1)}, f32[1,512,2048]{2,1,0:T(8,128)}, u32[]{:S(2)}) copy-start(f32[1,512,2048]{2,1,0:T(8,128)} %param.6) | copy-start | bytes 12582916
  152.8 20.6 %collective-permute-start.28 = (f32[1280,512]{1,0:T(8,128)}, f32[1280,512]{1,0:T(8,128)S(1)}, u32[]{:S(2)}, u32[]{:S(2)}) collective-permute-start(f32[1280,512]{1,0:T(8,128)} %shard_map.80.refs_3_), channel_id=1, source_target_pairs={{0,1},{1,0},{2,3},{3,2},{4,5},{5,4},{6,7},{7,6},{8,9},{9,8},{10,11... | collective-permute-start | bytes 7864328 | tf_op jit(solution)/shard_map/ppermute | solution.py:459
  170.9 5.5 %collective-permute-start.29 = (f32[1024,512]{1,0:T(8,128)}, f32[1024,512]{1,0:T(8,128)S(1)}, u32[]{:S(2)}, u32[]{:S(2)}) collective-permute-start(f32[1024,512]{1,0:T(8,128)} %shard_map.82.refs_2_), channel_id=1, source_target_pairs={{0,1},{1,0},{2,3},{3,2},{4,5},{5,4},{6,7},{7,6},{8,9},{9,8},{10,11... | collective-permute-start | bytes 6291464 | tf_op jit(solution)/shard_map/ppermute | solution.py:459
  173.4 1.5 copy-start.15
  175.5 49.9 %collective-permute-start.34 = (f32[256,2048]{1,0:T(8,128)}, f32[256,2048]{1,0:T(8,128)S(1)}, u32[]{:S(2)}, u32[]{:S(2)}) collective-permute-start(f32[256,2048]{1,0:T(8,128)} %shard_map.81), channel_id=1, source_target_pairs={{0,2},{1,3},{2,4},{3,5},{4,6},{5,7},{6,0},{7,1},{8,10},{9,11},{10,... | collective-permute-start | bytes 6291464 | tf_op jit(solution)/shard_map/ppermute | solution.py:467
  176.4 1.3 copy-start.18
  177.8 2.2 copy-start.8
  180.0 26.4 %copy-start.1 = (f32[1,512,2048]{2,1,0:T(8,128)S(1)}, f32[1,512,2048]{2,1,0:T(8,128)}, u32[]{:S(2)}) copy-start(f32[1,512,2048]{2,1,0:T(8,128)} %param.6) | copy-start | bytes 12582916
  206.3 3.4 %copy-start.3 = (bf16[4,512,512]{2,1,0:T(8,128)(2,1)}, bf16[4,512,512]{2,1,0:T(8,128)(2,1)S(1)}, u32[]{:S(2)}) copy-start(bf16[4,512,512]{2,1,0:T(8,128)(2,1)S(1)} %get-tuple-element.26.low) | copy-start | bytes 6291460
  206.3 3.4 %copy-start.9 = (f32[8,128]{1,0:T(8,128)}, f32[8,128]{1,0:T(8,128)S(1)}, u32[]{:S(2)}) copy-start(f32[8,128]{1,0:T(8,128)S(1)} %get-tuple-element.24.refs_0_.earlier.refs_1_) | copy-start | bytes 12292
  207.2 2.5 collective-permute-start.30
  217.0 10.5 %copy-start.10 = (f32[128,736]{1,0:T(8,128)}, f32[128,736]{1,0:T(8,128)S(1)}, u32[]{:S(2)}) copy-start(f32[128,736]{1,0:T(8,128)S(1)} %get-tuple-element.30) | copy-start | bytes 1130500
  217.0 10.5 %copy-start.12 = (f32[128,736]{1,0:T(8,128)}, f32[128,736]{1,0:T(8,128)S(1)}, u32[]{:S(2)}) copy-start(f32[128,736]{1,0:T(8,128)S(1)} %get-tuple-element.29) | copy-start | bytes 1130500
  217.0 10.6 %copy-start.14 = (f32[128,736]{1,0:T(8,128)}, f32[128,736]{1,0:T(8,128)S(1)}, u32[]{:S(2)}) copy-start(f32[128,736]{1,0:T(8,128)S(1)} %get-tuple-element.28) | copy-start | bytes 1130500
  225.4 2.1 copy-start.6
  227.6 4.8 %collective-permute-start.35 = (f32[256,2048]{1,0:T(8,128)}, f32[256,2048]{1,0:T(8,128)}, u32[]{:S(2)}, u32[]{:S(2)}) collective-permute-start(f32[256,2048]{1,0:T(8,128)} %shard_map.86), channel_id=1, source_target_pairs={{0,1},{1,0},{2,3},{3,2},{4,5},{5,4},{6,7},{7,6},{8,9},{9,8},{10,11... | collective-permute-start | bytes 6291464 | tf_op jit(solution)/shard_map/ppermute | solution.py:459
  227.7 2.8 copy-start.13
  227.7 4.7 %copy-start.11 = (f32[128,736]{1,0:T(8,128)S(1)}, f32[128,736]{1,0:T(8,128)}, u32[]{:S(2)}) copy-start(f32[128,736]{1,0:T(8,128)} %copy-done.10) | copy-start | bytes 1130500
  228.8 33.0 %collective-permute-start.39 = (f32[144,2048]{1,0:T(8,128)}, f32[144,2048]{1,0:T(8,128)S(1)}, u32[]{:S(2)}, u32[]{:S(2)}) collective-permute-start(f32[144,2048]{1,0:T(8,128)} %shard_map.88), channel_id=1, source_target_pairs={{0,2},{1,3},{2,4},{3,5},{4,6},{5,7},{6,0},{7,1},{8,10},{9,11},{10,... | collective-permute-start | bytes 3538952 | tf_op jit(solution)/shard_map/ppermute | solution.py:467
  228.8 15.2 %collective-permute-start.31 = (f32[128,736]{1,0:T(8,128)}, f32[128,736]{1,0:T(8,128)S(1)}, u32[]{:S(2)}, u32[]{:S(2)}) collective-permute-start(f32[128,736]{1,0:T(8,128)} %copy-done.14), channel_id=1, source_target_pairs={{0,8},{8,0},{16,24},{24,16},{1,9},{9,1},{17,25},{25,17},{2,10},{10... | collective-permute-start | bytes 1130504 | tf_op jit(solution)/shard_map/ppermute | solution.py:508
  230.5 19.8 %collective-permute-start.32 = (f32[128,736]{1,0:T(8,128)S(1)}, f32[128,736]{1,0:T(8,128)S(1)}, u32[]{:S(2)}, u32[]{:S(2)}) collective-permute-start(f32[128,736]{1,0:T(8,128)S(1)} %copy-done.13), channel_id=1, source_target_pairs={{0,16},{8,24},{16,0},{24,8},{1,17},{9,25},{17,1},{25,9},{2,18},{10... | collective-permute-start | bytes 1130504 | tf_op jit(solution)/shard_map/ppermute | solution.py:508
  232.4 19.9 %collective-permute-start.33 = (f32[128,736]{1,0:T(8,128)S(1)}, f32[128,736]{1,0:T(8,128)S(1)}, u32[]{:S(2)}, u32[]{:S(2)}) collective-permute-start(f32[128,736]{1,0:T(8,128)S(1)} %copy-done.11), channel_id=1, source_target_pairs={{0,24},{8,16},{16,8},{24,0},{1,25},{9,17},{17,9},{25,1},{2,26},{10... | collective-permute-start | bytes 1130504 | tf_op jit(solution)/shard_map/ppermute | solution.py:508
  232.4 1.6 copy-start.4
  234.0 1.6 copy-start.7
  235.6 26.2 %copy-start.2 = (f32[1,512,2048]{2,1,0:T(8,128)S(1)}, f32[1,512,2048]{2,1,0:T(8,128)}, u32[]{:S(2)}) copy-start(f32[1,512,2048]{2,1,0:T(8,128)} %param.6) | copy-start | bytes 12582916
  242.3 12.7 %collective-permute-start.36 = (f32[128,512]{1,0:T(8,128)S(1)}, f32[128,512]{1,0:T(8,128)S(1)}, u32[]{:S(2)}, u32[]{:S(2)}) collective-permute-start(f32[128,512]{1,0:T(8,128)S(1)} %get-tuple-element.32), channel_id=1, source_target_pairs={{0,8},{8,0},{16,24},{24,16},{1,9},{9,1},{17,25},{25,17},{2,10},{10... | collective-permute-start | bytes 786440 | tf_op jit(solution)/shard_map/ppermute | solution.py:508
  243.9 16.8 %collective-permute-start.37 = (f32[128,512]{1,0:T(8,128)S(1)}, f32[128,512]{1,0:T(8,128)S(1)}, u32[]{:S(2)}, u32[]{:S(2)}) collective-permute-start(f32[128,512]{1,0:T(8,128)S(1)} %get-tuple-element.33), channel_id=1, source_target_pairs={{0,16},{8,24},{16,0},{24,8},{1,17},{9,25},{17,1},{25,9},{2,18},{10... | collective-permute-start | bytes 786440 | tf_op jit(solution)/shard_map/ppermute | solution.py:508
  250.3 11.4 %collective-permute-start.38 = (f32[128,512]{1,0:T(8,128)S(1)}, f32[128,512]{1,0:T(8,128)S(1)}, u32[]{:S(2)}, u32[]{:S(2)}) collective-permute-start(f32[128,512]{1,0:T(8,128)S(1)} %get-tuple-element.34), channel_id=1, source_target_pairs={{0,24},{8,16},{16,8},{24,0},{1,25},{9,17},{17,9},{25,1},{2,26},{10... | collective-permute-start | bytes 786440 | tf_op jit(solution)/shard_map/ppermute | solution.py:508
  252.3 10.4 %copy-start.19 = (f32[128,736]{1,0:T(8,128)}, f32[128,736]{1,0:T(8,128)S(1)}, u32[]{:S(2)}) copy-start(f32[128,736]{1,0:T(8,128)S(1)} %add_add_fusion) | copy-start | bytes 1130500
  262.6 2.9 %collective-permute-start.40 = (f32[144,2048]{1,0:T(8,128)S(1)}, f32[144,2048]{1,0:T(8,128)S(1)}, u32[]{:S(2)}, u32[]{:S(2)}) collective-permute-start(f32[144,2048]{1,0:T(8,128)S(1)} %shard_map.89), channel_id=1, source_target_pairs={{0,1},{1,0},{2,3},{3,2},{4,5},{5,4},{6,7},{7,6},{8,9},{9,8},{10,11... | collective-permute-start | bytes 3538952 | tf_op jit(solution)/shard_map/ppermute | solution.py:459
  270.5 12.6 %slice-start = ((f32[128,736]{1,0:T(8,128)}), f32[128,624]{1,0:T(8,128)S(1)}, s32[]{:S(2)}) async-start(f32[128,736]{1,0:T(8,128)} %copy-done.19), calls=%async_computation | async-start | bytes 655360 | tf_op jit(solution)/shard_map/slice | solution.py:525
  270.5 7.8 %collective-permute-start.41 = (f32[128,288]{1,0:T(8,128)S(1)}, f32[128,288]{1,0:T(8,128)S(1)}, u32[]{:S(2)}, u32[]{:S(2)}) collective-permute-start(f32[128,288]{1,0:T(8,128)S(1)} %get-tuple-element.36), channel_id=1, source_target_pairs={{0,8},{8,0},{16,24},{24,16},{1,9},{9,1},{17,25},{25,17},{2,10},{10... | collective-permute-start | bytes 442376 | tf_op jit(solution)/shard_map/ppermute | solution.py:508
  272.1 10.9 %collective-permute-start.42 = (f32[128,288]{1,0:T(8,128)S(1)}, f32[128,288]{1,0:T(8,128)S(1)}, u32[]{:S(2)}, u32[]{:S(2)}) collective-permute-start(f32[128,288]{1,0:T(8,128)S(1)} %get-tuple-element.37), channel_id=1, source_target_pairs={{0,16},{8,24},{16,0},{24,8},{1,17},{9,25},{17,1},{25,9},{2,18},{10... | collective-permute-start | bytes 442376 | tf_op jit(solution)/shard_map/ppermute | solution.py:508
  272.6 10.3 %collective-permute-start.43 = (f32[128,288]{1,0:T(8,128)S(1)}, f32[128,288]{1,0:T(8,128)S(1)}, u32[]{:S(2)}, u32[]{:S(2)}) collective-permute-start(f32[128,288]{1,0:T(8,128)S(1)} %get-tuple-element.38), channel_id=1, source_target_pairs={{0,24},{8,16},{16,8},{24,0},{1,25},{9,17},{17,9},{25,1},{2,26},{10... | collective-permute-start | bytes 442376 | tf_op jit(solution)/shard_map/ppermute | solution.py:508
  (1 other events, 1.3 us)
